TPU v7x, 32 devices: a whole 2x2x4 slice. The times are simulated.
32 devices in a mesh: dp: 2 (over y), expert: 16 (over z, x, core).
Axes of the slice: x: 2, y: 2, z: 4, core: 2. Of those that a mesh axis runs over, the one named last changes fastest.
Arguments:
- tokens: bfloat16 [2048, 3584], P('expert', 'dp'), may hold values from -6 to 6
- cotangent: bfloat16 [2048, 3584], P('expert', 'dp'), may hold values from -12 to 12
- expert_ids: int32 [2048, 8], P('expert'), may hold values from 0 to 15, all different within a row; in each aligned block of 128 rows (0 to 127, 128 to 255, ...) at most 64 rows name the same one
- gate_levels: int32 [2048, 8], P('expert'), may hold values from 1 to 15
- capacity: int32 [16], replicated, may hold values from 16 to 64, as said below
- up_weight: bfloat16 [16, 3584, 1024], P('expert', 'dp'), may hold values from -0.09375 to 0.09375
- down_weight: bfloat16 [16, 3584, 1024], P('expert', 'dp'), may hold values from -0.1875 to 0.1875
Outputs:
- token_grad: bfloat16 [2048, 3584], P('expert', 'dp')
- up_grad: bfloat16 [16, 3584, 1024], P('expert', 'dp')
- down_grad: bfloat16 [16, 3584, 1024], P('expert', 'dp')
Inputs may be any that keep to these rules, and one draw needn't show every extreme that they name: `expert_ids`: in each aligned block of 128 tokens every expert is named by exactly 64 choices. `capacity`: some expert accepts 64 rows and some only 4.
All inputs are finite; a program needn't handle non-finite values.
Results may differ from a plain program's by a relative error of at most 0.023.
Values may be sent and summed in bfloat16 or wider, within the bound.
No kernel may reach another device: no remote copies, remote signals or barrier semaphores. Data moves between devices by JAX's collectives and lax.ppermute only.
A program may use at most 64 MiB of HBM per device.

v0:
```python
import jax
import jax.numpy as jnp
from jax import lax
from jax.sharding import PartitionSpec as P


def silu_slope(preact):
    sigmoid = jax.nn.sigmoid(preact)
    return sigmoid * (1.0 + preact * (1.0 - sigmoid))


def per_device(tokens, cotangent, expert_ids, gate_levels, capacity, up_weight, down_weight):
    tok_rows, width_dev = tokens.shape
    top_count = expert_ids.shape[1]
    expert_count = capacity.shape[0]
    slots = tok_rows * top_count // expert_count
    row_count = expert_count * slots
    flat_ids = expert_ids.reshape(-1)
    expert_column = jnp.arange(expert_count, dtype=jnp.int32)[:, None]
    onehot = (flat_ids[None, :] == expert_column).astype(jnp.int32)
    earlier = jnp.cumsum(onehot, axis=1) - onehot
    slot_rank = jnp.sum(earlier * onehot, axis=0)
    limits = jnp.sum(onehot * capacity[:, None], axis=0)
    slot_index = jnp.where(slot_rank < limits, flat_ids * slots + slot_rank, -1).reshape(
        tok_rows, top_count
    )
    levels = gate_levels.astype(jnp.float32)
    gate_weights = levels / jnp.sum(levels, axis=1, keepdims=True)
    targets = jnp.arange(row_count, dtype=jnp.int32)[:, None]
    placing = jnp.zeros((row_count, tok_rows), jnp.float32)
    weighted = jnp.zeros((row_count, tok_rows), jnp.float32)
    for choice_index in range(top_count):
        matched = slot_index[:, choice_index][None, :] == targets
        placing = placing + matched.astype(jnp.float32)
        weighted = weighted + jnp.where(matched, gate_weights[:, choice_index][None, :], 0.0)
    slot_gate = jnp.sum(weighted, axis=1)
    placing_half = placing.astype(jnp.bfloat16)
    send_rows = jnp.dot(placing_half, tokens, preferred_element_type=jnp.float32).astype(
        jnp.bfloat16
    )
    placed_cot = jnp.dot(placing_half, cotangent, preferred_element_type=jnp.float32)
    send_cot = (slot_gate[:, None] * placed_cot).astype(jnp.bfloat16)
    block_shape = (expert_count, slots, width_dev)
    arrived_rows, arrived_cot = (
        lax.all_to_all(
            send_rows.reshape(block_shape), "expert", split_axis=0, concat_axis=0, tiled=True
        ),
        lax.all_to_all(
            send_cot.reshape(block_shape), "expert", split_axis=0, concat_axis=0, tiled=True
        ),
    )
    expert_in = arrived_rows.reshape(row_count, width_dev)
    expert_cot = arrived_cot.reshape(row_count, width_dev)
    weight_up = up_weight[0]
    weight_down = down_weight[0]
    pre_part = jnp.dot(expert_in, weight_up, preferred_element_type=jnp.float32)
    cot_part = jnp.dot(expert_cot, weight_down, preferred_element_type=jnp.float32)
    contract_rows = (((0,), (0,)), ((), ()))
    contract_hidden = (((1,), (1,)), ((), ()))
    preact, hidden_cot = (
        lax.psum_scatter(
            pre_part.astype(jnp.bfloat16), "dp", scatter_dimension=1, tiled=True
        ).astype(jnp.float32),
        lax.psum_scatter(
            cot_part.astype(jnp.bfloat16), "dp", scatter_dimension=1, tiled=True
        ).astype(jnp.float32),
    )
    hidden = jax.nn.silu(preact).astype(jnp.bfloat16)
    act_cot = (hidden_cot * silu_slope(preact)).astype(jnp.bfloat16)
    hidden_piece = lax.all_gather(hidden, "dp", axis=1, tiled=True)
    cot_piece = lax.all_gather(act_cot, "dp", axis=1, tiled=True)
    up_term = lax.dot_general(
        expert_in, cot_piece, contract_rows, preferred_element_type=jnp.float32
    )
    down_term = lax.dot_general(
        expert_cot, hidden_piece, contract_rows, preferred_element_type=jnp.float32
    )
    back_term = lax.dot_general(
        cot_piece, weight_up, contract_hidden, preferred_element_type=jnp.float32
    )
    back_rows = back_term.astype(jnp.bfloat16).reshape(block_shape)
    returned = lax.all_to_all(back_rows, "expert", split_axis=0, concat_axis=0, tiled=True)
    token_grad = lax.dot_general(
        placing_half,
        returned.reshape(row_count, width_dev),
        contract_rows,
        preferred_element_type=jnp.float32,
    ).astype(jnp.bfloat16)
    up_grad = up_term.astype(jnp.bfloat16)[None]
    down_grad = down_term.astype(jnp.bfloat16)[None]
    return (token_grad, up_grad, down_grad)


def solution(mesh):
    return jax.shard_map(
        per_device,
        mesh=mesh,
        in_specs=(
            P("expert", "dp"),
            P("expert", "dp"),
            P("expert", None),
            P("expert", None),
            P(),
            P("expert", "dp", None),
            P("expert", "dp", None),
        ),
        out_specs=(P("expert", "dp"), P("expert", "dp", None), P("expert", "dp", None)),
        check_vma=False,
    )
```

profile of v0, /device:TPU:8, one launch (start us, length us, event | category | flops | bytes accessed | tf_op | source)
XLA Modules:
  0.0 375.8 jit_solution(5692956285758743864)
XLA Ops:
  7.2 0.8 copy.30
  8.0 0.1 eq.145
  8.1 0.1 eq.149
  8.2 0.7 convert_reduce_fusion
  8.9 0.7 convert_divide_fusion
  9.6 0.7 select_reduce_fusion
  10.5 4.5 %reduce-window.6 = s32[16,8,128]{2,1,0:T(8,128)S(1)} reduce-window(s32[16,8,128]{2,1,0:T(8,128)S(1)} %fusion.21, s32[]{:T(128)} %constant.5.clone.1), window={size=1x1x128 pad=0_0x0_0x127_0}, to_apply=%region_0.0 | reduce-window | flops 2080768 | bytes 131076 | tf_op jit(solution)/shard_map/reduce-window
  15.1 0.1 copy.31
  15.3 0.1 select_reduce_fusion.1
  15.4 0.1 reduce_sum.41
  15.6 0.7 add_select_fusion
  16.3 0.5 add_reduce_fusion
  16.8 3.2 multiply_convert_fusion
  20.1 6.4 %all-to-all-start = ((bf16[16,64,1792]{2,1,0:T(8,128)(2,1)}), bf16[16,64,1792]{2,1,0:T(8,128)(2,1)}, u32[]{:S(2)}, u32[]{:S(2)}) async-start(bf16[16,64,1792]{2,1,0:T(8,128)(2,1)} %bitcast.67), calls=%async_computation | async-start | bytes 7340032 | tf_op jit(solution)/shard_map/all_to_all | solution.py:48
  26.5 3.2 convolution_convert_fusion
  29.7 76.3 %all-to-all-done = bf16[16,64,1792]{2,1,0:T(8,128)(2,1)} async-done(((bf16[16,64,1792]{2,1,0:T(8,128)(2,1)}), bf16[16,64,1792]{2,1,0:T(8,128)(2,1)}, u32[]{:S(2)}, u32[]{:S(2)}) %all-to-all-start) | async-done | bytes 3670048 | tf_op jit(solution)/shard_map/all_to_all | solution.py:48
  106.1 6.6 %all-to-all-start.1 = ((bf16[16,64,1792]{2,1,0:T(8,128)(2,1)}), bf16[16,64,1792]{2,1,0:T(8,128)(2,1)}, u32[]{:S(2)}, u32[]{:S(2)}) async-start(bf16[16,64,1792]{2,1,0:T(8,128)(2,1)} %bitcast.65), calls=%async_computation.2 | async-start | bytes 7340032 | tf_op jit(solution)/shard_map/all_to_all | solution.py:45
  112.7 8.4 %fusion.15 = bf16[1024,1024]{1,0:T(8,128)(2,1)} fusion(bf16[1024,1792]{1,0:T(8,128)(2,1)} %bitcast.18, bf16[1,1792,1024]{2,1,0:T(8,128)(2,1)} %param.13), kind=kOutput, calls=%fused_computation.24 | convolution fusion | flops 3759144960 | bytes 9437184 | tf_op jit(solution)/shard_map/dot_general | solution.py:57
  121.2 71.0 %all-to-all-done.1 = bf16[16,64,1792]{2,1,0:T(8,128)(2,1)} async-done(((bf16[16,64,1792]{2,1,0:T(8,128)(2,1)}), bf16[16,64,1792]{2,1,0:T(8,128)(2,1)}, u32[]{:S(2)}, u32[]{:S(2)}) %all-to-all-start.1) | async-done | bytes 3670048 | tf_op jit(solution)/shard_map/all_to_all | solution.py:45
  192.2 8.4 %fusion.18 = bf16[1024,1024]{1,0:T(8,128)(2,1)} fusion(bf16[1024,1792]{1,0:T(8,128)(2,1)} %bitcast.21, bf16[1,1792,1024]{2,1,0:T(8,128)(2,1)} %param.12), kind=kOutput, calls=%fused_computation.25 | convolution fusion | flops 3759144960 | bytes 9437184 | tf_op jit(solution)/shard_map/dot_general | solution.py:56
  200.7 0.2 all-gather.3.cloned.1.call-start
  200.9 33.2 %reduce-scatter.5.cloned.1.call-done = bf16[1024,512]{1,0:T(8,128)(2,1)} async-done(((bf16[1024,1024]{1,0:T(8,128)(2,1)}), bf16[1024,512]{1,0:T(8,128)(2,1)}) %reduce-scatter.5.cloned.1.call-update) | async-done | bytes 1048592 | tf_op jit(solution)/shard_map/reduce_scatter | solution.py:61
  234.1 3.8 %fusion.14 = (bf16[1024,512]{1,0:T(8,128)(2,1)}, bf16[1024,512]{1,0:T(8,128)(2,1)}) fusion(bf16[1024,512]{1,0:T(8,128)(2,1)} %reduce-scatter.5.cloned.1.call-done, bf16[1024,512]{1,0:T(8,128)(2,1)} %reduce-scatter.3.cloned.1.call-done), kind=kLoop, calls=%fused_computation.23 | loop fusion | flops 6815744 | bytes 4194304 | tf_op jit(solution)/shard_map/convert_element_type | solution.py:68
  237.9 33.3 %all-gather.3.cloned.1.call-done = bf16[1024,1024]{1,0:T(8,128)(2,1)} async-done(((bf16[1024,512]{1,0:T(8,128)(2,1)}), bf16[1024,1024]{1,0:T(8,128)(2,1)}) %all-gather.3.cloned.1.call-update) | async-done | bytes 2097168 | tf_op jit(solution)/shard_map/all_gather | solution.py:71
  271.2 8.6 %convolution_convert_fusion.3 = bf16[1024,1792]{1,0:T(8,128)(2,1)} fusion(bf16[1024,1024]{1,0:T(8,128)(2,1)} %all-gather.3.cloned.1.call-done, bf16[1,1792,1024]{2,1,0:T(8,128)(2,1)} %param.12), kind=kOutput, calls=%fused_computation.4 | convolution fusion | flops 3759931392 | bytes 9437184 | tf_op jit(solution)/shard_map/dot_general | solution.py:78
  279.8 6.2 %all-to-all-start.2 = ((bf16[16,64,1792]{2,1,0:T(8,128)(2,1)}), bf16[16,64,1792]{2,1,0:T(8,128)(2,1)}, u32[]{:S(2)}, u32[]{:S(2)}) async-start(bf16[16,64,1792]{2,1,0:T(8,128)(2,1)} %bitcast.66), calls=%async_computation.4 | async-start | bytes 7340032 | tf_op jit(solution)/shard_map/all_to_all | solution.py:82
  286.0 0.5 all-gather.5.cloned.1.call-update
  286.6 7.5 %fusion.5 = bf16[1,1792,1024]{2,1,0:T(8,128)(2,1)} fusion(bf16[1024,1792]{1,0:T(8,128)(2,1)} %bitcast.21, bf16[1024,1024]{1,0:T(8,128)(2,1)S(1)} %copy-done.2), kind=kOutput, calls=%fused_computation.10 | convolution fusion | flops 3759931392 | bytes 9437184 | tf_op jit(solution)/shard_map/dot_general | solution.py:72
  294.1 27.6 %all-gather.5.cloned.1.call-done = bf16[1024,1024]{1,0:T(8,128)(2,1)} async-done(((bf16[1024,512]{1,0:T(8,128)(2,1)}), bf16[1024,1024]{1,0:T(8,128)(2,1)}) %all-gather.5.cloned.1.call-update) | async-done | bytes 2097168 | tf_op jit(solution)/shard_map/all_gather | solution.py:70
  321.7 8.6 %fusion.6 = bf16[1,1792,1024]{2,1,0:T(8,128)(2,1)} fusion(bf16[1024,1792]{1,0:T(8,128)(2,1)} %bitcast.18, bf16[1024,1024]{1,0:T(8,128)(2,1)} %all-gather.5.cloned.1.call-done), kind=kOutput, calls=%fused_computation.11 | convolution fusion | flops 3759931392 | bytes 9437184 | tf_op jit(solution)/shard_map/dot_general | solution.py:75
  330.3 35.3 %all-to-all-done.2 = bf16[16,64,1792]{2,1,0:T(8,128)(2,1)} async-done(((bf16[16,64,1792]{2,1,0:T(8,128)(2,1)}), bf16[16,64,1792]{2,1,0:T(8,128)(2,1)}, u32[]{:S(2)}, u32[]{:S(2)}) %all-to-all-start.2) | async-done | bytes 3670048 | tf_op jit(solution)/shard_map/all_to_all | solution.py:82
  365.6 3.7 convolution_convert_fusion.4
  (23 shorter events, 0.6 us)
Async XLA Ops:
  7.2 9.7 %copy-start = (bf16[128,1792]{1,0:T(8,128)(2,1)S(1)}, bf16[128,1792]{1,0:T(8,128)(2,1)}, u32[]{:S(2)}) copy-start(bf16[128,1792]{1,0:T(8,128)(2,1)} %param.8) | copy-start | bytes 1376260
  20.1 6.4 %copy-start.1 = (bf16[128,1792]{1,0:T(8,128)(2,1)S(1)}, bf16[128,1792]{1,0:T(8,128)(2,1)}, u32[]{:S(2)}) copy-start(bf16[128,1792]{1,0:T(8,128)(2,1)} %param.7) | copy-start | bytes 1376260
  20.1 86.0 %all-to-all-start = ((bf16[16,64,1792]{2,1,0:T(8,128)(2,1)}), bf16[16,64,1792]{2,1,0:T(8,128)(2,1)}, u32[]{:S(2)}, u32[]{:S(2)}) async-start(bf16[16,64,1792]{2,1,0:T(8,128)(2,1)} %bitcast.67), calls=%async_computation | async-start | bytes 7340032 | tf_op jit(solution)/shard_map/all_to_all | solution.py:48
  106.1 86.1 %all-to-all-start.1 = ((bf16[16,64,1792]{2,1,0:T(8,128)(2,1)}), bf16[16,64,1792]{2,1,0:T(8,128)(2,1)}, u32[]{:S(2)}, u32[]{:S(2)}) async-start(bf16[16,64,1792]{2,1,0:T(8,128)(2,1)} %bitcast.65), calls=%async_computation.2 | async-start | bytes 7340032 | tf_op jit(solution)/shard_map/all_to_all | solution.py:45
  112.6 88.3 %reduce-scatter.3.cloned.1.call-start = ((), (), s32[]{:S(2)}) async-start(), calls=%async_computation.5 | async-start | bytes 3145728 | tf_op jit(solution)/shard_map/reduce_scatter | solution.py:64
  121.1 113.0 %reduce-scatter.5.cloned.1.call-start = ((), (), s32[]{:S(2)}) async-start(), calls=%async_computation.6 | async-start | bytes 3145728 | tf_op jit(solution)/shard_map/reduce_scatter | solution.py:61
  200.7 70.6 %all-gather.3.cloned.1.call-start = ((), (), s32[]{:S(2)}) async-start(), calls=%async_computation.7 | async-start | bytes 3145728 | tf_op jit(solution)/shard_map/all_gather | solution.py:71
  279.8 6.8 %copy-start.2 = (bf16[1024,1024]{1,0:T(8,128)(2,1)S(1)}, bf16[1024,1024]{1,0:T(8,128)(2,1)}, u32[]{:S(2)}) copy-start(bf16[1024,1024]{1,0:T(8,128)(2,1)} %all-gather.3.cloned.1.call-done) | copy-start | bytes 6291460
  279.8 85.8 %all-to-all-start.2 = ((bf16[16,64,1792]{2,1,0:T(8,128)(2,1)}), bf16[16,64,1792]{2,1,0:T(8,128)(2,1)}, u32[]{:S(2)}, u32[]{:S(2)}) async-start(bf16[16,64,1792]{2,1,0:T(8,128)(2,1)} %bitcast.66), calls=%async_computation.4 | async-start | bytes 7340032 | tf_op jit(solution)/shard_map/all_to_all | solution.py:82
  286.0 35.8 %all-gather.5.cloned.1.call-start = ((), (), s32[]{:S(2)}) async-start(), calls=%async_computation.8 | async-start | bytes 3145728 | tf_op jit(solution)/shard_map/all_gather | solution.py:70
Sparse Core Ops, SparseCore 0:
  121.2 32.7 reduce-scatter.2
  200.8 33.2 reduce-scatter.4
  238.0 33.1 all-gather.2
  288.6 33.0 all-gather.4
where the time goes:
time: 378 us; the launch traced here: 376 us
  waiting for transfers between devices  277 us (73%)
  matrix products  51.7 us (14%)
  starting transfers between devices  19.5 us (5%)
  between operations  13.8 us (4%)
  other arithmetic  11.8 us (3%)
    all_to_all x1, waiting for transfers between devices, per_device(): lax.all_to_all(send_cot.reshape(block_shape), 'expert', split_axis=0, con...  76.3 us
    all_to_all x1, waiting for transfers between devices, per_device(): lax.all_to_all(send_rows.reshape(block_shape), 'expert', split_axis=0, co...  71 us
    all_to_all x1, waiting for transfers between devices, per_device(): lax.all_to_all(back_rows, 'expert', split_axis=0, concat_axis=0, tiled=True)  35.3 us
    all_gather x1, waiting for transfers between devices, per_device(): cot_piece = lax.all_gather(act_cot, 'dp', axis=1, tiled=True)  33.3 us
    reduce_scatter x1, waiting for transfers between devices, per_device(): lax.psum_scatter(pre_part.astype(jnp.bfloat16), 'dp', scatter_dimension=1...  33.2 us
    all_gather x1, waiting for transfers between devices, per_device(): hidden_piece = lax.all_gather(hidden, 'dp', axis=1, tiled=True)  27.6 us
    dot_general x1, matrix products, per_device(): lax.dot_general(cot_piece, weight_up, contract_hidden, preferred_element_...  8.57 us
    dot_general x1, matrix products, per_device(): lax.dot_general(expert_cot, hidden_piece, contract_rows, preferred_elemen...  8.55 us
  transfers between devices with their start and end apart: 7, of which 6 were waited for; matrix products, arithmetic and copies ran while one was open for 10% of the time, Pallas kernels for 0%

commit v1 on v0

v1 whole, which is shorter than its diff:
```python
import functools

import jax
import jax.numpy as jnp
from jax import lax
from jax.sharding import PartitionSpec as P


def dot_f32(left, right, dims):
    return lax.dot_general(left, right, dims, preferred_element_type=jnp.float32)


def dp_sum(part, n_dp):
    part = part.astype(jnp.bfloat16)
    if n_dp == 2:
        other = lax.ppermute(part, "dp", [(0, 1), (1, 0)])
        return part.astype(jnp.float32) + other.astype(jnp.float32)
    return lax.psum(part.astype(jnp.float32), "dp")


def per_device(
    n_dp, n_expert, tokens, cotangent, expert_ids, gate_levels, capacity, up_weight, down_weight
):
    tok_rows, width_dev = tokens.shape
    top_count = expert_ids.shape[1]
    expert_count = capacity.shape[0]
    slots = tok_rows * top_count // expert_count
    row_count = n_expert * slots
    own = lax.axis_index("expert")

    routing = lax.all_gather(
        jnp.concatenate([expert_ids, gate_levels], axis=1), "expert", axis=0, tiled=True
    )
    tok_all = lax.all_gather(tokens, "expert", axis=0, tiled=False)
    cot_all = lax.all_gather(cotangent, "expert", axis=0, tiled=False)

    ids = routing[:, :top_count].reshape(n_expert, tok_rows, top_count)
    levels = routing[:, top_count:].reshape(n_expert, tok_rows, top_count).astype(jnp.float32)
    named = ids == own
    match = jnp.any(named, axis=2)
    gates = jnp.sum(jnp.where(named, levels, 0.0), axis=2) / jnp.sum(levels, axis=2)
    before = jnp.arange(tok_rows)[:, None] < jnp.arange(tok_rows)[None, :]
    rank = jnp.dot(
        match.astype(jnp.bfloat16), before.astype(jnp.bfloat16), preferred_element_type=jnp.float32
    ).astype(jnp.int32)
    kept = match & (rank < capacity[own])
    slot_of = jnp.where(kept, rank, -1)
    placing = slot_of[:, None, :] == jnp.arange(slots, dtype=jnp.int32)[None, :, None]
    slot_gate = jnp.sum(jnp.where(placing, gates[:, None, :], 0.0), axis=2)
    placing = placing.astype(jnp.bfloat16)

    pick = (((2,), (1,)), ((0,), (0,)))
    weight_up = up_weight[0]
    weight_down = down_weight[0]
    expert_in = dot_f32(placing, tok_all, pick).astype(jnp.bfloat16).reshape(row_count, width_dev)
    preact = dp_sum(jnp.dot(expert_in, weight_up, preferred_element_type=jnp.float32), n_dp)
    placed_cot = dot_f32(placing, cot_all, pick)
    expert_cot = (slot_gate[:, :, None] * placed_cot).astype(jnp.bfloat16)
    expert_cot = expert_cot.reshape(row_count, width_dev)
    hidden_cot = dp_sum(jnp.dot(expert_cot, weight_down, preferred_element_type=jnp.float32), n_dp)
    sigmoid = jax.nn.sigmoid(preact)
    hidden = (preact * sigmoid).astype(jnp.bfloat16)
    act_cot = (hidden_cot * (sigmoid * (1.0 + preact * (1.0 - sigmoid)))).astype(jnp.bfloat16)

    contract_rows = (((0,), (0,)), ((), ()))
    contract_hidden = (((1,), (1,)), ((), ()))
    back = dot_f32(act_cot, weight_up, contract_hidden).astype(jnp.bfloat16)
    back = back.reshape(n_expert, slots, width_dev)
    spread = dot_f32(placing, back, (((1,), (1,)), ((0,), (0,)))).astype(jnp.bfloat16)
    token_grad = lax.psum_scatter(
        spread.reshape(n_expert * tok_rows, width_dev), "expert", scatter_dimension=0, tiled=True
    )
    up_grad = dot_f32(expert_in, act_cot, contract_rows).astype(jnp.bfloat16)[None]
    down_grad = dot_f32(expert_cot, hidden, contract_rows).astype(jnp.bfloat16)[None]
    return (token_grad, up_grad, down_grad)


def solution(mesh):
    return jax.shard_map(
        functools.partial(per_device, mesh.shape["dp"], mesh.shape["expert"]),
        mesh=mesh,
        in_specs=(
            P("expert", "dp"),
            P("expert", "dp"),
            P("expert", None),
            P("expert", None),
            P(),
            P("expert", "dp", None),
            P("expert", "dp", None),
        ),
        out_specs=(P("expert", "dp"), P("expert", "dp", None), P("expert", "dp", None)),
        check_vma=False,
    )
```

time: 378 us -> 362 us (0.958)
  blocking collectives: 0 us -> 19.5 us
  starting transfers between devices: 19.5 us -> 2.27 us
  other arithmetic: 11.8 us -> 3.26 us
  matrix products: 51.7 us -> 43.5 us
    all_to_all x3 -> x0, waiting for transfers between devices: 183 us -> none  [the longest x1 76.3 us: per_device(): lax.all_to_all(send_cot.reshape(block_shape), 'expert', split_axis=0, con...]
    ppermute x0 -> x2, waiting for transfers between devices: none -> 86.5 us  [dp_sum(): other = lax.ppermute(part, 'dp', [(0, 1), (1, 0)])]
    all_gather x2, waiting for transfers between devices: 60.9 us -> 111 us  [the longest x1 63 us: per_device(): cot_all = lax.all_gather(cotangent, 'expert', axis=0, tiled=False)]
    reduce_scatter x2 -> x1, waiting for transfers between devices: 33.2 us -> 76.3 us  [per_device(): lax.psum_scatter(spread.reshape(n_expert * tok_rows, width_dev), 'expert'...]
    all_gather x0 -> x1, blocking collectives: none -> 19.5 us  [per_device(): lax.all_gather(jnp.concatenate([expert_ids, gate_levels], axis=1), 'exper...]
    all_to_all x3 -> x0, starting transfers between devices: 19.1 us -> none  [the longest x1 6.55 us: per_device(): lax.all_to_all(send_rows.reshape(block_shape), 'expert', split_axis=0, co...]
    another operation x2 -> x0, other arithmetic: 4.56 us -> none
    dot_general x7 -> x8, matrix products: 43.3 us -> 39.1 us  [the longest x6 34.2 us: dot_f32(): lax.dot_general(left, right, dims, preferred_element_type=jnp.float32)]
  transfers between devices with their start and end apart: 7 -> 5, of which waited for: 6 -> 5; matrix products, arithmetic and copies ran while one was open for 10% -> 8% of each run, Pallas kernels for 0% -> 0%
where the time goes in v1:
time: 362 us; the launch traced here: 361 us
  waiting for transfers between devices  276 us (76%)
  matrix products  43.5 us (12%)
  blocking collectives  19.5 us (5%)
  between operations  13.9 us (4%)
    ppermute x2, waiting for transfers between devices, dp_sum(): other = lax.ppermute(part, 'dp', [(0, 1), (1, 0)])  86.5 us
    reduce_scatter x1, waiting for transfers between devices, per_device(): lax.psum_scatter(spread.reshape(n_expert * tok_rows, width_dev), 'expert'...  76.3 us
    all_gather x1, waiting for transfers between devices, per_device(): cot_all = lax.all_gather(cotangent, 'expert', axis=0, tiled=False)  63 us
    all_gather x1, waiting for transfers between devices, per_device(): tok_all = lax.all_gather(tokens, 'expert', axis=0, tiled=False)  48.5 us
    dot_general x6, matrix products, dot_f32(): lax.dot_general(left, right, dims, preferred_element_type=jnp.float32)  34.2 us
    all_gather x1, blocking collectives, per_device(): lax.all_gather(jnp.concatenate([expert_ids, gate_levels], axis=1), 'exper...  19.5 us
  transfers between devices with their start and end apart: 5, of which 5 were waited for; matrix products, arithmetic and copies ran while one was open for 8% of the time, Pallas kernels for 0%

profile of v1, /device:TPU:8, one launch (start us, length us, event | category | flops | bytes accessed | tf_op | source)
XLA Modules:
  0.0 360.7 jit_solution(14400012649658591996)
XLA Ops:
  7.2 0.0 all-gather.7.cloned.1.call-start
  7.2 0.7 all-gather.7.cloned.1.call-update
  7.9 0.0 all-gather.5.cloned.1.call-start
  7.9 0.7 all-gather.5.cloned.1.call-update
  8.6 0.0 reduce-scatter.2.cloned.1.call-start
  8.7 1.2 dynamic_slice.3
  9.9 0.7 pad_add_fusion
  10.6 19.5 %all_gather.15 = s32[2048,16]{0,1:T(8,128)S(1)} all-gather(s32[128,16]{0,1:T(8,128)S(1)} %pad_add_fusion), channel_id=1, replica_groups=mesh['dp'=2,'expert'=16] {'expert'}, dimensions={0}, use_global_device_ids=true | all-gather | bytes 139264 | tf_op jit(solution)/shard_map/all_gather | solution.py:31
  30.3 0.8 fusion.19
  31.1 0.2 select_reduce_fusion
  31.3 48.5 %all-gather.7.cloned.1.call-done = bf16[2048,1792]{1,0:T(8,128)(2,1)} async-done(((bf16[128,1792]{1,0:T(8,128)(2,1)}), bf16[2048,1792]{1,0:T(8,128)(2,1)}) %all-gather.7.cloned.1.call-update) | async-done | bytes 7340048 | tf_op jit(solution)/shard_map/all_gather | solution.py:34
  79.7 6.0 %convolution_convert_fusion.1 = bf16[16,64,1792]{2,1,0:T(8,128)(2,1)} fusion(bf16[16,128,1792]{2,1,0:T(8,128)(2,1)} %bitcast.43, s32[16,128]{1,0:T(8,128)S(1)} %fusion.19), kind=kOutput, calls=%fused_computation.6 | convolution fusion | flops 471728128 | bytes 11018240 | tf_op jit(solution)/shard_map/dot_general | solution.py:10
  85.8 63.0 %all-gather.5.cloned.1.call-done = bf16[2048,1792]{1,0:T(8,128)(2,1)} async-done(((bf16[128,1792]{1,0:T(8,128)(2,1)}), bf16[2048,1792]{1,0:T(8,128)(2,1)}) %all-gather.5.cloned.1.call-update) | async-done | bytes 7340048 | tf_op jit(solution)/shard_map/all_gather | solution.py:35
  148.8 4.4 %multiply_convert_fusion = bf16[16,64,1792]{2,1,0:T(8,128)(2,1)S(1)} fusion(bf16[16,128,1792]{2,1,0:T(8,128)(2,1)} %bitcast.44, f32[16,64]{1,0:T(8,128)S(1)} %select_reduce_fusion, s32[16,128]{1,0:T(8,128)S(1)} %fusion.19), kind=kOutput, calls=%fused_computation | convolution fusion | flops 473563136 | bytes 11022336 | tf_op jit(solution)/shard_map/dot_general | solution.py:10
  153.1 0.0 copy-start.1
  153.1 0.0 copy-done.6
  153.2 0.0 copy-start
  153.2 0.0 copy-start.7
  153.2 4.4 %fusion.8 = bf16[1024,1024]{1,0:T(8,128)(2,1)S(1)} fusion(bf16[1024,1792]{1,0:T(8,128)(2,1)S(1)} %bitcast.48, bf16[1,1792,1024]{2,1,0:T(8,128)(2,1)S(1)} %copy-done.6), kind=kOutput, calls=%fused_computation.18 | convolution fusion | flops 3759144960 | bytes 9437184 | tf_op jit(solution)/shard_map/dot_general | solution.py:60
  157.6 1.5 collective-permute-start
  159.1 4.2 %fusion.11 = bf16[1024,1024]{1,0:T(8,128)(2,1)S(1)} fusion(bf16[1024,1792]{1,0:T(8,128)(2,1)S(1)} %bitcast.46, bf16[1,1792,1024]{2,1,0:T(8,128)(2,1)S(1)} %copy-done.7), kind=kOutput, calls=%fused_computation.19 | convolution fusion | flops 3759144960 | bytes 9437184 | tf_op jit(solution)/shard_map/dot_general | solution.py:56
  163.3 0.6 collective-permute-start.1
  163.9 42.2 %collective-permute-done = bf16[1024,1024]{1,0:T(8,128)(2,1)S(1)} collective-permute-done((bf16[1024,1024]{1,0:T(8,128)(2,1)S(1)}, bf16[1024,1024]{1,0:T(8,128)(2,1)S(1)}, u32[]{:S(2)}, u32[]{:S(2)}) %collective-permute-start) | collective-permute-done | bytes 2097184 | tf_op jit(solution)/shard_map/ppermute | solution.py:16
  206.1 44.3 %collective-permute-done.1 = bf16[1024,1024]{1,0:T(8,128)(2,1)S(1)} collective-permute-done((bf16[1024,1024]{1,0:T(8,128)(2,1)S(1)}, bf16[1024,1024]{1,0:T(8,128)(2,1)S(1)}, u32[]{:S(2)}, u32[]{:S(2)}) %collective-permute-start.1) | collective-permute-done | bytes 2097184 | tf_op jit(solution)/shard_map/ppermute | solution.py:16
  250.4 1.4 copy-done.3
  251.7 2.3 multiply_convert_fusion.2
  254.0 4.3 %convolution_convert_fusion.4 = bf16[1024,1792]{1,0:T(8,128)(2,1)S(1)} fusion(bf16[1024,1024]{1,0:T(8,128)(2,1)S(1)} %multiply_convert_fusion.2, bf16[1,1792,1024]{2,1,0:T(8,128)(2,1)S(1)} %copy-done.7), kind=kOutput, calls=%fused_computation.9 | convolution fusion | flops 3759931392 | bytes 9437184 | tf_op jit(solution)/shard_map/dot_general | solution.py:10
  258.3 5.1 %convolution_convert_fusion = bf16[16,128,1792]{2,1,0:T(8,128)(2,1)} fusion(bf16[16,64,1792]{2,1,0:T(8,128)(2,1)S(1)} %bitcast.47, s32[16,128]{1,0:T(8,128)S(1)} %fusion.19), kind=kOutput, calls=%fused_computation.1 | convolution fusion | flops 473563136 | bytes 11018240 | tf_op jit(solution)/shard_map/dot_general | solution.py:10
  263.4 0.0 reduce-scatter.2.cloned.1.call-update
  263.4 8.7 %fusion.5 = bf16[1,1792,1024]{2,1,0:T(8,128)(2,1)} fusion(bf16[1024,1792]{1,0:T(8,128)(2,1)} %bitcast.45, bf16[1024,1024]{1,0:T(8,128)(2,1)} %copy-done.5), kind=kOutput, calls=%fused_computation.15 | convolution fusion | flops 3759931392 | bytes 9437184 | tf_op jit(solution)/shard_map/dot_general | solution.py:10
  272.1 5.7 %fusion.6 = bf16[1,1792,1024]{2,1,0:T(8,128)(2,1)} fusion(bf16[1024,1792]{1,0:T(8,128)(2,1)S(1)} %bitcast.49, bf16[1024,1024]{1,0:T(8,128)(2,1)S(1)} %copy-done.4, bf16[1024,1024]{1,0:T(8,128)(2,1)S(1)} %fusion.11), kind=kOutput, calls=%fused_computation.16 | convolution fusion | flops 3768320000 | bytes 11534336 | tf_op jit(solution)/shard_map/dot_general | solution.py:10
  277.8 76.3 %reduce-scatter.2.cloned.1.call-done = bf16[128,1792]{1,0:T(8,128)(2,1)} async-done(((bf16[2048,1792]{1,0:T(8,128)(2,1)}), bf16[128,1792]{1,0:T(8,128)(2,1)}) %reduce-scatter.2.cloned.1.call-update) | async-done | bytes 458768 | tf_op jit(solution)/shard_map/reduce_scatter | solution.py:70
  (14 shorter events, 0.1 us)
Async XLA Ops:
  7.2 72.6 %all-gather.7.cloned.1.call-start = ((), (), s32[]{:S(2)}) async-start(), calls=%async_computation.3 | async-start | bytes 7798784 | tf_op jit(solution)/shard_map/all_gather | solution.py:34
  7.9 140.9 %all-gather.5.cloned.1.call-start = ((), (), s32[]{:S(2)}) async-start(), calls=%async_computation.2 | async-start | bytes 7798784 | tf_op jit(solution)/shard_map/all_gather | solution.py:35
  8.6 345.5 %reduce-scatter.2.cloned.1.call-start = ((), (), s32[]{:S(2)}) async-start(), calls=%async_computation.1 | async-start | bytes 7798784 | tf_op jit(solution)/shard_map/reduce_scatter | solution.py:70
  148.8 4.4 %copy-start.6 = (bf16[1,1792,1024]{2,1,0:T(8,128)(2,1)S(1)}, bf16[1,1792,1024]{2,1,0:T(8,128)(2,1)}, u32[]{:S(2)}) copy-start(bf16[1,1792,1024]{2,1,0:T(8,128)(2,1)} %param.13) | copy-start | bytes 11010052
  153.1 4.4 %copy-start.1 = (bf16[16,64,1792]{2,1,0:T(8,128)(2,1)}, bf16[16,64,1792]{2,1,0:T(8,128)(2,1)S(1)}, u32[]{:S(2)}) copy-start(bf16[16,64,1792]{2,1,0:T(8,128)(2,1)S(1)} %multiply_convert_fusion) | copy-start | bytes 11010052
  153.2 5.9 %copy-start = (bf16[16,64,1792]{2,1,0:T(8,128)(2,1)S(1)}, bf16[16,64,1792]{2,1,0:T(8,128)(2,1)}, u32[]{:S(2)}) copy-start(bf16[16,64,1792]{2,1,0:T(8,128)(2,1)} %convolution_convert_fusion.1) | copy-start | bytes 11010052
  153.2 5.9 %copy-start.7 = (bf16[1,1792,1024]{2,1,0:T(8,128)(2,1)S(1)}, bf16[1,1792,1024]{2,1,0:T(8,128)(2,1)}, u32[]{:S(2)}) copy-start(bf16[1,1792,1024]{2,1,0:T(8,128)(2,1)} %param.12) | copy-start | bytes 11010052
  157.6 48.5 %collective-permute-start = (bf16[1024,1024]{1,0:T(8,128)(2,1)S(1)}, bf16[1024,1024]{1,0:T(8,128)(2,1)S(1)}, u32[]{:S(2)}, u32[]{:S(2)}) collective-permute-start(bf16[1024,1024]{1,0:T(8,128)(2,1)S(1)} %fusion.8), channel_id=1, source_target_pairs={{0,16},{16,0},{1,17},{17,1},{2,18},{18,2},{3,19},{19,3},{4,20},{20... | collective-permute-start | bytes 6291464 | tf_op jit(solution)/shard_map/ppermute | solution.py:16
  163.3 87.1 %collective-permute-start.1 = (bf16[1024,1024]{1,0:T(8,128)(2,1)S(1)}, bf16[1024,1024]{1,0:T(8,128)(2,1)S(1)}, u32[]{:S(2)}, u32[]{:S(2)}) collective-permute-start(bf16[1024,1024]{1,0:T(8,128)(2,1)S(1)} %fusion.11), channel_id=1, source_target_pairs={{0,16},{16,0},{1,17},{17,1},{2,18},{18,2},{3,19},{19,3},{4,20},{20... | collective-permute-start | bytes 6291464 | tf_op jit(solution)/shard_map/ppermute | solution.py:16
  250.4 1.4 copy-start.3
  254.0 4.3 %copy-start.5 = (bf16[1024,1024]{1,0:T(8,128)(2,1)}, bf16[1024,1024]{1,0:T(8,128)(2,1)S(1)}, u32[]{:S(2)}) copy-start(bf16[1024,1024]{1,0:T(8,128)(2,1)S(1)} %multiply_convert_fusion.2) | copy-start | bytes 6291460
  263.4 8.7 %copy-start.2 = (bf16[16,64,1792]{2,1,0:T(8,128)(2,1)S(1)}, bf16[16,64,1792]{2,1,0:T(8,128)(2,1)}, u32[]{:S(2)}) copy-start(bf16[16,64,1792]{2,1,0:T(8,128)(2,1)} %copy-done.1) | copy-start | bytes 11010052
  263.4 8.7 %copy-start.4 = (bf16[1024,1024]{1,0:T(8,128)(2,1)S(1)}, bf16[1024,1024]{1,0:T(8,128)(2,1)}, u32[]{:S(2)}) copy-start(bf16[1024,1024]{1,0:T(8,128)(2,1)} %copy-done.3) | copy-start | bytes 6291460
Sparse Core Ops, SparseCore 0:
  10.3 69.4 all-gather.6
  82.0 66.6 all-gather.4
  263.5 90.6 reduce-scatter.1

commit v2 on v1

v2 whole, which is shorter than its diff:
```python
import functools

import jax
import jax.numpy as jnp
from jax import lax
from jax.experimental import pallas as pl
from jax.experimental.pallas import tpu as pltpu
from jax.sharding import PartitionSpec as P

F32 = jnp.float32
BF16 = jnp.bfloat16
CONTRACT_ROWS = (((0,), (0,)), ((), ()))
CONTRACT_LAST = (((1,), (1,)), ((), ()))

NZ, NX, NC = 4, 2, 2
ORDER = ((0, 1, 2, 3), (1, 0, 2, 3), (2, 3, 1, 0), (3, 2, 1, 0))


def dot_f32(left, right, dims=(((1,), (0,)), ((), ()))):
    return lax.dot_general(left, right, dims, preferred_element_type=F32)


def along_z(value, pairs):
    perm = [
        ((a * NX + x) * NC + c, (b * NX + x) * NC + c)
        for a, b in pairs
        for x in range(NX)
        for c in range(NC)
    ]
    return lax.ppermute(value, "expert", perm)


def swap_x(value):
    return lax.ppermute(value, "expert", [(i, i ^ NC) for i in range(NZ * NX * NC)])


def swap_core(value):
    return lax.ppermute(value, "expert", [(i, i ^ 1) for i in range(NZ * NX * NC)])


def swap_dp(value):
    return lax.ppermute(value, "dp", [(0, 1), (1, 0)])


NEIGHBOUR = ((0, 1), (1, 0), (2, 3), (3, 2))
MIDDLE = ((1, 2), (2, 1))
OUTWARD = ((1, 0), (2, 3))
INWARD = ((0, 1), (3, 2))


def gather_groups(block, inner):
    near = along_z(block, NEIGHBOUR)
    across = along_z(block, MIDDLE)
    outer_two = along_z(across, OUTWARD)
    far = along_z(near, MIDDLE)
    outer_three = along_z(far, OUTWARD)
    columns = [
        block,
        near,
        jnp.where(inner, across, outer_two),
        jnp.where(inner, far, outer_three),
    ]
    groups = []
    for own in columns:
        other = swap_x(own)
        groups.append((own, swap_core(own), other, swap_core(other)))
    return groups


def add(left, right):
    return (left.astype(F32) + right.astype(F32)).astype(BF16)


def scatter_groups(keep, send):
    sums = [None] * NZ
    for s in reversed(range(NZ)):
        chip = add(keep[s], swap_core(send[s]))
        sums[s] = add(chip[0], swap_x(chip[1]))
    far = add(sums[3], along_z(sums[3], INWARD))
    near = add(sums[1], along_z(far, MIDDLE))
    across = add(sums[2], along_z(sums[2], INWARD))
    return (
        sums[0].astype(F32)
        + along_z(across, MIDDLE).astype(F32)
        + along_z(near, NEIGHBOUR).astype(F32)
    ).astype(BF16)


def placing_of(slot_row, slots):
    return slot_row == lax.broadcasted_iota(jnp.int32, (slots, slot_row.shape[1]), 0)


def front_kernel(scaled, slots, slot_ref, gate_ref, b0, b1, b2, b3, weight_ref, rows_ref, part_ref, total):
    step = pl.program_id(0)
    for index, block in enumerate((b0, b1, b2, b3)):
        hit = placing_of(slot_ref[index], slots)
        picked = dot_f32(jnp.where(hit, 1.0, 0.0).astype(BF16), block[...])
        if scaled:
            gate = jnp.sum(jnp.where(hit, gate_ref[index], 0.0), axis=1, keepdims=True)
            picked = picked * gate
        rows_ref[index * slots : (index + 1) * slots, :] = picked.astype(BF16)
    product = dot_f32(rows_ref[...], weight_ref[...])

    @pl.when(step == 0)
    def _():
        total[...] = product

    @pl.when(step > 0)
    def _():
        total[...] += product

    @pl.when(step == pl.num_programs(0) - 1)
    def _():
        part_ref[...] = total[...].astype(BF16)


def front(blocks, slot_of, gates, weight, slots, scaled):
    tok_rows, width = blocks[0].shape
    hidden = weight.shape[1]
    rows = 4 * slots
    tile = width // 2
    whole = pl.BlockSpec((4, 1, tok_rows), lambda k: (0, 0, 0))
    return pl.pallas_call(
        functools.partial(front_kernel, scaled, slots),
        grid=(width // tile,),
        in_specs=[whole, whole]
        + [pl.BlockSpec((tok_rows, tile), lambda k: (0, k))] * 4
        + [pl.BlockSpec((tile, hidden), lambda k: (k, 0))],
        out_specs=[
            pl.BlockSpec((rows, tile), lambda k: (0, k)),
            pl.BlockSpec((rows, hidden), lambda k: (0, 0)),
        ],
        out_shape=[
            jax.ShapeDtypeStruct((rows, width), BF16),
            jax.ShapeDtypeStruct((rows, hidden), BF16),
        ],
        scratch_shapes=[pltpu.VMEM((rows, hidden), F32)],
        compiler_params=pltpu.CompilerParams(vmem_limit_bytes=24 * 1024 * 1024),
        cost_estimate=pl.CostEstimate(
            flops=2 * rows * width * (hidden + tok_rows),
            bytes_accessed=2 * (width * hidden + 2 * rows * width + 4 * tok_rows * width),
            transcendentals=0,
        ),
    )(slot_of, gates, *blocks, weight)


def back_kernel(slots, slot_ref, pre_a, pre_b, cot_a, cot_b, weight_ref, hidden_ref, act_ref, keep_ref, send_ref):
    @pl.when(pl.program_id(0) == 0)
    def _():
        preact = pre_a[...].astype(F32) + pre_b[...].astype(F32)
        hidden_cot = cot_a[...].astype(F32) + cot_b[...].astype(F32)
        sigmoid = jax.nn.sigmoid(preact)
        hidden_ref[...] = (preact * sigmoid).astype(BF16)
        act_ref[...] = (hidden_cot * (sigmoid * (1.0 + preact * (1.0 - sigmoid)))).astype(BF16)

    back = dot_f32(act_ref[...], weight_ref[...], CONTRACT_LAST).astype(BF16)
    for index in range(4):
        hit = placing_of(slot_ref[index], slots)
        placing = jnp.where(hit, 1.0, 0.0).astype(BF16)
        spread = dot_f32(placing, back[index * slots : (index + 1) * slots], CONTRACT_ROWS)
        out_ref = send_ref if index % 2 else keep_ref
        out_ref[index // 2] = spread.astype(BF16)


def back(slot_of, parts, weight, slots):
    tok_rows = slot_of.shape[2]
    width, hidden = weight.shape
    rows = 4 * slots
    tile = width // 2
    full = pl.BlockSpec((rows, hidden), lambda n: (0, 0))
    spread = pl.BlockSpec((2, tok_rows, tile), lambda n: (0, 0, n))
    return pl.pallas_call(
        functools.partial(back_kernel, slots),
        grid=(width // tile,),
        in_specs=[pl.BlockSpec((4, 1, tok_rows), lambda n: (0, 0, 0))]
        + [full] * 4
        + [pl.BlockSpec((tile, hidden), lambda n: (n, 0))],
        out_specs=[full, full, spread, spread],
        out_shape=[
            jax.ShapeDtypeStruct((rows, hidden), BF16),
            jax.ShapeDtypeStruct((rows, hidden), BF16),
            jax.ShapeDtypeStruct((2, tok_rows, width), BF16),
            jax.ShapeDtypeStruct((2, tok_rows, width), BF16),
        ],
        compiler_params=pltpu.CompilerParams(vmem_limit_bytes=32 * 1024 * 1024),
        cost_estimate=pl.CostEstimate(
            flops=2 * rows * width * (hidden + tok_rows),
            bytes_accessed=2 * (width * hidden + 6 * rows * hidden + 4 * tok_rows * width),
            transcendentals=rows * hidden,
        ),
    )(slot_of, *parts, weight)


def grad_kernel(*refs):
    out_ref = refs[-1]
    half = (len(refs) - 1) // 2
    total = None
    for left, right in zip(refs[:half], refs[half:-1]):
        term = dot_f32(left[...], right[...], CONTRACT_ROWS)
        total = term if total is None else total + term
    out_ref[...] = total.astype(BF16)


def grad(lefts, rights):
    rows, width = lefts[0].shape
    hidden = rights[0].shape[1]
    count = len(lefts)
    tile = 256
    return pl.pallas_call(
        grad_kernel,
        grid=(width // tile,),
        in_specs=[pl.BlockSpec((rows, tile), lambda n: (0, n))] * count
        + [pl.BlockSpec((rows, hidden), lambda n: (0, 0))] * count,
        out_specs=pl.BlockSpec((tile, hidden), lambda n: (n, 0)),
        out_shape=jax.ShapeDtypeStruct((width, hidden), BF16),
        compiler_params=pltpu.CompilerParams(vmem_limit_bytes=24 * 1024 * 1024),
        cost_estimate=pl.CostEstimate(
            flops=2 * count * rows * width * hidden,
            bytes_accessed=2 * (width * hidden + count * rows * (width + hidden)),
            transcendentals=0,
        ),
    )(*lefts, *rights)


def slots_and_gates(routing, own, limit, top_count):
    ids = routing[:, :, :top_count]
    levels = routing[:, :, top_count:].astype(F32)
    tok_rows = ids.shape[1]
    named = ids == own
    match = jnp.any(named, axis=2)
    gates = jnp.sum(jnp.where(named, levels, 0.0), axis=2) / jnp.sum(levels, axis=2)
    before = jnp.arange(tok_rows)[:, None] < jnp.arange(tok_rows)[None, :]
    rank = dot_f32(match.astype(BF16), before.astype(BF16)).astype(jnp.int32)
    return jnp.where(match & (rank < limit), rank, -1), gates


def grouped(tokens, cotangent, expert_ids, gate_levels, capacity, up_weight, down_weight):
    tok_rows, width = tokens.shape
    top_count = expert_ids.shape[1]
    slots = tok_rows * top_count // capacity.shape[0]
    own = lax.axis_index("expert")
    z, x, c = own // (NX * NC), (own // NC) % NX, own % NC
    inner = (z > 0) & (z < NZ - 1)
    weight_up, weight_down = up_weight[0], down_weight[0]

    routing = lax.all_gather(
        jnp.concatenate([expert_ids, gate_levels], axis=1), "expert", axis=0, tiled=False
    )
    order = jnp.array(ORDER, jnp.int32)[z]
    flip = jnp.arange(2, dtype=jnp.int32)
    block_ids = (order[:, None, None] * NX + (x ^ flip)[None, :, None]) * NC + (c ^ flip)
    slot_of, gates = slots_and_gates(routing, own, capacity[own], top_count)
    slot_of = slot_of[block_ids.reshape(-1)].reshape(NZ, 4, 1, tok_rows)
    gates = gates[block_ids.reshape(-1)].reshape(NZ, 4, 1, tok_rows)

    tok_groups = gather_groups(tokens, inner)
    cot_groups = gather_groups(cotangent, inner)
    rows_in, pre = [], []
    for s in range(NZ):
        rows, part = front(tok_groups[s], slot_of[s], gates[s], weight_up, slots, False)
        rows_in.append(rows)
        pre.append((part, swap_dp(part)))
    rows_cot, cot = [], []
    for s in range(NZ):
        rows, part = front(cot_groups[s], slot_of[s], gates[s], weight_down, slots, True)
        rows_cot.append(rows)
        cot.append((part, swap_dp(part)))
    hidden, act, keep, send = [], [], [], []
    for s in range(NZ):
        h, a, k, d = back(slot_of[s], pre[s] + cot[s], weight_up, slots)
        hidden.append(h)
        act.append(a)
        keep.append(k)
        send.append(d)
    token_grad = scatter_groups(keep, send)
    up_grad = grad(rows_in, act)[None]
    down_grad = grad(rows_cot, hidden)[None]
    return token_grad, up_grad, down_grad


def general(n_expert, tokens, cotangent, expert_ids, gate_levels, capacity, up_weight, down_weight):
    tok_rows, width = tokens.shape
    top_count = expert_ids.shape[1]
    slots = tok_rows * top_count // capacity.shape[0]
    row_count = n_expert * slots
    own = lax.axis_index("expert")
    weight_up, weight_down = up_weight[0], down_weight[0]

    routing = lax.all_gather(
        jnp.concatenate([expert_ids, gate_levels], axis=1), "expert", axis=0, tiled=False
    )
    tok_all = lax.all_gather(tokens, "expert", axis=0, tiled=False)
    cot_all = lax.all_gather(cotangent, "expert", axis=0, tiled=False)
    slot_of, gates = slots_and_gates(routing, own, capacity[own], top_count)
    placing = slot_of[:, None, :] == jnp.arange(slots, dtype=jnp.int32)[None, :, None]
    slot_gate = jnp.sum(jnp.where(placing, gates[:, None, :], 0.0), axis=2)
    placing = placing.astype(BF16)
    pick = (((2,), (1,)), ((0,), (0,)))
    rows_in = dot_f32(placing, tok_all, pick).astype(BF16).reshape(row_count, width)
    rows_cot = (slot_gate[:, :, None] * dot_f32(placing, cot_all, pick)).astype(BF16)
    rows_cot = rows_cot.reshape(row_count, width)
    preact = lax.psum(dot_f32(rows_in, weight_up).astype(BF16).astype(F32), "dp")
    hidden_cot = lax.psum(dot_f32(rows_cot, weight_down).astype(BF16).astype(F32), "dp")
    sigmoid = jax.nn.sigmoid(preact)
    hidden = (preact * sigmoid).astype(BF16)
    act = (hidden_cot * (sigmoid * (1.0 + preact * (1.0 - sigmoid)))).astype(BF16)
    row_grad = dot_f32(act, weight_up, CONTRACT_LAST).astype(BF16)
    spread = dot_f32(
        placing, row_grad.reshape(n_expert, slots, width), (((1,), (1,)), ((0,), (0,)))
    ).astype(BF16)
    token_grad = lax.psum_scatter(
        spread.reshape(n_expert * tok_rows, width), "expert", scatter_dimension=0, tiled=True
    )
    up_grad = dot_f32(rows_in, act, CONTRACT_ROWS).astype(BF16)[None]
    down_grad = dot_f32(rows_cot, hidden, CONTRACT_ROWS).astype(BF16)[None]
    return token_grad, up_grad, down_grad


def solution(mesh):
    n_dp, n_expert = mesh.shape["dp"], mesh.shape["expert"]
    if n_dp == 2 and n_expert == NZ * NX * NC:
        body = grouped
    else:
        body = functools.partial(general, n_expert)
    return jax.shard_map(
        body,
        mesh=mesh,
        in_specs=(
            P("expert", "dp"),
            P("expert", "dp"),
            P("expert", None),
            P("expert", None),
            P(),
            P("expert", "dp", None),
            P("expert", "dp", None),
        ),
        out_specs=(P("expert", "dp"), P("expert", "dp", None), P("expert", "dp", None)),
        check_vma=False,
    )
```

time: 362 us -> 269 us (0.74)
  waiting for transfers between devices: 276 us -> 118 us
  starting transfers between devices: 2.27 us -> 60.5 us
  Pallas kernels: 0 us -> 43.1 us
  matrix products: 43.5 us -> 0.78 us
  between operations: 13.9 us -> 1.25 us
  blocking collectives: 19.5 us -> 29.9 us
    all_gather x2 -> x0, waiting for transfers between devices: 111 us -> none  [the longest x1 63 us: per_device(): cot_all = lax.all_gather(cotangent, 'expert', axis=0, tiled=False)]
    reduce_scatter x1 -> x0, waiting for transfers between devices: 76.3 us -> none  [per_device(): lax.psum_scatter(spread.reshape(n_expert * tok_rows, width_dev), 'expert'...]
    ppermute x2 -> x55, starting transfers between devices: 2.16 us -> 60.5 us  [the longest x15 34.8 us: along_z(): return lax.ppermute(value, 'expert', perm)]
    pallas_call x0 -> x14, Pallas kernels: none -> 43.1 us  [the longest x8 19.3 us: front(): pl.pallas_call(functools.partial(front_kernel, scaled, slots), grid=(widt...]
    dot_general x9 -> x1, matrix products: 43.5 us -> 0.78 us  [dot_f32(): return lax.dot_general(left, right, dims, preferred_element_type=F32)]
    ppermute x2 -> x55, waiting for transfers between devices: 86.5 us -> 118 us  [the longest x8 48.8 us: swap_dp(): return lax.ppermute(value, 'dp', [(0, 1), (1, 0)])]
    all_gather x1, blocking collectives: 19.5 us -> 29.9 us  [grouped(): lax.all_gather(jnp.concatenate([expert_ids, gate_levels], axis=1), 'exper...]
  transfers between devices with their start and end apart: 5 -> 55, of which waited for: 5 -> 20; matrix products, arithmetic and copies ran while one was open for 8% -> 3% of each run, Pallas kernels for 0% -> 16%
where the time goes in v2:
time: 269 us; the launch traced here: 266 us
  waiting for transfers between devices  118 us (44%)
  starting transfers between devices  60.5 us (22%)
  Pallas kernels  43.1 us (16%)
  blocking collectives  29.9 us (11%)
  other arithmetic  6.32 us (2%)
  local copies, waits for them, and re-layouts  5.68 us (2%)
    ppermute x8, waiting for transfers between devices, swap_dp(): return lax.ppermute(value, 'dp', [(0, 1), (1, 0)])  48.8 us
    ppermute x12, waiting for transfers between devices, swap_x(): lax.ppermute(value, 'expert', [(i, i ^ NC) for i in range(NZ * NX * NC)])  43.2 us
    ppermute x15, starting transfers between devices, along_z(): return lax.ppermute(value, 'expert', perm)  34.8 us
    all_gather x1, blocking collectives, grouped(): lax.all_gather(jnp.concatenate([expert_ids, gate_levels], axis=1), 'exper...  29.9 us
    ppermute x15, waiting for transfers between devices, along_z(): return lax.ppermute(value, 'expert', perm)  25.5 us
    pallas_call x8, Pallas kernels, front(): pl.pallas_call(functools.partial(front_kernel, scaled, slots), grid=(widt...  19.3 us
    ppermute x12, starting transfers between devices, swap_x(): lax.ppermute(value, 'expert', [(i, i ^ NC) for i in range(NZ * NX * NC)])  14.2 us
    pallas_call x2, Pallas kernels, grad(): pl.pallas_call(grad_kernel, grid=(width // tile,), in_specs=[pl.BlockSpec...  12.6 us
  transfers between devices with their start and end apart: 55, of which 20 were waited for; matrix products, arithmetic and copies ran while one was open for 3% of the time, Pallas kernels for 16%

profile of v2, /device:TPU:8, one launch (start us, length us, event | category | flops | bytes accessed | tf_op | source)
XLA Modules:
  0.0 265.6 jit_solution(4695119106907910445)
XLA Ops:
  0.7 5.0 %collective-permute-start.10 = (bf16[128,1792]{1,0:T(8,128)(2,1)}, bf16[128,1792]{1,0:T(8,128)(2,1)}, u32[]{:S(2)}, u32[]{:S(2)}) collective-permute-start(bf16[128,1792]{1,0:T(8,128)(2,1)} %b0.2), channel_id=1, source_target_pairs={{4,8},{5,9},{6,10},{7,11},{8,4},{9,5},{10,6},{11,7},{20,24},{21,25... | collective-permute-start | bytes 1376264 | tf_op jit(solution)/shard_map/ppermute | solution.py:30
  9.4 29.9 %all-gather = s32[2048,16]{0,1:T(8,128)S(1)} all-gather(s32[128,16]{0,1:T(8,128)S(1)} %pad_add_fusion), channel_id=2, replica_groups=mesh['dp'=2,'expert'=16] {'expert'}, dimensions={0}, use_global_device_ids=true | all-gather | bytes 139264 | tf_op jit(solution)/shard_map/all_gather | solution.py:246
  46.6 2.3 collective-permute-start.11
  55.2 3.9 %collective-permute-start.38 = (bf16[128,1792]{1,0:T(8,128)(2,1)S(1)}, bf16[128,1792]{1,0:T(8,128)(2,1)S(1)}, u32[]{:S(2)}, u32[]{:S(2)}) collective-permute-start(bf16[128,1792]{1,0:T(8,128)(2,1)S(1)} %collective-permute-done.26.b0), channel_id=1, source_target_pairs={{4,8},{5,9},{6,10},{7,11},{8,4},{9,5},{10,6},{11,7},{20,24},{21,25... | collective-permute-start | bytes 1376264 | tf_op jit(solution)/shard_map/ppermute | solution.py:30
  59.2 3.1 %shard_map.104 = (bf16[256,1792]{1,0:T(8,128)(2,1)S(1)}, bf16[256,1024]{1,0:T(8,128)(2,1)S(1)}) custom-call(s32[4,1,128]{2,1,0:T(1,128)S(1)} %bitcast.72, f32[4,1,128]{2,1,0:T(1,128)S(1)} %bitcast.81, bf16[128,1792]{1,0:T(8,128)(2,1)S(1)} %copy-done.4, bf16[128,1792]{1,0:T(8,128)(2,1)S(1)} %collective-permute-done.4.b1, ...), custom_call_target="tpu_custom_call" | custom-call | flops 1056964608 | bytes 7340032 | tf_op jit(solution)/shard_map/pallas_call | solution.py:123
  62.4 2.3 collective-permute-start.44
  64.9 4.4 %collective-permute-start.17 = (bf16[128,1792]{1,0:T(8,128)(2,1)}, bf16[128,1792]{1,0:T(8,128)(2,1)S(1)}, u32[]{:S(2)}, u32[]{:S(2)}) collective-permute-start(bf16[128,1792]{1,0:T(8,128)(2,1)} %collective-permute-done.16), channel_id=1, source_target_pairs={{4,0},{5,1},{6,2},{7,3},{8,12},{9,13},{10,14},{11,15},{20,16},{21,... | collective-permute-start | bytes 1376264 | tf_op jit(solution)/shard_map/ppermute | solution.py:30
  70.5 9.2 %collective-permute-done.44 = bf16[128,1792]{1,0:T(8,128)(2,1)S(1)} collective-permute-done((bf16[128,1792]{1,0:T(8,128)(2,1)S(1)}, bf16[128,1792]{1,0:T(8,128)(2,1)S(1)}, u32[]{:S(2)}, u32[]{:S(2)}) %collective-permute-start.44) | collective-permute-done | bytes 458784 | tf_op jit(solution)/shard_map/ppermute | solution.py:30
  85.6 7.5 %collective-permute-done.33.b2 = bf16[128,1792]{1,0:T(8,128)(2,1)S(1)} collective-permute-done((bf16[128,1792]{1,0:T(8,128)(2,1)S(1)}, bf16[128,1792]{1,0:T(8,128)(2,1)S(1)}, u32[]{:S(2)}, u32[]{:S(2)}) %collective-permute-start.33) | collective-permute-done | bytes 458784 | tf_op jit(solution)/shard_map/ppermute | solution.py:34
  93.6 7.0 %collective-permute-done.45 = bf16[128,1792]{1,0:T(8,128)(2,1)S(1)} collective-permute-done((bf16[128,1792]{1,0:T(8,128)(2,1)S(1)}, bf16[128,1792]{1,0:T(8,128)(2,1)S(1)}, u32[]{:S(2)}, u32[]{:S(2)}) %collective-permute-start.45) | collective-permute-done | bytes 458784 | tf_op jit(solution)/shard_map/ppermute | solution.py:30
  106.2 7.9 %collective-permute-done.19.b2 = bf16[128,1792]{1,0:T(8,128)(2,1)S(1)} collective-permute-done((bf16[128,1792]{1,0:T(8,128)(2,1)S(1)}, bf16[128,1792]{1,0:T(8,128)(2,1)S(1)}, u32[]{:S(2)}, u32[]{:S(2)}) %collective-permute-start.19) | collective-permute-done | bytes 458784 | tf_op jit(solution)/shard_map/ppermute | solution.py:34
  119.5 8.1 %collective-permute-done.7.cot_b = bf16[256,1024]{1,0:T(8,128)(2,1)S(1)} collective-permute-done((bf16[256,1024]{1,0:T(8,128)(2,1)S(1)}, bf16[256,1024]{1,0:T(8,128)(2,1)S(1)}, u32[]{:S(2)}, u32[]{:S(2)}) %collective-permute-start.7) | collective-permute-done | bytes 524320 | tf_op jit(solution)/shard_map/ppermute | solution.py:42
  133.3 2.8 %shard_map.105 = (bf16[256,1024]{1,0:T(8,128)(2,1)S(1)}, bf16[256,1024]{1,0:T(8,128)(2,1)S(1)}, bf16[2,128,1792]{2,1,0:T(8,128)(2,1)S(1)}, bf16[2,128,1792]{2,1,0:T(8,128)(2,1)S(1)}) custom-call(s32[4,1,128]{2,1,0:T(1,128)S(1)} %bitcast.73, bf16[256,1024]{1,0:T(8,128)(2,1)S(1)} %get-tuple-element.35.pre_a, ...), custom_call_target="tpu_custom_call" | custom-call | flops 1056964608 | bytes 8650752 | tf_op jit(solution)/shard_map/pallas_call | solution.py:172
  136.7 2.3 shard_map.106
  139.1 3.4 %collective-permute-done.30.pre_b = bf16[256,1024]{1,0:T(8,128)(2,1)S(1)} collective-permute-done((bf16[256,1024]{1,0:T(8,128)(2,1)S(1)}, bf16[256,1024]{1,0:T(8,128)(2,1)S(1)}, u32[]{:S(2)}, u32[]{:S(2)}) %collective-permute-start.30) | collective-permute-done | bytes 524320 | tf_op jit(solution)/shard_map/ppermute | solution.py:42
  144.8 7.2 %collective-permute-done.35.cot_b = bf16[256,1024]{1,0:T(8,128)(2,1)S(1)} collective-permute-done((bf16[256,1024]{1,0:T(8,128)(2,1)S(1)}, bf16[256,1024]{1,0:T(8,128)(2,1)S(1)}, u32[]{:S(2)}, u32[]{:S(2)}) %collective-permute-start.35) | collective-permute-done | bytes 524320 | tf_op jit(solution)/shard_map/ppermute | solution.py:42
  154.1 2.8 %shard_map.111 = (bf16[256,1024]{1,0:T(8,128)(2,1)S(1)}, bf16[256,1024]{1,0:T(8,128)(2,1)S(1)}, bf16[2,128,1792]{2,1,0:T(8,128)(2,1)S(1)}, bf16[2,128,1792]{2,1,0:T(8,128)(2,1)S(1)}) custom-call(s32[4,1,128]{2,1,0:T(1,128)S(1)} %bitcast.70, bf16[256,1024]{1,0:T(8,128)(2,1)S(1)} %get-tuple-element.43.pre_a, ...), custom_call_target="tpu_custom_call" | custom-call | flops 1056964608 | bytes 8650752 | tf_op jit(solution)/shard_map/pallas_call | solution.py:172
  156.9 2.3 shard_map.112
  163.2 3.7 %collective-permute-done.15.pre_b = bf16[256,1024]{1,0:T(8,128)(2,1)S(1)} collective-permute-done((bf16[256,1024]{1,0:T(8,128)(2,1)S(1)}, bf16[256,1024]{1,0:T(8,128)(2,1)S(1)}, u32[]{:S(2)}, u32[]{:S(2)}) %collective-permute-start.15) | collective-permute-done | bytes 524320 | tf_op jit(solution)/shard_map/ppermute | solution.py:42
  168.4 9.8 %collective-permute-done.21.cot_b = bf16[256,1024]{1,0:T(8,128)(2,1)S(1)} collective-permute-done((bf16[256,1024]{1,0:T(8,128)(2,1)S(1)}, bf16[256,1024]{1,0:T(8,128)(2,1)S(1)}, u32[]{:S(2)}, u32[]{:S(2)}) %collective-permute-start.21) | collective-permute-done | bytes 524320 | tf_op jit(solution)/shard_map/ppermute | solution.py:42
  178.1 2.8 %shard_map.108 = (bf16[256,1024]{1,0:T(8,128)(2,1)S(1)}, bf16[256,1024]{1,0:T(8,128)(2,1)S(1)}, bf16[2,128,1792]{2,1,0:T(8,128)(2,1)S(1)}, bf16[2,128,1792]{2,1,0:T(8,128)(2,1)S(1)}) custom-call(s32[4,1,128]{2,1,0:T(1,128)S(1)} %bitcast.67, bf16[256,1024]{1,0:T(8,128)(2,1)S(1)} %get-tuple-element.39.pre_a, ...), custom_call_target="tpu_custom_call" | custom-call | flops 1056964608 | bytes 8650752 | tf_op jit(solution)/shard_map/pallas_call | solution.py:172
  182.9 6.4 %collective-permute-done.43.pre_b = bf16[256,1024]{1,0:T(8,128)(2,1)S(1)} collective-permute-done((bf16[256,1024]{1,0:T(8,128)(2,1)S(1)}, bf16[256,1024]{1,0:T(8,128)(2,1)S(1)}, u32[]{:S(2)}, u32[]{:S(2)}) %collective-permute-start.43) | collective-permute-done | bytes 524320 | tf_op jit(solution)/shard_map/ppermute | solution.py:42
  189.4 8.6 %collective-permute-done.49.cot_b = bf16[256,1024]{1,0:T(8,128)(2,1)S(1)} collective-permute-done((bf16[256,1024]{1,0:T(8,128)(2,1)S(1)}, bf16[256,1024]{1,0:T(8,128)(2,1)S(1)}, u32[]{:S(2)}, u32[]{:S(2)}) %collective-permute-start.49) | collective-permute-done | bytes 524320 | tf_op jit(solution)/shard_map/ppermute | solution.py:42
  198.0 2.8 %shard_map.114 = (bf16[256,1024]{1,0:T(8,128)(2,1)S(1)}, bf16[256,1024]{1,0:T(8,128)(2,1)S(1)}, bf16[2,128,1792]{2,1,0:T(8,128)(2,1)S(1)}, bf16[2,128,1792]{2,1,0:T(8,128)(2,1)S(1)}) custom-call(s32[4,1,128]{2,1,0:T(1,128)S(1)} %bitcast.64, bf16[256,1024]{1,0:T(8,128)(2,1)S(1)} %get-tuple-element.47.pre_a, ...), custom_call_target="tpu_custom_call" | custom-call | flops 1056964608 | bytes 8650752 | tf_op jit(solution)/shard_map/pallas_call | solution.py:172
  205.8 18.6 %collective-permute-done.51 = bf16[128,1792]{1,0:T(8,128)(2,1)S(1)} collective-permute-done((bf16[128,1792]{1,0:T(8,128)(2,1)S(1)}, bf16[128,1792]{1,0:T(8,128)(2,1)S(1)}, u32[]{:S(2)}, u32[]{:S(2)}) %collective-permute-start.51) | collective-permute-done | bytes 458784 | tf_op jit(solution)/shard_map/ppermute | solution.py:34
  225.8 8.0 %collective-permute-done.23 = bf16[128,1792]{1,0:T(8,128)(2,1)S(1)} collective-permute-done((bf16[128,1792]{1,0:T(8,128)(2,1)S(1)}, bf16[128,1792]{1,0:T(8,128)(2,1)S(1)}, u32[]{:S(2)}, u32[]{:S(2)}) %collective-permute-start.23) | collective-permute-done | bytes 458784 | tf_op jit(solution)/shard_map/ppermute | solution.py:34
  235.2 3.0 %collective-permute-done.52 = bf16[128,1792]{1,0:T(8,128)(2,1)S(1)} collective-permute-done((bf16[128,1792]{1,0:T(8,128)(2,1)S(1)}, bf16[128,1792]{1,0:T(8,128)(2,1)S(1)}, u32[]{:S(2)}, u32[]{:S(2)}) %collective-permute-start.52) | collective-permute-done | bytes 458784 | tf_op jit(solution)/shard_map/ppermute | solution.py:30
  238.3 3.5 %collective-permute-start.53 = (bf16[128,1792]{1,0:T(8,128)(2,1)S(1)}, bf16[128,1792]{1,0:T(8,128)(2,1)S(1)}, u32[]{:S(2)}, u32[]{:S(2)}) collective-permute-start(bf16[128,1792]{1,0:T(8,128)(2,1)S(1)} %add_convert_fusion.6), channel_id=1, source_target_pairs={{4,8},{5,9},{6,10},{7,11},{8,4},{9,5},{10,6},{11,7},{20,24},{21,25... | collective-permute-start | bytes 1376264 | tf_op jit(solution)/shard_map/ppermute | solution.py:30
  241.8 6.2 %collective-permute-done.24 = bf16[128,1792]{1,0:T(8,128)(2,1)S(1)} collective-permute-done((bf16[128,1792]{1,0:T(8,128)(2,1)S(1)}, bf16[128,1792]{1,0:T(8,128)(2,1)S(1)}, u32[]{:S(2)}, u32[]{:S(2)}) %collective-permute-start.24) | collective-permute-done | bytes 458784 | tf_op jit(solution)/shard_map/ppermute | solution.py:30
  248.1 3.5 %collective-permute-start.25 = (bf16[128,1792]{1,0:T(8,128)(2,1)S(1)}, bf16[128,1792]{1,0:T(8,128)(2,1)S(1)}, u32[]{:S(2)}, u32[]{:S(2)}) collective-permute-start(bf16[128,1792]{1,0:T(8,128)(2,1)S(1)} %add_convert_fusion.7), channel_id=1, source_target_pairs={{4,8},{5,9},{6,10},{7,11},{8,4},{9,5},{10,6},{11,7},{20,24},{21,25... | collective-permute-start | bytes 1376264 | tf_op jit(solution)/shard_map/ppermute | solution.py:30
  251.9 6.3 %shard_map.115 = bf16[1792,1024]{1,0:T(8,128)(2,1)} custom-call(bf16[256,1792]{1,0:T(8,128)(2,1)S(1)} %get-tuple-element.51.refs_0_, bf16[256,1792]{1,0:T(8,128)(2,1)S(1)} %get-tuple-element.52.refs_1_, bf16[256,1792]{1,0:T(8,128)(2,1)S(1)} %get-tuple-element.53.refs_2_, bf16[256,1792]{1,0:T(8,128)(2,1)S(1)} %get-tuple-element.54.refs_3_, ...), custom_call_target="tpu_custom_call" | custom-call | flops 3758096384 | bytes 9437184 | tf_op jit(solution)/shard_map/pallas_call | solution.py:209
  258.2 6.3 %shard_map.116 = bf16[1792,1024]{1,0:T(8,128)(2,1)} custom-call(bf16[256,1792]{1,0:T(8,128)(2,1)S(1)} %get-tuple-element.59.refs_0_, bf16[256,1792]{1,0:T(8,128)(2,1)S(1)} %get-tuple-element.60.refs_1_, bf16[256,1792]{1,0:T(8,128)(2,1)S(1)} %get-tuple-element.61.refs_2_, bf16[256,1792]{1,0:T(8,128)(2,1)S(1)} %get-tuple-element.62.refs_3_, ...), custom_call_target="tpu_custom_call" | custom-call | flops 3758096384 | bytes 9437184 | tf_op jit(solution)/shard_map/pallas_call | solution.py:209
  (140 shorter events, 63.2 us)
Async XLA Ops:
  0.6 41.9 %collective-permute-start.26 = (bf16[128,1792]{1,0:T(8,128)(2,1)}, bf16[128,1792]{1,0:T(8,128)(2,1)S(1)}, u32[]{:S(2)}, u32[]{:S(2)}) collective-permute-start(bf16[128,1792]{1,0:T(8,128)(2,1)} %b0.2), channel_id=1, source_target_pairs={{0,4},{1,5},{2,6},{3,7},{4,0},{5,1},{6,2},{7,3},{8,12},{9,13},{10,... | collective-permute-start | bytes 1376264 | tf_op jit(solution)/shard_map/ppermute | solution.py:30
  0.7 43.9 %collective-permute-start.10 = (bf16[128,1792]{1,0:T(8,128)(2,1)}, bf16[128,1792]{1,0:T(8,128)(2,1)}, u32[]{:S(2)}, u32[]{:S(2)}) collective-permute-start(bf16[128,1792]{1,0:T(8,128)(2,1)} %b0.2), channel_id=1, source_target_pairs={{4,8},{5,9},{6,10},{7,11},{8,4},{9,5},{10,6},{11,7},{20,24},{21,25... | collective-permute-start | bytes 1376264 | tf_op jit(solution)/shard_map/ppermute | solution.py:30
  5.8 40.8 %collective-permute-start = (bf16[128,1792]{1,0:T(8,128)(2,1)}, bf16[128,1792]{1,0:T(8,128)(2,1)S(1)}, u32[]{:S(2)}, u32[]{:S(2)}) collective-permute-start(bf16[128,1792]{1,0:T(8,128)(2,1)} %b0.2), channel_id=1, source_target_pairs={{0,1},{1,0},{2,3},{3,2},{4,5},{5,4},{6,7},{7,6},{8,9},{9,8},{10,11... | collective-permute-start | bytes 1376264 | tf_op jit(solution)/shard_map/ppermute | solution.py:38
  5.8 34.9 %collective-permute-start.1 = (bf16[128,1792]{1,0:T(8,128)(2,1)}, bf16[128,1792]{1,0:T(8,128)(2,1)S(1)}, u32[]{:S(2)}, u32[]{:S(2)}) collective-permute-start(bf16[128,1792]{1,0:T(8,128)(2,1)} %b0.2), channel_id=1, source_target_pairs={{0,2},{1,3},{2,0},{3,1},{4,6},{5,7},{6,4},{7,5},{8,10},{9,11},{10,... | collective-permute-start | bytes 1376264 | tf_op jit(solution)/shard_map/ppermute | solution.py:34
  7.4 39.2 %collective-permute-start.5 = (bf16[128,1792]{1,0:T(8,128)(2,1)}, bf16[128,1792]{1,0:T(8,128)(2,1)S(1)}, u32[]{:S(2)}, u32[]{:S(2)}) collective-permute-start(bf16[128,1792]{1,0:T(8,128)(2,1)} %b0.3), channel_id=1, source_target_pairs={{0,2},{1,3},{2,0},{3,1},{4,6},{5,7},{6,4},{7,5},{8,10},{9,11},{10,... | collective-permute-start | bytes 1376264 | tf_op jit(solution)/shard_map/ppermute | solution.py:34
  42.5 19.9 %collective-permute-start.31 = (bf16[128,1792]{1,0:T(8,128)(2,1)}, bf16[128,1792]{1,0:T(8,128)(2,1)S(1)}, u32[]{:S(2)}, u32[]{:S(2)}) collective-permute-start(bf16[128,1792]{1,0:T(8,128)(2,1)} %b0.3), channel_id=1, source_target_pairs={{0,4},{1,5},{2,6},{3,7},{4,0},{5,1},{6,2},{7,3},{8,12},{9,13},{10,... | collective-permute-start | bytes 1376264 | tf_op jit(solution)/shard_map/ppermute | solution.py:30
  44.6 17.8 %collective-permute-start.16 = (bf16[128,1792]{1,0:T(8,128)(2,1)}, bf16[128,1792]{1,0:T(8,128)(2,1)}, u32[]{:S(2)}, u32[]{:S(2)}) collective-permute-start(bf16[128,1792]{1,0:T(8,128)(2,1)} %b0.3), channel_id=1, source_target_pairs={{4,8},{5,9},{6,10},{7,11},{8,4},{9,5},{10,6},{11,7},{20,24},{21,25... | collective-permute-start | bytes 1376264 | tf_op jit(solution)/shard_map/ppermute | solution.py:30
  46.6 18.2 %collective-permute-start.11 = (bf16[128,1792]{1,0:T(8,128)(2,1)}, bf16[128,1792]{1,0:T(8,128)(2,1)}, u32[]{:S(2)}, u32[]{:S(2)}) collective-permute-start(bf16[128,1792]{1,0:T(8,128)(2,1)} %collective-permute-done.10), channel_id=1, source_target_pairs={{4,0},{5,1},{6,2},{7,3},{8,12},{9,13},{10,14},{11,15},{20,16},{21,... | collective-permute-start | bytes 1376264 | tf_op jit(solution)/shard_map/ppermute | solution.py:30
  59.1 21.0 %collective-permute-start.27 = (bf16[128,1792]{1,0:T(8,128)(2,1)S(1)}, bf16[128,1792]{1,0:T(8,128)(2,1)S(1)}, u32[]{:S(2)}, u32[]{:S(2)}) collective-permute-start(bf16[128,1792]{1,0:T(8,128)(2,1)S(1)} %collective-permute-done.26.b0), channel_id=1, source_target_pairs={{0,1},{1,0},{2,3},{3,2},{4,5},{5,4},{6,7},{7,6},{8,9},{9,8},{10,11... | collective-permute-start | bytes 1376264 | tf_op jit(solution)/shard_map/ppermute | solution.py:38
  62.4 21.9 %collective-permute-start.28 = (bf16[128,1792]{1,0:T(8,128)(2,1)S(1)}, bf16[128,1792]{1,0:T(8,128)(2,1)S(1)}, u32[]{:S(2)}, u32[]{:S(2)}) collective-permute-start(bf16[128,1792]{1,0:T(8,128)(2,1)S(1)} %collective-permute-done.26.b0), channel_id=1, source_target_pairs={{0,2},{1,3},{2,0},{3,1},{4,6},{5,7},{6,4},{7,5},{8,10},{9,11},{10,... | collective-permute-start | bytes 1376264 | tf_op jit(solution)/shard_map/ppermute | solution.py:34
  62.4 17.2 %collective-permute-start.44 = (bf16[128,1792]{1,0:T(8,128)(2,1)S(1)}, bf16[128,1792]{1,0:T(8,128)(2,1)S(1)}, u32[]{:S(2)}, u32[]{:S(2)}) collective-permute-start(bf16[128,1792]{1,0:T(8,128)(2,1)S(1)} %collective-permute-done.31.b0), channel_id=1, source_target_pairs={{4,8},{5,9},{6,10},{7,11},{8,4},{9,5},{10,6},{11,7},{20,24},{21,25... | collective-permute-start | bytes 1376264 | tf_op jit(solution)/shard_map/ppermute | solution.py:30
  81.4 19.2 %collective-permute-start.45 = (bf16[128,1792]{1,0:T(8,128)(2,1)S(1)}, bf16[128,1792]{1,0:T(8,128)(2,1)S(1)}, u32[]{:S(2)}, u32[]{:S(2)}) collective-permute-start(bf16[128,1792]{1,0:T(8,128)(2,1)S(1)} %collective-permute-done.44), channel_id=1, source_target_pairs={{4,0},{5,1},{6,2},{7,3},{8,12},{9,13},{10,14},{11,15},{20,16},{21,... | collective-permute-start | bytes 1376264 | tf_op jit(solution)/shard_map/ppermute | solution.py:30
  84.2 19.7 %collective-permute-start.12 = (bf16[128,1792]{1,0:T(8,128)(2,1)S(1)}, bf16[128,1792]{1,0:T(8,128)(2,1)S(1)}, u32[]{:S(2)}, u32[]{:S(2)}) collective-permute-start(bf16[128,1792]{1,0:T(8,128)(2,1)S(1)} %broadcast_select_fusion.3.b0), channel_id=1, source_target_pairs={{0,1},{1,0},{2,3},{3,2},{4,5},{5,4},{6,7},{7,6},{8,9},{9,8},{10,11... | collective-permute-start | bytes 1376264 | tf_op jit(solution)/shard_map/ppermute | solution.py:38
  84.3 20.1 %collective-permute-start.13 = (bf16[128,1792]{1,0:T(8,128)(2,1)S(1)}, bf16[128,1792]{1,0:T(8,128)(2,1)S(1)}, u32[]{:S(2)}, u32[]{:S(2)}) collective-permute-start(bf16[128,1792]{1,0:T(8,128)(2,1)S(1)} %broadcast_select_fusion.3.b0), channel_id=1, source_target_pairs={{0,2},{1,3},{2,0},{3,1},{4,6},{5,7},{6,4},{7,5},{8,10},{9,11},{10,... | collective-permute-start | bytes 1376264 | tf_op jit(solution)/shard_map/ppermute | solution.py:34
  104.0 23.7 %collective-permute-start.7 = (bf16[256,1024]{1,0:T(8,128)(2,1)S(1)}, bf16[256,1024]{1,0:T(8,128)(2,1)S(1)}, u32[]{:S(2)}, u32[]{:S(2)}) collective-permute-start(bf16[256,1024]{1,0:T(8,128)(2,1)S(1)} %get-tuple-element.36.cot_a), channel_id=1, source_target_pairs={{0,16},{16,0},{1,17},{17,1},{2,18},{18,2},{3,19},{19,3},{4,20},{20... | collective-permute-start | bytes 1572872 | tf_op jit(solution)/shard_map/ppermute | solution.py:42
  104.4 24.7 %collective-permute-start.40 = (bf16[128,1792]{1,0:T(8,128)(2,1)S(1)}, bf16[128,1792]{1,0:T(8,128)(2,1)S(1)}, u32[]{:S(2)}, u32[]{:S(2)}) collective-permute-start(bf16[128,1792]{1,0:T(8,128)(2,1)S(1)} %broadcast_select_fusion.1.b0), channel_id=1, source_target_pairs={{0,1},{1,0},{2,3},{3,2},{4,5},{5,4},{6,7},{7,6},{8,9},{9,8},{10,11... | collective-permute-start | bytes 1376264 | tf_op jit(solution)/shard_map/ppermute | solution.py:38
  104.5 27.0 %collective-permute-start.41 = (bf16[128,1792]{1,0:T(8,128)(2,1)S(1)}, bf16[128,1792]{1,0:T(8,128)(2,1)S(1)}, u32[]{:S(2)}, u32[]{:S(2)}) collective-permute-start(bf16[128,1792]{1,0:T(8,128)(2,1)S(1)} %broadcast_select_fusion.1.b0), channel_id=1, source_target_pairs={{0,2},{1,3},{2,0},{3,1},{4,6},{5,7},{6,4},{7,5},{8,10},{9,11},{10,... | collective-permute-start | bytes 1376264 | tf_op jit(solution)/shard_map/ppermute | solution.py:34
  114.0 19.3 %collective-permute-start.47 = (bf16[128,1792]{1,0:T(8,128)(2,1)S(1)}, bf16[128,1792]{1,0:T(8,128)(2,1)S(1)}, u32[]{:S(2)}, u32[]{:S(2)}) collective-permute-start(bf16[128,1792]{1,0:T(8,128)(2,1)S(1)} %broadcast_select_fusion.b0), channel_id=1, source_target_pairs={{0,2},{1,3},{2,0},{3,1},{4,6},{5,7},{6,4},{7,5},{8,10},{9,11},{10,... | collective-permute-start | bytes 1376264 | tf_op jit(solution)/shard_map/ppermute | solution.py:34
  117.2 19.0 %collective-permute-start.14 = (bf16[128,1792]{1,0:T(8,128)(2,1)S(1)}, bf16[128,1792]{1,0:T(8,128)(2,1)S(1)}, u32[]{:S(2)}, u32[]{:S(2)}) collective-permute-start(bf16[128,1792]{1,0:T(8,128)(2,1)S(1)} %collective-permute-done.13.b2), channel_id=1, source_target_pairs={{0,1},{1,0},{2,3},{3,2},{4,5},{5,4},{6,7},{7,6},{8,9},{9,8},{10,11... | collective-permute-start | bytes 1376264 | tf_op jit(solution)/shard_map/ppermute | solution.py:38
  131.5 20.5 %collective-permute-start.35 = (bf16[256,1024]{1,0:T(8,128)(2,1)S(1)}, bf16[256,1024]{1,0:T(8,128)(2,1)S(1)}, u32[]{:S(2)}, u32[]{:S(2)}) collective-permute-start(bf16[256,1024]{1,0:T(8,128)(2,1)S(1)} %get-tuple-element.44.cot_a), channel_id=1, source_target_pairs={{0,16},{16,0},{1,17},{17,1},{2,18},{18,2},{3,19},{19,3},{4,20},{20... | collective-permute-start | bytes 1572872 | tf_op jit(solution)/shard_map/ppermute | solution.py:42
  133.3 20.2 %collective-permute-start.42 = (bf16[128,1792]{1,0:T(8,128)(2,1)S(1)}, bf16[128,1792]{1,0:T(8,128)(2,1)S(1)}, u32[]{:S(2)}, u32[]{:S(2)}) collective-permute-start(bf16[128,1792]{1,0:T(8,128)(2,1)S(1)} %collective-permute-done.41.b2), channel_id=1, source_target_pairs={{0,1},{1,0},{2,3},{3,2},{4,5},{5,4},{6,7},{7,6},{8,9},{9,8},{10,11... | collective-permute-start | bytes 1376264 | tf_op jit(solution)/shard_map/ppermute | solution.py:38
  136.2 44.9 %collective-permute-start.8 = (bf16[2,128,1792]{2,1,0:T(8,128)(2,1)S(1)}, bf16[2,128,1792]{2,1,0:T(8,128)(2,1)S(1)}, u32[]{:S(2)}, u32[]{:S(2)}) collective-permute-start(bf16[2,128,1792]{2,1,0:T(8,128)(2,1)S(1)} %get-tuple-element.38), channel_id=1, source_target_pairs={{0,1},{1,0},{2,3},{3,2},{4,5},{5,4},{6,7},{7,6},{8,9},{9,8},{10,11... | collective-permute-start | bytes 2752520 | tf_op jit(solution)/shard_map/ppermute | solution.py:38
  139.1 20.2 %collective-permute-start.46 = (bf16[128,1792]{1,0:T(8,128)(2,1)S(1)}, bf16[128,1792]{1,0:T(8,128)(2,1)S(1)}, u32[]{:S(2)}, u32[]{:S(2)}) collective-permute-start(bf16[128,1792]{1,0:T(8,128)(2,1)S(1)} %broadcast_select_fusion.b0), channel_id=1, source_target_pairs={{0,1},{1,0},{2,3},{3,2},{4,5},{5,4},{6,7},{7,6},{8,9},{9,8},{10,11... | collective-permute-start | bytes 1376264 | tf_op jit(solution)/shard_map/ppermute | solution.py:38
  153.5 24.6 %collective-permute-start.21 = (bf16[256,1024]{1,0:T(8,128)(2,1)S(1)}, bf16[256,1024]{1,0:T(8,128)(2,1)S(1)}, u32[]{:S(2)}, u32[]{:S(2)}) collective-permute-start(bf16[256,1024]{1,0:T(8,128)(2,1)S(1)} %get-tuple-element.40.cot_a), channel_id=1, source_target_pairs={{0,16},{16,0},{1,17},{17,1},{2,18},{18,2},{3,19},{19,3},{4,20},{20... | collective-permute-start | bytes 1572872 | tf_op jit(solution)/shard_map/ppermute | solution.py:42
  159.2 41.6 %collective-permute-start.36 = (bf16[2,128,1792]{2,1,0:T(8,128)(2,1)S(1)}, bf16[2,128,1792]{2,1,0:T(8,128)(2,1)S(1)}, u32[]{:S(2)}, u32[]{:S(2)}) collective-permute-start(bf16[2,128,1792]{2,1,0:T(8,128)(2,1)S(1)} %get-tuple-element.46), channel_id=1, source_target_pairs={{0,1},{1,0},{2,3},{3,2},{4,5},{5,4},{6,7},{7,6},{8,9},{9,8},{10,11... | collective-permute-start | bytes 2752520 | tf_op jit(solution)/shard_map/ppermute | solution.py:38
  159.3 30.0 %collective-permute-start.43 = (bf16[256,1024]{1,0:T(8,128)(2,1)S(1)}, bf16[256,1024]{1,0:T(8,128)(2,1)S(1)}, u32[]{:S(2)}, u32[]{:S(2)}) collective-permute-start(bf16[256,1024]{1,0:T(8,128)(2,1)S(1)} %get-tuple-element.47.pre_a), channel_id=1, source_target_pairs={{0,16},{16,0},{1,17},{17,1},{2,18},{18,2},{3,19},{19,3},{4,20},{20... | collective-permute-start | bytes 1572872 | tf_op jit(solution)/shard_map/ppermute | solution.py:42
  166.9 31.1 %collective-permute-start.49 = (bf16[256,1024]{1,0:T(8,128)(2,1)S(1)}, bf16[256,1024]{1,0:T(8,128)(2,1)S(1)}, u32[]{:S(2)}, u32[]{:S(2)}) collective-permute-start(bf16[256,1024]{1,0:T(8,128)(2,1)S(1)} %get-tuple-element.48.cot_a), channel_id=1, source_target_pairs={{0,16},{16,0},{1,17},{17,1},{2,18},{18,2},{3,19},{19,3},{4,20},{20... | collective-permute-start | bytes 1572872 | tf_op jit(solution)/shard_map/ppermute | solution.py:42
  180.9 21.8 %collective-permute-start.22 = (bf16[2,128,1792]{2,1,0:T(8,128)(2,1)S(1)}, bf16[2,128,1792]{2,1,0:T(8,128)(2,1)S(1)}, u32[]{:S(2)}, u32[]{:S(2)}) collective-permute-start(bf16[2,128,1792]{2,1,0:T(8,128)(2,1)S(1)} %get-tuple-element.42), channel_id=1, source_target_pairs={{0,1},{1,0},{2,3},{3,2},{4,5},{5,4},{6,7},{7,6},{8,9},{9,8},{10,11... | collective-permute-start | bytes 2752520 | tf_op jit(solution)/shard_map/ppermute | solution.py:38
  181.3 83.3 %collective-permute-start.9 = (bf16[128,1792]{1,0:T(8,128)(2,1)S(1)}, bf16[128,1792]{1,0:T(8,128)(2,1)S(1)}, u32[]{:S(2)}, u32[]{:S(2)}) collective-permute-start(bf16[128,1792]{1,0:T(8,128)(2,1)S(1)} %slice_bitcast_fusion.6), channel_id=1, source_target_pairs={{0,2},{1,3},{2,0},{3,1},{4,6},{5,7},{6,4},{7,5},{8,10},{9,11},{10,... | collective-permute-start | bytes 1376264 | tf_op jit(solution)/shard_map/ppermute | solution.py:34
  201.1 50.5 %collective-permute-start.37 = (bf16[128,1792]{1,0:T(8,128)(2,1)S(1)}, bf16[128,1792]{1,0:T(8,128)(2,1)S(1)}, u32[]{:S(2)}, u32[]{:S(2)}) collective-permute-start(bf16[128,1792]{1,0:T(8,128)(2,1)S(1)} %slice_bitcast_fusion.2), channel_id=1, source_target_pairs={{0,2},{1,3},{2,0},{3,1},{4,6},{5,7},{6,4},{7,5},{8,10},{9,11},{10,... | collective-permute-start | bytes 1376264 | tf_op jit(solution)/shard_map/ppermute | solution.py:34
  203.6 20.8 %collective-permute-start.51 = (bf16[128,1792]{1,0:T(8,128)(2,1)S(1)}, bf16[128,1792]{1,0:T(8,128)(2,1)S(1)}, u32[]{:S(2)}, u32[]{:S(2)}) collective-permute-start(bf16[128,1792]{1,0:T(8,128)(2,1)S(1)} %slice_bitcast_fusion), channel_id=1, source_target_pairs={{0,2},{1,3},{2,0},{3,1},{4,6},{5,7},{6,4},{7,5},{8,10},{9,11},{10,... | collective-permute-start | bytes 1376264 | tf_op jit(solution)/shard_map/ppermute | solution.py:34
  205.2 28.5 %collective-permute-start.23 = (bf16[128,1792]{1,0:T(8,128)(2,1)S(1)}, bf16[128,1792]{1,0:T(8,128)(2,1)S(1)}, u32[]{:S(2)}, u32[]{:S(2)}) collective-permute-start(bf16[128,1792]{1,0:T(8,128)(2,1)S(1)} %slice_bitcast_fusion.4), channel_id=1, source_target_pairs={{0,2},{1,3},{2,0},{3,1},{4,6},{5,7},{6,4},{7,5},{8,10},{9,11},{10,... | collective-permute-start | bytes 1376264 | tf_op jit(solution)/shard_map/ppermute | solution.py:34
  (28 other events, 339.9 us)

commit v3 on v2

v3 whole, which is shorter than its diff:
```python
import functools

import jax
import jax.numpy as jnp
from jax import lax
from jax.experimental import pallas as pl
from jax.experimental.pallas import tpu as pltpu
from jax.sharding import PartitionSpec as P

F32 = jnp.float32
BF16 = jnp.bfloat16
CONTRACT_ROWS = (((0,), (0,)), ((), ()))
CONTRACT_LAST = (((1,), (1,)), ((), ()))

NO_COST = pl.CostEstimate(flops=0, bytes_accessed=0, transcendentals=0)

NZ, NX, NC = 4, 2, 2


def dot_f32(left, right, dims=(((1,), (0,)), ((), ()))):
    return lax.dot_general(left, right, dims, preferred_element_type=F32)


def along_z(value, pairs):
    perm = [
        ((a * NX + x) * NC + c, (b * NX + x) * NC + c)
        for a, b in pairs
        for x in range(NX)
        for c in range(NC)
    ]
    return lax.ppermute(value, "expert", perm)


def swap_x(value):
    return lax.ppermute(value, "expert", [(i, i ^ NC) for i in range(NZ * NX * NC)])


def swap_core(value):
    return lax.ppermute(value, "expert", [(i, i ^ 1) for i in range(NZ * NX * NC)])


def swap_dp(value):
    return lax.ppermute(value, "dp", [(0, 1), (1, 0)])


NEIGHBOUR = ((0, 1), (1, 0), (2, 3), (3, 2))
MIDDLE = ((1, 2), (2, 1))
OUTWARD = ((1, 0), (2, 3))
INWARD = ((0, 1), (3, 2))


def tie(value, *earlier):
    return lax.optimization_barrier((value, earlier))[0]


def add(left, right):
    return (left.astype(F32) + right.astype(F32)).astype(BF16)


def placing_of(slot_row, slots):
    return slot_row == lax.broadcasted_iota(jnp.int32, (slots, slot_row.shape[1]), 0)


LANES = 128


def with_routing(tokens, expert_ids, gate_levels):
    half = LANES // 2
    room = ((0, 0), (0, half - expert_ids.shape[1]))
    parts = [tokens, jnp.pad(expert_ids, room).astype(BF16), jnp.pad(gate_levels, room).astype(BF16)]
    return jnp.concatenate(parts, axis=1)


def read_routing(meta, own, limit, top_count):
    tok_rows = meta.shape[0]
    ids = meta.astype(F32)
    levels = pltpu.roll(ids, LANES // 2, 1)
    choice = lax.broadcasted_iota(jnp.int32, ids.shape, 1) < top_count
    named = choice & (ids == own)
    ones = jnp.ones((8, LANES), BF16)
    match = dot_f32(ones, jnp.where(named, 1.0, 0.0).astype(BF16), CONTRACT_LAST)
    level = dot_f32(ones, jnp.where(named, levels, 0.0).astype(BF16), CONTRACT_LAST)
    total = dot_f32(ones, jnp.where(choice, levels, 0.0).astype(BF16), CONTRACT_LAST)
    square = (tok_rows, tok_rows)
    before = lax.broadcasted_iota(jnp.int32, square, 0) < lax.broadcasted_iota(jnp.int32, square, 1)
    rank = dot_f32(match.astype(BF16), jnp.where(before, 1.0, 0.0).astype(BF16))
    kept = (match > 0.5) & (rank < limit)
    return jnp.where(kept, rank, -1.0).astype(jnp.int32), level / total


def add_up(total, part_ref, product):
    step = pl.program_id(0)

    @pl.when(step == 0)
    def _():
        total[...] = product

    @pl.when(step > 0)
    def _():
        total[...] += product

    @pl.when(step == pl.num_programs(0) - 1)
    def _():
        part_ref[...] = total[...].astype(BF16)


def tokens_kernel(top_count, slots, own_ref, m0, m1, m2, m3, b0, b1, b2, b3, weight_ref, rows_ref, part_ref, slot_ref, gate_ref, total):
    @pl.when(pl.program_id(0) == 0)
    def _():
        own = own_ref[0].astype(F32)
        limit = own_ref[1].astype(F32)
        for index, meta in enumerate((m0, m1, m2, m3)):
            slot, gate = read_routing(meta[...], own, limit, top_count)
            slot_ref[index] = slot
            gate_ref[index] = gate

    for index, block in enumerate((b0, b1, b2, b3)):
        hit = placing_of(slot_ref[index, 0:1, :], slots)
        picked = dot_f32(jnp.where(hit, 1.0, 0.0).astype(BF16), block[...])
        rows_ref[index * slots : (index + 1) * slots, :] = picked.astype(BF16)
    add_up(total, part_ref, dot_f32(rows_ref[...], weight_ref[...]))


def cotangent_kernel(slots, slot_ref, gate_ref, b0, b1, b2, b3, weight_ref, rows_ref, part_ref, total):
    for index, block in enumerate((b0, b1, b2, b3)):
        hit = placing_of(slot_ref[index, 0:1, :], slots)
        picked = dot_f32(jnp.where(hit, 1.0, 0.0).astype(BF16), block[...])
        gate = jnp.sum(jnp.where(hit, gate_ref[index, 0:1, :], 0.0), axis=1, keepdims=True)
        rows_ref[index * slots : (index + 1) * slots, :] = (picked * gate).astype(BF16)
    add_up(total, part_ref, dot_f32(rows_ref[...], weight_ref[...]))


def front_specs(tok_rows, width, hidden, rows):
    tile = width // 2
    table = pl.BlockSpec((4, 8, tok_rows), lambda k: (0, 0, 0))
    blocks = [pl.BlockSpec((tok_rows, tile), lambda k: (0, k))] * 4
    weight = pl.BlockSpec((tile, hidden), lambda k: (k, 0))
    outs = [
        pl.BlockSpec((rows, tile), lambda k: (0, k)),
        pl.BlockSpec((rows, hidden), lambda k: (0, 0)),
    ]
    shapes = [jax.ShapeDtypeStruct((rows, width), BF16), jax.ShapeDtypeStruct((rows, hidden), BF16)]
    rest = dict(
        grid=(width // tile,),
        scratch_shapes=[pltpu.VMEM((rows, hidden), F32)],
        compiler_params=pltpu.CompilerParams(vmem_limit_bytes=24 * 1024 * 1024),
        cost_estimate=NO_COST,
    )
    return table, blocks, weight, outs, shapes, rest


def front_tokens(blocks, own, weight, slots, top_count):
    tok_rows = blocks[0].shape[0]
    width, hidden = weight.shape
    table, block_specs, weight_spec, outs, shapes, rest = front_specs(tok_rows, width, hidden, 4 * slots)
    meta = pl.BlockSpec((tok_rows, LANES), lambda k: (0, width // LANES))
    return pl.pallas_call(
        functools.partial(tokens_kernel, top_count, slots),
        in_specs=[pl.BlockSpec(memory_space=pltpu.SMEM)] + [meta] * 4 + block_specs + [weight_spec],
        out_specs=outs + [table, table],
        out_shape=shapes
        + [
            jax.ShapeDtypeStruct((4, 8, tok_rows), jnp.int32),
            jax.ShapeDtypeStruct((4, 8, tok_rows), F32),
        ],
        **rest,
    )(own, *blocks, *blocks, weight)


def front_cotangent(blocks, tables, weight, slots):
    tok_rows = blocks[0].shape[0]
    width, hidden = weight.shape
    table, block_specs, weight_spec, outs, shapes, rest = front_specs(tok_rows, width, hidden, 4 * slots)
    return pl.pallas_call(
        functools.partial(cotangent_kernel, slots),
        in_specs=[table, table] + block_specs + [weight_spec],
        out_specs=outs,
        out_shape=shapes,
        **rest,
    )(*tables, *blocks, weight)


def back_kernel(slots, slot_ref, pre_a, pre_b, cot_a, cot_b, weight_ref, act_ref, keep_ref, send_ref):
    @pl.when(pl.program_id(0) == 0)
    def _():
        preact = pre_a[...].astype(F32) + pre_b[...].astype(F32)
        hidden_cot = cot_a[...].astype(F32) + cot_b[...].astype(F32)
        sigmoid = jax.nn.sigmoid(preact)
        act_ref[...] = (hidden_cot * (sigmoid * (1.0 + preact * (1.0 - sigmoid)))).astype(BF16)

    back = dot_f32(act_ref[...], weight_ref[...], CONTRACT_LAST).astype(BF16)
    for index in range(4):
        hit = placing_of(slot_ref[index, 0:1, :], slots)
        placing = jnp.where(hit, 1.0, 0.0).astype(BF16)
        spread = dot_f32(placing, back[index * slots : (index + 1) * slots], CONTRACT_ROWS)
        out_ref = send_ref if index % 2 else keep_ref
        out_ref[index // 2] = spread.astype(BF16)


def back(slot_of, parts, weight, slots):
    tok_rows = slot_of.shape[2]
    width, hidden = weight.shape
    rows = 4 * slots
    tile = width // 2
    full = pl.BlockSpec((rows, hidden), lambda n: (0, 0))
    spread = pl.BlockSpec((2, tok_rows, tile), lambda n: (0, 0, n))
    return pl.pallas_call(
        functools.partial(back_kernel, slots),
        grid=(width // tile,),
        in_specs=[pl.BlockSpec((4, 8, tok_rows), lambda n: (0, 0, 0))]
        + [full] * 4
        + [pl.BlockSpec((tile, hidden), lambda n: (n, 0))],
        out_specs=[full, spread, spread],
        out_shape=[
            jax.ShapeDtypeStruct((rows, hidden), BF16),
            jax.ShapeDtypeStruct((2, tok_rows, width), BF16),
            jax.ShapeDtypeStruct((2, tok_rows, width), BF16),
        ],
        compiler_params=pltpu.CompilerParams(vmem_limit_bytes=32 * 1024 * 1024),
        cost_estimate=NO_COST,
    )(slot_of, *parts, weight)


def up_grad_kernel(*refs):
    count = (len(refs) - 1) // 2
    total = None
    for left, right in zip(refs[:count], refs[count:-1]):
        term = dot_f32(left[...], right[...], CONTRACT_ROWS)
        total = term if total is None else total + term
    refs[-1][...] = total.astype(BF16)


def down_grad_kernel(*refs):
    count = (len(refs) - 2) // 3
    out_ref, hidden_ref = refs[-2:]

    @pl.when(pl.program_id(0) == 0)
    def _():
        for index, (first, second) in enumerate(zip(refs[count : 2 * count], refs[2 * count : -2])):
            preact = first[...].astype(F32) + second[...].astype(F32)
            hidden_ref[index] = (preact * jax.nn.sigmoid(preact)).astype(BF16)

    total = None
    for index, left in enumerate(refs[:count]):
        term = dot_f32(left[...], hidden_ref[index], CONTRACT_ROWS)
        total = term if total is None else total + term
    out_ref[...] = total.astype(BF16)


def weight_grad(kernel, lefts, rights, scratch_shapes):
    rows, width = lefts[0].shape
    hidden = rights[0].shape[1]
    count = len(lefts)
    tile = 256
    return pl.pallas_call(
        kernel,
        grid=(width // tile,),
        in_specs=[pl.BlockSpec((rows, tile), lambda n: (0, n))] * count
        + [pl.BlockSpec((rows, hidden), lambda n: (0, 0))] * len(rights),
        out_specs=pl.BlockSpec((tile, hidden), lambda n: (n, 0)),
        out_shape=jax.ShapeDtypeStruct((width, hidden), BF16),
        scratch_shapes=scratch_shapes,
        compiler_params=pltpu.CompilerParams(vmem_limit_bytes=32 * 1024 * 1024),
        cost_estimate=NO_COST,
    )(*lefts, *rights)


def slots_and_gates(routing, own, limit, top_count):
    ids = routing[:, :, :top_count]
    levels = routing[:, :, top_count:].astype(F32)
    tok_rows = ids.shape[1]
    named = ids == own
    match = jnp.any(named, axis=2)
    gates = jnp.sum(jnp.where(named, levels, 0.0), axis=2) / jnp.sum(levels, axis=2)
    before = jnp.arange(tok_rows)[:, None] < jnp.arange(tok_rows)[None, :]
    rank = dot_f32(match.astype(BF16), before.astype(BF16)).astype(jnp.int32)
    return jnp.where(match & (rank < limit), rank, -1), gates


def grouped(tokens, cotangent, expert_ids, gate_levels, capacity, up_weight, down_weight):
    top_count = expert_ids.shape[1]
    slots = tokens.shape[0] * top_count // capacity.shape[0]
    own = lax.axis_index("expert")
    z = own // (NX * NC)
    inner = (z > 0) & (z < NZ - 1)
    who = jnp.stack([own.astype(jnp.int32), capacity[own]])
    weight_up, weight_down = up_weight[0], down_weight[0]

    rows_in, rows_cot, tables, pre, cot = ([None] * NZ for _ in range(5))

    def first(s, mine, mine_core, other):
        blocks = (mine, mine_core, other, swap_core(other))
        rows_in[s], part, slot, gate = front_tokens(blocks, who, weight_up, slots, top_count)
        tables[s] = (slot, gate)
        pre[s] = (part, swap_dp(part))

    def second(s, mine, mine_core, other):
        blocks = (mine, mine_core, other, swap_core(other))
        rows_cot[s], part = front_cotangent(blocks, tables[s], weight_down, slots)
        cot[s] = (part, swap_dp(part))

    tok = with_routing(tokens, expert_ids, gate_levels)
    x0 = swap_x(tok)
    near = along_z(tok, NEIGHBOUR)
    two_in = along_z(tok, MIDDLE)
    tok_core = swap_core(tok)

    near, two_in = tie((near, two_in), x0)
    x1 = swap_x(near)
    far_in = along_z(near, MIDDLE)
    two_out = along_z(two_in, OUTWARD)
    first(0, tok, tok_core, x0)

    two, far_in, cot_own = tie((jnp.where(inner, two_in, two_out), far_in, cotangent), x1, pre[0][0])
    x2 = swap_x(two)
    far_out = along_z(far_in, OUTWARD)
    cot_near_in = along_z(cot_own, INWARD)
    cot_two_in = along_z(cot_own, MIDDLE)
    first(1, near, swap_core(near), x1)

    far, cot_own, cot_near_in = tie(
        (jnp.where(inner, far_in, far_out), cot_own, cot_near_in), x2, pre[1][0], pre[0][1]
    )
    x3 = swap_x(far)
    cot_near_out = along_z(cot_own, OUTWARD)
    cot_far_in = along_z(cot_near_in, MIDDLE)
    first(2, two, swap_core(two), x2)

    cot_near, cot_far_in = tie(
        (jnp.where(inner, cot_near_in, cot_near_out), cot_far_in), x3, pre[2][0], pre[1][1]
    )
    x4 = swap_x(cot_near)
    cot_far_out = along_z(cot_far_in, OUTWARD)
    first(3, far, swap_core(far), x3)

    cot_far, cot_two_in = tie(
        (jnp.where(inner, cot_far_in, cot_far_out), cot_two_in), x4, pre[3][0], pre[2][1]
    )
    x5 = swap_x(cot_far)
    cot_two_out = along_z(cot_two_in, OUTWARD)
    second(1, cot_near, swap_core(cot_near), x4)

    cot_two = tie(jnp.where(inner, cot_two_in, cot_two_out), x5, cot[1][0], pre[3][1])
    x6 = swap_x(cot_two)
    second(3, cot_far, swap_core(cot_far), x5)

    cot_own = tie(cot_own, x6, cot[3][0], cot[1][1])
    x7 = swap_x(cot_own)
    second(2, cot_two, swap_core(cot_two), x6)

    act, chip = [None] * NZ, [None] * NZ

    def last(s):
        act[s], keep, send = back(tables[s][0], pre[s] + cot[s], weight_up, slots)
        chip[s] = add(keep, swap_core(send))

    last(1)
    near_send, cot_own = tie((chip[1][1], cot_own), x7, cot[2][0], cot[3][1])
    x8 = swap_x(near_send)
    second(0, cot_own, swap_core(cot_own), x7)
    last(3)

    far_send = tie(chip[3][1], x8, cot[0][0], cot[2][1])
    x9 = swap_x(far_send)
    last(2)

    two_send, far_sum = tie((chip[2][1], add(chip[3][0], x9)), cot[0][1])
    x10 = swap_x(two_send)
    hop_far = along_z(far_sum, INWARD)
    last(0)

    own_send, far_sum, two_sum = tie((chip[0][1], add(far_sum, hop_far), add(chip[2][0], x10)))
    x11 = swap_x(own_send)
    hop_far = along_z(far_sum, MIDDLE)
    hop_two = along_z(two_sum, INWARD)
    down_grad = weight_grad(
        down_grad_kernel,
        rows_cot,
        [p[0] for p in pre] + [p[1] for p in pre],
        [pltpu.VMEM((NZ,) + pre[0][0].shape, BF16)],
    )

    near_sum, two_sum = tie(
        (add(add(chip[1][0], x8), hop_far), add(two_sum, hop_two)), x11, down_grad
    )
    hop_near = along_z(near_sum, NEIGHBOUR)
    hop_two = along_z(two_sum, MIDDLE)
    up_grad = weight_grad(up_grad_kernel, rows_in, act, [])
    token_grad = (
        add(chip[0][0], x11).astype(F32) + hop_near.astype(F32) + hop_two.astype(F32)
    ).astype(BF16)
    return token_grad, up_grad[None], down_grad[None]


def general(n_expert, tokens, cotangent, expert_ids, gate_levels, capacity, up_weight, down_weight):
    tok_rows, width = tokens.shape
    top_count = expert_ids.shape[1]
    slots = tok_rows * top_count // capacity.shape[0]
    row_count = n_expert * slots
    own = lax.axis_index("expert")
    weight_up, weight_down = up_weight[0], down_weight[0]

    routing = lax.all_gather(
        jnp.concatenate([expert_ids, gate_levels], axis=1), "expert", axis=0, tiled=False
    )
    tok_all = lax.all_gather(tokens, "expert", axis=0, tiled=False)
    cot_all = lax.all_gather(cotangent, "expert", axis=0, tiled=False)
    slot_of, gates = slots_and_gates(routing, own, capacity[own], top_count)
    placing = slot_of[:, None, :] == jnp.arange(slots, dtype=jnp.int32)[None, :, None]
    slot_gate = jnp.sum(jnp.where(placing, gates[:, None, :], 0.0), axis=2)
    placing = placing.astype(BF16)
    pick = (((2,), (1,)), ((0,), (0,)))
    rows_in = dot_f32(placing, tok_all, pick).astype(BF16).reshape(row_count, width)
    rows_cot = (slot_gate[:, :, None] * dot_f32(placing, cot_all, pick)).astype(BF16)
    rows_cot = rows_cot.reshape(row_count, width)
    preact = lax.psum(dot_f32(rows_in, weight_up).astype(BF16).astype(F32), "dp")
    hidden_cot = lax.psum(dot_f32(rows_cot, weight_down).astype(BF16).astype(F32), "dp")
    sigmoid = jax.nn.sigmoid(preact)
    hidden = (preact * sigmoid).astype(BF16)
    act = (hidden_cot * (sigmoid * (1.0 + preact * (1.0 - sigmoid)))).astype(BF16)
    row_grad = dot_f32(act, weight_up, CONTRACT_LAST).astype(BF16)
    spread = dot_f32(
        placing, row_grad.reshape(n_expert, slots, width), (((1,), (1,)), ((0,), (0,)))
    ).astype(BF16)
    token_grad = lax.psum_scatter(
        spread.reshape(n_expert * tok_rows, width), "expert", scatter_dimension=0, tiled=True
    )
    up_grad = dot_f32(rows_in, act, CONTRACT_ROWS).astype(BF16)[None]
    down_grad = dot_f32(rows_cot, hidden, CONTRACT_ROWS).astype(BF16)[None]
    return token_grad, up_grad, down_grad


def solution(mesh):
    n_dp, n_expert = mesh.shape["dp"], mesh.shape["expert"]
    if n_dp == 2 and n_expert == NZ * NX * NC:
        body = grouped
    else:
        body = functools.partial(general, n_expert)
    return jax.shard_map(
        body,
        mesh=mesh,
        in_specs=(
            P("expert", "dp"),
            P("expert", "dp"),
            P("expert", None),
            P("expert", None),
            P(),
            P("expert", "dp", None),
            P("expert", "dp", None),
        ),
        out_specs=(P("expert", "dp"), P("expert", "dp", None), P("expert", "dp", None)),
        check_vma=False,
    )
```

time: 269 us -> 241 us (0.90)
  blocking collectives: 29.9 us -> 0 us
  waiting for transfers between devices: 118 us -> 125 us
  Pallas kernels: 43.1 us -> 48.1 us
  starting transfers between devices: 60.5 us -> 55.5 us
    all_gather x1 -> x0, blocking collectives: 29.9 us -> none  [grouped(): lax.all_gather(jnp.concatenate([expert_ids, gate_levels], axis=1), 'exper...]
    ppermute x15 -> x16, waiting for transfers between devices: 25.5 us -> 53.7 us  [along_z(): return lax.ppermute(value, 'expert', perm)]
    ppermute x12, waiting for transfers between devices: 43.2 us -> 30.4 us  [swap_x(): lax.ppermute(value, 'expert', [(i, i ^ NC) for i in range(NZ * NX * NC)])]
    ppermute x8, waiting for transfers between devices: 48.8 us -> 40.6 us  [swap_dp(): return lax.ppermute(value, 'dp', [(0, 1), (1, 0)])]
    pallas_call x10, Pallas kernels: 31.9 us -> 37.5 us  [the longest x4 14.6 us: front_tokens(): pl.pallas_call(functools.partial(tokens_kernel, top_count, slots), in_spe...]
    ppermute x15 -> x16, starting transfers between devices: 34.8 us -> 29.6 us  [along_z(): return lax.ppermute(value, 'expert', perm)]
  transfers between devices with their start and end apart: 55 -> 56, of which waited for: 20 -> 25; matrix products, arithmetic and copies ran while one was open for 3% -> 2% of each run, Pallas kernels for 16% -> 20%
where the time goes in v3:
time: 241 us; the launch traced here: 240 us
  waiting for transfers between devices  125 us (52%)
  starting transfers between devices  55.5 us (23%)
  Pallas kernels  48.1 us (20%)
  other arithmetic  5.84 us (2%)
  local copies, waits for them, and re-layouts  4.81 us (2%)
    ppermute x16, waiting for transfers between devices, along_z(): return lax.ppermute(value, 'expert', perm)  53.7 us
    ppermute x8, waiting for transfers between devices, swap_dp(): return lax.ppermute(value, 'dp', [(0, 1), (1, 0)])  40.6 us
    ppermute x12, waiting for transfers between devices, swap_x(): lax.ppermute(value, 'expert', [(i, i ^ NC) for i in range(NZ * NX * NC)])  30.4 us
    ppermute x16, starting transfers between devices, along_z(): return lax.ppermute(value, 'expert', perm)  29.6 us
    pallas_call x4, Pallas kernels, front_tokens(): pl.pallas_call(functools.partial(tokens_kernel, top_count, slots), in_spe...  14.6 us
    pallas_call x2, Pallas kernels, weight_grad(): pl.pallas_call(kernel, grid=(width // tile,), in_specs=[pl.BlockSpec((row...  13.6 us
    ppermute x12, starting transfers between devices, swap_x(): lax.ppermute(value, 'expert', [(i, i ^ NC) for i in range(NZ * NX * NC)])  13.4 us
    pallas_call x4, Pallas kernels, back(): pl.pallas_call(functools.partial(back_kernel, slots), grid=(width // tile...  10.7 us
  transfers between devices with their start and end apart: 56, of which 25 were waited for; matrix products, arithmetic and copies ran while one was open for 2% of the time, Pallas kernels for 20%

profile of v3, /device:TPU:8, one launch (start us, length us, event | category | flops | bytes accessed | tf_op | source)
XLA Modules:
  0.0 240.2 jit_solution(10290286398586009387)
XLA Ops:
  5.0 3.5 %collective-permute-start.5 = (bf16[128,1920]{1,0:T(8,128)(2,1)S(1)}, bf16[128,1920]{1,0:T(8,128)(2,1)S(1)}, u32[]{:S(2)}, u32[]{:S(2)}) collective-permute-start(bf16[128,1920]{1,0:T(8,128)(2,1)S(1)} %concatenate.3.m0.b0), channel_id=1, source_target_pairs={{4,8},{5,9},{6,10},{7,11},{8,4},{9,5},{10,6},{11,7},{20,24},{21,25... | collective-permute-start | bytes 1474568 | tf_op jit(solution)/shard_map/ppermute | solution.py:31
  8.6 7.8 %collective-permute-done.1.m2.b2 = bf16[128,1920]{1,0:T(8,128)(2,1)S(1)} collective-permute-done((bf16[128,1920]{1,0:T(8,128)(2,1)S(1)}, bf16[128,1920]{1,0:T(8,128)(2,1)S(1)}, u32[]{:S(2)}, u32[]{:S(2)}) %collective-permute-start.1) | collective-permute-done | bytes 491552 | tf_op jit(solution)/shard_map/ppermute | solution.py:35
  16.5 3.1 %collective-permute-done.5 = bf16[128,1920]{1,0:T(8,128)(2,1)S(1)} collective-permute-done((bf16[128,1920]{1,0:T(8,128)(2,1)S(1)}, bf16[128,1920]{1,0:T(8,128)(2,1)S(1)}, u32[]{:S(2)}, u32[]{:S(2)}) %collective-permute-start.5) | collective-permute-done | bytes 491552 | tf_op jit(solution)/shard_map/ppermute | solution.py:31
  20.9 3.0 %collective-permute-start.10 = (bf16[128,1920]{1,0:T(8,128)(2,1)S(1)}, bf16[128,1920]{1,0:T(8,128)(2,1)}, u32[]{:S(2)}, u32[]{:S(2)}) collective-permute-start(bf16[128,1920]{1,0:T(8,128)(2,1)S(1)} %collective-permute-done.5), channel_id=1, source_target_pairs={{4,0},{5,1},{6,2},{7,3},{8,12},{9,13},{10,14},{11,15},{20,16},{21,... | collective-permute-start | bytes 1474568 | tf_op jit(solution)/shard_map/ppermute | solution.py:31
  30.9 3.6 %shard_map.94 = (bf16[256,1792]{1,0:T(8,128)(2,1)S(1)}, bf16[256,1024]{1,0:T(8,128)(2,1)S(1)}, s32[4,8,128]{2,1,0:T(8,128)S(1)}, f32[4,8,128]{2,1,0:T(8,128)S(1)}) custom-call(s32[2]{0:T(128)S(1)} %pad_add_fusion.own_ref, bf16[128,1920]{1,0:T(8,128)(2,1)S(1)} %concatenate.3.m0.b0, bf16[128,1920]{1,0:T(8,128)(2,1)S(1)} %collective-permute-done.m1.b1, ...), custom_call_target="tpu_custom_call" | custom-call | tf_op jit(solution)/shard_map/pallas_call | solution.py:157
  34.6 4.0 %collective-permute-done.11 = bf16[128,1920]{1,0:T(8,128)(2,1)} collective-permute-done((bf16[128,1920]{1,0:T(8,128)(2,1)S(1)}, bf16[128,1920]{1,0:T(8,128)(2,1)}, u32[]{:S(2)}, u32[]{:S(2)}) %collective-permute-start.11) | collective-permute-done | bytes 491552 | tf_op jit(solution)/shard_map/ppermute | solution.py:31
  43.2 5.4 %collective-permute-done.12 = bf16[128,1920]{1,0:T(8,128)(2,1)S(1)} collective-permute-done((bf16[128,1920]{1,0:T(8,128)(2,1)}, bf16[128,1920]{1,0:T(8,128)(2,1)S(1)}, u32[]{:S(2)}, u32[]{:S(2)}) %collective-permute-start.12) | collective-permute-done | bytes 491552 | tf_op jit(solution)/shard_map/ppermute | solution.py:31
  51.0 3.7 %shard_map.95 = (bf16[256,1792]{1,0:T(8,128)(2,1)S(1)}, bf16[256,1024]{1,0:T(8,128)(2,1)S(1)}, s32[4,8,128]{2,1,0:T(8,128)S(1)}, f32[4,8,128]{2,1,0:T(8,128)S(1)}) custom-call(s32[2]{0:T(128)S(1)} %pad_add_fusion.own_ref, bf16[128,1920]{1,0:T(8,128)(2,1)S(1)} %collective-permute-done.4.m0.b0, bf16[128,1920]{1,0:T(8,128)(2,1)S(1)} %collective-permute-done.6.m1.b1, ...), custom_call_target="tpu_custom_call" | custom-call | tf_op jit(solution)/shard_map/pallas_call | solution.py:157
  54.7 4.9 %collective-permute-done.13 = bf16[128,1792]{1,0:T(8,128)(2,1)S(1)} collective-permute-done((bf16[128,1792]{1,0:T(8,128)(2,1)S(1)}, bf16[128,1792]{1,0:T(8,128)(2,1)S(1)}, u32[]{:S(2)}, u32[]{:S(2)}) %collective-permute-start.13) | collective-permute-done | bytes 458784 | tf_op jit(solution)/shard_map/ppermute | solution.py:31
  62.6 2.8 %collective-permute-start.17 = (bf16[128,1920]{1,0:T(8,128)(2,1)S(1)}, bf16[128,1920]{1,0:T(8,128)(2,1)S(1)}, u32[]{:S(2)}, u32[]{:S(2)}) collective-permute-start(bf16[128,1920]{1,0:T(8,128)(2,1)S(1)} %broadcast_select_fusion.m0.b0), channel_id=1, source_target_pairs={{0,2},{1,3},{2,0},{3,1},{4,6},{5,7},{6,4},{7,5},{8,10},{9,11},{10,... | collective-permute-start | bytes 1474568 | tf_op jit(solution)/shard_map/ppermute | solution.py:35
  67.0 3.4 %collective-permute-start.16 = (bf16[128,1792]{1,0:T(8,128)(2,1)S(1)}, bf16[128,1792]{1,0:T(8,128)(2,1)S(1)}, u32[]{:S(2)}, u32[]{:S(2)}) collective-permute-start(bf16[128,1792]{1,0:T(8,128)(2,1)S(1)} %collective-permute-done.13), channel_id=1, source_target_pairs={{4,8},{5,9},{6,10},{7,11},{8,4},{9,5},{10,6},{11,7},{20,24},{21,25... | collective-permute-start | bytes 1376264 | tf_op jit(solution)/shard_map/ppermute | solution.py:31
  70.5 3.7 %shard_map.96 = (bf16[256,1792]{1,0:T(8,128)(2,1)S(1)}, bf16[256,1024]{1,0:T(8,128)(2,1)S(1)}, s32[4,8,128]{2,1,0:T(8,128)S(1)}, f32[4,8,128]{2,1,0:T(8,128)S(1)}) custom-call(s32[2]{0:T(128)S(1)} %pad_add_fusion.own_ref, bf16[128,1920]{1,0:T(8,128)(2,1)S(1)} %broadcast_select_fusion.1.m0.b0, bf16[128,1920]{1,0:T(8,128)(2,1)S(1)} %collective-permute-done.18.m1.b1, ...), custom_call_target="tpu_custom_call" | custom-call | tf_op jit(solution)/shard_map/pallas_call | solution.py:157
  74.2 6.1 %collective-permute-done.16 = bf16[128,1792]{1,0:T(8,128)(2,1)S(1)} collective-permute-done((bf16[128,1792]{1,0:T(8,128)(2,1)S(1)}, bf16[128,1792]{1,0:T(8,128)(2,1)S(1)}, u32[]{:S(2)}, u32[]{:S(2)}) %collective-permute-start.16) | collective-permute-done | bytes 458784 | tf_op jit(solution)/shard_map/ppermute | solution.py:31
  85.5 4.2 %collective-permute-done.25 = bf16[128,1792]{1,0:T(8,128)(2,1)S(1)} collective-permute-done((bf16[128,1792]{1,0:T(8,128)(2,1)S(1)}, bf16[128,1792]{1,0:T(8,128)(2,1)S(1)}, u32[]{:S(2)}, u32[]{:S(2)}) %collective-permute-start.25) | collective-permute-done | bytes 458784 | tf_op jit(solution)/shard_map/ppermute | solution.py:31
  92.2 3.7 %shard_map.99 = (bf16[256,1792]{1,0:T(8,128)(2,1)S(1)}, bf16[256,1024]{1,0:T(8,128)(2,1)S(1)}, s32[4,8,128]{2,1,0:T(8,128)S(1)}, f32[4,8,128]{2,1,0:T(8,128)S(1)}) custom-call(s32[2]{0:T(128)S(1)} %pad_add_fusion.own_ref, bf16[128,1920]{1,0:T(8,128)(2,1)S(1)} %broadcast_select_fusion.m0.b0, bf16[128,1920]{1,0:T(8,128)(2,1)S(1)} %collective-permute-done.27.m1.b1, ...), custom_call_target="tpu_custom_call" | custom-call | tf_op jit(solution)/shard_map/pallas_call | solution.py:157
  105.0 5.6 %collective-permute-done.31.b2 = bf16[128,1792]{1,0:T(8,128)(2,1)S(1)} collective-permute-done((bf16[128,1792]{1,0:T(8,128)(2,1)S(1)}, bf16[128,1792]{1,0:T(8,128)(2,1)S(1)}, u32[]{:S(2)}, u32[]{:S(2)}) %collective-permute-start.31) | collective-permute-done | bytes 458784 | tf_op jit(solution)/shard_map/ppermute | solution.py:35
  110.7 4.8 %collective-permute-done.32.pre_b.refs_11_ = bf16[256,1024]{1,0:T(8,128)(2,1)S(1)} collective-permute-done((bf16[256,1024]{1,0:T(8,128)(2,1)S(1)}, bf16[256,1024]{1,0:T(8,128)(2,1)S(1)}, u32[]{:S(2)}, u32[]{:S(2)}) %collective-permute-start.32) | collective-permute-done | bytes 524320 | tf_op jit(solution)/shard_map/ppermute | solution.py:43
  116.9 8.2 %collective-permute-done.23.cot_b = bf16[256,1024]{1,0:T(8,128)(2,1)S(1)} collective-permute-done((bf16[256,1024]{1,0:T(8,128)(2,1)S(1)}, bf16[256,1024]{1,0:T(8,128)(2,1)S(1)}, u32[]{:S(2)}, u32[]{:S(2)}) %collective-permute-start.23) | collective-permute-done | bytes 524320 | tf_op jit(solution)/shard_map/ppermute | solution.py:43
  125.1 2.7 %shard_map.98 = (bf16[256,1024]{1,0:T(8,128)(2,1)S(1)}, bf16[2,128,1792]{2,1,0:T(8,128)(2,1)S(1)}, bf16[2,128,1792]{2,1,0:T(8,128)(2,1)S(1)}) custom-call(s32[4,8,128]{2,1,0:T(8,128)S(1)} %get-tuple-element.67.slot_ref, bf16[256,1024]{1,0:T(8,128)(2,1)S(1)} %get-tuple-element.68.pre_a.refs_5_, bf16[256,1024]{1,0:T(8,128)(2,1)S(1)} %collective-permute-done.9.pre_b.refs_9_, ...), custom_call_target="tpu_custom_call" | custom-call | tf_op jit(solution)/shard_map/pallas_call | solution.py:207
  132.7 11.8 %collective-permute-done.39.cot_b = bf16[256,1024]{1,0:T(8,128)(2,1)S(1)} collective-permute-done((bf16[256,1024]{1,0:T(8,128)(2,1)S(1)}, bf16[256,1024]{1,0:T(8,128)(2,1)S(1)}, u32[]{:S(2)}, u32[]{:S(2)}) %collective-permute-start.39) | collective-permute-done | bytes 524320 | tf_op jit(solution)/shard_map/ppermute | solution.py:43
  144.5 2.7 %shard_map.105 = (bf16[256,1024]{1,0:T(8,128)(2,1)S(1)}, bf16[2,128,1792]{2,1,0:T(8,128)(2,1)S(1)}, bf16[2,128,1792]{2,1,0:T(8,128)(2,1)S(1)}) custom-call(s32[4,8,128]{2,1,0:T(8,128)S(1)} %get-tuple-element.87.slot_ref, bf16[256,1024]{1,0:T(8,128)(2,1)S(1)} %get-tuple-element.83.pre_a.refs_7_, bf16[256,1024]{1,0:T(8,128)(2,1)S(1)} %collective-permute-done.32.pre_b.refs_11_, ...), custom_call_target="tpu_custom_call" | custom-call | tf_op jit(solution)/shard_map/pallas_call | solution.py:207
  155.1 9.7 %collective-permute-done.44.cot_b = bf16[256,1024]{1,0:T(8,128)(2,1)S(1)} collective-permute-done((bf16[256,1024]{1,0:T(8,128)(2,1)S(1)}, bf16[256,1024]{1,0:T(8,128)(2,1)S(1)}, u32[]{:S(2)}, u32[]{:S(2)}) %collective-permute-start.44) | collective-permute-done | bytes 524320 | tf_op jit(solution)/shard_map/ppermute | solution.py:43
  166.3 2.7 %shard_map.104 = (bf16[256,1024]{1,0:T(8,128)(2,1)S(1)}, bf16[2,128,1792]{2,1,0:T(8,128)(2,1)S(1)}, bf16[2,128,1792]{2,1,0:T(8,128)(2,1)S(1)}) custom-call(s32[4,8,128]{2,1,0:T(8,128)S(1)} %get-tuple-element.91.slot_ref, bf16[256,1024]{1,0:T(8,128)(2,1)S(1)} %get-tuple-element.77.pre_a.refs_6_, bf16[256,1024]{1,0:T(8,128)(2,1)S(1)} %collective-permute-done.29.pre_b.refs_10_, ...), custom_call_target="tpu_custom_call" | custom-call | tf_op jit(solution)/shard_map/pallas_call | solution.py:207
  169.6 7.3 %collective-permute-done.48 = bf16[128,1792]{1,0:T(8,128)(2,1)S(1)} collective-permute-done((bf16[128,1792]{1,0:T(8,128)(2,1)S(1)}, bf16[128,1792]{1,0:T(8,128)(2,1)S(1)}, u32[]{:S(2)}, u32[]{:S(2)}) %collective-permute-start.48) | collective-permute-done | bytes 458784 | tf_op jit(solution)/shard_map/ppermute | solution.py:35
  177.3 6.1 %collective-permute-done.42.cot_b = bf16[256,1024]{1,0:T(8,128)(2,1)S(1)} collective-permute-done((bf16[256,1024]{1,0:T(8,128)(2,1)S(1)}, bf16[256,1024]{1,0:T(8,128)(2,1)S(1)}, u32[]{:S(2)}, u32[]{:S(2)}) %collective-permute-start.42) | collective-permute-done | bytes 524320 | tf_op jit(solution)/shard_map/ppermute | solution.py:43
  183.9 2.7 %shard_map.103 = (bf16[256,1024]{1,0:T(8,128)(2,1)S(1)}, bf16[2,128,1792]{2,1,0:T(8,128)(2,1)S(1)}, bf16[2,128,1792]{2,1,0:T(8,128)(2,1)S(1)}) custom-call(s32[4,8,128]{2,1,0:T(8,128)S(1)} %get-tuple-element.63.slot_ref, bf16[256,1024]{1,0:T(8,128)(2,1)S(1)} %get-tuple-element.64.pre_a.refs_4_, bf16[256,1024]{1,0:T(8,128)(2,1)S(1)} %collective-permute-done.3.pre_b.refs_8_, ...), custom_call_target="tpu_custom_call" | custom-call | tf_op jit(solution)/shard_map/pallas_call | solution.py:207
  188.2 7.2 %collective-permute-done.50 = bf16[128,1792]{1,0:T(8,128)(2,1)S(1)} collective-permute-done((bf16[128,1792]{1,0:T(8,128)(2,1)S(1)}, bf16[128,1792]{1,0:T(8,128)(2,1)S(1)}, u32[]{:S(2)}, u32[]{:S(2)}) %collective-permute-start.50) | collective-permute-done | bytes 458784 | tf_op jit(solution)/shard_map/ppermute | solution.py:35
  195.6 5.9 %collective-permute-done.49 = bf16[128,1792]{1,0:T(8,128)(2,1)S(1)} collective-permute-done((bf16[128,1792]{1,0:T(8,128)(2,1)S(1)}, bf16[128,1792]{1,0:T(8,128)(2,1)S(1)}, u32[]{:S(2)}, u32[]{:S(2)}) %collective-permute-start.49) | collective-permute-done | bytes 458784 | tf_op jit(solution)/shard_map/ppermute | solution.py:31
  204.1 7.3 %shard_map.106 = bf16[1792,1024]{1,0:T(8,128)(2,1)} custom-call(bf16[256,1792]{1,0:T(8,128)(2,1)S(1)} %get-tuple-element.109.refs_0_, bf16[256,1792]{1,0:T(8,128)(2,1)S(1)} %get-tuple-element.110.refs_1_, bf16[256,1792]{1,0:T(8,128)(2,1)S(1)} %get-tuple-element.111.refs_2_, bf16[256,1792]{1,0:T(8,128)(2,1)S(1)} %get-tuple-element.112.refs_3_, ...), custom_call_target="tpu_custom_call" | custom-call | tf_op jit(solution)/shard_map/pallas_call | solution.py:255
  216.1 10.4 %collective-permute-done.53 = bf16[128,1792]{1,0:T(8,128)(2,1)S(1)} collective-permute-done((bf16[128,1792]{1,0:T(8,128)(2,1)S(1)}, bf16[128,1792]{1,0:T(8,128)(2,1)S(1)}, u32[]{:S(2)}, u32[]{:S(2)}) %collective-permute-start.53) | collective-permute-done | bytes 458784 | tf_op jit(solution)/shard_map/ppermute | solution.py:31
  226.7 3.4 %collective-permute-start.55 = (bf16[128,1792]{1,0:T(8,128)(2,1)S(1)}, bf16[128,1792]{1,0:T(8,128)(2,1)S(1)}, u32[]{:S(2)}, u32[]{:S(2)}) collective-permute-start(bf16[128,1792]{1,0:T(8,128)(2,1)S(1)} %add_convert_fusion.5), channel_id=1, source_target_pairs={{4,8},{5,9},{6,10},{7,11},{8,4},{9,5},{10,6},{11,7},{20,24},{21,25... | collective-permute-start | bytes 1376264 | tf_op jit(solution)/shard_map/ppermute | solution.py:31
  230.2 6.3 %shard_map.107 = bf16[1792,1024]{1,0:T(8,128)(2,1)} custom-call(bf16[256,1792]{1,0:T(8,128)(2,1)S(1)} %get-tuple-element.115.refs_0_, bf16[256,1792]{1,0:T(8,128)(2,1)S(1)} %get-tuple-element.116.refs_1_, bf16[256,1792]{1,0:T(8,128)(2,1)S(1)} %get-tuple-element.117.refs_2_, bf16[256,1792]{1,0:T(8,128)(2,1)S(1)} %get-tuple-element.118.refs_3_, ...), custom_call_target="tpu_custom_call" | custom-call | tf_op jit(solution)/shard_map/pallas_call | solution.py:255
  (130 shorter events, 71.5 us)
Async XLA Ops:
  3.4 13.0 %collective-permute-start.1 = (bf16[128,1920]{1,0:T(8,128)(2,1)S(1)}, bf16[128,1920]{1,0:T(8,128)(2,1)S(1)}, u32[]{:S(2)}, u32[]{:S(2)}) collective-permute-start(bf16[128,1920]{1,0:T(8,128)(2,1)S(1)} %concatenate.3.m0.b0), channel_id=1, source_target_pairs={{0,2},{1,3},{2,0},{3,1},{4,6},{5,7},{6,4},{7,5},{8,10},{9,11},{10,... | collective-permute-start | bytes 1474568 | tf_op jit(solution)/shard_map/ppermute | solution.py:35
  5.0 14.6 %collective-permute-start.5 = (bf16[128,1920]{1,0:T(8,128)(2,1)S(1)}, bf16[128,1920]{1,0:T(8,128)(2,1)S(1)}, u32[]{:S(2)}, u32[]{:S(2)}) collective-permute-start(bf16[128,1920]{1,0:T(8,128)(2,1)S(1)} %concatenate.3.m0.b0), channel_id=1, source_target_pairs={{4,8},{5,9},{6,10},{7,11},{8,4},{9,5},{10,6},{11,7},{20,24},{21,25... | collective-permute-start | bytes 1474568 | tf_op jit(solution)/shard_map/ppermute | solution.py:31
  8.5 20.3 %collective-permute-start = (bf16[128,1920]{1,0:T(8,128)(2,1)S(1)}, bf16[128,1920]{1,0:T(8,128)(2,1)S(1)}, u32[]{:S(2)}, u32[]{:S(2)}) collective-permute-start(bf16[128,1920]{1,0:T(8,128)(2,1)S(1)} %concatenate.3.m0.b0), channel_id=1, source_target_pairs={{0,1},{1,0},{2,3},{3,2},{4,5},{5,4},{6,7},{7,6},{8,9},{9,8},{10,11... | collective-permute-start | bytes 1474568 | tf_op jit(solution)/shard_map/ppermute | solution.py:39
  20.9 13.6 %collective-permute-start.10 = (bf16[128,1920]{1,0:T(8,128)(2,1)S(1)}, bf16[128,1920]{1,0:T(8,128)(2,1)}, u32[]{:S(2)}, u32[]{:S(2)}) collective-permute-start(bf16[128,1920]{1,0:T(8,128)(2,1)S(1)} %collective-permute-done.5), channel_id=1, source_target_pairs={{4,0},{5,1},{6,2},{7,3},{8,12},{9,13},{10,14},{11,15},{20,16},{21,... | collective-permute-start | bytes 1474568 | tf_op jit(solution)/shard_map/ppermute | solution.py:31
  25.2 13.5 %collective-permute-start.11 = (bf16[128,1920]{1,0:T(8,128)(2,1)S(1)}, bf16[128,1920]{1,0:T(8,128)(2,1)}, u32[]{:S(2)}, u32[]{:S(2)}) collective-permute-start(bf16[128,1920]{1,0:T(8,128)(2,1)S(1)} %collective-permute-done.4.m0.b0), channel_id=1, source_target_pairs={{4,8},{5,9},{6,10},{7,11},{8,4},{9,5},{10,6},{11,7},{20,24},{21,25... | collective-permute-start | bytes 1474568 | tf_op jit(solution)/shard_map/ppermute | solution.py:31
  28.8 14.2 %collective-permute-start.6 = (bf16[128,1920]{1,0:T(8,128)(2,1)S(1)}, bf16[128,1920]{1,0:T(8,128)(2,1)S(1)}, u32[]{:S(2)}, u32[]{:S(2)}) collective-permute-start(bf16[128,1920]{1,0:T(8,128)(2,1)S(1)} %collective-permute-done.4.m0.b0), channel_id=1, source_target_pairs={{0,1},{1,0},{2,3},{3,2},{4,5},{5,4},{6,7},{7,6},{8,9},{9,8},{10,11... | collective-permute-start | bytes 1474568 | tf_op jit(solution)/shard_map/ppermute | solution.py:39
  40.1 19.5 %collective-permute-start.3 = (bf16[256,1024]{1,0:T(8,128)(2,1)S(1)}, bf16[256,1024]{1,0:T(8,128)(2,1)S(1)}, u32[]{:S(2)}, u32[]{:S(2)}) collective-permute-start(bf16[256,1024]{1,0:T(8,128)(2,1)S(1)} %get-tuple-element.64.pre_a.refs_4_), channel_id=1, source_target_pairs={{0,16},{16,0},{1,17},{17,1},{2,18},{18,2},{3,19},{19,3},{4,20},{20... | collective-permute-start | bytes 1572872 | tf_op jit(solution)/shard_map/ppermute | solution.py:43
  41.7 17.9 %collective-permute-start.14 = (bf16[128,1920]{1,0:T(8,128)(2,1)S(1)}, bf16[128,1920]{1,0:T(8,128)(2,1)S(1)}, u32[]{:S(2)}, u32[]{:S(2)}) collective-permute-start(bf16[128,1920]{1,0:T(8,128)(2,1)S(1)} %broadcast_select_fusion.1.m0.b0), channel_id=1, source_target_pairs={{0,2},{1,3},{2,0},{3,1},{4,6},{5,7},{6,4},{7,5},{8,10},{9,11},{10,... | collective-permute-start | bytes 1474568 | tf_op jit(solution)/shard_map/ppermute | solution.py:35
  43.0 22.4 %collective-permute-start.18 = (bf16[128,1920]{1,0:T(8,128)(2,1)S(1)}, bf16[128,1920]{1,0:T(8,128)(2,1)S(1)}, u32[]{:S(2)}, u32[]{:S(2)}) collective-permute-start(bf16[128,1920]{1,0:T(8,128)(2,1)S(1)} %broadcast_select_fusion.1.m0.b0), channel_id=1, source_target_pairs={{0,1},{1,0},{2,3},{3,2},{4,5},{5,4},{6,7},{7,6},{8,9},{9,8},{10,11... | collective-permute-start | bytes 1474568 | tf_op jit(solution)/shard_map/ppermute | solution.py:39
  61.0 19.2 %collective-permute-start.9 = (bf16[256,1024]{1,0:T(8,128)(2,1)S(1)}, bf16[256,1024]{1,0:T(8,128)(2,1)S(1)}, u32[]{:S(2)}, u32[]{:S(2)}) collective-permute-start(bf16[256,1024]{1,0:T(8,128)(2,1)S(1)} %get-tuple-element.68.pre_a.refs_5_), channel_id=1, source_target_pairs={{0,16},{16,0},{1,17},{17,1},{2,18},{18,2},{3,19},{19,3},{4,20},{20... | collective-permute-start | bytes 1572872 | tf_op jit(solution)/shard_map/ppermute | solution.py:43
  62.6 17.6 %collective-permute-start.17 = (bf16[128,1920]{1,0:T(8,128)(2,1)S(1)}, bf16[128,1920]{1,0:T(8,128)(2,1)S(1)}, u32[]{:S(2)}, u32[]{:S(2)}) collective-permute-start(bf16[128,1920]{1,0:T(8,128)(2,1)S(1)} %broadcast_select_fusion.m0.b0), channel_id=1, source_target_pairs={{0,2},{1,3},{2,0},{3,1},{4,6},{5,7},{6,4},{7,5},{8,10},{9,11},{10,... | collective-permute-start | bytes 1474568 | tf_op jit(solution)/shard_map/ppermute | solution.py:35
  65.4 18.2 %collective-permute-start.27 = (bf16[128,1920]{1,0:T(8,128)(2,1)S(1)}, bf16[128,1920]{1,0:T(8,128)(2,1)S(1)}, u32[]{:S(2)}, u32[]{:S(2)}) collective-permute-start(bf16[128,1920]{1,0:T(8,128)(2,1)S(1)} %broadcast_select_fusion.m0.b0), channel_id=1, source_target_pairs={{0,1},{1,0},{2,3},{3,2},{4,5},{5,4},{6,7},{7,6},{8,9},{9,8},{10,11... | collective-permute-start | bytes 1474568 | tf_op jit(solution)/shard_map/ppermute | solution.py:39
  67.0 13.2 %collective-permute-start.16 = (bf16[128,1792]{1,0:T(8,128)(2,1)S(1)}, bf16[128,1792]{1,0:T(8,128)(2,1)S(1)}, u32[]{:S(2)}, u32[]{:S(2)}) collective-permute-start(bf16[128,1792]{1,0:T(8,128)(2,1)S(1)} %collective-permute-done.13), channel_id=1, source_target_pairs={{4,8},{5,9},{6,10},{7,11},{8,4},{9,5},{10,6},{11,7},{20,24},{21,25... | collective-permute-start | bytes 1376264 | tf_op jit(solution)/shard_map/ppermute | solution.py:31
  82.1 16.3 %collective-permute-start.29 = (bf16[256,1024]{1,0:T(8,128)(2,1)S(1)}, bf16[256,1024]{1,0:T(8,128)(2,1)S(1)}, u32[]{:S(2)}, u32[]{:S(2)}) collective-permute-start(bf16[256,1024]{1,0:T(8,128)(2,1)S(1)} %get-tuple-element.77.pre_a.refs_6_), channel_id=1, source_target_pairs={{0,16},{16,0},{1,17},{17,1},{2,18},{18,2},{3,19},{19,3},{4,20},{20... | collective-permute-start | bytes 1572872 | tf_op jit(solution)/shard_map/ppermute | solution.py:43
  83.6 14.8 %collective-permute-start.26 = (bf16[128,1792]{1,0:T(8,128)(2,1)S(1)}, bf16[128,1792]{1,0:T(8,128)(2,1)S(1)}, u32[]{:S(2)}, u32[]{:S(2)}) collective-permute-start(bf16[128,1792]{1,0:T(8,128)(2,1)S(1)} %copy-done.3), channel_id=1, source_target_pairs={{4,8},{5,9},{6,10},{7,11},{8,4},{9,5},{10,6},{11,7},{20,24},{21,25... | collective-permute-start | bytes 1376264 | tf_op jit(solution)/shard_map/ppermute | solution.py:31
  100.5 14.9 %collective-permute-start.32 = (bf16[256,1024]{1,0:T(8,128)(2,1)S(1)}, bf16[256,1024]{1,0:T(8,128)(2,1)S(1)}, u32[]{:S(2)}, u32[]{:S(2)}) collective-permute-start(bf16[256,1024]{1,0:T(8,128)(2,1)S(1)} %get-tuple-element.83.pre_a.refs_7_), channel_id=1, source_target_pairs={{0,16},{16,0},{1,17},{17,1},{2,18},{18,2},{3,19},{19,3},{4,20},{20... | collective-permute-start | bytes 1572872 | tf_op jit(solution)/shard_map/ppermute | solution.py:43
  104.4 20.7 %collective-permute-start.23 = (bf16[256,1024]{1,0:T(8,128)(2,1)S(1)}, bf16[256,1024]{1,0:T(8,128)(2,1)S(1)}, u32[]{:S(2)}, u32[]{:S(2)}) collective-permute-start(bf16[256,1024]{1,0:T(8,128)(2,1)S(1)} %get-tuple-element.79.cot_a), channel_id=1, source_target_pairs={{0,16},{16,0},{1,17},{17,1},{2,18},{18,2},{3,19},{19,3},{4,20},{20... | collective-permute-start | bytes 1572872 | tf_op jit(solution)/shard_map/ppermute | solution.py:43
  105.0 22.8 %collective-permute-start.34 = (bf16[128,1792]{1,0:T(8,128)(2,1)S(1)}, bf16[128,1792]{1,0:T(8,128)(2,1)S(1)}, u32[]{:S(2)}, u32[]{:S(2)}) collective-permute-start(bf16[128,1792]{1,0:T(8,128)(2,1)S(1)} %broadcast_select_fusion.3.b0), channel_id=1, source_target_pairs={{0,1},{1,0},{2,3},{3,2},{4,5},{5,4},{6,7},{7,6},{8,9},{9,8},{10,11... | collective-permute-start | bytes 1376264 | tf_op jit(solution)/shard_map/ppermute | solution.py:39
  110.6 17.2 %collective-permute-start.35 = (bf16[128,1792]{1,0:T(8,128)(2,1)S(1)}, bf16[128,1792]{1,0:T(8,128)(2,1)S(1)}, u32[]{:S(2)}, u32[]{:S(2)}) collective-permute-start(bf16[128,1792]{1,0:T(8,128)(2,1)S(1)} %collective-permute-done.31.b2), channel_id=1, source_target_pairs={{0,1},{1,0},{2,3},{3,2},{4,5},{5,4},{6,7},{7,6},{8,9},{9,8},{10,11... | collective-permute-start | bytes 1376264 | tf_op jit(solution)/shard_map/ppermute | solution.py:39
  115.4 16.3 %collective-permute-start.33 = (bf16[128,1792]{1,0:T(8,128)(2,1)S(1)}, bf16[128,1792]{1,0:T(8,128)(2,1)S(1)}, u32[]{:S(2)}, u32[]{:S(2)}) collective-permute-start(bf16[128,1792]{1,0:T(8,128)(2,1)S(1)} %broadcast_select_fusion.2.b0), channel_id=1, source_target_pairs={{0,2},{1,3},{2,0},{3,1},{4,6},{5,7},{6,4},{7,5},{8,10},{9,11},{10,... | collective-permute-start | bytes 1376264 | tf_op jit(solution)/shard_map/ppermute | solution.py:35
  127.7 22.4 %collective-permute-start.24 = (bf16[2,128,1792]{2,1,0:T(8,128)(2,1)S(1)}, bf16[2,128,1792]{2,1,0:T(8,128)(2,1)S(1)}, u32[]{:S(2)}, u32[]{:S(2)}) collective-permute-start(bf16[2,128,1792]{2,1,0:T(8,128)(2,1)S(1)} %get-tuple-element.81), channel_id=1, source_target_pairs={{0,1},{1,0},{2,3},{3,2},{4,5},{5,4},{6,7},{7,6},{8,9},{9,8},{10,11... | collective-permute-start | bytes 2752520 | tf_op jit(solution)/shard_map/ppermute | solution.py:39
  130.2 14.4 %collective-permute-start.39 = (bf16[256,1024]{1,0:T(8,128)(2,1)S(1)}, bf16[256,1024]{1,0:T(8,128)(2,1)S(1)}, u32[]{:S(2)}, u32[]{:S(2)}) collective-permute-start(bf16[256,1024]{1,0:T(8,128)(2,1)S(1)} %get-tuple-element.89.cot_a), channel_id=1, source_target_pairs={{0,16},{16,0},{1,17},{17,1},{2,18},{18,2},{3,19},{19,3},{4,20},{20... | collective-permute-start | bytes 1572872 | tf_op jit(solution)/shard_map/ppermute | solution.py:43
  131.8 15.5 %collective-permute-start.36 = (bf16[128,1792]{1,0:T(8,128)(2,1)S(1)}, bf16[128,1792]{1,0:T(8,128)(2,1)S(1)}, u32[]{:S(2)}, u32[]{:S(2)}) collective-permute-start(bf16[128,1792]{1,0:T(8,128)(2,1)S(1)} %copy-done.3), channel_id=1, source_target_pairs={{0,2},{1,3},{2,0},{3,1},{4,6},{5,7},{6,4},{7,5},{8,10},{9,11},{10,... | collective-permute-start | bytes 1376264 | tf_op jit(solution)/shard_map/ppermute | solution.py:35
  132.2 15.6 %collective-permute-start.37 = (bf16[128,1792]{1,0:T(8,128)(2,1)S(1)}, bf16[128,1792]{1,0:T(8,128)(2,1)S(1)}, u32[]{:S(2)}, u32[]{:S(2)}) collective-permute-start(bf16[128,1792]{1,0:T(8,128)(2,1)S(1)} %broadcast_select_fusion.2.b0), channel_id=1, source_target_pairs={{0,1},{1,0},{2,3},{3,2},{4,5},{5,4},{6,7},{7,6},{8,9},{9,8},{10,11... | collective-permute-start | bytes 1376264 | tf_op jit(solution)/shard_map/ppermute | solution.py:39
  132.2 15.6 %collective-permute-start.38 = (bf16[128,1792]{1,0:T(8,128)(2,1)S(1)}, bf16[128,1792]{1,0:T(8,128)(2,1)S(1)}, u32[]{:S(2)}, u32[]{:S(2)}) collective-permute-start(bf16[128,1792]{1,0:T(8,128)(2,1)S(1)} %collective-permute-done.33.b2), channel_id=1, source_target_pairs={{0,1},{1,0},{2,3},{3,2},{4,5},{5,4},{6,7},{7,6},{8,9},{9,8},{10,11... | collective-permute-start | bytes 1376264 | tf_op jit(solution)/shard_map/ppermute | solution.py:39
  150.5 14.3 %collective-permute-start.44 = (bf16[256,1024]{1,0:T(8,128)(2,1)S(1)}, bf16[256,1024]{1,0:T(8,128)(2,1)S(1)}, u32[]{:S(2)}, u32[]{:S(2)}) collective-permute-start(bf16[256,1024]{1,0:T(8,128)(2,1)S(1)} %get-tuple-element.93.cot_a), channel_id=1, source_target_pairs={{0,16},{16,0},{1,17},{17,1},{2,18},{18,2},{3,19},{19,3},{4,20},{20... | collective-permute-start | bytes 1572872 | tf_op jit(solution)/shard_map/ppermute | solution.py:43
  169.0 14.3 %collective-permute-start.42 = (bf16[256,1024]{1,0:T(8,128)(2,1)S(1)}, bf16[256,1024]{1,0:T(8,128)(2,1)S(1)}, u32[]{:S(2)}, u32[]{:S(2)}) collective-permute-start(bf16[256,1024]{1,0:T(8,128)(2,1)S(1)} %get-tuple-element.95.cot_a), channel_id=1, source_target_pairs={{0,16},{16,0},{1,17},{17,1},{2,18},{18,2},{3,19},{19,3},{4,20},{20... | collective-permute-start | bytes 1572872 | tf_op jit(solution)/shard_map/ppermute | solution.py:43
  186.6 15.0 %collective-permute-start.43 = (bf16[2,128,1792]{2,1,0:T(8,128)(2,1)S(1)}, bf16[2,128,1792]{2,1,0:T(8,128)(2,1)S(1)}, u32[]{:S(2)}, u32[]{:S(2)}) collective-permute-start(bf16[2,128,1792]{2,1,0:T(8,128)(2,1)S(1)} %get-tuple-element.97), channel_id=1, source_target_pairs={{0,1},{1,0},{2,3},{3,2},{4,5},{5,4},{6,7},{7,6},{8,9},{9,8},{10,11... | collective-permute-start | bytes 2752520 | tf_op jit(solution)/shard_map/ppermute | solution.py:39
  186.7 14.8 %collective-permute-start.49 = (bf16[128,1792]{1,0:T(8,128)(2,1)S(1)}, bf16[128,1792]{1,0:T(8,128)(2,1)S(1)}, u32[]{:S(2)}, u32[]{:S(2)}) collective-permute-start(bf16[128,1792]{1,0:T(8,128)(2,1)S(1)} %fusion.2), channel_id=1, source_target_pairs={{0,4},{1,5},{2,6},{3,7},{12,8},{13,9},{14,10},{15,11},{16,20},{17,... | collective-permute-start | bytes 1376264 | tf_op jit(solution)/shard_map/ppermute | solution.py:31
  201.9 14.0 %collective-permute-start.52 = (bf16[128,1792]{1,0:T(8,128)(2,1)S(1)}, bf16[128,1792]{1,0:T(8,128)(2,1)S(1)}, u32[]{:S(2)}, u32[]{:S(2)}) collective-permute-start(bf16[128,1792]{1,0:T(8,128)(2,1)S(1)} %add_convert_fusion.7), channel_id=1, source_target_pairs={{4,8},{5,9},{6,10},{7,11},{8,4},{9,5},{10,6},{11,7},{20,24},{21,25... | collective-permute-start | bytes 1376264 | tf_op jit(solution)/shard_map/ppermute | solution.py:31
  211.4 15.2 %collective-permute-start.51 = (bf16[128,1792]{1,0:T(8,128)(2,1)S(1)}, bf16[128,1792]{1,0:T(8,128)(2,1)S(1)}, u32[]{:S(2)}, u32[]{:S(2)}) collective-permute-start(bf16[128,1792]{1,0:T(8,128)(2,1)S(1)} %slice_bitcast_fusion.5), channel_id=1, source_target_pairs={{0,2},{1,3},{2,0},{3,1},{4,6},{5,7},{6,4},{7,5},{8,10},{9,11},{10,... | collective-permute-start | bytes 1376264 | tf_op jit(solution)/shard_map/ppermute | solution.py:35
  213.1 13.4 %collective-permute-start.53 = (bf16[128,1792]{1,0:T(8,128)(2,1)S(1)}, bf16[128,1792]{1,0:T(8,128)(2,1)S(1)}, u32[]{:S(2)}, u32[]{:S(2)}) collective-permute-start(bf16[128,1792]{1,0:T(8,128)(2,1)S(1)} %fusion.1), channel_id=1, source_target_pairs={{0,4},{1,5},{2,6},{3,7},{12,8},{13,9},{14,10},{15,11},{16,20},{17,... | collective-permute-start | bytes 1376264 | tf_op jit(solution)/shard_map/ppermute | solution.py:31
  (28 other events, 288.4 us)

commit v4 on v3

--- a/solution.py
+++ b/solution.py
@@ -21,14 +21,9 @@
     return lax.dot_general(left, right, dims, preferred_element_type=F32)
 
 
-def along_z(value, pairs):
-    perm = [
-        ((a * NX + x) * NC + c, (b * NX + x) * NC + c)
-        for a, b in pairs
-        for x in range(NX)
-        for c in range(NC)
-    ]
-    return lax.ppermute(value, "expert", perm)
+def swap_z(value, distance):
+    step = distance * NX * NC
+    return lax.ppermute(value, "expert", [(i, i ^ step) for i in range(NZ * NX * NC)])
 
 
 def swap_x(value):
@@ -41,12 +36,6 @@
 
 def swap_dp(value):
     return lax.ppermute(value, "dp", [(0, 1), (1, 0)])
-
-
-NEIGHBOUR = ((0, 1), (1, 0), (2, 3), (3, 2))
-MIDDLE = ((1, 2), (2, 1))
-OUTWARD = ((1, 0), (2, 3))
-INWARD = ((0, 1), (3, 2))
 
 
 def tie(value, *earlier):
@@ -281,8 +270,6 @@
     top_count = expert_ids.shape[1]
     slots = tokens.shape[0] * top_count // capacity.shape[0]
     own = lax.axis_index("expert")
-    z = own // (NX * NC)
-    inner = (z > 0) & (z < NZ - 1)
     who = jnp.stack([own.astype(jnp.int32), capacity[own]])
     weight_up, weight_down = up_weight[0], down_weight[0]
 
@@ -299,95 +286,73 @@
         rows_cot[s], part = front_cotangent(blocks, tables[s], weight_down, slots)
         cot[s] = (part, swap_dp(part))
 
+    act, chip = [None] * NZ, [None] * NZ
+
+    def last(s, *earlier):
+        parts = tie(pre[s] + cot[s], *earlier)
+        act[s], keep, send = back(tables[s][0], parts, weight_up, slots)
+        chip[s] = add(keep, swap_core(send))
+
+    z = own // (NX * NC)
+    columns = [[(k * NX + x) * NC + c for k in range(NZ)] for x in range(NX) for c in range(NC)]
+
+    def along_z(value):
+        return lax.all_gather(value, "expert", axis_index_groups=columns)
+
+    def at_distance(column, distance):
+        return lax.dynamic_index_in_dim(column, z ^ distance, 0, keepdims=False)
+
     tok = with_routing(tokens, expert_ids, gate_levels)
-    x0 = swap_x(tok)
-    near = along_z(tok, NEIGHBOUR)
-    two_in = along_z(tok, MIDDLE)
+    tok_column = along_z(tok)
+    cot_column = along_z(cotangent)
+    x_own = swap_x(tok)
     tok_core = swap_core(tok)
-
-    near, two_in = tie((near, two_in), x0)
-    x1 = swap_x(near)
-    far_in = along_z(near, MIDDLE)
-    two_out = along_z(two_in, OUTWARD)
-    first(0, tok, tok_core, x0)
-
-    two, far_in, cot_own = tie((jnp.where(inner, two_in, two_out), far_in, cotangent), x1, pre[0][0])
-    x2 = swap_x(two)
-    far_out = along_z(far_in, OUTWARD)
-    cot_near_in = along_z(cot_own, INWARD)
-    cot_two_in = along_z(cot_own, MIDDLE)
-    first(1, near, swap_core(near), x1)
-
-    far, cot_own, cot_near_in = tie(
-        (jnp.where(inner, far_in, far_out), cot_own, cot_near_in), x2, pre[1][0], pre[0][1]
-    )
-    x3 = swap_x(far)
-    cot_near_out = along_z(cot_own, OUTWARD)
-    cot_far_in = along_z(cot_near_in, MIDDLE)
-    first(2, two, swap_core(two), x2)
-
-    cot_near, cot_far_in = tie(
-        (jnp.where(inner, cot_near_in, cot_near_out), cot_far_in), x3, pre[2][0], pre[1][1]
-    )
-    x4 = swap_x(cot_near)
-    cot_far_out = along_z(cot_far_in, OUTWARD)
-    first(3, far, swap_core(far), x3)
-
-    cot_far, cot_two_in = tie(
-        (jnp.where(inner, cot_far_in, cot_far_out), cot_two_in), x4, pre[3][0], pre[2][1]
-    )
-    x5 = swap_x(cot_far)
-    cot_two_out = along_z(cot_two_in, OUTWARD)
-    second(1, cot_near, swap_core(cot_near), x4)
-
-    cot_two = tie(jnp.where(inner, cot_two_in, cot_two_out), x5, cot[1][0], pre[3][1])
-    x6 = swap_x(cot_two)
-    second(3, cot_far, swap_core(cot_far), x5)
-
-    cot_own = tie(cot_own, x6, cot[3][0], cot[1][1])
-    x7 = swap_x(cot_own)
-    second(2, cot_two, swap_core(cot_two), x6)
-
-    act, chip = [None] * NZ, [None] * NZ
-
-    def last(s):
-        act[s], keep, send = back(tables[s][0], pre[s] + cot[s], weight_up, slots)
-        chip[s] = add(keep, swap_core(send))
-
-    last(1)
-    near_send, cot_own = tie((chip[1][1], cot_own), x7, cot[2][0], cot[3][1])
-    x8 = swap_x(near_send)
-    second(0, cot_own, swap_core(cot_own), x7)
+    cot_own = tie(cotangent, x_own)
+    x_cot = swap_x(cot_own)
+    cot_core = swap_core(cot_own)
+    first(0, tok, tok_core, x_own)
+    second(0, cot_own, cot_core, tie(x_cot, pre[0][1]))
+
+    near = at_distance(tok_column, 1)
+    x_near = swap_x(tie(near, x_cot, cot[0][0]))
+    two = at_distance(tok_column, 2)
+    far = at_distance(tok_column, 3)
+    x_two = swap_x(tie(two, x_near))
+    first(1, near, swap_core(near), x_near)
+    x_far = swap_x(tie(far, x_two, pre[1][0], cot[0][1]))
+    first(2, two, swap_core(two), x_two)
+    last(0)
+
+    cot_far = tie(at_distance(cot_column, 3), x_far, pre[2][0], pre[1][1])
+    x_next = swap_x(cot_far)
+    first(3, far, swap_core(far), x_far)
+    cot_two = tie(at_distance(cot_column, 2), x_next, pre[3][0], pre[2][1])
+    x_then = swap_x(cot_two)
+    second(3, cot_far, swap_core(cot_far), x_next)
+    cot_near = tie(at_distance(cot_column, 1), x_then, cot[3][0], pre[3][1])
+    x_next = swap_x(cot_near)
+    second(2, cot_two, swap_core(cot_two), x_then)
+    x_own = swap_x(tie(chip[0][1], x_next, cot[2][0], cot[3][1]))
+    second(1, cot_near, swap_core(cot_near), x_next)
     last(3)
-
-    far_send = tie(chip[3][1], x8, cot[0][0], cot[2][1])
-    x9 = swap_x(far_send)
-    last(2)
-
-    two_send, far_sum = tie((chip[2][1], add(chip[3][0], x9)), cot[0][1])
-    x10 = swap_x(two_send)
-    hop_far = along_z(far_sum, INWARD)
-    last(0)
-
-    own_send, far_sum, two_sum = tie((chip[0][1], add(far_sum, hop_far), add(chip[2][0], x10)))
-    x11 = swap_x(own_send)
-    hop_far = along_z(far_sum, MIDDLE)
-    hop_two = along_z(two_sum, INWARD)
+    x_far = swap_x(tie(chip[3][1], cot[1][0]))
+    last(2, cot[1][0])
+    x_two = swap_x(tie(chip[2][1], x_far))
+    hop_far = swap_z(add(chip[3][0], x_far), 3)
     down_grad = weight_grad(
         down_grad_kernel,
         rows_cot,
         [p[0] for p in pre] + [p[1] for p in pre],
         [pltpu.VMEM((NZ,) + pre[0][0].shape, BF16)],
     )
-
-    near_sum, two_sum = tie(
-        (add(add(chip[1][0], x8), hop_far), add(two_sum, hop_two)), x11, down_grad
-    )
-    hop_near = along_z(near_sum, NEIGHBOUR)
-    hop_two = along_z(two_sum, MIDDLE)
+    last(1, down_grad)
+    x_near = swap_x(tie(chip[1][1], x_two))
+    hop_two = swap_z(add(chip[2][0], x_two), 2)
+    hop_near = swap_z(add(chip[1][0], x_near), 1)
     up_grad = weight_grad(up_grad_kernel, rows_in, act, [])
+    own_sum = chip[0][0].astype(F32) + x_own.astype(F32)
     token_grad = (
-        add(chip[0][0], x11).astype(F32) + hop_near.astype(F32) + hop_two.astype(F32)
+        own_sum + hop_near.astype(F32) + hop_two.astype(F32) + hop_far.astype(F32)
     ).astype(BF16)
     return token_grad, up_grad[None], down_grad[None]
 

time: 241 us -> 246 us (1.021); the launches traced: 240 us -> 242 us
  starting transfers between devices: 55.5 us -> 34.9 us
  local copies, waits for them, and re-layouts: 4.81 us -> 18.5 us
  between operations: 1.2 us -> 14.5 us
  waiting for transfers between devices: 125 us -> 120 us
  Pallas kernels: 48.1 us -> 50.7 us
    ppermute x12, waiting for transfers between devices: 30.4 us -> 73.4 us  [swap_x(): lax.ppermute(value, 'expert', [(i, i ^ NC) for i in range(NZ * NX * NC)])]
    ppermute x16 -> x3, waiting for transfers between devices: 53.7 us -> 12.2 us  [swap_z(): lax.ppermute(value, 'expert', [(i, i ^ step) for i in range(NZ * NX * NC)])]
    ppermute x16 -> x3, starting transfers between devices: 29.6 us -> 5.8 us  [swap_z(): lax.ppermute(value, 'expert', [(i, i ^ step) for i in range(NZ * NX * NC)])]
    ppermute x8, waiting for transfers between devices: 40.6 us -> 18.7 us  [swap_dp(): return lax.ppermute(value, 'dp', [(0, 1), (1, 0)])]
    all_gather x0 -> x2, waiting for transfers between devices: none -> 10.9 us  [along_z(): return lax.all_gather(value, 'expert', axis_index_groups=columns)]
    unnamed x8 -> x38, local copies, waits for them, and re-layouts: 2.05 us -> 12.8 us
    ppermute x20, waiting for transfers between devices: 0.05 us -> 4.31 us  [swap_core(): lax.ppermute(value, 'expert', [(i, i ^ 1) for i in range(NZ * NX * NC)])]
    ppermute x12, starting transfers between devices: 13.4 us -> 17.2 us  [swap_x(): lax.ppermute(value, 'expert', [(i, i ^ NC) for i in range(NZ * NX * NC)])]
  transfers between devices with their start and end apart: 56 -> 45, of which waited for: 25 -> 20; matrix products, arithmetic and copies ran while one was open for 2% -> 2% of each run, Pallas kernels for 20% -> 21%
where the time goes in v4:
time: 246 us; the launch traced here: 242 us
  waiting for transfers between devices  120 us (49%)
  Pallas kernels  50.7 us (21%)
  starting transfers between devices  34.9 us (14%)
  local copies, waits for them, and re-layouts  18.5 us (8%)
  between operations  14.5 us (6%)
  other arithmetic  4.32 us (2%)
    ppermute x12, waiting for transfers between devices, swap_x(): lax.ppermute(value, 'expert', [(i, i ^ NC) for i in range(NZ * NX * NC)])  73.4 us
    ppermute x8, waiting for transfers between devices, swap_dp(): return lax.ppermute(value, 'dp', [(0, 1), (1, 0)])  18.7 us
    ppermute x12, starting transfers between devices, swap_x(): lax.ppermute(value, 'expert', [(i, i ^ NC) for i in range(NZ * NX * NC)])  17.2 us
    pallas_call x4, Pallas kernels, front_tokens(): pl.pallas_call(functools.partial(tokens_kernel, top_count, slots), in_spe...  15.4 us
    pallas_call x2, Pallas kernels, weight_grad(): pl.pallas_call(kernel, grid=(width // tile,), in_specs=[pl.BlockSpec((row...  13.5 us
    unnamed x38, local copies, waits for them, and re-layouts  12.8 us
    ppermute x3, waiting for transfers between devices, swap_z(): lax.ppermute(value, 'expert', [(i, i ^ step) for i in range(NZ * NX * NC)])  12.2 us
    pallas_call x4, Pallas kernels, back(): pl.pallas_call(functools.partial(back_kernel, slots), grid=(width // tile...  11.7 us
  transfers between devices with their start and end apart: 45, of which 20 were waited for; matrix products, arithmetic and copies ran while one was open for 2% of the time, Pallas kernels for 21%

profile of v4, /device:TPU:8, one launch (start us, length us, event | category | flops | bytes accessed | tf_op | source)
XLA Modules:
  0.0 242.5 jit_solution(17320439166452200377)
XLA Ops:
  12.4 11.7 %collective-permute-done.1.m2.b2 = bf16[128,1920]{1,0:T(8,128)(2,1)S(1)} collective-permute-done((bf16[128,1920]{1,0:T(8,128)(2,1)}, bf16[128,1920]{1,0:T(8,128)(2,1)S(1)}, u32[]{:S(2)}, u32[]{:S(2)}) %collective-permute-start.1) | collective-permute-done | bytes 491552 | tf_op jit(solution)/shard_map/ppermute | solution.py:30
  26.0 2.0 copy-done
  29.1 3.6 %shard_map.94 = (bf16[256,1792]{1,0:T(8,128)(2,1)S(1)}, bf16[256,1024]{1,0:T(8,128)(2,1)S(1)}, s32[4,8,128]{2,1,0:T(8,128)S(1)}, f32[4,8,128]{2,1,0:T(8,128)S(1)}) custom-call(s32[2]{0:T(128)S(1)} %pad_add_fusion.own_ref, bf16[128,1920]{1,0:T(8,128)(2,1)S(1)} %copy-done.6, bf16[128,1920]{1,0:T(8,128)(2,1)S(1)} %collective-permute-done.m1.b1, ...), custom_call_target="tpu_custom_call" | custom-call | tf_op jit(solution)/shard_map/pallas_call | solution.py:146
  36.6 10.8 %collective-permute-done.5.b2 = bf16[128,1792]{1,0:T(8,128)(2,1)S(1)} collective-permute-done((bf16[128,1792]{1,0:T(8,128)(2,1)S(1)}, bf16[128,1792]{1,0:T(8,128)(2,1)S(1)}, u32[]{:S(2)}, u32[]{:S(2)}) %collective-permute-start.5) | collective-permute-done | bytes 458784 | tf_op jit(solution)/shard_map/ppermute | solution.py:30
  49.4 2.0 copy-done.4
  51.4 3.1 %shard_map.95 = (bf16[256,1792]{1,0:T(8,128)(2,1)S(1)}, bf16[256,1024]{1,0:T(8,128)(2,1)}) custom-call(s32[4,8,128]{2,1,0:T(8,128)S(1)} %get-tuple-element.67.slot_ref, f32[4,8,128]{2,1,0:T(8,128)S(1)} %get-tuple-element.69.gate_ref, bf16[128,1792]{1,0:T(8,128)(2,1)S(1)} %copy-done.7, bf16[128,1792]{1,0:T(8,128)(2,1)S(1)} %collective-permute-done.4.b1, ...), custom_call_target="tpu_custom_call" | custom-call | tf_op jit(solution)/shard_map/pallas_call | solution.py:163
  60.0 10.2 %collective-permute-done.9.m2.b2 = bf16[128,1920]{1,0:T(8,128)(2,1)S(1)} collective-permute-done((bf16[128,1920]{1,0:T(8,128)(2,1)S(1)}, bf16[128,1920]{1,0:T(8,128)(2,1)S(1)}, u32[]{:S(2)}, u32[]{:S(2)}) %collective-permute-start.9) | collective-permute-done | bytes 491552 | tf_op jit(solution)/shard_map/ppermute | solution.py:30
  72.1 2.1 copy-done.1
  74.2 3.6 %shard_map.97 = (bf16[256,1792]{1,0:T(8,128)(2,1)S(1)}, bf16[256,1024]{1,0:T(8,128)(2,1)S(1)}, s32[4,8,128]{2,1,0:T(8,128)S(1)}, f32[4,8,128]{2,1,0:T(8,128)S(1)}) custom-call(s32[2]{0:T(128)S(1)} %pad_add_fusion.own_ref, bf16[128,1920]{1,0:T(8,128)(2,1)S(1)} %get-tuple-element.79.m0.b0, bf16[128,1920]{1,0:T(8,128)(2,1)S(1)} %collective-permute-done.11.m1.b1, ...), custom_call_target="tpu_custom_call" | custom-call | tf_op jit(solution)/shard_map/pallas_call | solution.py:146
  81.0 2.9 %collective-permute-done.10.m2.b2 = bf16[128,1920]{1,0:T(8,128)(2,1)} collective-permute-done((bf16[128,1920]{1,0:T(8,128)(2,1)S(1)}, bf16[128,1920]{1,0:T(8,128)(2,1)}, u32[]{:S(2)}, u32[]{:S(2)}) %collective-permute-start.10) | collective-permute-done | bytes 491552 | tf_op jit(solution)/shard_map/ppermute | solution.py:30
  85.5 10.9 %all-gather.5.cloned.1.call-done = bf16[512,1792]{1,0:T(8,128)(2,1)} async-done(((bf16[128,1792]{1,0:T(8,128)(2,1)}), bf16[512,1792]{1,0:T(8,128)(2,1)}) %all-gather.5.cloned.1.call-update) | async-done | bytes 1835024 | tf_op jit(solution)/shard_map/all_gather | solution.py:300
  97.8 2.0 copy-done.2
  99.8 4.2 %shard_map.98 = (bf16[256,1792]{1,0:T(8,128)(2,1)S(1)}, bf16[256,1024]{1,0:T(8,128)(2,1)S(1)}, s32[4,8,128]{2,1,0:T(8,128)S(1)}, f32[4,8,128]{2,1,0:T(8,128)S(1)}) custom-call(s32[2]{0:T(128)S(1)} %copy-done.17, bf16[128,1920]{1,0:T(8,128)(2,1)S(1)} %get-tuple-element.80.m0.b0, bf16[128,1920]{1,0:T(8,128)(2,1)} %collective-permute-done.14.m1.b1, ...), custom_call_target="tpu_custom_call" | custom-call | tf_op jit(solution)/shard_map/pallas_call | solution.py:146
  107.6 8.6 %collective-permute-done.17.b2 = bf16[128,1792]{1,0:T(8,128)(2,1)S(1)} collective-permute-done((bf16[128,1792]{1,0:T(8,128)(2,1)S(1)}, bf16[128,1792]{1,0:T(8,128)(2,1)S(1)}, u32[]{:S(2)}, u32[]{:S(2)}) %collective-permute-start.17) | collective-permute-done | bytes 458784 | tf_op jit(solution)/shard_map/ppermute | solution.py:30
  116.2 4.0 %shard_map.99 = (bf16[256,1792]{1,0:T(8,128)(2,1)S(1)}, bf16[256,1024]{1,0:T(8,128)(2,1)S(1)}, s32[4,8,128]{2,1,0:T(8,128)S(1)}, f32[4,8,128]{2,1,0:T(8,128)S(1)}) custom-call(s32[2]{0:T(128)S(1)} %copy-done.17, bf16[128,1920]{1,0:T(8,128)(2,1)S(1)} %get-tuple-element.82.m0.b0, bf16[128,1920]{1,0:T(8,128)(2,1)S(1)} %collective-permute-done.18.m1.b1, ...), custom_call_target="tpu_custom_call" | custom-call | tf_op jit(solution)/shard_map/pallas_call | solution.py:146
  123.2 3.7 %shard_map.96 = (bf16[256,1024]{1,0:T(8,128)(2,1)S(1)}, bf16[2,128,1792]{2,1,0:T(8,128)(2,1)S(1)}, bf16[2,128,1792]{2,1,0:T(8,128)(2,1)S(1)}) custom-call(s32[4,8,128]{2,1,0:T(8,128)S(1)} %get-tuple-element.67.slot_ref, bf16[256,1024]{1,0:T(8,128)(2,1)S(1)} %get-tuple-element.73.pre_a.refs_4_, bf16[256,1024]{1,0:T(8,128)(2,1)S(1)} %collective-permute-done.3.pre_b.refs_8_, ...), custom_call_target="tpu_custom_call" | custom-call | tf_op jit(solution)/shard_map/pallas_call | solution.py:196
  127.0 2.3 shard_map.100
  130.2 4.2 %collective-permute-done.21.b2 = bf16[128,1792]{1,0:T(8,128)(2,1)S(1)} collective-permute-done((bf16[128,1792]{1,0:T(8,128)(2,1)S(1)}, bf16[128,1792]{1,0:T(8,128)(2,1)S(1)}, u32[]{:S(2)}, u32[]{:S(2)}) %collective-permute-start.21) | collective-permute-done | bytes 458784 | tf_op jit(solution)/shard_map/ppermute | solution.py:30
  136.4 9.4 %collective-permute-done.28.cot_b = bf16[256,1024]{1,0:T(8,128)(2,1)S(1)} collective-permute-done((bf16[256,1024]{1,0:T(8,128)(2,1)S(1)}, bf16[256,1024]{1,0:T(8,128)(2,1)S(1)}, u32[]{:S(2)}, u32[]{:S(2)}) %collective-permute-start.28) | collective-permute-done | bytes 524320 | tf_op jit(solution)/shard_map/ppermute | solution.py:38
  145.8 2.7 %shard_map.106 = (bf16[256,1024]{1,0:T(8,128)(2,1)S(1)}, bf16[2,128,1792]{2,1,0:T(8,128)(2,1)S(1)}, bf16[2,128,1792]{2,1,0:T(8,128)(2,1)S(1)}) custom-call(s32[4,8,128]{2,1,0:T(8,128)S(1)} %get-tuple-element.87.slot_ref, bf16[256,1024]{1,0:T(8,128)(2,1)S(1)} %get-tuple-element.114.refs_7_.pre_a, ...), custom_call_target="tpu_custom_call" | custom-call | tf_op jit(solution)/shard_map/pallas_call | solution.py:196
  149.1 2.3 shard_map.101
  154.7 2.3 shard_map.102
  157.7 8.6 %collective-permute-done.34.cot_b = bf16[256,1024]{1,0:T(8,128)(2,1)S(1)} collective-permute-done((bf16[256,1024]{1,0:T(8,128)(2,1)S(1)}, bf16[256,1024]{1,0:T(8,128)(2,1)S(1)}, u32[]{:S(2)}, u32[]{:S(2)}) %collective-permute-start.34) | collective-permute-done | bytes 524320 | tf_op jit(solution)/shard_map/ppermute | solution.py:38
  166.2 2.7 %shard_map.105 = (bf16[256,1024]{1,0:T(8,128)(2,1)S(1)}, bf16[2,128,1792]{2,1,0:T(8,128)(2,1)S(1)}, bf16[2,128,1792]{2,1,0:T(8,128)(2,1)S(1)}) custom-call(s32[4,8,128]{2,1,0:T(8,128)S(1)} %get-tuple-element.91.slot_ref, bf16[256,1024]{1,0:T(8,128)(2,1)S(1)} %get-tuple-element.108.refs_6_.pre_a, ...), custom_call_target="tpu_custom_call" | custom-call | tf_op jit(solution)/shard_map/pallas_call | solution.py:196
  171.4 7.3 %shard_map.103 = bf16[1792,1024]{1,0:T(8,128)(2,1)} custom-call(bf16[256,1792]{1,0:T(8,128)(2,1)S(1)} %copy-done.13, bf16[256,1792]{1,0:T(8,128)(2,1)S(1)} %get-tuple-element.99.refs_1_, bf16[256,1792]{1,0:T(8,128)(2,1)S(1)} %get-tuple-element.100.refs_2_, bf16[256,1792]{1,0:T(8,128)(2,1)S(1)} %get-tuple-element.101.refs_3_, ...), custom_call_target="tpu_custom_call" | custom-call | tf_op jit(solution)/shard_map/pallas_call | solution.py:244
  178.7 2.7 %shard_map.104 = (bf16[256,1024]{1,0:T(8,128)(2,1)S(1)}, bf16[2,128,1792]{2,1,0:T(8,128)(2,1)S(1)}, bf16[2,128,1792]{2,1,0:T(8,128)(2,1)S(1)}) custom-call(s32[4,8,128]{2,1,0:T(8,128)S(1)} %get-tuple-element.95.slot_ref, bf16[256,1024]{1,0:T(8,128)(2,1)S(1)} %get-tuple-element.102.refs_5_.pre_a, bf16[256,1024]{1,0:T(8,128)(2,1)S(1)} %collective-permute-done.16.refs_9_.pre_b, ...), custom_call_target="tpu_custom_call" | custom-call | tf_op jit(solution)/shard_map/pallas_call | solution.py:196
  186.7 15.2 %collective-permute-done.38 = bf16[128,1792]{1,0:T(8,128)(2,1)S(1)} collective-permute-done((bf16[128,1792]{1,0:T(8,128)(2,1)S(1)}, bf16[128,1792]{1,0:T(8,128)(2,1)S(1)}, u32[]{:S(2)}, u32[]{:S(2)}) %collective-permute-start.38) | collective-permute-done | bytes 458784 | tf_op jit(solution)/shard_map/ppermute | solution.py:30
  205.4 8.6 %collective-permute-done.39 = bf16[128,1792]{1,0:T(8,128)(2,1)S(1)} collective-permute-done((bf16[128,1792]{1,0:T(8,128)(2,1)S(1)}, bf16[128,1792]{1,0:T(8,128)(2,1)S(1)}, u32[]{:S(2)}, u32[]{:S(2)}) %collective-permute-start.39) | collective-permute-done | bytes 458784 | tf_op jit(solution)/shard_map/ppermute | solution.py:30
  214.1 2.0 collective-permute-start.40
  216.1 6.3 %shard_map.107 = bf16[1792,1024]{1,0:T(8,128)(2,1)} custom-call(bf16[256,1792]{1,0:T(8,128)(2,1)S(1)} %copy-done.9, bf16[256,1792]{1,0:T(8,128)(2,1)S(1)} %copy-done.11, bf16[256,1792]{1,0:T(8,128)(2,1)S(1)} %get-tuple-element.125.refs_2_, bf16[256,1792]{1,0:T(8,128)(2,1)S(1)} %get-tuple-element.126.refs_3_, ...), custom_call_target="tpu_custom_call" | custom-call | tf_op jit(solution)/shard_map/pallas_call | solution.py:244
  222.4 2.2 collective-permute-done.41
  224.6 10.0 %collective-permute-done.40 = bf16[128,1792]{1,0:T(8,128)(2,1)S(1)} collective-permute-done((bf16[128,1792]{1,0:T(8,128)(2,1)S(1)}, bf16[128,1792]{1,0:T(8,128)(2,1)S(1)}, u32[]{:S(2)}, u32[]{:S(2)}) %collective-permute-start.40) | collective-permute-done | bytes 458784 | tf_op jit(solution)/shard_map/ppermute | solution.py:26
  (135 shorter events, 53.9 us)
Async XLA Ops:
  7.2 48.3 %all-gather.7.cloned.1.call-start = ((), (), s32[]{:S(2)}) async-start(), calls=%async_computation.1 | async-start | bytes 2457600 | tf_op jit(solution)/shard_map/all_gather | solution.py:300
  10.8 85.5 %all-gather.5.cloned.1.call-start = ((), (), s32[]{:S(2)}) async-start(), calls=%async_computation | async-start | bytes 2293760 | tf_op jit(solution)/shard_map/all_gather | solution.py:300
  10.9 13.2 %collective-permute-start.1 = (bf16[128,1920]{1,0:T(8,128)(2,1)}, bf16[128,1920]{1,0:T(8,128)(2,1)S(1)}, u32[]{:S(2)}, u32[]{:S(2)}) collective-permute-start(bf16[128,1920]{1,0:T(8,128)(2,1)} %concatenate.3.m0.b0), channel_id=1, source_target_pairs={{0,2},{1,3},{2,0},{3,1},{4,6},{5,7},{6,4},{7,5},{8,10},{9,11},{10,... | collective-permute-start | bytes 1474568 | tf_op jit(solution)/shard_map/ppermute | solution.py:30
  12.4 13.0 %collective-permute-start = (bf16[128,1920]{1,0:T(8,128)(2,1)}, bf16[128,1920]{1,0:T(8,128)(2,1)S(1)}, u32[]{:S(2)}, u32[]{:S(2)}) collective-permute-start(bf16[128,1920]{1,0:T(8,128)(2,1)} %concatenate.3.m0.b0), channel_id=1, source_target_pairs={{0,1},{1,0},{2,3},{3,2},{4,5},{5,4},{6,7},{7,6},{8,9},{9,8},{10,11... | collective-permute-start | bytes 1474568 | tf_op jit(solution)/shard_map/ppermute | solution.py:34
  33.6 14.0 %collective-permute-start.3 = (bf16[256,1024]{1,0:T(8,128)(2,1)S(1)}, bf16[256,1024]{1,0:T(8,128)(2,1)S(1)}, u32[]{:S(2)}, u32[]{:S(2)}) collective-permute-start(bf16[256,1024]{1,0:T(8,128)(2,1)S(1)} %get-tuple-element.73.pre_a.refs_4_), channel_id=1, source_target_pairs={{0,16},{16,0},{1,17},{17,1},{2,18},{18,2},{3,19},{19,3},{4,20},{20... | collective-permute-start | bytes 1572872 | tf_op jit(solution)/shard_map/ppermute | solution.py:38
  35.1 12.3 %collective-permute-start.5 = (bf16[128,1792]{1,0:T(8,128)(2,1)S(1)}, bf16[128,1792]{1,0:T(8,128)(2,1)S(1)}, u32[]{:S(2)}, u32[]{:S(2)}) collective-permute-start(bf16[128,1792]{1,0:T(8,128)(2,1)S(1)} %copy-done.7), channel_id=1, source_target_pairs={{0,2},{1,3},{2,0},{3,1},{4,6},{5,7},{6,4},{7,5},{8,10},{9,11},{10,... | collective-permute-start | bytes 1376264 | tf_op jit(solution)/shard_map/ppermute | solution.py:30
  56.9 13.3 %collective-permute-start.9 = (bf16[128,1920]{1,0:T(8,128)(2,1)S(1)}, bf16[128,1920]{1,0:T(8,128)(2,1)S(1)}, u32[]{:S(2)}, u32[]{:S(2)}) collective-permute-start(bf16[128,1920]{1,0:T(8,128)(2,1)S(1)} %get-tuple-element.79.m0.b0), channel_id=1, source_target_pairs={{0,2},{1,3},{2,0},{3,1},{4,6},{5,7},{6,4},{7,5},{8,10},{9,11},{10,... | collective-permute-start | bytes 1474568 | tf_op jit(solution)/shard_map/ppermute | solution.py:30
  58.4 21.8 %collective-permute-start.7 = (bf16[256,1024]{1,0:T(8,128)(2,1)}, bf16[256,1024]{1,0:T(8,128)(2,1)S(1)}, u32[]{:S(2)}, u32[]{:S(2)}) collective-permute-start(bf16[256,1024]{1,0:T(8,128)(2,1)} %get-tuple-element.75.cot_a), channel_id=1, source_target_pairs={{0,16},{16,0},{1,17},{17,1},{2,18},{18,2},{3,19},{19,3},{4,20},{20... | collective-permute-start | bytes 1572872 | tf_op jit(solution)/shard_map/ppermute | solution.py:38
  70.2 13.7 %collective-permute-start.10 = (bf16[128,1920]{1,0:T(8,128)(2,1)S(1)}, bf16[128,1920]{1,0:T(8,128)(2,1)}, u32[]{:S(2)}, u32[]{:S(2)}) collective-permute-start(bf16[128,1920]{1,0:T(8,128)(2,1)S(1)} %get-tuple-element.80.m0.b0), channel_id=1, source_target_pairs={{0,2},{1,3},{2,0},{3,1},{4,6},{5,7},{6,4},{7,5},{8,10},{9,11},{10,... | collective-permute-start | bytes 1474568 | tf_op jit(solution)/shard_map/ppermute | solution.py:30
  78.7 25.3 %collective-permute-start.16 = (bf16[256,1024]{1,0:T(8,128)(2,1)S(1)}, bf16[256,1024]{1,0:T(8,128)(2,1)S(1)}, u32[]{:S(2)}, u32[]{:S(2)}) collective-permute-start(bf16[256,1024]{1,0:T(8,128)(2,1)S(1)} %get-tuple-element.102.refs_5_.pre_a), channel_id=1, source_target_pairs={{0,16},{16,0},{1,17},{17,1},{2,18},{18,2},{3,19},{19,3},{4,20},{20... | collective-permute-start | bytes 1572872 | tf_op jit(solution)/shard_map/ppermute | solution.py:38
  80.2 17.5 %collective-permute-start.14 = (bf16[128,1920]{1,0:T(8,128)(2,1)S(1)}, bf16[128,1920]{1,0:T(8,128)(2,1)}, u32[]{:S(2)}, u32[]{:S(2)}) collective-permute-start(bf16[128,1920]{1,0:T(8,128)(2,1)S(1)} %get-tuple-element.80.m0.b0), channel_id=1, source_target_pairs={{0,1},{1,0},{2,3},{3,2},{4,5},{5,4},{6,7},{7,6},{8,9},{9,8},{10,11... | collective-permute-start | bytes 1474568 | tf_op jit(solution)/shard_map/ppermute | solution.py:34
  84.0 13.8 %collective-permute-start.15 = (bf16[128,1920]{1,0:T(8,128)(2,1)}, bf16[128,1920]{1,0:T(8,128)(2,1)}, u32[]{:S(2)}, u32[]{:S(2)}) collective-permute-start(bf16[128,1920]{1,0:T(8,128)(2,1)} %collective-permute-done.10.m2.b2), channel_id=1, source_target_pairs={{0,1},{1,0},{2,3},{3,2},{4,5},{5,4},{6,7},{7,6},{8,9},{9,8},{10,11... | collective-permute-start | bytes 1474568 | tf_op jit(solution)/shard_map/ppermute | solution.py:34
  84.0 20.1 %collective-permute-start.13 = (bf16[128,1920]{1,0:T(8,128)(2,1)S(1)}, bf16[128,1920]{1,0:T(8,128)(2,1)}, u32[]{:S(2)}, u32[]{:S(2)}) collective-permute-start(bf16[128,1920]{1,0:T(8,128)(2,1)S(1)} %get-tuple-element.82.m0.b0), channel_id=1, source_target_pairs={{0,2},{1,3},{2,0},{3,1},{4,6},{5,7},{6,4},{7,5},{8,10},{9,11},{10,... | collective-permute-start | bytes 1474568 | tf_op jit(solution)/shard_map/ppermute | solution.py:30
  106.1 15.6 %collective-permute-start.20 = (bf16[256,1024]{1,0:T(8,128)(2,1)S(1)}, bf16[256,1024]{1,0:T(8,128)(2,1)S(1)}, u32[]{:S(2)}, u32[]{:S(2)}) collective-permute-start(bf16[256,1024]{1,0:T(8,128)(2,1)S(1)} %get-tuple-element.108.refs_6_.pre_a), channel_id=1, source_target_pairs={{0,16},{16,0},{1,17},{17,1},{2,18},{18,2},{3,19},{19,3},{4,20},{20... | collective-permute-start | bytes 1572872 | tf_op jit(solution)/shard_map/ppermute | solution.py:38
  107.6 19.4 %collective-permute-start.22 = (bf16[128,1792]{1,0:T(8,128)(2,1)S(1)}, bf16[128,1792]{1,0:T(8,128)(2,1)S(1)}, u32[]{:S(2)}, u32[]{:S(2)}) collective-permute-start(bf16[128,1792]{1,0:T(8,128)(2,1)S(1)} %get-tuple-element.84.b0), channel_id=1, source_target_pairs={{0,1},{1,0},{2,3},{3,2},{4,5},{5,4},{6,7},{7,6},{8,9},{9,8},{10,11... | collective-permute-start | bytes 1376264 | tf_op jit(solution)/shard_map/ppermute | solution.py:34
  120.2 14.8 %collective-permute-start.24 = (bf16[256,1024]{1,0:T(8,128)(2,1)S(1)}, bf16[256,1024]{1,0:T(8,128)(2,1)S(1)}, u32[]{:S(2)}, u32[]{:S(2)}) collective-permute-start(bf16[256,1024]{1,0:T(8,128)(2,1)S(1)} %get-tuple-element.114.refs_7_.pre_a), channel_id=1, source_target_pairs={{0,16},{16,0},{1,17},{17,1},{2,18},{18,2},{3,19},{19,3},{4,20},{20... | collective-permute-start | bytes 1572872 | tf_op jit(solution)/shard_map/ppermute | solution.py:38
  121.7 12.6 %collective-permute-start.21 = (bf16[128,1792]{1,0:T(8,128)(2,1)S(1)}, bf16[128,1792]{1,0:T(8,128)(2,1)S(1)}, u32[]{:S(2)}, u32[]{:S(2)}) collective-permute-start(bf16[128,1792]{1,0:T(8,128)(2,1)S(1)} %get-tuple-element.86.b0), channel_id=1, source_target_pairs={{0,2},{1,3},{2,0},{3,1},{4,6},{5,7},{6,4},{7,5},{8,10},{9,11},{10,... | collective-permute-start | bytes 1376264 | tf_op jit(solution)/shard_map/ppermute | solution.py:30
  126.9 26.0 %collective-permute-start.8 = (bf16[2,128,1792]{2,1,0:T(8,128)(2,1)S(1)}, bf16[2,128,1792]{2,1,0:T(8,128)(2,1)S(1)}, u32[]{:S(2)}, u32[]{:S(2)}) collective-permute-start(bf16[2,128,1792]{2,1,0:T(8,128)(2,1)S(1)} %get-tuple-element.78), channel_id=1, source_target_pairs={{0,1},{1,0},{2,3},{3,2},{4,5},{5,4},{6,7},{7,6},{8,9},{9,8},{10,11... | collective-permute-start | bytes 2752520 | tf_op jit(solution)/shard_map/ppermute | solution.py:34
  129.3 16.5 %collective-permute-start.28 = (bf16[256,1024]{1,0:T(8,128)(2,1)S(1)}, bf16[256,1024]{1,0:T(8,128)(2,1)S(1)}, u32[]{:S(2)}, u32[]{:S(2)}) collective-permute-start(bf16[256,1024]{1,0:T(8,128)(2,1)S(1)} %get-tuple-element.116.cot_a), channel_id=1, source_target_pairs={{0,16},{16,0},{1,17},{17,1},{2,18},{18,2},{3,19},{19,3},{4,20},{20... | collective-permute-start | bytes 1572872 | tf_op jit(solution)/shard_map/ppermute | solution.py:38
  130.0 18.6 %collective-permute-start.26 = (bf16[128,1792]{1,0:T(8,128)(2,1)S(1)}, bf16[128,1792]{1,0:T(8,128)(2,1)S(1)}, u32[]{:S(2)}, u32[]{:S(2)}) collective-permute-start(bf16[128,1792]{1,0:T(8,128)(2,1)S(1)} %get-tuple-element.86.b0), channel_id=1, source_target_pairs={{0,1},{1,0},{2,3},{3,2},{4,5},{5,4},{6,7},{7,6},{8,9},{9,8},{10,11... | collective-permute-start | bytes 1376264 | tf_op jit(solution)/shard_map/ppermute | solution.py:34
  134.4 14.7 %collective-permute-start.27 = (bf16[128,1792]{1,0:T(8,128)(2,1)S(1)}, bf16[128,1792]{1,0:T(8,128)(2,1)S(1)}, u32[]{:S(2)}, u32[]{:S(2)}) collective-permute-start(bf16[128,1792]{1,0:T(8,128)(2,1)S(1)} %collective-permute-done.21.b2), channel_id=1, source_target_pairs={{0,1},{1,0},{2,3},{3,2},{4,5},{5,4},{6,7},{7,6},{8,9},{9,8},{10,11... | collective-permute-start | bytes 1376264 | tf_op jit(solution)/shard_map/ppermute | solution.py:34
  135.0 18.0 %collective-permute-start.25 = (bf16[128,1792]{1,0:T(8,128)(2,1)S(1)}, bf16[128,1792]{1,0:T(8,128)(2,1)S(1)}, u32[]{:S(2)}, u32[]{:S(2)}) collective-permute-start(bf16[128,1792]{1,0:T(8,128)(2,1)S(1)} %get-tuple-element.90.b0), channel_id=1, source_target_pairs={{0,2},{1,3},{2,0},{3,1},{4,6},{5,7},{6,4},{7,5},{8,10},{9,11},{10,... | collective-permute-start | bytes 1376264 | tf_op jit(solution)/shard_map/ppermute | solution.py:30
  148.5 20.5 %collective-permute-start.36 = (bf16[2,128,1792]{2,1,0:T(8,128)(2,1)S(1)}, bf16[2,128,1792]{2,1,0:T(8,128)(2,1)S(1)}, u32[]{:S(2)}, u32[]{:S(2)}) collective-permute-start(bf16[2,128,1792]{2,1,0:T(8,128)(2,1)S(1)} %get-tuple-element.119), channel_id=1, source_target_pairs={{0,1},{1,0},{2,3},{3,2},{4,5},{5,4},{6,7},{7,6},{8,9},{9,8},{10,11... | collective-permute-start | bytes 2752520 | tf_op jit(solution)/shard_map/ppermute | solution.py:34
  151.4 14.8 %collective-permute-start.34 = (bf16[256,1024]{1,0:T(8,128)(2,1)S(1)}, bf16[256,1024]{1,0:T(8,128)(2,1)S(1)}, u32[]{:S(2)}, u32[]{:S(2)}) collective-permute-start(bf16[256,1024]{1,0:T(8,128)(2,1)S(1)} %get-tuple-element.110.cot_a), channel_id=1, source_target_pairs={{0,16},{16,0},{1,17},{17,1},{2,18},{18,2},{3,19},{19,3},{4,20},{20... | collective-permute-start | bytes 1572872 | tf_op jit(solution)/shard_map/ppermute | solution.py:38
  157.0 21.7 %collective-permute-start.32 = (bf16[256,1024]{1,0:T(8,128)(2,1)S(1)}, bf16[256,1024]{1,0:T(8,128)(2,1)S(1)}, u32[]{:S(2)}, u32[]{:S(2)}) collective-permute-start(bf16[256,1024]{1,0:T(8,128)(2,1)S(1)} %get-tuple-element.104.cot_a), channel_id=1, source_target_pairs={{0,16},{16,0},{1,17},{17,1},{2,18},{18,2},{3,19},{19,3},{4,20},{20... | collective-permute-start | bytes 1572872 | tf_op jit(solution)/shard_map/ppermute | solution.py:38
  168.9 15.7 %collective-permute-start.35 = (bf16[2,128,1792]{2,1,0:T(8,128)(2,1)S(1)}, bf16[2,128,1792]{2,1,0:T(8,128)(2,1)S(1)}, u32[]{:S(2)}, u32[]{:S(2)}) collective-permute-start(bf16[2,128,1792]{2,1,0:T(8,128)(2,1)S(1)} %get-tuple-element.113), channel_id=1, source_target_pairs={{0,1},{1,0},{2,3},{3,2},{4,5},{5,4},{6,7},{7,6},{8,9},{9,8},{10,11... | collective-permute-start | bytes 2752520 | tf_op jit(solution)/shard_map/ppermute | solution.py:34
  169.3 13.4 %collective-permute-start.37 = (bf16[128,1792]{1,0:T(8,128)(2,1)S(1)}, bf16[128,1792]{1,0:T(8,128)(2,1)S(1)}, u32[]{:S(2)}, u32[]{:S(2)}) collective-permute-start(bf16[128,1792]{1,0:T(8,128)(2,1)S(1)} %slice_bitcast_fusion.2), channel_id=1, source_target_pairs={{0,2},{1,3},{2,0},{3,1},{4,6},{5,7},{6,4},{7,5},{8,10},{9,11},{10,... | collective-permute-start | bytes 1376264 | tf_op jit(solution)/shard_map/ppermute | solution.py:30
  170.8 51.6 %collective-permute-start.29 = (bf16[128,1792]{1,0:T(8,128)(2,1)S(1)}, bf16[128,1792]{1,0:T(8,128)(2,1)S(1)}, u32[]{:S(2)}, u32[]{:S(2)}) collective-permute-start(bf16[128,1792]{1,0:T(8,128)(2,1)S(1)} %slice_bitcast_fusion.6), channel_id=1, source_target_pairs={{0,2},{1,3},{2,0},{3,1},{4,6},{5,7},{6,4},{7,5},{8,10},{9,11},{10,... | collective-permute-start | bytes 1376264 | tf_op jit(solution)/shard_map/ppermute | solution.py:30
  182.8 39.6 %collective-permute-start.42 = (bf16[128,1792]{1,0:T(8,128)(2,1)S(1)}, bf16[128,1792]{1,0:T(8,128)(2,1)S(1)}, u32[]{:S(2)}, u32[]{:S(2)}) collective-permute-start(bf16[128,1792]{1,0:T(8,128)(2,1)S(1)} %fusion), channel_id=1, source_target_pairs={{0,12},{1,13},{2,14},{3,15},{4,8},{5,9},{6,10},{7,11},{8,4},{9,5},... | collective-permute-start | bytes 1376264 | tf_op jit(solution)/shard_map/ppermute | solution.py:26
  184.8 17.0 %collective-permute-start.38 = (bf16[128,1792]{1,0:T(8,128)(2,1)S(1)}, bf16[128,1792]{1,0:T(8,128)(2,1)S(1)}, u32[]{:S(2)}, u32[]{:S(2)}) collective-permute-start(bf16[128,1792]{1,0:T(8,128)(2,1)S(1)} %slice_bitcast_fusion.3), channel_id=1, source_target_pairs={{0,2},{1,3},{2,0},{3,1},{4,6},{5,7},{6,4},{7,5},{8,10},{9,11},{10,... | collective-permute-start | bytes 1376264 | tf_op jit(solution)/shard_map/ppermute | solution.py:30
  203.5 21.2 %collective-permute-start.41 = (bf16[128,1792]{1,0:T(8,128)(2,1)S(1)}, bf16[128,1792]{1,0:T(8,128)(2,1)S(1)}, u32[]{:S(2)}, u32[]{:S(2)}) collective-permute-start(bf16[128,1792]{1,0:T(8,128)(2,1)S(1)} %fusion.1), channel_id=1, source_target_pairs={{0,8},{1,9},{2,10},{3,11},{4,12},{5,13},{6,14},{7,15},{8,0},{9,1},... | collective-permute-start | bytes 1376264 | tf_op jit(solution)/shard_map/ppermute | solution.py:26
  214.1 20.5 %collective-permute-start.40 = (bf16[128,1792]{1,0:T(8,128)(2,1)S(1)}, bf16[128,1792]{1,0:T(8,128)(2,1)S(1)}, u32[]{:S(2)}, u32[]{:S(2)}) collective-permute-start(bf16[128,1792]{1,0:T(8,128)(2,1)S(1)} %fusion.2), channel_id=1, source_target_pairs={{0,4},{1,5},{2,6},{3,7},{4,0},{5,1},{6,2},{7,3},{8,12},{9,13},{10,... | collective-permute-start | bytes 1376264 | tf_op jit(solution)/shard_map/ppermute | solution.py:26
  (32 other events, 299.6 us)
Sparse Core Ops, SparseCore 0:
  10.9 43.4 all-gather.6
  56.0 40.3 all-gather.4

commit v5 on v3

--- a/solution.py
+++ b/solution.py
@@ -46,7 +46,9 @@
 NEIGHBOUR = ((0, 1), (1, 0), (2, 3), (3, 2))
 MIDDLE = ((1, 2), (2, 1))
 OUTWARD = ((1, 0), (2, 3))
-INWARD = ((0, 1), (3, 2))
+TWO_INWARD = ((0, 2), (3, 1))
+TWO_OUTWARD = ((1, 3), (2, 0))
+THREE = ((0, 3), (3, 0))
 
 
 def tie(value, *earlier):
@@ -64,11 +66,10 @@
 LANES = 128
 
 
-def with_routing(tokens, expert_ids, gate_levels):
-    half = LANES // 2
-    room = ((0, 0), (0, half - expert_ids.shape[1]))
-    parts = [tokens, jnp.pad(expert_ids, room).astype(BF16), jnp.pad(gate_levels, room).astype(BF16)]
-    return jnp.concatenate(parts, axis=1)
+def joined(tokens, cotangent, expert_ids, gate_levels):
+    room = ((0, 0), (0, LANES // 2 - expert_ids.shape[1]))
+    tables = [jnp.pad(table.astype(BF16), room) for table in (expert_ids, gate_levels)]
+    return jnp.concatenate([tokens, cotangent] + tables, axis=1)
 
 
 def read_routing(meta, own, limit, top_count):
@@ -88,103 +89,87 @@
     return jnp.where(kept, rank, -1.0).astype(jnp.int32), level / total
 
 
-def add_up(total, part_ref, product):
-    step = pl.program_id(0)
+def front_kernel(top_count, slots, own_ref, *refs):
+    metas, tok_blocks, cot_blocks = refs[:4], refs[4:8], refs[8:12]
+    up_ref, down_ref, rows_ref, rows_cot_ref, part_ref, slot_ref, gates, total = refs[12:]
+    step, hidden = pl.program_id(0), up_ref.shape[1]
 
     @pl.when(step == 0)
-    def _():
-        total[...] = product
-
-    @pl.when(step > 0)
-    def _():
-        total[...] += product
-
-    @pl.when(step == pl.num_programs(0) - 1)
-    def _():
-        part_ref[...] = total[...].astype(BF16)
-
-
-def tokens_kernel(top_count, slots, own_ref, m0, m1, m2, m3, b0, b1, b2, b3, weight_ref, rows_ref, part_ref, slot_ref, gate_ref, total):
-    @pl.when(pl.program_id(0) == 0)
     def _():
         own = own_ref[0].astype(F32)
         limit = own_ref[1].astype(F32)
-        for index, meta in enumerate((m0, m1, m2, m3)):
+        for index, meta in enumerate(metas):
             slot, gate = read_routing(meta[...], own, limit, top_count)
             slot_ref[index] = slot
-            gate_ref[index] = gate
-
-    for index, block in enumerate((b0, b1, b2, b3)):
+            gates[index] = gate
+
+    for index in range(4):
         hit = placing_of(slot_ref[index, 0:1, :], slots)
-        picked = dot_f32(jnp.where(hit, 1.0, 0.0).astype(BF16), block[...])
-        rows_ref[index * slots : (index + 1) * slots, :] = picked.astype(BF16)
-    add_up(total, part_ref, dot_f32(rows_ref[...], weight_ref[...]))
-
-
-def cotangent_kernel(slots, slot_ref, gate_ref, b0, b1, b2, b3, weight_ref, rows_ref, part_ref, total):
-    for index, block in enumerate((b0, b1, b2, b3)):
-        hit = placing_of(slot_ref[index, 0:1, :], slots)
-        picked = dot_f32(jnp.where(hit, 1.0, 0.0).astype(BF16), block[...])
-        gate = jnp.sum(jnp.where(hit, gate_ref[index, 0:1, :], 0.0), axis=1, keepdims=True)
-        rows_ref[index * slots : (index + 1) * slots, :] = (picked * gate).astype(BF16)
-    add_up(total, part_ref, dot_f32(rows_ref[...], weight_ref[...]))
-
-
-def front_specs(tok_rows, width, hidden, rows):
+        placing = jnp.where(hit, 1.0, 0.0).astype(BF16)
+        gate = jnp.sum(jnp.where(hit, gates[index, 0:1, :], 0.0), axis=1, keepdims=True)
+        here = slice(index * slots, (index + 1) * slots)
+        rows_ref[here, :] = dot_f32(placing, tok_blocks[index][...]).astype(BF16)
+        rows_cot_ref[here, :] = (gate * dot_f32(placing, cot_blocks[index][...])).astype(BF16)
+    products = (dot_f32(rows_ref[...], up_ref[...]), dot_f32(rows_cot_ref[...], down_ref[...]))
+
+    @pl.when(step == 0)
+    def _():
+        for half, product in enumerate(products):
+            total[half] = product
+
+    @pl.when(step > 0)
+    def _():
+        for half, product in enumerate(products):
+            total[half] += product
+
+    @pl.when(step == pl.num_programs(0) - 1)
+    def _():
+        for half in range(2):
+            part_ref[:, half * hidden : (half + 1) * hidden] = total[half].astype(BF16)
+
+
+def front(blocks, own, weight_up, weight_down, slots, top_count):
+    tok_rows = blocks[0].shape[0]
+    width, hidden = weight_up.shape
+    rows = 4 * slots
     tile = width // 2
-    table = pl.BlockSpec((4, 8, tok_rows), lambda k: (0, 0, 0))
-    blocks = [pl.BlockSpec((tok_rows, tile), lambda k: (0, k))] * 4
     weight = pl.BlockSpec((tile, hidden), lambda k: (k, 0))
-    outs = [
-        pl.BlockSpec((rows, tile), lambda k: (0, k)),
-        pl.BlockSpec((rows, hidden), lambda k: (0, 0)),
-    ]
-    shapes = [jax.ShapeDtypeStruct((rows, width), BF16), jax.ShapeDtypeStruct((rows, hidden), BF16)]
-    rest = dict(
+    picked = pl.BlockSpec((rows, tile), lambda k: (0, k))
+    return pl.pallas_call(
+        functools.partial(front_kernel, top_count, slots),
         grid=(width // tile,),
-        scratch_shapes=[pltpu.VMEM((rows, hidden), F32)],
-        compiler_params=pltpu.CompilerParams(vmem_limit_bytes=24 * 1024 * 1024),
+        in_specs=[pl.BlockSpec(memory_space=pltpu.SMEM)]
+        + [pl.BlockSpec((tok_rows, LANES), lambda k: (0, 2 * width // LANES))] * 4
+        + [pl.BlockSpec((tok_rows, tile), lambda k: (0, k))] * 4
+        + [pl.BlockSpec((tok_rows, tile), lambda k: (0, width // tile + k))] * 4
+        + [weight, weight],
+        out_specs=[
+            picked,
+            picked,
+            pl.BlockSpec((rows, 2 * hidden), lambda k: (0, 0)),
+            pl.BlockSpec((4, 8, tok_rows), lambda k: (0, 0, 0)),
+        ],
+        out_shape=[
+            jax.ShapeDtypeStruct((rows, width), BF16),
+            jax.ShapeDtypeStruct((rows, width), BF16),
+            jax.ShapeDtypeStruct((rows, 2 * hidden), BF16),
+            jax.ShapeDtypeStruct((4, 8, tok_rows), jnp.int32),
+        ],
+        scratch_shapes=[
+            pltpu.VMEM((4, 8, tok_rows), F32),
+            pltpu.VMEM((2, rows, hidden), F32),
+        ],
+        compiler_params=pltpu.CompilerParams(vmem_limit_bytes=32 * 1024 * 1024),
         cost_estimate=NO_COST,
-    )
-    return table, blocks, weight, outs, shapes, rest
-
-
-def front_tokens(blocks, own, weight, slots, top_count):
-    tok_rows = blocks[0].shape[0]
-    width, hidden = weight.shape
-    table, block_specs, weight_spec, outs, shapes, rest = front_specs(tok_rows, width, hidden, 4 * slots)
-    meta = pl.BlockSpec((tok_rows, LANES), lambda k: (0, width // LANES))
-    return pl.pallas_call(
-        functools.partial(tokens_kernel, top_count, slots),
-        in_specs=[pl.BlockSpec(memory_space=pltpu.SMEM)] + [meta] * 4 + block_specs + [weight_spec],
-        out_specs=outs + [table, table],
-        out_shape=shapes
-        + [
-            jax.ShapeDtypeStruct((4, 8, tok_rows), jnp.int32),
-            jax.ShapeDtypeStruct((4, 8, tok_rows), F32),
-        ],
-        **rest,
-    )(own, *blocks, *blocks, weight)
-
-
-def front_cotangent(blocks, tables, weight, slots):
-    tok_rows = blocks[0].shape[0]
-    width, hidden = weight.shape
-    table, block_specs, weight_spec, outs, shapes, rest = front_specs(tok_rows, width, hidden, 4 * slots)
-    return pl.pallas_call(
-        functools.partial(cotangent_kernel, slots),
-        in_specs=[table, table] + block_specs + [weight_spec],
-        out_specs=outs,
-        out_shape=shapes,
-        **rest,
-    )(*tables, *blocks, weight)
-
-
-def back_kernel(slots, slot_ref, pre_a, pre_b, cot_a, cot_b, weight_ref, act_ref, keep_ref, send_ref):
+    )(own, *blocks, *blocks, *blocks, weight_up, weight_down)
+
+
+def back_kernel(slots, slot_ref, part_a, part_b, weight_ref, act_ref, keep_ref, send_ref):
     @pl.when(pl.program_id(0) == 0)
     def _():
-        preact = pre_a[...].astype(F32) + pre_b[...].astype(F32)
-        hidden_cot = cot_a[...].astype(F32) + cot_b[...].astype(F32)
+        hidden = act_ref.shape[1]
+        preact = part_a[:, :hidden].astype(F32) + part_b[:, :hidden].astype(F32)
+        hidden_cot = part_a[:, hidden:].astype(F32) + part_b[:, hidden:].astype(F32)
         sigmoid = jax.nn.sigmoid(preact)
         act_ref[...] = (hidden_cot * (sigmoid * (1.0 + preact * (1.0 - sigmoid)))).astype(BF16)
 
@@ -208,7 +193,7 @@
         functools.partial(back_kernel, slots),
         grid=(width // tile,),
         in_specs=[pl.BlockSpec((4, 8, tok_rows), lambda n: (0, 0, 0))]
-        + [full] * 4
+        + [pl.BlockSpec((rows, 2 * hidden), lambda n: (0, 0))] * 2
         + [pl.BlockSpec((tile, hidden), lambda n: (n, 0))],
         out_specs=[full, spread, spread],
         out_shape=[
@@ -247,9 +232,8 @@
     out_ref[...] = total.astype(BF16)
 
 
-def weight_grad(kernel, lefts, rights, scratch_shapes):
+def weight_grad(kernel, hidden, lefts, rights, scratch_shapes):
     rows, width = lefts[0].shape
-    hidden = rights[0].shape[1]
     count = len(lefts)
     tile = 256
     return pl.pallas_call(
@@ -286,109 +270,79 @@
     who = jnp.stack([own.astype(jnp.int32), capacity[own]])
     weight_up, weight_down = up_weight[0], down_weight[0]
 
-    rows_in, rows_cot, tables, pre, cot = ([None] * NZ for _ in range(5))
-
-    def first(s, mine, mine_core, other):
-        blocks = (mine, mine_core, other, swap_core(other))
-        rows_in[s], part, slot, gate = front_tokens(blocks, who, weight_up, slots, top_count)
-        tables[s] = (slot, gate)
-        pre[s] = (part, swap_dp(part))
-
-    def second(s, mine, mine_core, other):
-        blocks = (mine, mine_core, other, swap_core(other))
-        rows_cot[s], part = front_cotangent(blocks, tables[s], weight_down, slots)
-        cot[s] = (part, swap_dp(part))
-
-    tok = with_routing(tokens, expert_ids, gate_levels)
-    x0 = swap_x(tok)
-    near = along_z(tok, NEIGHBOUR)
-    two_in = along_z(tok, MIDDLE)
-    tok_core = swap_core(tok)
-
-    near, two_in = tie((near, two_in), x0)
-    x1 = swap_x(near)
+    hidden_units = weight_up.shape[1]
+
+    rows_in, rows_cot, slot_of, parts, act, chip = ([None] * NZ for _ in range(6))
+
+    def forth(s, *blocks):
+        rows_in[s], rows_cot[s], part, slot_of[s] = front(
+            blocks, who, weight_up, weight_down, slots, top_count
+        )
+        parts[s] = (part, swap_dp(part))
+
+    def back_again(s, *earlier):
+        pair = tie(parts[s], *earlier)
+        act[s], keep, send = back(slot_of[s], pair, weight_up, slots)
+        chip[s] = add(keep, swap_core(send))
+
+    block = joined(tokens, cotangent, expert_ids, gate_levels)
+    x_own = swap_x(block)
+    near = along_z(block, NEIGHBOUR)
+    two_in = along_z(block, MIDDLE)
+    own_core = swap_core(block)
+
+    near, two_in = tie((near, two_in), x_own)
+    x_near = swap_x(near)
     far_in = along_z(near, MIDDLE)
     two_out = along_z(two_in, OUTWARD)
-    first(0, tok, tok_core, x0)
-
-    two, far_in, cot_own = tie((jnp.where(inner, two_in, two_out), far_in, cotangent), x1, pre[0][0])
-    x2 = swap_x(two)
+    near_core = swap_core(near)
+    forth(0, block, own_core, x_own, swap_core(x_own))
+
+    two, far_in = tie((jnp.where(inner, two_in, two_out), far_in), x_near, parts[0][0])
+    x_two = swap_x(two)
     far_out = along_z(far_in, OUTWARD)
-    cot_near_in = along_z(cot_own, INWARD)
-    cot_two_in = along_z(cot_own, MIDDLE)
-    first(1, near, swap_core(near), x1)
-
-    far, cot_own, cot_near_in = tie(
-        (jnp.where(inner, far_in, far_out), cot_own, cot_near_in), x2, pre[1][0], pre[0][1]
-    )
-    x3 = swap_x(far)
-    cot_near_out = along_z(cot_own, OUTWARD)
-    cot_far_in = along_z(cot_near_in, MIDDLE)
-    first(2, two, swap_core(two), x2)
-
-    cot_near, cot_far_in = tie(
-        (jnp.where(inner, cot_near_in, cot_near_out), cot_far_in), x3, pre[2][0], pre[1][1]
-    )
-    x4 = swap_x(cot_near)
-    cot_far_out = along_z(cot_far_in, OUTWARD)
-    first(3, far, swap_core(far), x3)
-
-    cot_far, cot_two_in = tie(
-        (jnp.where(inner, cot_far_in, cot_far_out), cot_two_in), x4, pre[3][0], pre[2][1]
-    )
-    x5 = swap_x(cot_far)
-    cot_two_out = along_z(cot_two_in, OUTWARD)
-    second(1, cot_near, swap_core(cot_near), x4)
-
-    cot_two = tie(jnp.where(inner, cot_two_in, cot_two_out), x5, cot[1][0], pre[3][1])
-    x6 = swap_x(cot_two)
-    second(3, cot_far, swap_core(cot_far), x5)
-
-    cot_own = tie(cot_own, x6, cot[3][0], cot[1][1])
-    x7 = swap_x(cot_own)
-    second(2, cot_two, swap_core(cot_two), x6)
-
-    act, chip = [None] * NZ, [None] * NZ
-
-    def last(s):
-        act[s], keep, send = back(tables[s][0], pre[s] + cot[s], weight_up, slots)
-        chip[s] = add(keep, swap_core(send))
-
-    last(1)
-    near_send, cot_own = tie((chip[1][1], cot_own), x7, cot[2][0], cot[3][1])
-    x8 = swap_x(near_send)
-    second(0, cot_own, swap_core(cot_own), x7)
-    last(3)
-
-    far_send = tie(chip[3][1], x8, cot[0][0], cot[2][1])
-    x9 = swap_x(far_send)
-    last(2)
-
-    two_send, far_sum = tie((chip[2][1], add(chip[3][0], x9)), cot[0][1])
-    x10 = swap_x(two_send)
-    hop_far = along_z(far_sum, INWARD)
-    last(0)
-
-    own_send, far_sum, two_sum = tie((chip[0][1], add(far_sum, hop_far), add(chip[2][0], x10)))
-    x11 = swap_x(own_send)
-    hop_far = along_z(far_sum, MIDDLE)
-    hop_two = along_z(two_sum, INWARD)
+    two_core = swap_core(two)
+    forth(1, near, near_core, x_near, swap_core(x_near))
+
+    far = tie(jnp.where(inner, far_in, far_out), x_two, parts[1][0], parts[0][1])
+    x_far = swap_x(far)
+    far_core = swap_core(far)
+    forth(2, two, two_core, x_two, swap_core(x_two))
+    back_again(0)
+
+    own_send = tie(chip[0][1], x_far, parts[2][0], parts[1][1])
+    back_own = swap_x(own_send)
+    forth(3, far, far_core, x_far, swap_core(x_far))
+    back_again(1)
+
+    near_send = tie(chip[1][1], back_own, parts[3][0])
+    back_near = swap_x(near_send)
+    back_again(2)
+    near_sum = add(chip[1][0], back_near)
+    hop_near = along_z(near_sum, NEIGHBOUR)
+
+    two_send = tie(chip[2][1], back_near)
+    back_two = swap_x(two_send)
+    two_sum = add(chip[2][0], back_two)
+    hops_two = (along_z(two_sum, MIDDLE), along_z(two_sum, TWO_INWARD))
+    back_again(3, near_sum)
     down_grad = weight_grad(
         down_grad_kernel,
-        rows_cot,
-        [p[0] for p in pre] + [p[1] for p in pre],
-        [pltpu.VMEM((NZ,) + pre[0][0].shape, BF16)],
+        hidden_units,
+        tie(rows_cot, chip[3]),
+        [p[0] for p in parts] + [p[1] for p in parts],
+        [pltpu.VMEM((NZ, parts[0][0].shape[0], hidden_units), BF16)],
     )
 
-    near_sum, two_sum = tie(
-        (add(add(chip[1][0], x8), hop_far), add(two_sum, hop_two)), x11, down_grad
-    )
-    hop_near = along_z(near_sum, NEIGHBOUR)
-    hop_two = along_z(two_sum, MIDDLE)
-    up_grad = weight_grad(up_grad_kernel, rows_in, act, [])
-    token_grad = (
-        add(chip[0][0], x11).astype(F32) + hop_near.astype(F32) + hop_two.astype(F32)
-    ).astype(BF16)
+    far_send = tie(chip[3][1], back_two)
+    back_far = swap_x(far_send)
+    far_sum = tie(add(chip[3][0], back_far), *hops_two)
+    hops_far = (along_z(far_sum, THREE), along_z(far_sum, TWO_OUTWARD))
+    up_grad = weight_grad(up_grad_kernel, hidden_units, rows_in, act, [])
+    own_sum = chip[0][0].astype(F32) + back_own.astype(F32)
+    for hop in (hop_near, *hops_two, *hops_far):
+        own_sum = own_sum + hop.astype(F32)
+    token_grad = own_sum.astype(BF16)
     return token_grad, up_grad[None], down_grad[None]
 
 

time: 241 us -> 211 us (0.88)
  starting transfers between devices: 55.5 us -> 34.1 us
  waiting for transfers between devices: 125 us -> 115 us
    ppermute x12 -> x8, waiting for transfers between devices: 30.4 us -> 63.6 us  [swap_x(): lax.ppermute(value, 'expert', [(i, i ^ NC) for i in range(NZ * NX * NC)])]
    ppermute x8 -> x4, waiting for transfers between devices: 40.6 us -> 17.7 us  [swap_dp(): return lax.ppermute(value, 'dp', [(0, 1), (1, 0)])]
    ppermute x16 -> x10, waiting for transfers between devices: 53.7 us -> 31.7 us  [along_z(): return lax.ppermute(value, 'expert', perm)]
    ppermute x16 -> x10, starting transfers between devices: 29.6 us -> 18 us  [along_z(): return lax.ppermute(value, 'expert', perm)]
    ppermute x12 -> x8, starting transfers between devices: 13.4 us -> 8.82 us  [swap_x(): lax.ppermute(value, 'expert', [(i, i ^ NC) for i in range(NZ * NX * NC)])]
    ppermute x8 -> x4, starting transfers between devices: 10.5 us -> 6.34 us  [swap_dp(): return lax.ppermute(value, 'dp', [(0, 1), (1, 0)])]
    pallas_call x8 -> x4, Pallas kernels: 23.9 us -> 22.7 us  [front(): pl.pallas_call(functools.partial(front_kernel, top_count, slots), grid=(w...]
  transfers between devices with their start and end apart: 56 -> 34, of which waited for: 25 -> 17; matrix products, arithmetic and copies ran while one was open for 2% -> 2% of each run, Pallas kernels for 20% -> 23%
where the time goes in v5:
time: 211 us; the launch traced here: 210 us
  waiting for transfers between devices  115 us (55%)
  Pallas kernels  47.4 us (22%)
  starting transfers between devices  34.1 us (16%)
  local copies, waits for them, and re-layouts  6.5 us (3%)
  other arithmetic  5.96 us (3%)
    ppermute x8, waiting for transfers between devices, swap_x(): lax.ppermute(value, 'expert', [(i, i ^ NC) for i in range(NZ * NX * NC)])  63.6 us
    ppermute x10, waiting for transfers between devices, along_z(): return lax.ppermute(value, 'expert', perm)  31.7 us
    pallas_call x4, Pallas kernels, front(): pl.pallas_call(functools.partial(front_kernel, top_count, slots), grid=(w...  22.7 us
    ppermute x10, starting transfers between devices, along_z(): return lax.ppermute(value, 'expert', perm)  18 us
    ppermute x4, waiting for transfers between devices, swap_dp(): return lax.ppermute(value, 'dp', [(0, 1), (1, 0)])  17.7 us
    pallas_call x2, Pallas kernels, weight_grad(): pl.pallas_call(kernel, grid=(width // tile,), in_specs=[pl.BlockSpec((row...  14 us
    pallas_call x4, Pallas kernels, back(): pl.pallas_call(functools.partial(back_kernel, slots), grid=(width // tile...  10.8 us
    ppermute x8, starting transfers between devices, swap_x(): lax.ppermute(value, 'expert', [(i, i ^ NC) for i in range(NZ * NX * NC)])  8.82 us
  transfers between devices with their start and end apart: 34, of which 17 were waited for; matrix products, arithmetic and copies ran while one was open for 2% of the time, Pallas kernels for 23%

profile of v5, /device:TPU:8, one launch (start us, length us, event | category | flops | bytes accessed | tf_op | source)
XLA Modules:
  0.0 210.2 jit_solution(16822656957617208288)
XLA Ops:
  5.7 4.6 %collective-permute-start.6 = (bf16[128,3712]{1,0:T(8,128)(2,1)S(1)}, bf16[128,3712]{1,0:T(8,128)(2,1)}, u32[]{:S(2)}, u32[]{:S(2)}) collective-permute-start(bf16[128,3712]{1,0:T(8,128)(2,1)S(1)} %concatenate.3.refs_0_.refs_4_.refs_8_), channel_id=1, source_target_pairs={{4,8},{5,9},{6,10},{7,11},{8,4},{9,5},{10,6},{11,7},{20,24},{21,25... | collective-permute-start | bytes 2850824 | tf_op jit(solution)/shard_map/ppermute | solution.py:31
  10.4 16.3 %collective-permute-done.1.refs_2_.refs_6_.refs_10_ = bf16[128,3712]{1,0:T(8,128)(2,1)} collective-permute-done((bf16[128,3712]{1,0:T(8,128)(2,1)S(1)}, bf16[128,3712]{1,0:T(8,128)(2,1)}, u32[]{:S(2)}, u32[]{:S(2)}) %collective-permute-start.1) | collective-permute-done | bytes 950304 | tf_op jit(solution)/shard_map/ppermute | solution.py:35
  27.8 3.1 %collective-permute-done.6 = bf16[128,3712]{1,0:T(8,128)(2,1)} collective-permute-done((bf16[128,3712]{1,0:T(8,128)(2,1)S(1)}, bf16[128,3712]{1,0:T(8,128)(2,1)}, u32[]{:S(2)}, u32[]{:S(2)}) %collective-permute-start.6) | collective-permute-done | bytes 950304 | tf_op jit(solution)/shard_map/ppermute | solution.py:31
  31.5 2.2 %collective-permute-start.7 = (bf16[128,3712]{1,0:T(8,128)(2,1)}, bf16[128,3712]{1,0:T(8,128)(2,1)}, u32[]{:S(2)}, u32[]{:S(2)}) collective-permute-start(bf16[128,3712]{1,0:T(8,128)(2,1)} %collective-permute-done.6), channel_id=1, source_target_pairs={{4,0},{5,1},{6,2},{7,3},{8,12},{9,13},{10,14},{11,15},{20,16},{21,... | collective-permute-start | bytes 2850824 | tf_op jit(solution)/shard_map/ppermute | solution.py:31
  35.0 3.6 %collective-permute-start.8 = (bf16[128,3712]{1,0:T(8,128)(2,1)S(1)}, bf16[128,3712]{1,0:T(8,128)(2,1)S(1)}, u32[]{:S(2)}, u32[]{:S(2)}) collective-permute-start(bf16[128,3712]{1,0:T(8,128)(2,1)S(1)} %collective-permute-done.5.refs_0_.refs_4_.refs_8_), channel_id=1, source_target_pairs={{4,8},{5,9},{6,10},{7,11},{8,4},{9,5},{10,6},{11,7},{20,24},{21,25... | collective-permute-start | bytes 2850824 | tf_op jit(solution)/shard_map/ppermute | solution.py:31
  38.7 2.0 copy-done
  40.8 2.0 copy-done.2
  42.8 6.1 %shard_map.94 = (bf16[256,1792]{1,0:T(8,128)(2,1)S(1)}, bf16[256,1792]{1,0:T(8,128)(2,1)S(1)}, bf16[256,2048]{1,0:T(8,128)(2,1)S(1)}, s32[4,8,128]{2,1,0:T(8,128)S(1)}) custom-call(s32[2]{0:T(128)S(1)} %pad_add_fusion.own_ref, bf16[128,3712]{1,0:T(8,128)(2,1)S(1)} %concatenate.3.refs_0_.refs_4_.refs_8_, ...), custom_call_target="tpu_custom_call" | custom-call | tf_op jit(solution)/shard_map/pallas_call | solution.py:138
  50.5 2.1 collective-permute-done.9.refs_2_.refs_6_.refs_10_
  53.8 4.7 %collective-permute-done.8 = bf16[128,3712]{1,0:T(8,128)(2,1)S(1)} collective-permute-done((bf16[128,3712]{1,0:T(8,128)(2,1)S(1)}, bf16[128,3712]{1,0:T(8,128)(2,1)S(1)}, u32[]{:S(2)}, u32[]{:S(2)}) %collective-permute-start.8) | collective-permute-done | bytes 950304 | tf_op jit(solution)/shard_map/ppermute | solution.py:31
  61.3 5.6 %shard_map.96 = (bf16[256,1792]{1,0:T(8,128)(2,1)S(1)}, bf16[256,1792]{1,0:T(8,128)(2,1)S(1)}, bf16[256,2048]{1,0:T(8,128)(2,1)S(1)}, s32[4,8,128]{2,1,0:T(8,128)S(1)}) custom-call(s32[2]{0:T(128)S(1)} %pad_add_fusion.own_ref, bf16[128,3712]{1,0:T(8,128)(2,1)S(1)} %collective-permute-done.5.refs_0_.refs_4_.refs_8_, ...), custom_call_target="tpu_custom_call" | custom-call | tf_op jit(solution)/shard_map/pallas_call | solution.py:138
  66.9 1.6 collective-permute-start.17
  68.5 10.8 %collective-permute-done.11.refs_2_.refs_6_.refs_10_ = bf16[128,3712]{1,0:T(8,128)(2,1)S(1)} collective-permute-done((bf16[128,3712]{1,0:T(8,128)(2,1)S(1)}, bf16[128,3712]{1,0:T(8,128)(2,1)S(1)}, u32[]{:S(2)}, u32[]{:S(2)}) %collective-permute-start.11) | collective-permute-done | bytes 950304 | tf_op jit(solution)/shard_map/ppermute | solution.py:35
  79.3 2.7 %shard_map.95 = (bf16[256,1024]{1,0:T(8,128)(2,1)S(1)}, bf16[2,128,1792]{2,1,0:T(8,128)(2,1)S(1)}, bf16[2,128,1792]{2,1,0:T(8,128)(2,1)S(1)}) custom-call(s32[4,8,128]{2,1,0:T(8,128)S(1)} %get-tuple-element.53.slot_ref, bf16[256,2048]{1,0:T(8,128)(2,1)S(1)} %get-tuple-element.55.part_a.refs_4_, bf16[256,2048]{1,0:T(8,128)(2,1)S(1)} %collective-permute-done.3.part_b.refs_8_, ...), custom_call_target="tpu_custom_call" | custom-call | tf_op jit(solution)/shard_map/pallas_call | solution.py:192
  83.6 5.6 %shard_map.97 = (bf16[256,1792]{1,0:T(8,128)(2,1)S(1)}, bf16[256,1792]{1,0:T(8,128)(2,1)S(1)}, bf16[256,2048]{1,0:T(8,128)(2,1)S(1)}, s32[4,8,128]{2,1,0:T(8,128)S(1)}) custom-call(s32[2]{0:T(128)S(1)} %pad_add_fusion.own_ref, bf16[128,3712]{1,0:T(8,128)(2,1)S(1)} %broadcast_select_fusion.1.refs_0_.refs_4_.refs_8_, ...), custom_call_target="tpu_custom_call" | custom-call | tf_op jit(solution)/shard_map/pallas_call | solution.py:138
  89.2 1.6 collective-permute-start.24
  90.7 6.7 %collective-permute-done.17.part_b.refs_9_ = bf16[256,2048]{1,0:T(8,128)(2,1)S(1)} collective-permute-done((bf16[256,2048]{1,0:T(8,128)(2,1)S(1)}, bf16[256,2048]{1,0:T(8,128)(2,1)S(1)}, u32[]{:S(2)}, u32[]{:S(2)}) %collective-permute-start.17) | collective-permute-done | bytes 1048608 | tf_op jit(solution)/shard_map/ppermute | solution.py:43
  97.4 2.7 %shard_map.98 = (bf16[256,1024]{1,0:T(8,128)(2,1)S(1)}, bf16[2,128,1792]{2,1,0:T(8,128)(2,1)S(1)}, bf16[2,128,1792]{2,1,0:T(8,128)(2,1)S(1)}) custom-call(s32[4,8,128]{2,1,0:T(8,128)S(1)} %get-tuple-element.67.slot_ref, bf16[256,2048]{1,0:T(8,128)(2,1)S(1)} %get-tuple-element.68.part_a.refs_5_, bf16[256,2048]{1,0:T(8,128)(2,1)S(1)} %collective-permute-done.17.part_b.refs_9_, ...), custom_call_target="tpu_custom_call" | custom-call | tf_op jit(solution)/shard_map/pallas_call | solution.py:192
  100.4 5.4 %collective-permute-done.14.refs_2_.refs_6_.refs_10_ = bf16[128,3712]{1,0:T(8,128)(2,1)S(1)} collective-permute-done((bf16[128,3712]{1,0:T(8,128)(2,1)S(1)}, bf16[128,3712]{1,0:T(8,128)(2,1)S(1)}, u32[]{:S(2)}, u32[]{:S(2)}) %collective-permute-start.14) | collective-permute-done | bytes 950304 | tf_op jit(solution)/shard_map/ppermute | solution.py:35
  108.3 5.5 %shard_map.99 = (bf16[256,1792]{1,0:T(8,128)(2,1)S(1)}, bf16[256,1792]{1,0:T(8,128)(2,1)S(1)}, bf16[256,2048]{1,0:T(8,128)(2,1)S(1)}, s32[4,8,128]{2,1,0:T(8,128)S(1)}) custom-call(s32[2]{0:T(128)S(1)} %pad_add_fusion.own_ref, bf16[128,3712]{1,0:T(8,128)(2,1)S(1)} %broadcast_select_fusion.refs_0_.refs_4_.refs_8_, ...), custom_call_target="tpu_custom_call" | custom-call | tf_op jit(solution)/shard_map/pallas_call | solution.py:138
  113.8 1.6 collective-permute-start.29
  115.4 3.4 %collective-permute-done.18 = bf16[128,1792]{1,0:T(8,128)(2,1)S(1)} collective-permute-done((bf16[128,1792]{1,0:T(8,128)(2,1)S(1)}, bf16[128,1792]{1,0:T(8,128)(2,1)S(1)}, u32[]{:S(2)}, u32[]{:S(2)}) %collective-permute-start.18) | collective-permute-done | bytes 458784 | tf_op jit(solution)/shard_map/ppermute | solution.py:35
  119.9 2.7 %shard_map.100 = (bf16[256,1024]{1,0:T(8,128)(2,1)S(1)}, bf16[2,128,1792]{2,1,0:T(8,128)(2,1)S(1)}, bf16[2,128,1792]{2,1,0:T(8,128)(2,1)S(1)}) custom-call(s32[4,8,128]{2,1,0:T(8,128)S(1)} %get-tuple-element.74.slot_ref, bf16[256,2048]{1,0:T(8,128)(2,1)S(1)} %get-tuple-element.75.part_a.refs_6_, ...), custom_call_target="tpu_custom_call" | custom-call | tf_op jit(solution)/shard_map/pallas_call | solution.py:192
  122.6 8.3 %collective-permute-done.22 = bf16[128,1792]{1,0:T(8,128)(2,1)S(1)} collective-permute-done((bf16[128,1792]{1,0:T(8,128)(2,1)S(1)}, bf16[128,1792]{1,0:T(8,128)(2,1)S(1)}, u32[]{:S(2)}, u32[]{:S(2)}) %collective-permute-start.22) | collective-permute-done | bytes 458784 | tf_op jit(solution)/shard_map/ppermute | solution.py:35
  131.1 10.8 %collective-permute-done.29.part_b.refs_11_ = bf16[256,2048]{1,0:T(8,128)(2,1)S(1)} collective-permute-done((bf16[256,2048]{1,0:T(8,128)(2,1)S(1)}, bf16[256,2048]{1,0:T(8,128)(2,1)S(1)}, u32[]{:S(2)}, u32[]{:S(2)}) %collective-permute-start.29) | collective-permute-done | bytes 1048608 | tf_op jit(solution)/shard_map/ppermute | solution.py:43
  141.9 2.7 %shard_map.101 = (bf16[256,1024]{1,0:T(8,128)(2,1)S(1)}, bf16[2,128,1792]{2,1,0:T(8,128)(2,1)S(1)}, bf16[2,128,1792]{2,1,0:T(8,128)(2,1)S(1)}) custom-call(s32[4,8,128]{2,1,0:T(8,128)S(1)} %get-tuple-element.80.slot_ref, bf16[256,2048]{1,0:T(8,128)(2,1)S(1)} %get-tuple-element.81.part_a.refs_7_, ...), custom_call_target="tpu_custom_call" | custom-call | tf_op jit(solution)/shard_map/pallas_call | solution.py:192
  147.5 10.5 %collective-permute-done.26 = bf16[128,1792]{1,0:T(8,128)(2,1)S(1)} collective-permute-done((bf16[128,1792]{1,0:T(8,128)(2,1)S(1)}, bf16[128,1792]{1,0:T(8,128)(2,1)S(1)}, u32[]{:S(2)}, u32[]{:S(2)}) %collective-permute-start.26) | collective-permute-done | bytes 458784 | tf_op jit(solution)/shard_map/ppermute | solution.py:35
  159.6 2.2 %collective-permute-start.27 = (bf16[128,1792]{1,0:T(8,128)(2,1)S(1)}, bf16[128,1792]{1,0:T(8,128)(2,1)S(1)}, u32[]{:S(2)}, u32[]{:S(2)}) collective-permute-start(bf16[128,1792]{1,0:T(8,128)(2,1)S(1)} %fusion.1), channel_id=1, source_target_pairs={{4,8},{5,9},{6,10},{7,11},{8,4},{9,5},{10,6},{11,7},{20,24},{21,25... | collective-permute-start | bytes 1376264 | tf_op jit(solution)/shard_map/ppermute | solution.py:31
  163.1 7.0 %collective-permute-done.31 = bf16[128,1792]{1,0:T(8,128)(2,1)S(1)} collective-permute-done((bf16[128,1792]{1,0:T(8,128)(2,1)S(1)}, bf16[128,1792]{1,0:T(8,128)(2,1)S(1)}, u32[]{:S(2)}, u32[]{:S(2)}) %collective-permute-start.31) | collective-permute-done | bytes 458784 | tf_op jit(solution)/shard_map/ppermute | solution.py:35
  170.2 22.8 %collective-permute-done.27 = bf16[128,1792]{1,0:T(8,128)(2,1)S(1)} collective-permute-done((bf16[128,1792]{1,0:T(8,128)(2,1)S(1)}, bf16[128,1792]{1,0:T(8,128)(2,1)S(1)}, u32[]{:S(2)}, u32[]{:S(2)}) %collective-permute-start.27) | collective-permute-done | bytes 458784 | tf_op jit(solution)/shard_map/ppermute | solution.py:31
  195.0 6.3 %shard_map.102 = bf16[1792,1024]{1,0:T(8,128)(2,1)} custom-call(bf16[256,1792]{1,0:T(8,128)(2,1)S(1)} %copy-done.5, bf16[256,1792]{1,0:T(8,128)(2,1)S(1)} %get-tuple-element.88.refs_1_, bf16[256,1792]{1,0:T(8,128)(2,1)S(1)} %get-tuple-element.89.refs_2_, bf16[256,1792]{1,0:T(8,128)(2,1)S(1)} %get-tuple-element.90.refs_3_, ...), custom_call_target="tpu_custom_call" | custom-call | tf_op jit(solution)/shard_map/pallas_call | solution.py:239
  201.3 7.7 %shard_map.103 = bf16[1792,1024]{1,0:T(8,128)(2,1)} custom-call(bf16[256,1792]{1,0:T(8,128)(2,1)S(1)} %copy-done.7, bf16[256,1792]{1,0:T(8,128)(2,1)S(1)} %copy-done.9, bf16[256,1792]{1,0:T(8,128)(2,1)S(1)} %get-tuple-element.101.refs_2_, bf16[256,1792]{1,0:T(8,128)(2,1)S(1)} %get-tuple-element.102.refs_3_, ...), custom_call_target="tpu_custom_call" | custom-call | tf_op jit(solution)/shard_map/pallas_call | solution.py:239
  (91 shorter events, 28.5 us)
Async XLA Ops:
  3.7 23.0 %collective-permute-start.1 = (bf16[128,3712]{1,0:T(8,128)(2,1)S(1)}, bf16[128,3712]{1,0:T(8,128)(2,1)}, u32[]{:S(2)}, u32[]{:S(2)}) collective-permute-start(bf16[128,3712]{1,0:T(8,128)(2,1)S(1)} %concatenate.3.refs_0_.refs_4_.refs_8_), channel_id=1, source_target_pairs={{0,2},{1,3},{2,0},{3,1},{4,6},{5,7},{6,4},{7,5},{8,10},{9,11},{10,... | collective-permute-start | bytes 2850824 | tf_op jit(solution)/shard_map/ppermute | solution.py:35
  5.3 22.5 %collective-permute-start.5 = (bf16[128,3712]{1,0:T(8,128)(2,1)S(1)}, bf16[128,3712]{1,0:T(8,128)(2,1)S(1)}, u32[]{:S(2)}, u32[]{:S(2)}) collective-permute-start(bf16[128,3712]{1,0:T(8,128)(2,1)S(1)} %concatenate.3.refs_0_.refs_4_.refs_8_), channel_id=1, source_target_pairs={{0,4},{1,5},{2,6},{3,7},{4,0},{5,1},{6,2},{7,3},{8,12},{9,13},{10,... | collective-permute-start | bytes 2850824 | tf_op jit(solution)/shard_map/ppermute | solution.py:31
  5.7 25.2 %collective-permute-start.6 = (bf16[128,3712]{1,0:T(8,128)(2,1)S(1)}, bf16[128,3712]{1,0:T(8,128)(2,1)}, u32[]{:S(2)}, u32[]{:S(2)}) collective-permute-start(bf16[128,3712]{1,0:T(8,128)(2,1)S(1)} %concatenate.3.refs_0_.refs_4_.refs_8_), channel_id=1, source_target_pairs={{4,8},{5,9},{6,10},{7,11},{8,4},{9,5},{10,6},{11,7},{20,24},{21,25... | collective-permute-start | bytes 2850824 | tf_op jit(solution)/shard_map/ppermute | solution.py:31
  10.3 28.3 %collective-permute-start = (bf16[128,3712]{1,0:T(8,128)(2,1)S(1)}, bf16[128,3712]{1,0:T(8,128)(2,1)}, u32[]{:S(2)}, u32[]{:S(2)}) collective-permute-start(bf16[128,3712]{1,0:T(8,128)(2,1)S(1)} %concatenate.3.refs_0_.refs_4_.refs_8_), channel_id=1, source_target_pairs={{0,1},{1,0},{2,3},{3,2},{4,5},{5,4},{6,7},{7,6},{8,9},{9,8},{10,11... | collective-permute-start | bytes 2850824 | tf_op jit(solution)/shard_map/ppermute | solution.py:39
  26.7 12.0 %collective-permute-start.2 = (bf16[128,3712]{1,0:T(8,128)(2,1)}, bf16[128,3712]{1,0:T(8,128)(2,1)}, u32[]{:S(2)}, u32[]{:S(2)}) collective-permute-start(bf16[128,3712]{1,0:T(8,128)(2,1)} %collective-permute-done.1.refs_2_.refs_6_.refs_10_), channel_id=1, source_target_pairs={{0,1},{1,0},{2,3},{3,2},{4,5},{5,4},{6,7},{7,6},{8,9},{9,8},{10,11... | collective-permute-start | bytes 2850824 | tf_op jit(solution)/shard_map/ppermute | solution.py:39
  30.9 21.6 %collective-permute-start.9 = (bf16[128,3712]{1,0:T(8,128)(2,1)S(1)}, bf16[128,3712]{1,0:T(8,128)(2,1)S(1)}, u32[]{:S(2)}, u32[]{:S(2)}) collective-permute-start(bf16[128,3712]{1,0:T(8,128)(2,1)S(1)} %collective-permute-done.5.refs_0_.refs_4_.refs_8_), channel_id=1, source_target_pairs={{0,2},{1,3},{2,0},{3,1},{4,6},{5,7},{6,4},{7,5},{8,10},{9,11},{10,... | collective-permute-start | bytes 2850824 | tf_op jit(solution)/shard_map/ppermute | solution.py:35
  31.5 21.1 %collective-permute-start.7 = (bf16[128,3712]{1,0:T(8,128)(2,1)}, bf16[128,3712]{1,0:T(8,128)(2,1)}, u32[]{:S(2)}, u32[]{:S(2)}) collective-permute-start(bf16[128,3712]{1,0:T(8,128)(2,1)} %collective-permute-done.6), channel_id=1, source_target_pairs={{4,0},{5,1},{6,2},{7,3},{8,12},{9,13},{10,14},{11,15},{20,16},{21,... | collective-permute-start | bytes 2850824 | tf_op jit(solution)/shard_map/ppermute | solution.py:31
  35.0 23.6 %collective-permute-start.8 = (bf16[128,3712]{1,0:T(8,128)(2,1)S(1)}, bf16[128,3712]{1,0:T(8,128)(2,1)S(1)}, u32[]{:S(2)}, u32[]{:S(2)}) collective-permute-start(bf16[128,3712]{1,0:T(8,128)(2,1)S(1)} %collective-permute-done.5.refs_0_.refs_4_.refs_8_), channel_id=1, source_target_pairs={{4,8},{5,9},{6,10},{7,11},{8,4},{9,5},{10,6},{11,7},{20,24},{21,25... | collective-permute-start | bytes 2850824 | tf_op jit(solution)/shard_map/ppermute | solution.py:31
  38.6 22.6 %collective-permute-start.12 = (bf16[128,3712]{1,0:T(8,128)(2,1)S(1)}, bf16[128,3712]{1,0:T(8,128)(2,1)S(1)}, u32[]{:S(2)}, u32[]{:S(2)}) collective-permute-start(bf16[128,3712]{1,0:T(8,128)(2,1)S(1)} %collective-permute-done.5.refs_0_.refs_4_.refs_8_), channel_id=1, source_target_pairs={{0,1},{1,0},{2,3},{3,2},{4,5},{5,4},{6,7},{7,6},{8,9},{9,8},{10,11... | collective-permute-start | bytes 2850824 | tf_op jit(solution)/shard_map/ppermute | solution.py:39
  48.9 30.4 %collective-permute-start.3 = (bf16[256,2048]{1,0:T(8,128)(2,1)S(1)}, bf16[256,2048]{1,0:T(8,128)(2,1)S(1)}, u32[]{:S(2)}, u32[]{:S(2)}) collective-permute-start(bf16[256,2048]{1,0:T(8,128)(2,1)S(1)} %get-tuple-element.55.part_a.refs_4_), channel_id=1, source_target_pairs={{0,16},{16,0},{1,17},{17,1},{2,18},{18,2},{3,19},{19,3},{4,20},{20... | collective-permute-start | bytes 3145736 | tf_op jit(solution)/shard_map/ppermute | solution.py:43
  52.5 8.8 %collective-permute-start.13 = (bf16[128,3712]{1,0:T(8,128)(2,1)S(1)}, bf16[128,3712]{1,0:T(8,128)(2,1)S(1)}, u32[]{:S(2)}, u32[]{:S(2)}) collective-permute-start(bf16[128,3712]{1,0:T(8,128)(2,1)S(1)} %collective-permute-done.9.refs_2_.refs_6_.refs_10_), channel_id=1, source_target_pairs={{0,1},{1,0},{2,3},{3,2},{4,5},{5,4},{6,7},{7,6},{8,9},{9,8},{10,11... | collective-permute-start | bytes 2850824 | tf_op jit(solution)/shard_map/ppermute | solution.py:39
  58.5 20.7 %collective-permute-start.11 = (bf16[128,3712]{1,0:T(8,128)(2,1)S(1)}, bf16[128,3712]{1,0:T(8,128)(2,1)S(1)}, u32[]{:S(2)}, u32[]{:S(2)}) collective-permute-start(bf16[128,3712]{1,0:T(8,128)(2,1)S(1)} %broadcast_select_fusion.1.refs_0_.refs_4_.refs_8_), channel_id=1, source_target_pairs={{0,2},{1,3},{2,0},{3,1},{4,6},{5,7},{6,4},{7,5},{8,10},{9,11},{10,... | collective-permute-start | bytes 2850824 | tf_op jit(solution)/shard_map/ppermute | solution.py:35
  59.7 22.9 %collective-permute-start.10 = (bf16[128,3712]{1,0:T(8,128)(2,1)S(1)}, bf16[128,3712]{1,0:T(8,128)(2,1)S(1)}, u32[]{:S(2)}, u32[]{:S(2)}) collective-permute-start(bf16[128,3712]{1,0:T(8,128)(2,1)S(1)} %collective-permute-done.8), channel_id=1, source_target_pairs={{4,0},{5,1},{6,2},{7,3},{8,12},{9,13},{10,14},{11,15},{20,16},{21,... | collective-permute-start | bytes 2850824 | tf_op jit(solution)/shard_map/ppermute | solution.py:31
  61.2 22.3 %collective-permute-start.15 = (bf16[128,3712]{1,0:T(8,128)(2,1)S(1)}, bf16[128,3712]{1,0:T(8,128)(2,1)S(1)}, u32[]{:S(2)}, u32[]{:S(2)}) collective-permute-start(bf16[128,3712]{1,0:T(8,128)(2,1)S(1)} %broadcast_select_fusion.1.refs_0_.refs_4_.refs_8_), channel_id=1, source_target_pairs={{0,1},{1,0},{2,3},{3,2},{4,5},{5,4},{6,7},{7,6},{8,9},{9,8},{10,11... | collective-permute-start | bytes 2850824 | tf_op jit(solution)/shard_map/ppermute | solution.py:39
  66.9 30.4 %collective-permute-start.17 = (bf16[256,2048]{1,0:T(8,128)(2,1)S(1)}, bf16[256,2048]{1,0:T(8,128)(2,1)S(1)}, u32[]{:S(2)}, u32[]{:S(2)}) collective-permute-start(bf16[256,2048]{1,0:T(8,128)(2,1)S(1)} %get-tuple-element.68.part_a.refs_5_), channel_id=1, source_target_pairs={{0,16},{16,0},{1,17},{17,1},{2,18},{18,2},{3,19},{19,3},{4,20},{20... | collective-permute-start | bytes 3145736 | tf_op jit(solution)/shard_map/ppermute | solution.py:43
  79.3 4.3 %collective-permute-start.16 = (bf16[128,3712]{1,0:T(8,128)(2,1)S(1)}, bf16[128,3712]{1,0:T(8,128)(2,1)S(1)}, u32[]{:S(2)}, u32[]{:S(2)}) collective-permute-start(bf16[128,3712]{1,0:T(8,128)(2,1)S(1)} %collective-permute-done.11.refs_2_.refs_6_.refs_10_), channel_id=1, source_target_pairs={{0,1},{1,0},{2,3},{3,2},{4,5},{5,4},{6,7},{7,6},{8,9},{9,8},{10,11... | collective-permute-start | bytes 2850824 | tf_op jit(solution)/shard_map/ppermute | solution.py:39
  82.0 18.1 %collective-permute-start.4 = (bf16[2,128,1792]{2,1,0:T(8,128)(2,1)S(1)}, bf16[2,128,1792]{2,1,0:T(8,128)(2,1)S(1)}, u32[]{:S(2)}, u32[]{:S(2)}) collective-permute-start(bf16[2,128,1792]{2,1,0:T(8,128)(2,1)S(1)} %get-tuple-element.58), channel_id=1, source_target_pairs={{0,1},{1,0},{2,3},{3,2},{4,5},{5,4},{6,7},{7,6},{8,9},{9,8},{10,11... | collective-permute-start | bytes 2752520 | tf_op jit(solution)/shard_map/ppermute | solution.py:39
  82.7 23.1 %collective-permute-start.14 = (bf16[128,3712]{1,0:T(8,128)(2,1)S(1)}, bf16[128,3712]{1,0:T(8,128)(2,1)S(1)}, u32[]{:S(2)}, u32[]{:S(2)}) collective-permute-start(bf16[128,3712]{1,0:T(8,128)(2,1)S(1)} %broadcast_select_fusion.refs_0_.refs_4_.refs_8_), channel_id=1, source_target_pairs={{0,2},{1,3},{2,0},{3,1},{4,6},{5,7},{6,4},{7,5},{8,10},{9,11},{10,... | collective-permute-start | bytes 2850824 | tf_op jit(solution)/shard_map/ppermute | solution.py:35
  83.6 23.3 %collective-permute-start.20 = (bf16[128,3712]{1,0:T(8,128)(2,1)S(1)}, bf16[128,3712]{1,0:T(8,128)(2,1)S(1)}, u32[]{:S(2)}, u32[]{:S(2)}) collective-permute-start(bf16[128,3712]{1,0:T(8,128)(2,1)S(1)} %broadcast_select_fusion.refs_0_.refs_4_.refs_8_), channel_id=1, source_target_pairs={{0,1},{1,0},{2,3},{3,2},{4,5},{5,4},{6,7},{7,6},{8,9},{9,8},{10,11... | collective-permute-start | bytes 2850824 | tf_op jit(solution)/shard_map/ppermute | solution.py:39
  89.2 30.7 %collective-permute-start.24 = (bf16[256,2048]{1,0:T(8,128)(2,1)S(1)}, bf16[256,2048]{1,0:T(8,128)(2,1)S(1)}, u32[]{:S(2)}, u32[]{:S(2)}) collective-permute-start(bf16[256,2048]{1,0:T(8,128)(2,1)S(1)} %get-tuple-element.75.part_a.refs_6_), channel_id=1, source_target_pairs={{0,16},{16,0},{1,17},{17,1},{2,18},{18,2},{3,19},{19,3},{4,20},{20... | collective-permute-start | bytes 3145736 | tf_op jit(solution)/shard_map/ppermute | solution.py:43
  100.1 6.6 %collective-permute-start.19 = (bf16[2,128,1792]{2,1,0:T(8,128)(2,1)S(1)}, bf16[2,128,1792]{2,1,0:T(8,128)(2,1)S(1)}, u32[]{:S(2)}, u32[]{:S(2)}) collective-permute-start(bf16[2,128,1792]{2,1,0:T(8,128)(2,1)S(1)} %get-tuple-element.71), channel_id=1, source_target_pairs={{0,1},{1,0},{2,3},{3,2},{4,5},{5,4},{6,7},{7,6},{8,9},{9,8},{10,11... | collective-permute-start | bytes 2752520 | tf_op jit(solution)/shard_map/ppermute | solution.py:39
  105.8 13.0 %collective-permute-start.18 = (bf16[128,1792]{1,0:T(8,128)(2,1)S(1)}, bf16[128,1792]{1,0:T(8,128)(2,1)S(1)}, u32[]{:S(2)}, u32[]{:S(2)}) collective-permute-start(bf16[128,1792]{1,0:T(8,128)(2,1)S(1)} %slice_bitcast_fusion.6), channel_id=1, source_target_pairs={{0,2},{1,3},{2,0},{3,1},{4,6},{5,7},{6,4},{7,5},{8,10},{9,11},{10,... | collective-permute-start | bytes 1376264 | tf_op jit(solution)/shard_map/ppermute | solution.py:35
  113.8 28.1 %collective-permute-start.29 = (bf16[256,2048]{1,0:T(8,128)(2,1)S(1)}, bf16[256,2048]{1,0:T(8,128)(2,1)S(1)}, u32[]{:S(2)}, u32[]{:S(2)}) collective-permute-start(bf16[256,2048]{1,0:T(8,128)(2,1)S(1)} %get-tuple-element.81.part_a.refs_7_), channel_id=1, source_target_pairs={{0,16},{16,0},{1,17},{17,1},{2,18},{18,2},{3,19},{19,3},{4,20},{20... | collective-permute-start | bytes 3145736 | tf_op jit(solution)/shard_map/ppermute | solution.py:43
  118.8 12.2 %collective-permute-start.22 = (bf16[128,1792]{1,0:T(8,128)(2,1)S(1)}, bf16[128,1792]{1,0:T(8,128)(2,1)S(1)}, u32[]{:S(2)}, u32[]{:S(2)}) collective-permute-start(bf16[128,1792]{1,0:T(8,128)(2,1)S(1)} %slice_bitcast_fusion.4), channel_id=1, source_target_pairs={{0,2},{1,3},{2,0},{3,1},{4,6},{5,7},{6,4},{7,5},{8,10},{9,11},{10,... | collective-permute-start | bytes 1376264 | tf_op jit(solution)/shard_map/ppermute | solution.py:35
  122.6 22.1 %collective-permute-start.25 = (bf16[2,128,1792]{2,1,0:T(8,128)(2,1)S(1)}, bf16[2,128,1792]{2,1,0:T(8,128)(2,1)S(1)}, u32[]{:S(2)}, u32[]{:S(2)}) collective-permute-start(bf16[2,128,1792]{2,1,0:T(8,128)(2,1)S(1)} %get-tuple-element.78), channel_id=1, source_target_pairs={{0,1},{1,0},{2,3},{3,2},{4,5},{5,4},{6,7},{7,6},{8,9},{9,8},{10,11... | collective-permute-start | bytes 2752520 | tf_op jit(solution)/shard_map/ppermute | solution.py:39
  131.0 78.0 %collective-permute-start.23 = (bf16[128,1792]{1,0:T(8,128)(2,1)S(1)}, bf16[128,1792]{1,0:T(8,128)(2,1)S(1)}, u32[]{:S(2)}, u32[]{:S(2)}) collective-permute-start(bf16[128,1792]{1,0:T(8,128)(2,1)S(1)} %fusion.2), channel_id=1, source_target_pairs={{0,4},{1,5},{2,6},{3,7},{4,0},{5,1},{6,2},{7,3},{8,12},{9,13},{10,... | collective-permute-start | bytes 1376264 | tf_op jit(solution)/shard_map/ppermute | solution.py:31
  145.0 13.0 %collective-permute-start.26 = (bf16[128,1792]{1,0:T(8,128)(2,1)S(1)}, bf16[128,1792]{1,0:T(8,128)(2,1)S(1)}, u32[]{:S(2)}, u32[]{:S(2)}) collective-permute-start(bf16[128,1792]{1,0:T(8,128)(2,1)S(1)} %slice_bitcast_fusion.2), channel_id=1, source_target_pairs={{0,2},{1,3},{2,0},{3,1},{4,6},{5,7},{6,4},{7,5},{8,10},{9,11},{10,... | collective-permute-start | bytes 1376264 | tf_op jit(solution)/shard_map/ppermute | solution.py:35
  158.0 12.1 %collective-permute-start.31 = (bf16[128,1792]{1,0:T(8,128)(2,1)S(1)}, bf16[128,1792]{1,0:T(8,128)(2,1)S(1)}, u32[]{:S(2)}, u32[]{:S(2)}) collective-permute-start(bf16[128,1792]{1,0:T(8,128)(2,1)S(1)} %slice_bitcast_fusion), channel_id=1, source_target_pairs={{0,2},{1,3},{2,0},{3,1},{4,6},{5,7},{6,4},{7,5},{8,10},{9,11},{10,... | collective-permute-start | bytes 1376264 | tf_op jit(solution)/shard_map/ppermute | solution.py:35
  159.6 33.4 %collective-permute-start.27 = (bf16[128,1792]{1,0:T(8,128)(2,1)S(1)}, bf16[128,1792]{1,0:T(8,128)(2,1)S(1)}, u32[]{:S(2)}, u32[]{:S(2)}) collective-permute-start(bf16[128,1792]{1,0:T(8,128)(2,1)S(1)} %fusion.1), channel_id=1, source_target_pairs={{4,8},{5,9},{6,10},{7,11},{8,4},{9,5},{10,6},{11,7},{20,24},{21,25... | collective-permute-start | bytes 1376264 | tf_op jit(solution)/shard_map/ppermute | solution.py:31
  161.8 31.2 %collective-permute-start.28 = (bf16[128,1792]{1,0:T(8,128)(2,1)S(1)}, bf16[128,1792]{1,0:T(8,128)(2,1)S(1)}, u32[]{:S(2)}, u32[]{:S(2)}) collective-permute-start(bf16[128,1792]{1,0:T(8,128)(2,1)S(1)} %fusion.1), channel_id=1, source_target_pairs={{0,8},{1,9},{2,10},{3,11},{12,4},{13,5},{14,6},{15,7},{16,24},{17,... | collective-permute-start | bytes 1376264 | tf_op jit(solution)/shard_map/ppermute | solution.py:31
  193.0 16.0 %collective-permute-start.32 = (bf16[128,1792]{1,0:T(8,128)(2,1)S(1)}, bf16[128,1792]{1,0:T(8,128)(2,1)S(1)}, u32[]{:S(2)}, u32[]{:S(2)}) collective-permute-start(bf16[128,1792]{1,0:T(8,128)(2,1)S(1)} %fusion), channel_id=1, source_target_pairs={{0,12},{1,13},{2,14},{3,15},{12,0},{13,1},{14,2},{15,3},{16,28},{1... | collective-permute-start | bytes 1376264 | tf_op jit(solution)/shard_map/ppermute | solution.py:31
  193.7 15.3 %collective-permute-start.33 = (bf16[128,1792]{1,0:T(8,128)(2,1)S(1)}, bf16[128,1792]{1,0:T(8,128)(2,1)S(1)}, u32[]{:S(2)}, u32[]{:S(2)}) collective-permute-start(bf16[128,1792]{1,0:T(8,128)(2,1)S(1)} %fusion), channel_id=1, source_target_pairs={{4,12},{5,13},{6,14},{7,15},{8,0},{9,1},{10,2},{11,3},{20,28},{21,... | collective-permute-start | bytes 1376264 | tf_op jit(solution)/shard_map/ppermute | solution.py:31
  (13 other events, 164.6 us)

commit v6 on v5

--- a/solution.py
+++ b/solution.py
@@ -31,6 +31,11 @@
     return lax.ppermute(value, "expert", perm)
 
 
+def swap_z(value, distance):
+    step = distance * NX * NC
+    return lax.ppermute(value, "expert", [(i, i ^ step) for i in range(NZ * NX * NC)])
+
+
 def swap_x(value):
     return lax.ppermute(value, "expert", [(i, i ^ NC) for i in range(NZ * NX * NC)])
 
@@ -46,9 +51,6 @@
 NEIGHBOUR = ((0, 1), (1, 0), (2, 3), (3, 2))
 MIDDLE = ((1, 2), (2, 1))
 OUTWARD = ((1, 0), (2, 3))
-TWO_INWARD = ((0, 2), (3, 1))
-TWO_OUTWARD = ((1, 3), (2, 0))
-THREE = ((0, 3), (3, 0))
 
 
 def tie(value, *earlier):
@@ -67,9 +69,10 @@
 
 
 def joined(tokens, cotangent, expert_ids, gate_levels):
-    room = ((0, 0), (0, LANES // 2 - expert_ids.shape[1]))
-    tables = [jnp.pad(table.astype(BF16), room) for table in (expert_ids, gate_levels)]
-    return jnp.concatenate([tokens, cotangent] + tables, axis=1)
+    gap = LANES // 2 - expert_ids.shape[1]
+    table = jnp.pad(expert_ids, ((0, 0), (0, gap + LANES // 2)))
+    table = table + jnp.pad(gate_levels, ((0, 0), (LANES // 2, gap)))
+    return jnp.concatenate([tokens, cotangent, table.astype(BF16)], axis=1)
 
 
 def read_routing(meta, own, limit, top_count):
@@ -89,7 +92,7 @@
     return jnp.where(kept, rank, -1.0).astype(jnp.int32), level / total
 
 
-def front_kernel(top_count, slots, own_ref, *refs):
+def front_kernel(top_count, slots, own_ref, capacity_ref, *refs):
     metas, tok_blocks, cot_blocks = refs[:4], refs[4:8], refs[8:12]
     up_ref, down_ref, rows_ref, rows_cot_ref, part_ref, slot_ref, gates, total = refs[12:]
     step, hidden = pl.program_id(0), up_ref.shape[1]
@@ -97,7 +100,7 @@
     @pl.when(step == 0)
     def _():
         own = own_ref[0].astype(F32)
-        limit = own_ref[1].astype(F32)
+        limit = capacity_ref[own_ref[0]].astype(F32)
         for index, meta in enumerate(metas):
             slot, gate = read_routing(meta[...], own, limit, top_count)
             slot_ref[index] = slot
@@ -128,7 +131,7 @@
             part_ref[:, half * hidden : (half + 1) * hidden] = total[half].astype(BF16)
 
 
-def front(blocks, own, weight_up, weight_down, slots, top_count):
+def front(blocks, own, capacity, weight_up, weight_down, slots, top_count):
     tok_rows = blocks[0].shape[0]
     width, hidden = weight_up.shape
     rows = 4 * slots
@@ -138,7 +141,7 @@
     return pl.pallas_call(
         functools.partial(front_kernel, top_count, slots),
         grid=(width // tile,),
-        in_specs=[pl.BlockSpec(memory_space=pltpu.SMEM)]
+        in_specs=[pl.BlockSpec(memory_space=pltpu.SMEM)] * 2
         + [pl.BlockSpec((tok_rows, LANES), lambda k: (0, 2 * width // LANES))] * 4
         + [pl.BlockSpec((tok_rows, tile), lambda k: (0, k))] * 4
         + [pl.BlockSpec((tok_rows, tile), lambda k: (0, width // tile + k))] * 4
@@ -161,7 +164,7 @@
         ],
         compiler_params=pltpu.CompilerParams(vmem_limit_bytes=32 * 1024 * 1024),
         cost_estimate=NO_COST,
-    )(own, *blocks, *blocks, *blocks, weight_up, weight_down)
+    )(own, capacity, *blocks, *blocks, *blocks, weight_up, weight_down)
 
 
 def back_kernel(slots, slot_ref, part_a, part_b, weight_ref, act_ref, keep_ref, send_ref):
@@ -267,7 +270,7 @@
     own = lax.axis_index("expert")
     z = own // (NX * NC)
     inner = (z > 0) & (z < NZ - 1)
-    who = jnp.stack([own.astype(jnp.int32), capacity[own]])
+    who = own.astype(jnp.int32).reshape(1)
     weight_up, weight_down = up_weight[0], down_weight[0]
 
     hidden_units = weight_up.shape[1]
@@ -276,7 +279,7 @@
 
     def forth(s, *blocks):
         rows_in[s], rows_cot[s], part, slot_of[s] = front(
-            blocks, who, weight_up, weight_down, slots, top_count
+            blocks, who, capacity, weight_up, weight_down, slots, top_count
         )
         parts[s] = (part, swap_dp(part))
 
@@ -298,13 +301,15 @@
     near_core = swap_core(near)
     forth(0, block, own_core, x_own, swap_core(x_own))
 
-    two, far_in = tie((jnp.where(inner, two_in, two_out), far_in), x_near, parts[0][0])
+    two, two_in, far_in = tie(
+        (jnp.where(inner, far_in, two_out), two_in, far_in), x_near, parts[0][0]
+    )
     x_two = swap_x(two)
     far_out = along_z(far_in, OUTWARD)
     two_core = swap_core(two)
     forth(1, near, near_core, x_near, swap_core(x_near))
 
-    far = tie(jnp.where(inner, far_in, far_out), x_two, parts[1][0], parts[0][1])
+    far = tie(jnp.where(inner, two_in, far_out), x_two, parts[1][0], parts[0][1])
     x_far = swap_x(far)
     far_core = swap_core(far)
     forth(2, two, two_core, x_two, swap_core(x_two))
@@ -319,12 +324,12 @@
     back_near = swap_x(near_send)
     back_again(2)
     near_sum = add(chip[1][0], back_near)
-    hop_near = along_z(near_sum, NEIGHBOUR)
-
-    two_send = tie(chip[2][1], back_near)
+    hop_near = swap_z(near_sum, 1)
+
+    two_send = tie(chip[2][1], near_sum)
     back_two = swap_x(two_send)
     two_sum = add(chip[2][0], back_two)
-    hops_two = (along_z(two_sum, MIDDLE), along_z(two_sum, TWO_INWARD))
+    hop_two = swap_z(two_sum, 2)
     back_again(3, near_sum)
     down_grad = weight_grad(
         down_grad_kernel,
@@ -334,13 +339,13 @@
         [pltpu.VMEM((NZ, parts[0][0].shape[0], hidden_units), BF16)],
     )
 
-    far_send = tie(chip[3][1], back_two)
+    far_send = tie(chip[3][1], two_sum)
     back_far = swap_x(far_send)
-    far_sum = tie(add(chip[3][0], back_far), *hops_two)
-    hops_far = (along_z(far_sum, THREE), along_z(far_sum, TWO_OUTWARD))
+    far_sum = add(chip[3][0], back_far)
+    hop_far = swap_z(far_sum, 3)
     up_grad = weight_grad(up_grad_kernel, hidden_units, rows_in, act, [])
     own_sum = chip[0][0].astype(F32) + back_own.astype(F32)
-    for hop in (hop_near, *hops_two, *hops_far):
+    for hop in (hop_near, hop_two, hop_far):
         own_sum = own_sum + hop.astype(F32)
     token_grad = own_sum.astype(BF16)
     return token_grad, up_grad[None], down_grad[None]

time: 211 us -> 198 us (0.938)
  waiting for transfers between devices: 115 us -> 103 us
    ppermute x10 -> x5, waiting for transfers between devices: 31.7 us -> 6.94 us  [along_z(): return lax.ppermute(value, 'expert', perm)]
    ppermute x0 -> x3, waiting for transfers between devices: none -> 17.2 us  [swap_z(): lax.ppermute(value, 'expert', [(i, i ^ step) for i in range(NZ * NX * NC)])]
    ppermute x8, waiting for transfers between devices: 63.6 us -> 49.8 us  [swap_x(): lax.ppermute(value, 'expert', [(i, i ^ NC) for i in range(NZ * NX * NC)])]
    ppermute x4, waiting for transfers between devices: 17.7 us -> 24.4 us  [swap_dp(): return lax.ppermute(value, 'dp', [(0, 1), (1, 0)])]
    ppermute x12, waiting for transfers between devices: 2 us -> 4.61 us  [swap_core(): lax.ppermute(value, 'expert', [(i, i ^ 1) for i in range(NZ * NX * NC)])]
    ppermute x0 -> x3, starting transfers between devices: none -> 2.59 us  [swap_z(): lax.ppermute(value, 'expert', [(i, i ^ step) for i in range(NZ * NX * NC)])]
    ppermute x10 -> x5, starting transfers between devices: 18 us -> 15.6 us  [along_z(): return lax.ppermute(value, 'expert', perm)]
    unnamed x22 -> x20, local copies, waits for them, and re-layouts: 4.12 us -> 5.69 us
  transfers between devices with their start and end apart: 34 -> 32, of which waited for: 17 -> 18; matrix products, arithmetic and copies ran while one was open for 2% -> 2% of each run, Pallas kernels for 23% -> 24%
where the time goes in v6:
time: 198 us; the launch traced here: 197 us
  waiting for transfers between devices  103 us (52%)
  Pallas kernels  47.4 us (24%)
  starting transfers between devices  34 us (17%)
  other arithmetic  6.18 us (3%)
  local copies, waits for them, and re-layouts  5.81 us (3%)
    ppermute x8, waiting for transfers between devices, swap_x(): lax.ppermute(value, 'expert', [(i, i ^ NC) for i in range(NZ * NX * NC)])  49.8 us
    ppermute x4, waiting for transfers between devices, swap_dp(): return lax.ppermute(value, 'dp', [(0, 1), (1, 0)])  24.4 us
    pallas_call x4, Pallas kernels, front(): pl.pallas_call(functools.partial(front_kernel, top_count, slots), grid=(w...  22.7 us
    ppermute x3, waiting for transfers between devices, swap_z(): lax.ppermute(value, 'expert', [(i, i ^ step) for i in range(NZ * NX * NC)])  17.2 us
    ppermute x5, starting transfers between devices, along_z(): return lax.ppermute(value, 'expert', perm)  15.6 us
    pallas_call x2, Pallas kernels, weight_grad(): pl.pallas_call(kernel, grid=(width // tile,), in_specs=[pl.BlockSpec((row...  14 us
    pallas_call x4, Pallas kernels, back(): pl.pallas_call(functools.partial(back_kernel, slots), grid=(width // tile...  10.7 us
    ppermute x8, starting transfers between devices, swap_x(): lax.ppermute(value, 'expert', [(i, i ^ NC) for i in range(NZ * NX * NC)])  8.67 us
  transfers between devices with their start and end apart: 32, of which 18 were waited for; matrix products, arithmetic and copies ran while one was open for 2% of the time, Pallas kernels for 24%

profile of v6, /device:TPU:8, one launch (start us, length us, event | category | flops | bytes accessed | tf_op | source)
XLA Modules:
  0.0 197.4 jit_solution(14110790198262844833)
XLA Ops:
  5.5 4.6 %collective-permute-start.6 = (bf16[128,3712]{1,0:T(8,128)(2,1)S(1)}, bf16[128,3712]{1,0:T(8,128)(2,1)}, u32[]{:S(2)}, u32[]{:S(2)}) collective-permute-start(bf16[128,3712]{1,0:T(8,128)(2,1)S(1)} %pad_maximum_fusion.refs_0_.refs_4_.refs_8_), channel_id=1, source_target_pairs={{4,8},{5,9},{6,10},{7,11},{8,4},{9,5},{10,6},{11,7},{20,24},{21,25... | collective-permute-start | bytes 2850824 | tf_op jit(solution)/shard_map/ppermute | solution.py:31
  10.2 16.3 %collective-permute-done.1.refs_2_.refs_6_.refs_10_ = bf16[128,3712]{1,0:T(8,128)(2,1)} collective-permute-done((bf16[128,3712]{1,0:T(8,128)(2,1)S(1)}, bf16[128,3712]{1,0:T(8,128)(2,1)}, u32[]{:S(2)}, u32[]{:S(2)}) %collective-permute-start.1) | collective-permute-done | bytes 950304 | tf_op jit(solution)/shard_map/ppermute | solution.py:40
  27.6 3.1 %collective-permute-done.6 = bf16[128,3712]{1,0:T(8,128)(2,1)} collective-permute-done((bf16[128,3712]{1,0:T(8,128)(2,1)S(1)}, bf16[128,3712]{1,0:T(8,128)(2,1)}, u32[]{:S(2)}, u32[]{:S(2)}) %collective-permute-start.6) | collective-permute-done | bytes 950304 | tf_op jit(solution)/shard_map/ppermute | solution.py:31
  31.3 3.6 %collective-permute-start.7 = (bf16[128,3712]{1,0:T(8,128)(2,1)S(1)}, bf16[128,3712]{1,0:T(8,128)(2,1)}, u32[]{:S(2)}, u32[]{:S(2)}) collective-permute-start(bf16[128,3712]{1,0:T(8,128)(2,1)S(1)} %collective-permute-done.5.refs_0_.refs_4_.refs_8_), channel_id=1, source_target_pairs={{4,8},{5,9},{6,10},{7,11},{8,4},{9,5},{10,6},{11,7},{20,24},{21,25... | collective-permute-start | bytes 2850824 | tf_op jit(solution)/shard_map/ppermute | solution.py:31
  34.9 2.3 %collective-permute-start.8 = (bf16[128,3712]{1,0:T(8,128)(2,1)}, bf16[128,3712]{1,0:T(8,128)(2,1)}, u32[]{:S(2)}, u32[]{:S(2)}) collective-permute-start(bf16[128,3712]{1,0:T(8,128)(2,1)} %collective-permute-done.6), channel_id=1, source_target_pairs={{4,0},{5,1},{6,2},{7,3},{8,12},{9,13},{10,14},{11,15},{20,16},{21,... | collective-permute-start | bytes 2850824 | tf_op jit(solution)/shard_map/ppermute | solution.py:31
  37.2 2.0 %copy-done = bf16[1,1792,1024]{2,1,0:T(8,128)(2,1)S(1)} copy-done((bf16[1,1792,1024]{2,1,0:T(8,128)(2,1)S(1)}, bf16[1,1792,1024]{2,1,0:T(8,128)(2,1)}, u32[]{:S(2)}) %copy-start) | copy-done | bytes 3670040
  39.2 2.0 %copy-done.2 = bf16[1,1792,1024]{2,1,0:T(8,128)(2,1)S(1)} copy-done((bf16[1,1792,1024]{2,1,0:T(8,128)(2,1)S(1)}, bf16[1,1792,1024]{2,1,0:T(8,128)(2,1)}, u32[]{:S(2)}) %copy-start.2) | copy-done | bytes 3670040
  41.3 6.1 %shard_map.94 = (bf16[256,1792]{1,0:T(8,128)(2,1)S(1)}, bf16[256,1792]{1,0:T(8,128)(2,1)S(1)}, bf16[256,2048]{1,0:T(8,128)(2,1)S(1)}, s32[4,8,128]{2,1,0:T(8,128)S(1)}) custom-call(s32[1]{0:T(128)} %bitcast.own_ref, s32[16]{0:T(128)S(1)} %copy-done.8, bf16[128,3712]{1,0:T(8,128)(2,1)S(1)} %pad_maximum_fusion.refs_0_.refs_4_.refs_8_, ...), custom_call_target="tpu_custom_call" | custom-call | tf_op jit(solution)/shard_map/pallas_call | solution.py:141
  48.9 3.4 %collective-permute-done.9.refs_2_.refs_6_.refs_10_ = bf16[128,3712]{1,0:T(8,128)(2,1)S(1)} collective-permute-done((bf16[128,3712]{1,0:T(8,128)(2,1)S(1)}, bf16[128,3712]{1,0:T(8,128)(2,1)S(1)}, u32[]{:S(2)}, u32[]{:S(2)}) %collective-permute-start.9) | collective-permute-done | bytes 950304 | tf_op jit(solution)/shard_map/ppermute | solution.py:40
  52.3 2.2 %collective-permute-done.7 = bf16[128,3712]{1,0:T(8,128)(2,1)} collective-permute-done((bf16[128,3712]{1,0:T(8,128)(2,1)S(1)}, bf16[128,3712]{1,0:T(8,128)(2,1)}, u32[]{:S(2)}, u32[]{:S(2)}) %collective-permute-start.7) | collective-permute-done | bytes 950304 | tf_op jit(solution)/shard_map/ppermute | solution.py:31
  57.9 4.6 %collective-permute-start.10 = (bf16[128,3712]{1,0:T(8,128)(2,1)}, bf16[128,3712]{1,0:T(8,128)(2,1)S(1)}, u32[]{:S(2)}, u32[]{:S(2)}) collective-permute-start(bf16[128,3712]{1,0:T(8,128)(2,1)} %collective-permute-done.7), channel_id=1, source_target_pairs={{4,0},{5,1},{6,2},{7,3},{8,12},{9,13},{10,14},{11,15},{20,16},{21,... | collective-permute-start | bytes 2850824 | tf_op jit(solution)/shard_map/ppermute | solution.py:31
  62.6 5.6 %shard_map.96 = (bf16[256,1792]{1,0:T(8,128)(2,1)S(1)}, bf16[256,1792]{1,0:T(8,128)(2,1)S(1)}, bf16[256,2048]{1,0:T(8,128)(2,1)S(1)}, s32[4,8,128]{2,1,0:T(8,128)S(1)}) custom-call(s32[1]{0:T(128)} %bitcast.own_ref, s32[16]{0:T(128)S(1)} %copy-done.8, bf16[128,3712]{1,0:T(8,128)(2,1)S(1)} %collective-permute-done.5.refs_0_.refs_4_.refs_8_, ...), custom_call_target="tpu_custom_call" | custom-call | tf_op jit(solution)/shard_map/pallas_call | solution.py:141
  69.8 7.4 %collective-permute-done.11.refs_2_.refs_6_.refs_10_ = bf16[128,3712]{1,0:T(8,128)(2,1)S(1)} collective-permute-done((bf16[128,3712]{1,0:T(8,128)(2,1)S(1)}, bf16[128,3712]{1,0:T(8,128)(2,1)S(1)}, u32[]{:S(2)}, u32[]{:S(2)}) %collective-permute-start.11) | collective-permute-done | bytes 950304 | tf_op jit(solution)/shard_map/ppermute | solution.py:40
  77.2 2.7 %shard_map.95 = (bf16[256,1024]{1,0:T(8,128)(2,1)S(1)}, bf16[2,128,1792]{2,1,0:T(8,128)(2,1)S(1)}, bf16[2,128,1792]{2,1,0:T(8,128)(2,1)S(1)}) custom-call(s32[4,8,128]{2,1,0:T(8,128)S(1)} %get-tuple-element.53.slot_ref, bf16[256,2048]{1,0:T(8,128)(2,1)S(1)} %get-tuple-element.55.part_a.refs_4_, bf16[256,2048]{1,0:T(8,128)(2,1)S(1)} %collective-permute-done.3.part_b.refs_8_, ...), custom_call_target="tpu_custom_call" | custom-call | tf_op jit(solution)/shard_map/pallas_call | solution.py:195
  82.7 5.6 %shard_map.97 = (bf16[256,1792]{1,0:T(8,128)(2,1)S(1)}, bf16[256,1792]{1,0:T(8,128)(2,1)S(1)}, bf16[256,2048]{1,0:T(8,128)(2,1)S(1)}, s32[4,8,128]{2,1,0:T(8,128)S(1)}) custom-call(s32[1]{0:T(128)} %bitcast.own_ref, s32[16]{0:T(128)S(1)} %copy-done.8, bf16[128,3712]{1,0:T(8,128)(2,1)S(1)} %broadcast_select_fusion.1.refs_0_.refs_4_.refs_8_, ...), custom_call_target="tpu_custom_call" | custom-call | tf_op jit(solution)/shard_map/pallas_call | solution.py:141
  89.9 5.9 %collective-permute-done.17.part_b.refs_9_ = bf16[256,2048]{1,0:T(8,128)(2,1)S(1)} collective-permute-done((bf16[256,2048]{1,0:T(8,128)(2,1)S(1)}, bf16[256,2048]{1,0:T(8,128)(2,1)S(1)}, u32[]{:S(2)}, u32[]{:S(2)}) %collective-permute-start.17) | collective-permute-done | bytes 1048608 | tf_op jit(solution)/shard_map/ppermute | solution.py:48
  95.9 2.7 %shard_map.98 = (bf16[256,1024]{1,0:T(8,128)(2,1)S(1)}, bf16[2,128,1792]{2,1,0:T(8,128)(2,1)S(1)}, bf16[2,128,1792]{2,1,0:T(8,128)(2,1)S(1)}) custom-call(s32[4,8,128]{2,1,0:T(8,128)S(1)} %get-tuple-element.68.slot_ref, bf16[256,2048]{1,0:T(8,128)(2,1)S(1)} %get-tuple-element.69.part_a.refs_5_, bf16[256,2048]{1,0:T(8,128)(2,1)S(1)} %collective-permute-done.17.part_b.refs_9_, ...), custom_call_target="tpu_custom_call" | custom-call | tf_op jit(solution)/shard_map/pallas_call | solution.py:195
  98.9 6.0 %collective-permute-done.14.refs_2_.refs_6_.refs_10_ = bf16[128,3712]{1,0:T(8,128)(2,1)S(1)} collective-permute-done((bf16[128,3712]{1,0:T(8,128)(2,1)S(1)}, bf16[128,3712]{1,0:T(8,128)(2,1)S(1)}, u32[]{:S(2)}, u32[]{:S(2)}) %collective-permute-start.14) | collective-permute-done | bytes 950304 | tf_op jit(solution)/shard_map/ppermute | solution.py:40
  106.0 2.2 %collective-permute-done.21.refs_3_.refs_7_.refs_11_ = bf16[128,3712]{1,0:T(8,128)(2,1)S(1)} collective-permute-done((bf16[128,3712]{1,0:T(8,128)(2,1)S(1)}, bf16[128,3712]{1,0:T(8,128)(2,1)S(1)}, u32[]{:S(2)}, u32[]{:S(2)}) %collective-permute-start.21) | collective-permute-done | bytes 950304 | tf_op jit(solution)/shard_map/ppermute | solution.py:44
  108.2 5.5 %shard_map.99 = (bf16[256,1792]{1,0:T(8,128)(2,1)S(1)}, bf16[256,1792]{1,0:T(8,128)(2,1)S(1)}, bf16[256,2048]{1,0:T(8,128)(2,1)S(1)}, s32[4,8,128]{2,1,0:T(8,128)S(1)}) custom-call(s32[1]{0:T(128)} %bitcast.own_ref, s32[16]{0:T(128)S(1)} %copy-done.8, bf16[128,3712]{1,0:T(8,128)(2,1)S(1)} %broadcast_select_fusion.refs_0_.refs_4_.refs_8_, ...), custom_call_target="tpu_custom_call" | custom-call | tf_op jit(solution)/shard_map/pallas_call | solution.py:141
  113.8 2.7 %collective-permute-done.18 = bf16[128,1792]{1,0:T(8,128)(2,1)S(1)} collective-permute-done((bf16[128,1792]{1,0:T(8,128)(2,1)S(1)}, bf16[128,1792]{1,0:T(8,128)(2,1)S(1)}, u32[]{:S(2)}, u32[]{:S(2)}) %collective-permute-start.18) | collective-permute-done | bytes 458784 | tf_op jit(solution)/shard_map/ppermute | solution.py:40
  117.9 2.7 %shard_map.100 = (bf16[256,1024]{1,0:T(8,128)(2,1)S(1)}, bf16[2,128,1792]{2,1,0:T(8,128)(2,1)S(1)}, bf16[2,128,1792]{2,1,0:T(8,128)(2,1)S(1)}) custom-call(s32[4,8,128]{2,1,0:T(8,128)S(1)} %get-tuple-element.75.slot_ref, bf16[256,2048]{1,0:T(8,128)(2,1)S(1)} %get-tuple-element.76.part_a.refs_6_, ...), custom_call_target="tpu_custom_call" | custom-call | tf_op jit(solution)/shard_map/pallas_call | solution.py:195
  122.3 4.9 %collective-permute-done.22 = bf16[128,1792]{1,0:T(8,128)(2,1)S(1)} collective-permute-done((bf16[128,1792]{1,0:T(8,128)(2,1)S(1)}, bf16[128,1792]{1,0:T(8,128)(2,1)S(1)}, u32[]{:S(2)}, u32[]{:S(2)}) %collective-permute-start.22) | collective-permute-done | bytes 458784 | tf_op jit(solution)/shard_map/ppermute | solution.py:40
  128.4 17.8 %collective-permute-done.28.part_b.refs_11_ = bf16[256,2048]{1,0:T(8,128)(2,1)S(1)} collective-permute-done((bf16[256,2048]{1,0:T(8,128)(2,1)S(1)}, bf16[256,2048]{1,0:T(8,128)(2,1)S(1)}, u32[]{:S(2)}, u32[]{:S(2)}) %collective-permute-start.28) | collective-permute-done | bytes 1048608 | tf_op jit(solution)/shard_map/ppermute | solution.py:48
  146.3 2.7 %shard_map.101 = (bf16[256,1024]{1,0:T(8,128)(2,1)S(1)}, bf16[2,128,1792]{2,1,0:T(8,128)(2,1)S(1)}, bf16[2,128,1792]{2,1,0:T(8,128)(2,1)S(1)}) custom-call(s32[4,8,128]{2,1,0:T(8,128)S(1)} %get-tuple-element.81.slot_ref, bf16[256,2048]{1,0:T(8,128)(2,1)S(1)} %get-tuple-element.82.part_a.refs_7_, ...), custom_call_target="tpu_custom_call" | custom-call | tf_op jit(solution)/shard_map/pallas_call | solution.py:195
  149.1 2.3 %collective-permute-done.29 = bf16[2,128,1792]{2,1,0:T(8,128)(2,1)S(1)} collective-permute-done((bf16[2,128,1792]{2,1,0:T(8,128)(2,1)S(1)}, bf16[2,128,1792]{2,1,0:T(8,128)(2,1)S(1)}, u32[]{:S(2)}, u32[]{:S(2)}) %collective-permute-start.29) | collective-permute-done | bytes 917536 | tf_op jit(solution)/shard_map/ppermute | solution.py:44
  153.3 2.0 %collective-permute-start.27 = (bf16[128,1792]{1,0:T(8,128)(2,1)S(1)}, bf16[128,1792]{1,0:T(8,128)(2,1)S(1)}, u32[]{:S(2)}, u32[]{:S(2)}) collective-permute-start(bf16[128,1792]{1,0:T(8,128)(2,1)S(1)} %fusion.1), channel_id=1, source_target_pairs={{0,8},{1,9},{2,10},{3,11},{4,12},{5,13},{6,14},{7,15},{8,0},{9,1},... | collective-permute-start | bytes 1376264 | tf_op jit(solution)/shard_map/ppermute | solution.py:36
  155.3 9.1 %collective-permute-done.30 = bf16[128,1792]{1,0:T(8,128)(2,1)S(1)} collective-permute-done((bf16[128,1792]{1,0:T(8,128)(2,1)S(1)}, bf16[128,1792]{1,0:T(8,128)(2,1)S(1)}, u32[]{:S(2)}, u32[]{:S(2)}) %collective-permute-start.30) | collective-permute-done | bytes 458784 | tf_op jit(solution)/shard_map/ppermute | solution.py:40
  165.1 6.3 %shard_map.102 = bf16[1792,1024]{1,0:T(8,128)(2,1)} custom-call(bf16[256,1792]{1,0:T(8,128)(2,1)S(1)} %get-tuple-element.87.refs_0_, bf16[256,1792]{1,0:T(8,128)(2,1)S(1)} %get-tuple-element.88.refs_1_, bf16[256,1792]{1,0:T(8,128)(2,1)S(1)} %get-tuple-element.89.refs_2_, bf16[256,1792]{1,0:T(8,128)(2,1)S(1)} %get-tuple-element.90.refs_3_, ...), custom_call_target="tpu_custom_call" | custom-call | tf_op jit(solution)/shard_map/pallas_call | solution.py:242
  171.4 7.7 %shard_map.103 = bf16[1792,1024]{1,0:T(8,128)(2,1)} custom-call(bf16[256,1792]{1,0:T(8,128)(2,1)S(1)} %copy-done.5, bf16[256,1792]{1,0:T(8,128)(2,1)S(1)} %copy-done.7, bf16[256,1792]{1,0:T(8,128)(2,1)S(1)} %get-tuple-element.101.refs_2_, bf16[256,1792]{1,0:T(8,128)(2,1)S(1)} %get-tuple-element.102.refs_3_, ...), custom_call_target="tpu_custom_call" | custom-call | tf_op jit(solution)/shard_map/pallas_call | solution.py:242
  179.1 6.3 %collective-permute-done.27 = bf16[128,1792]{1,0:T(8,128)(2,1)S(1)} collective-permute-done((bf16[128,1792]{1,0:T(8,128)(2,1)S(1)}, bf16[128,1792]{1,0:T(8,128)(2,1)S(1)}, u32[]{:S(2)}, u32[]{:S(2)}) %collective-permute-start.27) | collective-permute-done | bytes 458784 | tf_op jit(solution)/shard_map/ppermute | solution.py:36
  185.3 11.0 %collective-permute-done.31 = bf16[128,1792]{1,0:T(8,128)(2,1)S(1)} collective-permute-done((bf16[128,1792]{1,0:T(8,128)(2,1)S(1)}, bf16[128,1792]{1,0:T(8,128)(2,1)S(1)}, u32[]{:S(2)}, u32[]{:S(2)}) %collective-permute-start.31) | collective-permute-done | bytes 458784 | tf_op jit(solution)/shard_map/ppermute | solution.py:36
  (78 shorter events, 27.1 us)
Async XLA Ops:
  3.5 23.0 %collective-permute-start.1 = (bf16[128,3712]{1,0:T(8,128)(2,1)S(1)}, bf16[128,3712]{1,0:T(8,128)(2,1)}, u32[]{:S(2)}, u32[]{:S(2)}) collective-permute-start(bf16[128,3712]{1,0:T(8,128)(2,1)S(1)} %pad_maximum_fusion.refs_0_.refs_4_.refs_8_), channel_id=1, source_target_pairs={{0,2},{1,3},{2,0},{3,1},{4,6},{5,7},{6,4},{7,5},{8,10},{9,11},{10,... | collective-permute-start | bytes 2850824 | tf_op jit(solution)/shard_map/ppermute | solution.py:40
  5.1 22.5 %collective-permute-start.5 = (bf16[128,3712]{1,0:T(8,128)(2,1)S(1)}, bf16[128,3712]{1,0:T(8,128)(2,1)S(1)}, u32[]{:S(2)}, u32[]{:S(2)}) collective-permute-start(bf16[128,3712]{1,0:T(8,128)(2,1)S(1)} %pad_maximum_fusion.refs_0_.refs_4_.refs_8_), channel_id=1, source_target_pairs={{0,4},{1,5},{2,6},{3,7},{4,0},{5,1},{6,2},{7,3},{8,12},{9,13},{10,... | collective-permute-start | bytes 2850824 | tf_op jit(solution)/shard_map/ppermute | solution.py:31
  5.5 25.2 %collective-permute-start.6 = (bf16[128,3712]{1,0:T(8,128)(2,1)S(1)}, bf16[128,3712]{1,0:T(8,128)(2,1)}, u32[]{:S(2)}, u32[]{:S(2)}) collective-permute-start(bf16[128,3712]{1,0:T(8,128)(2,1)S(1)} %pad_maximum_fusion.refs_0_.refs_4_.refs_8_), channel_id=1, source_target_pairs={{4,8},{5,9},{6,10},{7,11},{8,4},{9,5},{10,6},{11,7},{20,24},{21,25... | collective-permute-start | bytes 2850824 | tf_op jit(solution)/shard_map/ppermute | solution.py:31
  10.2 27.0 %collective-permute-start = (bf16[128,3712]{1,0:T(8,128)(2,1)S(1)}, bf16[128,3712]{1,0:T(8,128)(2,1)}, u32[]{:S(2)}, u32[]{:S(2)}) collective-permute-start(bf16[128,3712]{1,0:T(8,128)(2,1)S(1)} %pad_maximum_fusion.refs_0_.refs_4_.refs_8_), channel_id=1, source_target_pairs={{0,1},{1,0},{2,3},{3,2},{4,5},{5,4},{6,7},{7,6},{8,9},{9,8},{10,11... | collective-permute-start | bytes 2850824 | tf_op jit(solution)/shard_map/ppermute | solution.py:44
  26.5 10.7 %collective-permute-start.2 = (bf16[128,3712]{1,0:T(8,128)(2,1)}, bf16[128,3712]{1,0:T(8,128)(2,1)}, u32[]{:S(2)}, u32[]{:S(2)}) collective-permute-start(bf16[128,3712]{1,0:T(8,128)(2,1)} %collective-permute-done.1.refs_2_.refs_6_.refs_10_), channel_id=1, source_target_pairs={{0,1},{1,0},{2,3},{3,2},{4,5},{5,4},{6,7},{7,6},{8,9},{9,8},{10,11... | collective-permute-start | bytes 2850824 | tf_op jit(solution)/shard_map/ppermute | solution.py:44
  30.7 21.6 %collective-permute-start.9 = (bf16[128,3712]{1,0:T(8,128)(2,1)S(1)}, bf16[128,3712]{1,0:T(8,128)(2,1)S(1)}, u32[]{:S(2)}, u32[]{:S(2)}) collective-permute-start(bf16[128,3712]{1,0:T(8,128)(2,1)S(1)} %collective-permute-done.5.refs_0_.refs_4_.refs_8_), channel_id=1, source_target_pairs={{0,2},{1,3},{2,0},{3,1},{4,6},{5,7},{6,4},{7,5},{8,10},{9,11},{10,... | collective-permute-start | bytes 2850824 | tf_op jit(solution)/shard_map/ppermute | solution.py:40
  31.3 23.3 %collective-permute-start.7 = (bf16[128,3712]{1,0:T(8,128)(2,1)S(1)}, bf16[128,3712]{1,0:T(8,128)(2,1)}, u32[]{:S(2)}, u32[]{:S(2)}) collective-permute-start(bf16[128,3712]{1,0:T(8,128)(2,1)S(1)} %collective-permute-done.5.refs_0_.refs_4_.refs_8_), channel_id=1, source_target_pairs={{4,8},{5,9},{6,10},{7,11},{8,4},{9,5},{10,6},{11,7},{20,24},{21,25... | collective-permute-start | bytes 2850824 | tf_op jit(solution)/shard_map/ppermute | solution.py:31
  34.9 20.1 %collective-permute-start.8 = (bf16[128,3712]{1,0:T(8,128)(2,1)}, bf16[128,3712]{1,0:T(8,128)(2,1)}, u32[]{:S(2)}, u32[]{:S(2)}) collective-permute-start(bf16[128,3712]{1,0:T(8,128)(2,1)} %collective-permute-done.6), channel_id=1, source_target_pairs={{4,0},{5,1},{6,2},{7,3},{8,12},{9,13},{10,14},{11,15},{20,16},{21,... | collective-permute-start | bytes 2850824 | tf_op jit(solution)/shard_map/ppermute | solution.py:31
  37.2 25.4 %collective-permute-start.12 = (bf16[128,3712]{1,0:T(8,128)(2,1)S(1)}, bf16[128,3712]{1,0:T(8,128)(2,1)S(1)}, u32[]{:S(2)}, u32[]{:S(2)}) collective-permute-start(bf16[128,3712]{1,0:T(8,128)(2,1)S(1)} %collective-permute-done.5.refs_0_.refs_4_.refs_8_), channel_id=1, source_target_pairs={{0,1},{1,0},{2,3},{3,2},{4,5},{5,4},{6,7},{7,6},{8,9},{9,8},{10,11... | collective-permute-start | bytes 2850824 | tf_op jit(solution)/shard_map/ppermute | solution.py:44
  47.4 29.8 %collective-permute-start.3 = (bf16[256,2048]{1,0:T(8,128)(2,1)S(1)}, bf16[256,2048]{1,0:T(8,128)(2,1)S(1)}, u32[]{:S(2)}, u32[]{:S(2)}) collective-permute-start(bf16[256,2048]{1,0:T(8,128)(2,1)S(1)} %get-tuple-element.55.part_a.refs_4_), channel_id=1, source_target_pairs={{0,16},{16,0},{1,17},{17,1},{2,18},{18,2},{3,19},{19,3},{4,20},{20... | collective-permute-start | bytes 3145736 | tf_op jit(solution)/shard_map/ppermute | solution.py:48
  52.3 10.2 %collective-permute-start.13 = (bf16[128,3712]{1,0:T(8,128)(2,1)S(1)}, bf16[128,3712]{1,0:T(8,128)(2,1)S(1)}, u32[]{:S(2)}, u32[]{:S(2)}) collective-permute-start(bf16[128,3712]{1,0:T(8,128)(2,1)S(1)} %collective-permute-done.9.refs_2_.refs_6_.refs_10_), channel_id=1, source_target_pairs={{0,1},{1,0},{2,3},{3,2},{4,5},{5,4},{6,7},{7,6},{8,9},{9,8},{10,11... | collective-permute-start | bytes 2850824 | tf_op jit(solution)/shard_map/ppermute | solution.py:44
  56.4 20.8 %collective-permute-start.11 = (bf16[128,3712]{1,0:T(8,128)(2,1)S(1)}, bf16[128,3712]{1,0:T(8,128)(2,1)S(1)}, u32[]{:S(2)}, u32[]{:S(2)}) collective-permute-start(bf16[128,3712]{1,0:T(8,128)(2,1)S(1)} %broadcast_select_fusion.1.refs_0_.refs_4_.refs_8_), channel_id=1, source_target_pairs={{0,2},{1,3},{2,0},{3,1},{4,6},{5,7},{6,4},{7,5},{8,10},{9,11},{10,... | collective-permute-start | bytes 2850824 | tf_op jit(solution)/shard_map/ppermute | solution.py:40
  57.9 22.6 %collective-permute-start.10 = (bf16[128,3712]{1,0:T(8,128)(2,1)}, bf16[128,3712]{1,0:T(8,128)(2,1)S(1)}, u32[]{:S(2)}, u32[]{:S(2)}) collective-permute-start(bf16[128,3712]{1,0:T(8,128)(2,1)} %collective-permute-done.7), channel_id=1, source_target_pairs={{4,0},{5,1},{6,2},{7,3},{8,12},{9,13},{10,14},{11,15},{20,16},{21,... | collective-permute-start | bytes 2850824 | tf_op jit(solution)/shard_map/ppermute | solution.py:31
  68.2 27.7 %collective-permute-start.17 = (bf16[256,2048]{1,0:T(8,128)(2,1)S(1)}, bf16[256,2048]{1,0:T(8,128)(2,1)S(1)}, u32[]{:S(2)}, u32[]{:S(2)}) collective-permute-start(bf16[256,2048]{1,0:T(8,128)(2,1)S(1)} %get-tuple-element.69.part_a.refs_5_), channel_id=1, source_target_pairs={{0,16},{16,0},{1,17},{17,1},{2,18},{18,2},{3,19},{19,3},{4,20},{20... | collective-permute-start | bytes 3145736 | tf_op jit(solution)/shard_map/ppermute | solution.py:48
  69.8 13.0 %collective-permute-start.15 = (bf16[128,3712]{1,0:T(8,128)(2,1)S(1)}, bf16[128,3712]{1,0:T(8,128)(2,1)S(1)}, u32[]{:S(2)}, u32[]{:S(2)}) collective-permute-start(bf16[128,3712]{1,0:T(8,128)(2,1)S(1)} %broadcast_select_fusion.1.refs_0_.refs_4_.refs_8_), channel_id=1, source_target_pairs={{0,1},{1,0},{2,3},{3,2},{4,5},{5,4},{6,7},{7,6},{8,9},{9,8},{10,11... | collective-permute-start | bytes 2850824 | tf_op jit(solution)/shard_map/ppermute | solution.py:44
  77.2 5.5 %collective-permute-start.16 = (bf16[128,3712]{1,0:T(8,128)(2,1)S(1)}, bf16[128,3712]{1,0:T(8,128)(2,1)S(1)}, u32[]{:S(2)}, u32[]{:S(2)}) collective-permute-start(bf16[128,3712]{1,0:T(8,128)(2,1)S(1)} %collective-permute-done.11.refs_2_.refs_6_.refs_10_), channel_id=1, source_target_pairs={{0,1},{1,0},{2,3},{3,2},{4,5},{5,4},{6,7},{7,6},{8,9},{9,8},{10,11... | collective-permute-start | bytes 2850824 | tf_op jit(solution)/shard_map/ppermute | solution.py:44
  79.9 18.7 %collective-permute-start.4 = (bf16[2,128,1792]{2,1,0:T(8,128)(2,1)S(1)}, bf16[2,128,1792]{2,1,0:T(8,128)(2,1)S(1)}, u32[]{:S(2)}, u32[]{:S(2)}) collective-permute-start(bf16[2,128,1792]{2,1,0:T(8,128)(2,1)S(1)} %get-tuple-element.58), channel_id=1, source_target_pairs={{0,1},{1,0},{2,3},{3,2},{4,5},{5,4},{6,7},{7,6},{8,9},{9,8},{10,11... | collective-permute-start | bytes 2752520 | tf_op jit(solution)/shard_map/ppermute | solution.py:44
  81.8 23.1 %collective-permute-start.14 = (bf16[128,3712]{1,0:T(8,128)(2,1)S(1)}, bf16[128,3712]{1,0:T(8,128)(2,1)S(1)}, u32[]{:S(2)}, u32[]{:S(2)}) collective-permute-start(bf16[128,3712]{1,0:T(8,128)(2,1)S(1)} %broadcast_select_fusion.refs_0_.refs_4_.refs_8_), channel_id=1, source_target_pairs={{0,2},{1,3},{2,0},{3,1},{4,6},{5,7},{6,4},{7,5},{8,10},{9,11},{10,... | collective-permute-start | bytes 2850824 | tf_op jit(solution)/shard_map/ppermute | solution.py:40
  82.7 23.2 %collective-permute-start.20 = (bf16[128,3712]{1,0:T(8,128)(2,1)S(1)}, bf16[128,3712]{1,0:T(8,128)(2,1)S(1)}, u32[]{:S(2)}, u32[]{:S(2)}) collective-permute-start(bf16[128,3712]{1,0:T(8,128)(2,1)S(1)} %broadcast_select_fusion.refs_0_.refs_4_.refs_8_), channel_id=1, source_target_pairs={{0,1},{1,0},{2,3},{3,2},{4,5},{5,4},{6,7},{7,6},{8,9},{9,8},{10,11... | collective-permute-start | bytes 2850824 | tf_op jit(solution)/shard_map/ppermute | solution.py:44
  88.3 29.6 %collective-permute-start.24 = (bf16[256,2048]{1,0:T(8,128)(2,1)S(1)}, bf16[256,2048]{1,0:T(8,128)(2,1)S(1)}, u32[]{:S(2)}, u32[]{:S(2)}) collective-permute-start(bf16[256,2048]{1,0:T(8,128)(2,1)S(1)} %get-tuple-element.76.part_a.refs_6_), channel_id=1, source_target_pairs={{0,16},{16,0},{1,17},{17,1},{2,18},{18,2},{3,19},{19,3},{4,20},{20... | collective-permute-start | bytes 3145736 | tf_op jit(solution)/shard_map/ppermute | solution.py:48
  98.5 7.2 %collective-permute-start.19 = (bf16[2,128,1792]{2,1,0:T(8,128)(2,1)S(1)}, bf16[2,128,1792]{2,1,0:T(8,128)(2,1)S(1)}, u32[]{:S(2)}, u32[]{:S(2)}) collective-permute-start(bf16[2,128,1792]{2,1,0:T(8,128)(2,1)S(1)} %get-tuple-element.72), channel_id=1, source_target_pairs={{0,1},{1,0},{2,3},{3,2},{4,5},{5,4},{6,7},{7,6},{8,9},{9,8},{10,11... | collective-permute-start | bytes 2752520 | tf_op jit(solution)/shard_map/ppermute | solution.py:44
  104.9 11.6 %collective-permute-start.18 = (bf16[128,1792]{1,0:T(8,128)(2,1)S(1)}, bf16[128,1792]{1,0:T(8,128)(2,1)S(1)}, u32[]{:S(2)}, u32[]{:S(2)}) collective-permute-start(bf16[128,1792]{1,0:T(8,128)(2,1)S(1)} %slice_bitcast_fusion.6), channel_id=1, source_target_pairs={{0,2},{1,3},{2,0},{3,1},{4,6},{5,7},{6,4},{7,5},{8,10},{9,11},{10,... | collective-permute-start | bytes 1376264 | tf_op jit(solution)/shard_map/ppermute | solution.py:40
  105.7 2.5 %collective-permute-start.21 = (bf16[128,3712]{1,0:T(8,128)(2,1)S(1)}, bf16[128,3712]{1,0:T(8,128)(2,1)S(1)}, u32[]{:S(2)}, u32[]{:S(2)}) collective-permute-start(bf16[128,3712]{1,0:T(8,128)(2,1)S(1)} %collective-permute-done.14.refs_2_.refs_6_.refs_10_), channel_id=1, source_target_pairs={{0,1},{1,0},{2,3},{3,2},{4,5},{5,4},{6,7},{7,6},{8,9},{9,8},{10,11... | collective-permute-start | bytes 2850824 | tf_op jit(solution)/shard_map/ppermute | solution.py:44
  116.5 10.7 %collective-permute-start.22 = (bf16[128,1792]{1,0:T(8,128)(2,1)S(1)}, bf16[128,1792]{1,0:T(8,128)(2,1)S(1)}, u32[]{:S(2)}, u32[]{:S(2)}) collective-permute-start(bf16[128,1792]{1,0:T(8,128)(2,1)S(1)} %slice_bitcast_fusion.4), channel_id=1, source_target_pairs={{0,2},{1,3},{2,0},{3,1},{4,6},{5,7},{6,4},{7,5},{8,10},{9,11},{10,... | collective-permute-start | bytes 1376264 | tf_op jit(solution)/shard_map/ppermute | solution.py:40
  120.6 6.7 %collective-permute-start.25 = (bf16[2,128,1792]{2,1,0:T(8,128)(2,1)S(1)}, bf16[2,128,1792]{2,1,0:T(8,128)(2,1)S(1)}, u32[]{:S(2)}, u32[]{:S(2)}) collective-permute-start(bf16[2,128,1792]{2,1,0:T(8,128)(2,1)S(1)} %get-tuple-element.79), channel_id=1, source_target_pairs={{0,1},{1,0},{2,3},{3,2},{4,5},{5,4},{6,7},{7,6},{8,9},{9,8},{10,11... | collective-permute-start | bytes 2752520 | tf_op jit(solution)/shard_map/ppermute | solution.py:44
  120.7 25.6 %collective-permute-start.28 = (bf16[256,2048]{1,0:T(8,128)(2,1)S(1)}, bf16[256,2048]{1,0:T(8,128)(2,1)S(1)}, u32[]{:S(2)}, u32[]{:S(2)}) collective-permute-start(bf16[256,2048]{1,0:T(8,128)(2,1)S(1)} %get-tuple-element.82.part_a.refs_7_), channel_id=1, source_target_pairs={{0,16},{16,0},{1,17},{17,1},{2,18},{18,2},{3,19},{19,3},{4,20},{20... | collective-permute-start | bytes 3145736 | tf_op jit(solution)/shard_map/ppermute | solution.py:48
  127.5 21.5 %collective-permute-start.26 = (bf16[128,1792]{1,0:T(8,128)(2,1)S(1)}, bf16[128,1792]{1,0:T(8,128)(2,1)S(1)}, u32[]{:S(2)}, u32[]{:S(2)}) collective-permute-start(bf16[128,1792]{1,0:T(8,128)(2,1)S(1)} %slice_bitcast_fusion.2), channel_id=1, source_target_pairs={{0,2},{1,3},{2,0},{3,1},{4,6},{5,7},{6,4},{7,5},{8,10},{9,11},{10,... | collective-permute-start | bytes 1376264 | tf_op jit(solution)/shard_map/ppermute | solution.py:40
  148.9 2.5 %collective-permute-start.29 = (bf16[2,128,1792]{2,1,0:T(8,128)(2,1)S(1)}, bf16[2,128,1792]{2,1,0:T(8,128)(2,1)S(1)}, u32[]{:S(2)}, u32[]{:S(2)}) collective-permute-start(bf16[2,128,1792]{2,1,0:T(8,128)(2,1)S(1)} %get-tuple-element.85), channel_id=1, source_target_pairs={{0,1},{1,0},{2,3},{3,2},{4,5},{5,4},{6,7},{7,6},{8,9},{9,8},{10,11... | collective-permute-start | bytes 2752520 | tf_op jit(solution)/shard_map/ppermute | solution.py:44
  151.7 12.6 %collective-permute-start.30 = (bf16[128,1792]{1,0:T(8,128)(2,1)S(1)}, bf16[128,1792]{1,0:T(8,128)(2,1)S(1)}, u32[]{:S(2)}, u32[]{:S(2)}) collective-permute-start(bf16[128,1792]{1,0:T(8,128)(2,1)S(1)} %slice_bitcast_fusion), channel_id=1, source_target_pairs={{0,2},{1,3},{2,0},{3,1},{4,6},{5,7},{6,4},{7,5},{8,10},{9,11},{10,... | collective-permute-start | bytes 1376264 | tf_op jit(solution)/shard_map/ppermute | solution.py:40
  153.3 25.8 %collective-permute-start.23 = (bf16[128,1792]{1,0:T(8,128)(2,1)S(1)}, bf16[128,1792]{1,0:T(8,128)(2,1)S(1)}, u32[]{:S(2)}, u32[]{:S(2)}) collective-permute-start(bf16[128,1792]{1,0:T(8,128)(2,1)S(1)} %fusion.2), channel_id=1, source_target_pairs={{0,4},{1,5},{2,6},{3,7},{4,0},{5,1},{6,2},{7,3},{8,12},{9,13},{10,... | collective-permute-start | bytes 1376264 | tf_op jit(solution)/shard_map/ppermute | solution.py:36
  153.3 32.0 %collective-permute-start.27 = (bf16[128,1792]{1,0:T(8,128)(2,1)S(1)}, bf16[128,1792]{1,0:T(8,128)(2,1)S(1)}, u32[]{:S(2)}, u32[]{:S(2)}) collective-permute-start(bf16[128,1792]{1,0:T(8,128)(2,1)S(1)} %fusion.1), channel_id=1, source_target_pairs={{0,8},{1,9},{2,10},{3,11},{4,12},{5,13},{6,14},{7,15},{8,0},{9,1},... | collective-permute-start | bytes 1376264 | tf_op jit(solution)/shard_map/ppermute | solution.py:36
  164.5 31.8 %collective-permute-start.31 = (bf16[128,1792]{1,0:T(8,128)(2,1)S(1)}, bf16[128,1792]{1,0:T(8,128)(2,1)S(1)}, u32[]{:S(2)}, u32[]{:S(2)}) collective-permute-start(bf16[128,1792]{1,0:T(8,128)(2,1)S(1)} %fusion), channel_id=1, source_target_pairs={{0,12},{1,13},{2,14},{3,15},{4,8},{5,9},{6,10},{7,11},{8,4},{9,5},... | collective-permute-start | bytes 1376264 | tf_op jit(solution)/shard_map/ppermute | solution.py:36
  (9 other events, 106.0 us)

commit v7 on v6

--- a/solution.py
+++ b/solution.py
@@ -13,6 +13,7 @@
 CONTRACT_LAST = (((1,), (1,)), ((), ()))
 
 NO_COST = pl.CostEstimate(flops=0, bytes_accessed=0, transcendentals=0)
+SOME_COST = pl.CostEstimate(flops=0, bytes_accessed=1 << 23, transcendentals=0)
 
 NZ, NX, NC = 4, 2, 2
 
@@ -94,7 +95,8 @@
 
 def front_kernel(top_count, slots, own_ref, capacity_ref, *refs):
     metas, tok_blocks, cot_blocks = refs[:4], refs[4:8], refs[8:12]
-    up_ref, down_ref, rows_ref, rows_cot_ref, part_ref, slot_ref, gates, total = refs[12:]
+    up_ref, down_ref, rows_ref, rows_cot_ref, slot_ref = refs[12:17]
+    part_refs, (gates, total) = refs[17:-2], refs[-2:]
     step, hidden = pl.program_id(0), up_ref.shape[1]
 
     @pl.when(step == 0)
@@ -128,10 +130,13 @@
     @pl.when(step == pl.num_programs(0) - 1)
     def _():
         for half in range(2):
-            part_ref[:, half * hidden : (half + 1) * hidden] = total[half].astype(BF16)
-
-
-def front(blocks, own, capacity, weight_up, weight_down, slots, top_count):
+            for piece, part_ref in enumerate(part_refs):
+                height = part_ref.shape[0]
+                rows = slice(piece * height, (piece + 1) * height)
+                part_ref[:, half * hidden : (half + 1) * hidden] = total[half, rows].astype(BF16)
+
+
+def front(blocks, own, capacity, weight_up, weight_down, slots, top_count, pieces):
     tok_rows = blocks[0].shape[0]
     width, hidden = weight_up.shape
     rows = 4 * slots
@@ -149,15 +154,15 @@
         out_specs=[
             picked,
             picked,
-            pl.BlockSpec((rows, 2 * hidden), lambda k: (0, 0)),
             pl.BlockSpec((4, 8, tok_rows), lambda k: (0, 0, 0)),
-        ],
+        ]
+        + [pl.BlockSpec((rows // pieces, 2 * hidden), lambda k: (0, 0))] * pieces,
         out_shape=[
             jax.ShapeDtypeStruct((rows, width), BF16),
             jax.ShapeDtypeStruct((rows, width), BF16),
-            jax.ShapeDtypeStruct((rows, 2 * hidden), BF16),
             jax.ShapeDtypeStruct((4, 8, tok_rows), jnp.int32),
-        ],
+        ]
+        + [jax.ShapeDtypeStruct((rows // pieces, 2 * hidden), BF16)] * pieces,
         scratch_shapes=[
             pltpu.VMEM((4, 8, tok_rows), F32),
             pltpu.VMEM((2, rows, hidden), F32),
@@ -167,7 +172,7 @@
     )(own, capacity, *blocks, *blocks, *blocks, weight_up, weight_down)
 
 
-def back_kernel(slots, slot_ref, part_a, part_b, weight_ref, act_ref, keep_ref, send_ref):
+def back_kernel(slots, first, slot_ref, part_a, part_b, weight_ref, act_ref, keep_ref, send_ref):
     @pl.when(pl.program_id(0) == 0)
     def _():
         hidden = act_ref.shape[1]
@@ -177,23 +182,24 @@
         act_ref[...] = (hidden_cot * (sigmoid * (1.0 + preact * (1.0 - sigmoid)))).astype(BF16)
 
     back = dot_f32(act_ref[...], weight_ref[...], CONTRACT_LAST).astype(BF16)
-    for index in range(4):
-        hit = placing_of(slot_ref[index, 0:1, :], slots)
+    for index in range(act_ref.shape[0] // slots):
+        hit = placing_of(slot_ref[first + index, 0:1, :], slots)
         placing = jnp.where(hit, 1.0, 0.0).astype(BF16)
         spread = dot_f32(placing, back[index * slots : (index + 1) * slots], CONTRACT_ROWS)
         out_ref = send_ref if index % 2 else keep_ref
         out_ref[index // 2] = spread.astype(BF16)
 
 
-def back(slot_of, parts, weight, slots):
+def back(slot_of, parts, weight, slots, first=0, cost=None):
     tok_rows = slot_of.shape[2]
     width, hidden = weight.shape
-    rows = 4 * slots
+    rows = parts[0].shape[0]
+    pairs = rows // (2 * slots)
     tile = width // 2
     full = pl.BlockSpec((rows, hidden), lambda n: (0, 0))
-    spread = pl.BlockSpec((2, tok_rows, tile), lambda n: (0, 0, n))
+    spread = pl.BlockSpec((pairs, tok_rows, tile), lambda n: (0, 0, n))
     return pl.pallas_call(
-        functools.partial(back_kernel, slots),
+        functools.partial(back_kernel, slots, first),
         grid=(width // tile,),
         in_specs=[pl.BlockSpec((4, 8, tok_rows), lambda n: (0, 0, 0))]
         + [pl.BlockSpec((rows, 2 * hidden), lambda n: (0, 0))] * 2
@@ -201,11 +207,11 @@
         out_specs=[full, spread, spread],
         out_shape=[
             jax.ShapeDtypeStruct((rows, hidden), BF16),
-            jax.ShapeDtypeStruct((2, tok_rows, width), BF16),
-            jax.ShapeDtypeStruct((2, tok_rows, width), BF16),
+            jax.ShapeDtypeStruct((pairs, tok_rows, width), BF16),
+            jax.ShapeDtypeStruct((pairs, tok_rows, width), BF16),
         ],
         compiler_params=pltpu.CompilerParams(vmem_limit_bytes=32 * 1024 * 1024),
-        cost_estimate=NO_COST,
+        cost_estimate=cost or NO_COST,
     )(slot_of, *parts, weight)
 
 
@@ -221,35 +227,44 @@
 def down_grad_kernel(*refs):
     count = (len(refs) - 2) // 3
     out_ref, hidden_ref = refs[-2:]
+    heights = [left.shape[0] for left in refs[:count]]
+    spans = [slice(sum(heights[:i]), sum(heights[: i + 1])) for i in range(count)]
 
     @pl.when(pl.program_id(0) == 0)
     def _():
-        for index, (first, second) in enumerate(zip(refs[count : 2 * count], refs[2 * count : -2])):
+        for span, first, second in zip(spans, refs[count : 2 * count], refs[2 * count : -2]):
             preact = first[...].astype(F32) + second[...].astype(F32)
-            hidden_ref[index] = (preact * jax.nn.sigmoid(preact)).astype(BF16)
+            hidden_ref[span, :] = (preact * jax.nn.sigmoid(preact)).astype(BF16)
 
     total = None
-    for index, left in enumerate(refs[:count]):
-        term = dot_f32(left[...], hidden_ref[index], CONTRACT_ROWS)
+    for span, left in zip(spans, refs[:count]):
+        term = dot_f32(left[...], hidden_ref[span, :], CONTRACT_ROWS)
         total = term if total is None else total + term
     out_ref[...] = total.astype(BF16)
 
 
-def weight_grad(kernel, hidden, lefts, rights, scratch_shapes):
-    rows, width = lefts[0].shape
-    count = len(lefts)
+def weight_grad(kernel, hidden, lefts, pieces, rights, scratch_shapes):
+    width = lefts[0].shape[1]
     tile = 256
+    in_specs, operands = [], []
+    for index, left in enumerate(lefts):
+        count = pieces if index == len(lefts) - 1 else 1
+        for piece in range(count):
+            in_specs.append(pl.BlockSpec((left.shape[0] // count, tile), lambda n, piece=piece: (piece, n)))
+            operands.append(left)
+    for right in rights:
+        in_specs.append(pl.BlockSpec((right.shape[0], hidden), lambda n: (0, 0)))
+        operands.append(right)
     return pl.pallas_call(
         kernel,
         grid=(width // tile,),
-        in_specs=[pl.BlockSpec((rows, tile), lambda n: (0, n))] * count
-        + [pl.BlockSpec((rows, hidden), lambda n: (0, 0))] * len(rights),
+        in_specs=in_specs,
         out_specs=pl.BlockSpec((tile, hidden), lambda n: (n, 0)),
         out_shape=jax.ShapeDtypeStruct((width, hidden), BF16),
         scratch_shapes=scratch_shapes,
         compiler_params=pltpu.CompilerParams(vmem_limit_bytes=32 * 1024 * 1024),
         cost_estimate=NO_COST,
-    )(*lefts, *rights)
+    )(*operands)
 
 
 def slots_and_gates(routing, own, limit, top_count):
@@ -278,10 +293,14 @@
     rows_in, rows_cot, slot_of, parts, act, chip = ([None] * NZ for _ in range(6))
 
     def forth(s, *blocks):
-        rows_in[s], rows_cot[s], part, slot_of[s] = front(
-            blocks, who, capacity, weight_up, weight_down, slots, top_count
+        pieces = 2 if s == NZ - 1 else 1
+        rows_in[s], rows_cot[s], slot_of[s], *part = front(
+            blocks, who, capacity, weight_up, weight_down, slots, top_count, pieces
         )
-        parts[s] = (part, swap_dp(part))
+        swapped = [swap_dp(part[-1])]
+        if pieces == 2:
+            swapped.append(swap_dp(tie(part[0], swapped[0])))
+        parts[s] = (*part, *swapped)
 
     def back_again(s, *earlier):
         pair = tie(parts[s], *earlier)
@@ -330,20 +349,26 @@
     back_two = swap_x(two_send)
     two_sum = add(chip[2][0], back_two)
     hop_two = swap_z(two_sum, 2)
-    back_again(3, near_sum)
+    part_own, part_other, dp_other, dp_own = parts[3]
+    act_other, keep, send = back(
+        slot_of[3], tie((part_other, dp_other), near_sum, chip[2]), weight_up, slots, 2
+    )
+    other_sum = add(keep[0], swap_core(send)[0])
+    far_send = tie(other_sum, two_sum)
+    back_far = swap_x(far_send)
+    act_own, keep, send = back(slot_of[3], tie((part_own, dp_own), other_sum), weight_up, slots)
+    far_sum = add(add(keep[0], swap_core(send)[0]), back_far)
+    hop_far = swap_z(far_sum, 3)
+    whole = parts[:3]
     down_grad = weight_grad(
         down_grad_kernel,
         hidden_units,
-        tie(rows_cot, chip[3]),
-        [p[0] for p in parts] + [p[1] for p in parts],
-        [pltpu.VMEM((NZ, parts[0][0].shape[0], hidden_units), BF16)],
-    )
-
-    far_send = tie(chip[3][1], two_sum)
-    back_far = swap_x(far_send)
-    far_sum = add(chip[3][0], back_far)
-    hop_far = swap_z(far_sum, 3)
-    up_grad = weight_grad(up_grad_kernel, hidden_units, rows_in, act, [])
+        tie(rows_cot, far_sum),
+        2,
+        [p[0] for p in whole] + [part_own, part_other] + [p[1] for p in whole] + [dp_own, dp_other],
+        [pltpu.VMEM((NZ * parts[0][0].shape[0], hidden_units), BF16)],
+    )
+    up_grad = weight_grad(up_grad_kernel, hidden_units, rows_in, 2, act[:3] + [act_own, act_other], [])
     own_sum = chip[0][0].astype(F32) + back_own.astype(F32)
     for hop in (hop_near, hop_two, hop_far):
         own_sum = own_sum + hop.astype(F32)

time: 198 us -> 196 us (0.990)
  waiting for transfers between devices: 103 us -> 95.2 us
  Pallas kernels: 47.4 us -> 51.3 us
  starting transfers between devices: 34 us -> 36.5 us
    ppermute x8, waiting for transfers between devices: 49.8 us -> 42.8 us  [swap_x(): lax.ppermute(value, 'expert', [(i, i ^ NC) for i in range(NZ * NX * NC)])]
    ppermute x4 -> x5, waiting for transfers between devices: 24.4 us -> 17.8 us  [swap_dp(): return lax.ppermute(value, 'dp', [(0, 1), (1, 0)])]
    ppermute x3, waiting for transfers between devices: 17.2 us -> 23.7 us  [swap_z(): lax.ppermute(value, 'expert', [(i, i ^ step) for i in range(NZ * NX * NC)])]
    pallas_call x6 -> x7, Pallas kernels: 24.7 us -> 28.6 us  [the longest x2 16 us: weight_grad(): pl.pallas_call(kernel, grid=(width // tile,), in_specs=in_specs, out_spec...]
    ppermute x4 -> x5, starting transfers between devices: 6.35 us -> 7.86 us  [swap_dp(): return lax.ppermute(value, 'dp', [(0, 1), (1, 0)])]
    ppermute x12 -> x13, waiting for transfers between devices: 4.61 us -> 3.92 us  [swap_core(): lax.ppermute(value, 'expert', [(i, i ^ 1) for i in range(NZ * NX * NC)])]
    unnamed x20 -> x24, local copies, waits for them, and re-layouts: 5.69 us -> 5.7 us
  transfers between devices with their start and end apart: 32 -> 34, of which waited for: 18 -> 18; matrix products, arithmetic and copies ran while one was open for 2% -> 2% of each run, Pallas kernels for 24% -> 26%
where the time goes in v7:
time: 196 us
  waiting for transfers between devices  95.2 us (49%)
  Pallas kernels  51.3 us (26%)
  starting transfers between devices  36.5 us (19%)
  other arithmetic  6.17 us (3%)
  local copies, waits for them, and re-layouts  5.79 us (3%)
    ppermute x8, waiting for transfers between devices, swap_x(): lax.ppermute(value, 'expert', [(i, i ^ NC) for i in range(NZ * NX * NC)])  42.8 us
    ppermute x3, waiting for transfers between devices, swap_z(): lax.ppermute(value, 'expert', [(i, i ^ step) for i in range(NZ * NX * NC)])  23.7 us
    pallas_call x4, Pallas kernels, front(): pl.pallas_call(functools.partial(front_kernel, top_count, slots), grid=(w...  22.7 us
    ppermute x5, waiting for transfers between devices, swap_dp(): return lax.ppermute(value, 'dp', [(0, 1), (1, 0)])  17.8 us
    pallas_call x2, Pallas kernels, weight_grad(): pl.pallas_call(kernel, grid=(width // tile,), in_specs=in_specs, out_spec...  16 us
    ppermute x5, starting transfers between devices, along_z(): return lax.ppermute(value, 'expert', perm)  15.5 us
    pallas_call x5, Pallas kernels, back(): pl.pallas_call(functools.partial(back_kernel, slots, first), grid=(width...  12.6 us
    ppermute x8, starting transfers between devices, swap_x(): lax.ppermute(value, 'expert', [(i, i ^ NC) for i in range(NZ * NX * NC)])  8.38 us
  transfers between devices with their start and end apart: 34, of which 18 were waited for; matrix products, arithmetic and copies ran while one was open for 2% of the time, Pallas kernels for 26%

profile of v7, /device:TPU:8, one launch (start us, length us, event | category | flops | bytes accessed | tf_op | source)
XLA Modules:
  0.0 196.0 jit_solution(8966841984320108325)
XLA Ops:
  5.5 4.6 %collective-permute-start.6 = (bf16[128,3712]{1,0:T(8,128)(2,1)S(1)}, bf16[128,3712]{1,0:T(8,128)(2,1)}, u32[]{:S(2)}, u32[]{:S(2)}) collective-permute-start(bf16[128,3712]{1,0:T(8,128)(2,1)S(1)} %pad_maximum_fusion.refs_0_.refs_4_.refs_8_), channel_id=1, source_target_pairs={{4,8},{5,9},{6,10},{7,11},{8,4},{9,5},{10,6},{11,7},{20,24},{21,25... | collective-permute-start | bytes 2850824 | tf_op jit(solution)/shard_map/ppermute | solution.py:32
  10.2 16.3 %collective-permute-done.1.refs_2_.refs_6_.refs_10_ = bf16[128,3712]{1,0:T(8,128)(2,1)} collective-permute-done((bf16[128,3712]{1,0:T(8,128)(2,1)S(1)}, bf16[128,3712]{1,0:T(8,128)(2,1)}, u32[]{:S(2)}, u32[]{:S(2)}) %collective-permute-start.1) | collective-permute-done | bytes 950304 | tf_op jit(solution)/shard_map/ppermute | solution.py:41
  27.6 3.1 %collective-permute-done.6 = bf16[128,3712]{1,0:T(8,128)(2,1)} collective-permute-done((bf16[128,3712]{1,0:T(8,128)(2,1)S(1)}, bf16[128,3712]{1,0:T(8,128)(2,1)}, u32[]{:S(2)}, u32[]{:S(2)}) %collective-permute-start.6) | collective-permute-done | bytes 950304 | tf_op jit(solution)/shard_map/ppermute | solution.py:32
  31.3 3.6 %collective-permute-start.7 = (bf16[128,3712]{1,0:T(8,128)(2,1)S(1)}, bf16[128,3712]{1,0:T(8,128)(2,1)}, u32[]{:S(2)}, u32[]{:S(2)}) collective-permute-start(bf16[128,3712]{1,0:T(8,128)(2,1)S(1)} %collective-permute-done.5.refs_0_.refs_4_.refs_8_), channel_id=1, source_target_pairs={{4,8},{5,9},{6,10},{7,11},{8,4},{9,5},{10,6},{11,7},{20,24},{21,25... | collective-permute-start | bytes 2850824 | tf_op jit(solution)/shard_map/ppermute | solution.py:32
  34.9 2.2 %collective-permute-start.8 = (bf16[128,3712]{1,0:T(8,128)(2,1)}, bf16[128,3712]{1,0:T(8,128)(2,1)}, u32[]{:S(2)}, u32[]{:S(2)}) collective-permute-start(bf16[128,3712]{1,0:T(8,128)(2,1)} %collective-permute-done.6), channel_id=1, source_target_pairs={{4,0},{5,1},{6,2},{7,3},{8,12},{9,13},{10,14},{11,15},{20,16},{21,... | collective-permute-start | bytes 2850824 | tf_op jit(solution)/shard_map/ppermute | solution.py:32
  37.2 2.0 %copy-done = bf16[1,1792,1024]{2,1,0:T(8,128)(2,1)S(1)} copy-done((bf16[1,1792,1024]{2,1,0:T(8,128)(2,1)S(1)}, bf16[1,1792,1024]{2,1,0:T(8,128)(2,1)}, u32[]{:S(2)}) %copy-start) | copy-done | bytes 3670040
  39.2 2.0 %copy-done.2 = bf16[1,1792,1024]{2,1,0:T(8,128)(2,1)S(1)} copy-done((bf16[1,1792,1024]{2,1,0:T(8,128)(2,1)S(1)}, bf16[1,1792,1024]{2,1,0:T(8,128)(2,1)}, u32[]{:S(2)}) %copy-start.2) | copy-done | bytes 3670040
  41.2 6.0 %shard_map.94 = (bf16[256,1792]{1,0:T(8,128)(2,1)S(1)}, bf16[256,1792]{1,0:T(8,128)(2,1)S(1)}, s32[4,8,128]{2,1,0:T(8,128)S(1)}, bf16[256,2048]{1,0:T(8,128)(2,1)S(1)}) custom-call(s32[1]{0:T(128)} %bitcast.own_ref, s32[16]{0:T(128)S(1)} %copy-done.10, bf16[128,3712]{1,0:T(8,128)(2,1)S(1)} %pad_maximum_fusion.refs_0_.refs_4_.refs_8_, ...), custom_call_target="tpu_custom_call" | custom-call | tf_op jit(solution)/shard_map/pallas_call | solution.py:146
  48.9 3.4 %collective-permute-done.9.refs_2_.refs_6_.refs_10_ = bf16[128,3712]{1,0:T(8,128)(2,1)S(1)} collective-permute-done((bf16[128,3712]{1,0:T(8,128)(2,1)S(1)}, bf16[128,3712]{1,0:T(8,128)(2,1)S(1)}, u32[]{:S(2)}, u32[]{:S(2)}) %collective-permute-start.9) | collective-permute-done | bytes 950304 | tf_op jit(solution)/shard_map/ppermute | solution.py:41
  52.3 2.2 %collective-permute-done.7 = bf16[128,3712]{1,0:T(8,128)(2,1)} collective-permute-done((bf16[128,3712]{1,0:T(8,128)(2,1)S(1)}, bf16[128,3712]{1,0:T(8,128)(2,1)}, u32[]{:S(2)}, u32[]{:S(2)}) %collective-permute-start.7) | collective-permute-done | bytes 950304 | tf_op jit(solution)/shard_map/ppermute | solution.py:32
  57.9 4.6 %collective-permute-start.10 = (bf16[128,3712]{1,0:T(8,128)(2,1)}, bf16[128,3712]{1,0:T(8,128)(2,1)S(1)}, u32[]{:S(2)}, u32[]{:S(2)}) collective-permute-start(bf16[128,3712]{1,0:T(8,128)(2,1)} %collective-permute-done.7), channel_id=1, source_target_pairs={{4,0},{5,1},{6,2},{7,3},{8,12},{9,13},{10,14},{11,15},{20,16},{21,... | collective-permute-start | bytes 2850824 | tf_op jit(solution)/shard_map/ppermute | solution.py:32
  62.6 5.6 %shard_map.96 = (bf16[256,1792]{1,0:T(8,128)(2,1)S(1)}, bf16[256,1792]{1,0:T(8,128)(2,1)S(1)}, s32[4,8,128]{2,1,0:T(8,128)S(1)}, bf16[256,2048]{1,0:T(8,128)(2,1)S(1)}) custom-call(s32[1]{0:T(128)} %bitcast.own_ref, s32[16]{0:T(128)S(1)} %copy-done.10, bf16[128,3712]{1,0:T(8,128)(2,1)S(1)} %collective-permute-done.5.refs_0_.refs_4_.refs_8_, ...), custom_call_target="tpu_custom_call" | custom-call | tf_op jit(solution)/shard_map/pallas_call | solution.py:146
  69.8 7.4 %collective-permute-done.11.refs_2_.refs_6_.refs_10_ = bf16[128,3712]{1,0:T(8,128)(2,1)S(1)} collective-permute-done((bf16[128,3712]{1,0:T(8,128)(2,1)S(1)}, bf16[128,3712]{1,0:T(8,128)(2,1)S(1)}, u32[]{:S(2)}, u32[]{:S(2)}) %collective-permute-start.11) | collective-permute-done | bytes 950304 | tf_op jit(solution)/shard_map/ppermute | solution.py:41
  77.2 2.7 %shard_map.95 = (bf16[256,1024]{1,0:T(8,128)(2,1)S(1)}, bf16[2,128,1792]{2,1,0:T(8,128)(2,1)S(1)}, bf16[2,128,1792]{2,1,0:T(8,128)(2,1)S(1)}) custom-call(s32[4,8,128]{2,1,0:T(8,128)S(1)} %get-tuple-element.60.slot_ref, bf16[256,2048]{1,0:T(8,128)(2,1)S(1)} %get-tuple-element.62.part_a.refs_5_, bf16[256,2048]{1,0:T(8,128)(2,1)S(1)} %collective-permute-done.3.part_b.refs_10_, ...), custom_call_target="tpu_custom_call" | custom-call | tf_op jit(solution)/shard_map/pallas_call | solution.py:201
  82.8 5.5 %shard_map.97 = (bf16[256,1792]{1,0:T(8,128)(2,1)S(1)}, bf16[256,1792]{1,0:T(8,128)(2,1)S(1)}, s32[4,8,128]{2,1,0:T(8,128)S(1)}, bf16[256,2048]{1,0:T(8,128)(2,1)S(1)}) custom-call(s32[1]{0:T(128)} %bitcast.own_ref, s32[16]{0:T(128)S(1)} %copy-done.10, bf16[128,3712]{1,0:T(8,128)(2,1)S(1)} %broadcast_select_fusion.1.refs_0_.refs_4_.refs_8_, ...), custom_call_target="tpu_custom_call" | custom-call | tf_op jit(solution)/shard_map/pallas_call | solution.py:146
  89.9 5.9 %collective-permute-done.17.part_b.refs_11_ = bf16[256,2048]{1,0:T(8,128)(2,1)S(1)} collective-permute-done((bf16[256,2048]{1,0:T(8,128)(2,1)S(1)}, bf16[256,2048]{1,0:T(8,128)(2,1)S(1)}, u32[]{:S(2)}, u32[]{:S(2)}) %collective-permute-start.17) | collective-permute-done | bytes 1048608 | tf_op jit(solution)/shard_map/ppermute | solution.py:49
  95.8 2.7 %shard_map.98 = (bf16[256,1024]{1,0:T(8,128)(2,1)S(1)}, bf16[2,128,1792]{2,1,0:T(8,128)(2,1)S(1)}, bf16[2,128,1792]{2,1,0:T(8,128)(2,1)S(1)}) custom-call(s32[4,8,128]{2,1,0:T(8,128)S(1)} %get-tuple-element.75.slot_ref, bf16[256,2048]{1,0:T(8,128)(2,1)S(1)} %get-tuple-element.76.part_a.refs_6_, ...), custom_call_target="tpu_custom_call" | custom-call | tf_op jit(solution)/shard_map/pallas_call | solution.py:201
  98.9 6.5 %collective-permute-done.14.refs_2_.refs_6_.refs_10_ = bf16[128,3712]{1,0:T(8,128)(2,1)S(1)} collective-permute-done((bf16[128,3712]{1,0:T(8,128)(2,1)S(1)}, bf16[128,3712]{1,0:T(8,128)(2,1)S(1)}, u32[]{:S(2)}, u32[]{:S(2)}) %collective-permute-start.14) | collective-permute-done | bytes 950304 | tf_op jit(solution)/shard_map/ppermute | solution.py:41
  106.5 2.2 %collective-permute-done.21.refs_3_.refs_7_.refs_11_ = bf16[128,3712]{1,0:T(8,128)(2,1)S(1)} collective-permute-done((bf16[128,3712]{1,0:T(8,128)(2,1)S(1)}, bf16[128,3712]{1,0:T(8,128)(2,1)S(1)}, u32[]{:S(2)}, u32[]{:S(2)}) %collective-permute-start.21) | collective-permute-done | bytes 950304 | tf_op jit(solution)/shard_map/ppermute | solution.py:45
  108.7 5.5 %shard_map.99 = (bf16[256,1792]{1,0:T(8,128)(2,1)S(1)}, bf16[256,1792]{1,0:T(8,128)(2,1)S(1)}, s32[4,8,128]{2,1,0:T(8,128)S(1)}, bf16[128,2048]{1,0:T(8,128)(2,1)S(1)}, bf16[128,2048]{1,0:T(8,128)(2,1)S(1)}) custom-call(s32[1]{0:T(128)} %bitcast.own_ref, s32[16]{0:T(128)S(1)} %copy-done.10, ...), custom_call_target="tpu_custom_call" | custom-call | tf_op jit(solution)/shard_map/pallas_call | solution.py:146
  114.2 3.2 %collective-permute-done.18 = bf16[128,1792]{1,0:T(8,128)(2,1)S(1)} collective-permute-done((bf16[128,1792]{1,0:T(8,128)(2,1)S(1)}, bf16[128,1792]{1,0:T(8,128)(2,1)S(1)}, u32[]{:S(2)}, u32[]{:S(2)}) %collective-permute-start.18) | collective-permute-done | bytes 458784 | tf_op jit(solution)/shard_map/ppermute | solution.py:41
  118.3 2.7 %shard_map.100 = (bf16[256,1024]{1,0:T(8,128)(2,1)S(1)}, bf16[2,128,1792]{2,1,0:T(8,128)(2,1)S(1)}, bf16[2,128,1792]{2,1,0:T(8,128)(2,1)S(1)}) custom-call(s32[4,8,128]{2,1,0:T(8,128)S(1)} %get-tuple-element.82.slot_ref, bf16[256,2048]{1,0:T(8,128)(2,1)S(1)} %get-tuple-element.83.part_a.refs_7_, ...), custom_call_target="tpu_custom_call" | custom-call | tf_op jit(solution)/shard_map/pallas_call | solution.py:201
  122.6 6.0 %collective-permute-done.22 = bf16[128,1792]{1,0:T(8,128)(2,1)S(1)} collective-permute-done((bf16[128,1792]{1,0:T(8,128)(2,1)S(1)}, bf16[128,1792]{1,0:T(8,128)(2,1)S(1)}, u32[]{:S(2)}, u32[]{:S(2)}) %collective-permute-start.22) | collective-permute-done | bytes 458784 | tf_op jit(solution)/shard_map/ppermute | solution.py:41
  129.9 5.5 %collective-permute-done.28.part_b.refs_14_ = bf16[128,2048]{1,0:T(8,128)(2,1)S(1)} collective-permute-done((bf16[128,2048]{1,0:T(8,128)(2,1)S(1)}, bf16[128,2048]{1,0:T(8,128)(2,1)S(1)}, u32[]{:S(2)}, u32[]{:S(2)}) %collective-permute-start.28) | collective-permute-done | bytes 524320 | tf_op jit(solution)/shard_map/ppermute | solution.py:49
  136.9 2.3 %shard_map.101 = (bf16[128,1024]{1,0:T(8,128)(2,1)S(1)}, bf16[1,128,1792]{2,1,0:T(8,128)(2,1)S(1)}, bf16[1,128,1792]{2,1,0:T(8,128)(2,1)S(1)}) custom-call(s32[4,8,128]{2,1,0:T(8,128)S(1)} %get-tuple-element.88.slot_ref, bf16[128,2048]{1,0:T(8,128)(2,1)S(1)} %get-tuple-element.91.part_a.refs_9_, ...), custom_call_target="tpu_custom_call" | custom-call | tf_op jit(solution)/shard_map/pallas_call | solution.py:201
  139.4 1.6 collective-permute-done.30
  142.4 6.4 %collective-permute-done.29.part_b.refs_13_ = bf16[128,2048]{1,0:T(8,128)(2,1)S(1)} collective-permute-done((bf16[128,2048]{1,0:T(8,128)(2,1)S(1)}, bf16[128,2048]{1,0:T(8,128)(2,1)S(1)}, u32[]{:S(2)}, u32[]{:S(2)}) %collective-permute-start.29) | collective-permute-done | bytes 524320 | tf_op jit(solution)/shard_map/ppermute | solution.py:49
  148.9 2.3 %shard_map.102 = (bf16[128,1024]{1,0:T(8,128)(2,1)S(1)}, bf16[1,128,1792]{2,1,0:T(8,128)(2,1)S(1)}, bf16[1,128,1792]{2,1,0:T(8,128)(2,1)S(1)}) custom-call(s32[4,8,128]{2,1,0:T(8,128)S(1)} %get-tuple-element.88.slot_ref, bf16[128,2048]{1,0:T(8,128)(2,1)S(1)} %get-tuple-element.95.part_a.refs_8_, ...), custom_call_target="tpu_custom_call" | custom-call | tf_op jit(solution)/shard_map/pallas_call | solution.py:201
  155.2 7.3 %shard_map.103 = bf16[1792,1024]{1,0:T(8,128)(2,1)} custom-call(bf16[256,1792]{1,0:T(8,128)(2,1)S(1)} %copy-done.5, bf16[256,1792]{1,0:T(8,128)(2,1)S(1)} %get-tuple-element.101.refs_1_, bf16[256,1792]{1,0:T(8,128)(2,1)S(1)} %get-tuple-element.102.refs_2_, bf16[256,1792]{1,0:T(8,128)(2,1)S(1)} %get-tuple-element.103.refs_3_.refs_4_, ...), custom_call_target="tpu_custom_call" | custom-call | tf_op jit(solution)/shard_map/pallas_call | solution.py:258
  162.5 8.7 %shard_map.104 = bf16[1792,1024]{1,0:T(8,128)(2,1)} custom-call(bf16[256,1792]{1,0:T(8,128)(2,1)S(1)} %copy-done.7, bf16[256,1792]{1,0:T(8,128)(2,1)S(1)} %copy-done.9, bf16[256,1792]{1,0:T(8,128)(2,1)S(1)} %get-tuple-element.115.refs_2_, bf16[256,1792]{1,0:T(8,128)(2,1)S(1)} %get-tuple-element.116.refs_3_.refs_4_, ...), custom_call_target="tpu_custom_call" | custom-call | tf_op jit(solution)/shard_map/pallas_call | solution.py:258
  172.2 12.3 %collective-permute-done.27 = bf16[128,1792]{1,0:T(8,128)(2,1)S(1)} collective-permute-done((bf16[128,1792]{1,0:T(8,128)(2,1)S(1)}, bf16[128,1792]{1,0:T(8,128)(2,1)S(1)}, u32[]{:S(2)}, u32[]{:S(2)}) %collective-permute-start.27) | collective-permute-done | bytes 458784 | tf_op jit(solution)/shard_map/ppermute | solution.py:37
  184.5 10.4 %collective-permute-done.33 = bf16[128,1792]{1,0:T(8,128)(2,1)S(1)} collective-permute-done((bf16[128,1792]{1,0:T(8,128)(2,1)S(1)}, bf16[128,1792]{1,0:T(8,128)(2,1)S(1)}, u32[]{:S(2)}, u32[]{:S(2)}) %collective-permute-start.33) | collective-permute-done | bytes 458784 | tf_op jit(solution)/shard_map/ppermute | solution.py:37
  (86 shorter events, 32.0 us)
Async XLA Ops:
  3.5 23.0 %collective-permute-start.1 = (bf16[128,3712]{1,0:T(8,128)(2,1)S(1)}, bf16[128,3712]{1,0:T(8,128)(2,1)}, u32[]{:S(2)}, u32[]{:S(2)}) collective-permute-start(bf16[128,3712]{1,0:T(8,128)(2,1)S(1)} %pad_maximum_fusion.refs_0_.refs_4_.refs_8_), channel_id=1, source_target_pairs={{0,2},{1,3},{2,0},{3,1},{4,6},{5,7},{6,4},{7,5},{8,10},{9,11},{10,... | collective-permute-start | bytes 2850824 | tf_op jit(solution)/shard_map/ppermute | solution.py:41
  5.1 22.5 %collective-permute-start.5 = (bf16[128,3712]{1,0:T(8,128)(2,1)S(1)}, bf16[128,3712]{1,0:T(8,128)(2,1)S(1)}, u32[]{:S(2)}, u32[]{:S(2)}) collective-permute-start(bf16[128,3712]{1,0:T(8,128)(2,1)S(1)} %pad_maximum_fusion.refs_0_.refs_4_.refs_8_), channel_id=1, source_target_pairs={{0,4},{1,5},{2,6},{3,7},{4,0},{5,1},{6,2},{7,3},{8,12},{9,13},{10,... | collective-permute-start | bytes 2850824 | tf_op jit(solution)/shard_map/ppermute | solution.py:32
  5.5 25.2 %collective-permute-start.6 = (bf16[128,3712]{1,0:T(8,128)(2,1)S(1)}, bf16[128,3712]{1,0:T(8,128)(2,1)}, u32[]{:S(2)}, u32[]{:S(2)}) collective-permute-start(bf16[128,3712]{1,0:T(8,128)(2,1)S(1)} %pad_maximum_fusion.refs_0_.refs_4_.refs_8_), channel_id=1, source_target_pairs={{4,8},{5,9},{6,10},{7,11},{8,4},{9,5},{10,6},{11,7},{20,24},{21,25... | collective-permute-start | bytes 2850824 | tf_op jit(solution)/shard_map/ppermute | solution.py:32
  10.2 27.0 %collective-permute-start = (bf16[128,3712]{1,0:T(8,128)(2,1)S(1)}, bf16[128,3712]{1,0:T(8,128)(2,1)}, u32[]{:S(2)}, u32[]{:S(2)}) collective-permute-start(bf16[128,3712]{1,0:T(8,128)(2,1)S(1)} %pad_maximum_fusion.refs_0_.refs_4_.refs_8_), channel_id=1, source_target_pairs={{0,1},{1,0},{2,3},{3,2},{4,5},{5,4},{6,7},{7,6},{8,9},{9,8},{10,11... | collective-permute-start | bytes 2850824 | tf_op jit(solution)/shard_map/ppermute | solution.py:45
  26.5 10.6 %collective-permute-start.2 = (bf16[128,3712]{1,0:T(8,128)(2,1)}, bf16[128,3712]{1,0:T(8,128)(2,1)}, u32[]{:S(2)}, u32[]{:S(2)}) collective-permute-start(bf16[128,3712]{1,0:T(8,128)(2,1)} %collective-permute-done.1.refs_2_.refs_6_.refs_10_), channel_id=1, source_target_pairs={{0,1},{1,0},{2,3},{3,2},{4,5},{5,4},{6,7},{7,6},{8,9},{9,8},{10,11... | collective-permute-start | bytes 2850824 | tf_op jit(solution)/shard_map/ppermute | solution.py:45
  30.7 21.6 %collective-permute-start.9 = (bf16[128,3712]{1,0:T(8,128)(2,1)S(1)}, bf16[128,3712]{1,0:T(8,128)(2,1)S(1)}, u32[]{:S(2)}, u32[]{:S(2)}) collective-permute-start(bf16[128,3712]{1,0:T(8,128)(2,1)S(1)} %collective-permute-done.5.refs_0_.refs_4_.refs_8_), channel_id=1, source_target_pairs={{0,2},{1,3},{2,0},{3,1},{4,6},{5,7},{6,4},{7,5},{8,10},{9,11},{10,... | collective-permute-start | bytes 2850824 | tf_op jit(solution)/shard_map/ppermute | solution.py:41
  31.3 23.3 %collective-permute-start.7 = (bf16[128,3712]{1,0:T(8,128)(2,1)S(1)}, bf16[128,3712]{1,0:T(8,128)(2,1)}, u32[]{:S(2)}, u32[]{:S(2)}) collective-permute-start(bf16[128,3712]{1,0:T(8,128)(2,1)S(1)} %collective-permute-done.5.refs_0_.refs_4_.refs_8_), channel_id=1, source_target_pairs={{4,8},{5,9},{6,10},{7,11},{8,4},{9,5},{10,6},{11,7},{20,24},{21,25... | collective-permute-start | bytes 2850824 | tf_op jit(solution)/shard_map/ppermute | solution.py:32
  34.9 20.1 %collective-permute-start.8 = (bf16[128,3712]{1,0:T(8,128)(2,1)}, bf16[128,3712]{1,0:T(8,128)(2,1)}, u32[]{:S(2)}, u32[]{:S(2)}) collective-permute-start(bf16[128,3712]{1,0:T(8,128)(2,1)} %collective-permute-done.6), channel_id=1, source_target_pairs={{4,0},{5,1},{6,2},{7,3},{8,12},{9,13},{10,14},{11,15},{20,16},{21,... | collective-permute-start | bytes 2850824 | tf_op jit(solution)/shard_map/ppermute | solution.py:32
  37.1 25.4 %collective-permute-start.12 = (bf16[128,3712]{1,0:T(8,128)(2,1)S(1)}, bf16[128,3712]{1,0:T(8,128)(2,1)S(1)}, u32[]{:S(2)}, u32[]{:S(2)}) collective-permute-start(bf16[128,3712]{1,0:T(8,128)(2,1)S(1)} %collective-permute-done.5.refs_0_.refs_4_.refs_8_), channel_id=1, source_target_pairs={{0,1},{1,0},{2,3},{3,2},{4,5},{5,4},{6,7},{7,6},{8,9},{9,8},{10,11... | collective-permute-start | bytes 2850824 | tf_op jit(solution)/shard_map/ppermute | solution.py:45
  47.3 29.9 %collective-permute-start.3 = (bf16[256,2048]{1,0:T(8,128)(2,1)S(1)}, bf16[256,2048]{1,0:T(8,128)(2,1)S(1)}, u32[]{:S(2)}, u32[]{:S(2)}) collective-permute-start(bf16[256,2048]{1,0:T(8,128)(2,1)S(1)} %get-tuple-element.62.part_a.refs_5_), channel_id=1, source_target_pairs={{0,16},{16,0},{1,17},{17,1},{2,18},{18,2},{3,19},{19,3},{4,20},{20... | collective-permute-start | bytes 3145736 | tf_op jit(solution)/shard_map/ppermute | solution.py:49
  52.3 10.2 %collective-permute-start.13 = (bf16[128,3712]{1,0:T(8,128)(2,1)S(1)}, bf16[128,3712]{1,0:T(8,128)(2,1)S(1)}, u32[]{:S(2)}, u32[]{:S(2)}) collective-permute-start(bf16[128,3712]{1,0:T(8,128)(2,1)S(1)} %collective-permute-done.9.refs_2_.refs_6_.refs_10_), channel_id=1, source_target_pairs={{0,1},{1,0},{2,3},{3,2},{4,5},{5,4},{6,7},{7,6},{8,9},{9,8},{10,11... | collective-permute-start | bytes 2850824 | tf_op jit(solution)/shard_map/ppermute | solution.py:45
  56.4 20.8 %collective-permute-start.11 = (bf16[128,3712]{1,0:T(8,128)(2,1)S(1)}, bf16[128,3712]{1,0:T(8,128)(2,1)S(1)}, u32[]{:S(2)}, u32[]{:S(2)}) collective-permute-start(bf16[128,3712]{1,0:T(8,128)(2,1)S(1)} %broadcast_select_fusion.1.refs_0_.refs_4_.refs_8_), channel_id=1, source_target_pairs={{0,2},{1,3},{2,0},{3,1},{4,6},{5,7},{6,4},{7,5},{8,10},{9,11},{10,... | collective-permute-start | bytes 2850824 | tf_op jit(solution)/shard_map/ppermute | solution.py:41
  57.9 22.6 %collective-permute-start.10 = (bf16[128,3712]{1,0:T(8,128)(2,1)}, bf16[128,3712]{1,0:T(8,128)(2,1)S(1)}, u32[]{:S(2)}, u32[]{:S(2)}) collective-permute-start(bf16[128,3712]{1,0:T(8,128)(2,1)} %collective-permute-done.7), channel_id=1, source_target_pairs={{4,0},{5,1},{6,2},{7,3},{8,12},{9,13},{10,14},{11,15},{20,16},{21,... | collective-permute-start | bytes 2850824 | tf_op jit(solution)/shard_map/ppermute | solution.py:32
  68.2 27.6 %collective-permute-start.17 = (bf16[256,2048]{1,0:T(8,128)(2,1)S(1)}, bf16[256,2048]{1,0:T(8,128)(2,1)S(1)}, u32[]{:S(2)}, u32[]{:S(2)}) collective-permute-start(bf16[256,2048]{1,0:T(8,128)(2,1)S(1)} %get-tuple-element.76.part_a.refs_6_), channel_id=1, source_target_pairs={{0,16},{16,0},{1,17},{17,1},{2,18},{18,2},{3,19},{19,3},{4,20},{20... | collective-permute-start | bytes 3145736 | tf_op jit(solution)/shard_map/ppermute | solution.py:49
  69.8 12.1 %collective-permute-start.15 = (bf16[128,3712]{1,0:T(8,128)(2,1)S(1)}, bf16[128,3712]{1,0:T(8,128)(2,1)S(1)}, u32[]{:S(2)}, u32[]{:S(2)}) collective-permute-start(bf16[128,3712]{1,0:T(8,128)(2,1)S(1)} %broadcast_select_fusion.1.refs_0_.refs_4_.refs_8_), channel_id=1, source_target_pairs={{0,1},{1,0},{2,3},{3,2},{4,5},{5,4},{6,7},{7,6},{8,9},{9,8},{10,11... | collective-permute-start | bytes 2850824 | tf_op jit(solution)/shard_map/ppermute | solution.py:45
  77.2 5.6 %collective-permute-start.16 = (bf16[128,3712]{1,0:T(8,128)(2,1)S(1)}, bf16[128,3712]{1,0:T(8,128)(2,1)S(1)}, u32[]{:S(2)}, u32[]{:S(2)}) collective-permute-start(bf16[128,3712]{1,0:T(8,128)(2,1)S(1)} %collective-permute-done.11.refs_2_.refs_6_.refs_10_), channel_id=1, source_target_pairs={{0,1},{1,0},{2,3},{3,2},{4,5},{5,4},{6,7},{7,6},{8,9},{9,8},{10,11... | collective-permute-start | bytes 2850824 | tf_op jit(solution)/shard_map/ppermute | solution.py:45
  79.9 18.6 %collective-permute-start.4 = (bf16[2,128,1792]{2,1,0:T(8,128)(2,1)S(1)}, bf16[2,128,1792]{2,1,0:T(8,128)(2,1)S(1)}, u32[]{:S(2)}, u32[]{:S(2)}) collective-permute-start(bf16[2,128,1792]{2,1,0:T(8,128)(2,1)S(1)} %get-tuple-element.65), channel_id=1, source_target_pairs={{0,1},{1,0},{2,3},{3,2},{4,5},{5,4},{6,7},{7,6},{8,9},{9,8},{10,11... | collective-permute-start | bytes 2752520 | tf_op jit(solution)/shard_map/ppermute | solution.py:45
  81.8 24.7 %collective-permute-start.20 = (bf16[128,3712]{1,0:T(8,128)(2,1)S(1)}, bf16[128,3712]{1,0:T(8,128)(2,1)S(1)}, u32[]{:S(2)}, u32[]{:S(2)}) collective-permute-start(bf16[128,3712]{1,0:T(8,128)(2,1)S(1)} %broadcast_select_fusion.refs_0_.refs_4_.refs_8_), channel_id=1, source_target_pairs={{0,1},{1,0},{2,3},{3,2},{4,5},{5,4},{6,7},{7,6},{8,9},{9,8},{10,11... | collective-permute-start | bytes 2850824 | tf_op jit(solution)/shard_map/ppermute | solution.py:45
  81.9 23.5 %collective-permute-start.14 = (bf16[128,3712]{1,0:T(8,128)(2,1)S(1)}, bf16[128,3712]{1,0:T(8,128)(2,1)S(1)}, u32[]{:S(2)}, u32[]{:S(2)}) collective-permute-start(bf16[128,3712]{1,0:T(8,128)(2,1)S(1)} %broadcast_select_fusion.refs_0_.refs_4_.refs_8_), channel_id=1, source_target_pairs={{0,2},{1,3},{2,0},{3,1},{4,6},{5,7},{6,4},{7,5},{8,10},{9,11},{10,... | collective-permute-start | bytes 2850824 | tf_op jit(solution)/shard_map/ppermute | solution.py:41
  88.3 29.9 %collective-permute-start.24 = (bf16[256,2048]{1,0:T(8,128)(2,1)S(1)}, bf16[256,2048]{1,0:T(8,128)(2,1)S(1)}, u32[]{:S(2)}, u32[]{:S(2)}) collective-permute-start(bf16[256,2048]{1,0:T(8,128)(2,1)S(1)} %get-tuple-element.83.part_a.refs_7_), channel_id=1, source_target_pairs={{0,16},{16,0},{1,17},{17,1},{2,18},{18,2},{3,19},{19,3},{4,20},{20... | collective-permute-start | bytes 3145736 | tf_op jit(solution)/shard_map/ppermute | solution.py:49
  98.5 7.7 %collective-permute-start.19 = (bf16[2,128,1792]{2,1,0:T(8,128)(2,1)S(1)}, bf16[2,128,1792]{2,1,0:T(8,128)(2,1)S(1)}, u32[]{:S(2)}, u32[]{:S(2)}) collective-permute-start(bf16[2,128,1792]{2,1,0:T(8,128)(2,1)S(1)} %get-tuple-element.79), channel_id=1, source_target_pairs={{0,1},{1,0},{2,3},{3,2},{4,5},{5,4},{6,7},{7,6},{8,9},{9,8},{10,11... | collective-permute-start | bytes 2752520 | tf_op jit(solution)/shard_map/ppermute | solution.py:45
  105.4 12.1 %collective-permute-start.18 = (bf16[128,1792]{1,0:T(8,128)(2,1)S(1)}, bf16[128,1792]{1,0:T(8,128)(2,1)S(1)}, u32[]{:S(2)}, u32[]{:S(2)}) collective-permute-start(bf16[128,1792]{1,0:T(8,128)(2,1)S(1)} %slice_bitcast_fusion.4), channel_id=1, source_target_pairs={{0,2},{1,3},{2,0},{3,1},{4,6},{5,7},{6,4},{7,5},{8,10},{9,11},{10,... | collective-permute-start | bytes 1376264 | tf_op jit(solution)/shard_map/ppermute | solution.py:41
  117.4 11.2 %collective-permute-start.22 = (bf16[128,1792]{1,0:T(8,128)(2,1)S(1)}, bf16[128,1792]{1,0:T(8,128)(2,1)S(1)}, u32[]{:S(2)}, u32[]{:S(2)}) collective-permute-start(bf16[128,1792]{1,0:T(8,128)(2,1)S(1)} %slice_bitcast_fusion.2), channel_id=1, source_target_pairs={{0,2},{1,3},{2,0},{3,1},{4,6},{5,7},{6,4},{7,5},{8,10},{9,11},{10,... | collective-permute-start | bytes 1376264 | tf_op jit(solution)/shard_map/ppermute | solution.py:41
  121.0 7.8 %collective-permute-start.25 = (bf16[2,128,1792]{2,1,0:T(8,128)(2,1)S(1)}, bf16[2,128,1792]{2,1,0:T(8,128)(2,1)S(1)}, u32[]{:S(2)}, u32[]{:S(2)}) collective-permute-start(bf16[2,128,1792]{2,1,0:T(8,128)(2,1)S(1)} %get-tuple-element.86), channel_id=1, source_target_pairs={{0,1},{1,0},{2,3},{3,2},{4,5},{5,4},{6,7},{7,6},{8,9},{9,8},{10,11... | collective-permute-start | bytes 2752520 | tf_op jit(solution)/shard_map/ppermute | solution.py:45
  121.0 14.3 %collective-permute-start.28 = (bf16[128,2048]{1,0:T(8,128)(2,1)S(1)}, bf16[128,2048]{1,0:T(8,128)(2,1)S(1)}, u32[]{:S(2)}, u32[]{:S(2)}) collective-permute-start(bf16[128,2048]{1,0:T(8,128)(2,1)S(1)} %get-tuple-element.91.part_a.refs_9_), channel_id=1, source_target_pairs={{0,16},{16,0},{1,17},{17,1},{2,18},{18,2},{3,19},{19,3},{4,20},{20... | collective-permute-start | bytes 1572872 | tf_op jit(solution)/shard_map/ppermute | solution.py:49
  129.0 10.3 %collective-permute-start.26 = (bf16[128,1792]{1,0:T(8,128)(2,1)S(1)}, bf16[128,1792]{1,0:T(8,128)(2,1)S(1)}, u32[]{:S(2)}, u32[]{:S(2)}) collective-permute-start(bf16[128,1792]{1,0:T(8,128)(2,1)S(1)} %slice_bitcast_fusion), channel_id=1, source_target_pairs={{0,2},{1,3},{2,0},{3,1},{4,6},{5,7},{6,4},{7,5},{8,10},{9,11},{10,... | collective-permute-start | bytes 1376264 | tf_op jit(solution)/shard_map/ppermute | solution.py:41
  135.4 13.5 %collective-permute-start.29 = (bf16[128,2048]{1,0:T(8,128)(2,1)S(1)}, bf16[128,2048]{1,0:T(8,128)(2,1)S(1)}, u32[]{:S(2)}, u32[]{:S(2)}) collective-permute-start(bf16[128,2048]{1,0:T(8,128)(2,1)S(1)} %get-tuple-element.95.part_a.refs_8_), channel_id=1, source_target_pairs={{0,16},{16,0},{1,17},{17,1},{2,18},{18,2},{3,19},{19,3},{4,20},{20... | collective-permute-start | bytes 1572872 | tf_op jit(solution)/shard_map/ppermute | solution.py:49
  141.2 12.7 %collective-permute-start.32 = (bf16[128,1792]{1,0:T(8,128)(2,1)S(1)}, bf16[128,1792]{1,0:T(8,128)(2,1)S(1)}, u32[]{:S(2)}, u32[]{:S(2)}) collective-permute-start(bf16[128,1792]{1,0:T(8,128)(2,1)S(1)} %fusion.7), channel_id=1, source_target_pairs={{0,2},{1,3},{2,0},{3,1},{4,6},{5,7},{6,4},{7,5},{8,10},{9,11},{10,... | collective-permute-start | bytes 1376264 | tf_op jit(solution)/shard_map/ppermute | solution.py:41
  151.2 2.8 %collective-permute-start.31 = (bf16[1,128,1792]{2,1,0:T(8,128)(2,1)S(1)}, bf16[1,128,1792]{2,1,0:T(8,128)(2,1)S(1)}, u32[]{:S(2)}, u32[]{:S(2)}) collective-permute-start(bf16[1,128,1792]{2,1,0:T(8,128)(2,1)S(1)} %get-tuple-element.98), channel_id=1, source_target_pairs={{0,1},{1,0},{2,3},{3,2},{4,5},{5,4},{6,7},{7,6},{8,9},{9,8},{10,11... | collective-permute-start | bytes 1376264 | tf_op jit(solution)/shard_map/ppermute | solution.py:45
  151.3 20.9 %collective-permute-start.23 = (bf16[128,1792]{1,0:T(8,128)(2,1)S(1)}, bf16[128,1792]{1,0:T(8,128)(2,1)S(1)}, u32[]{:S(2)}, u32[]{:S(2)}) collective-permute-start(bf16[128,1792]{1,0:T(8,128)(2,1)S(1)} %fusion.2), channel_id=1, source_target_pairs={{0,4},{1,5},{2,6},{3,7},{4,0},{5,1},{6,2},{7,3},{8,12},{9,13},{10,... | collective-permute-start | bytes 1376264 | tf_op jit(solution)/shard_map/ppermute | solution.py:37
  152.6 31.9 %collective-permute-start.27 = (bf16[128,1792]{1,0:T(8,128)(2,1)S(1)}, bf16[128,1792]{1,0:T(8,128)(2,1)S(1)}, u32[]{:S(2)}, u32[]{:S(2)}) collective-permute-start(bf16[128,1792]{1,0:T(8,128)(2,1)S(1)} %fusion.1), channel_id=1, source_target_pairs={{0,8},{1,9},{2,10},{3,11},{4,12},{5,13},{6,14},{7,15},{8,0},{9,1},... | collective-permute-start | bytes 1376264 | tf_op jit(solution)/shard_map/ppermute | solution.py:37
  154.1 40.8 %collective-permute-start.33 = (bf16[128,1792]{1,0:T(8,128)(2,1)S(1)}, bf16[128,1792]{1,0:T(8,128)(2,1)S(1)}, u32[]{:S(2)}, u32[]{:S(2)}) collective-permute-start(bf16[128,1792]{1,0:T(8,128)(2,1)S(1)} %fusion), channel_id=1, source_target_pairs={{0,12},{1,13},{2,14},{3,15},{4,8},{5,9},{6,10},{7,11},{8,4},{9,5},... | collective-permute-start | bytes 1376264 | tf_op jit(solution)/shard_map/ppermute | solution.py:37
  (13 other events, 126.0 us)

commit v8 on v7

--- a/solution.py
+++ b/solution.py
@@ -357,7 +357,7 @@
     far_send = tie(other_sum, two_sum)
     back_far = swap_x(far_send)
     act_own, keep, send = back(slot_of[3], tie((part_own, dp_own), other_sum), weight_up, slots)
-    far_sum = add(add(keep[0], swap_core(send)[0]), back_far)
+    far_sum = add(add(keep[0], swap_core(tie(send, hop_two))[0]), back_far)
     hop_far = swap_z(far_sum, 3)
     whole = parts[:3]
     down_grad = weight_grad(

time: 196 us -> 190 us (0.969)
  waiting for transfers between devices: 95.2 us -> 85.6 us
    ppermute x3, waiting for transfers between devices: 23.7 us -> 15.7 us  [swap_z(): lax.ppermute(value, 'expert', [(i, i ^ step) for i in range(NZ * NX * NC)])]
  transfers between devices with their start and end apart: 34 -> 34, of which waited for: 18 -> 16; matrix products, arithmetic and copies ran while one was open for 2% -> 2% of each run, Pallas kernels for 26% -> 27%
where the time goes in v8:
time: 190 us; the launch traced here: 188 us
  waiting for transfers between devices  85.6 us (45%)
  Pallas kernels  51.3 us (27%)
  starting transfers between devices  38.4 us (20%)
  other arithmetic  6.17 us (3%)
  local copies, waits for them, and re-layouts  5.79 us (3%)
    ppermute x8, waiting for transfers between devices, swap_x(): lax.ppermute(value, 'expert', [(i, i ^ NC) for i in range(NZ * NX * NC)])  42.8 us
    pallas_call x4, Pallas kernels, front(): pl.pallas_call(functools.partial(front_kernel, top_count, slots), grid=(w...  22.7 us
    ppermute x5, waiting for transfers between devices, swap_dp(): return lax.ppermute(value, 'dp', [(0, 1), (1, 0)])  17.8 us
    pallas_call x2, Pallas kernels, weight_grad(): pl.pallas_call(kernel, grid=(width // tile,), in_specs=in_specs, out_spec...  16 us
    ppermute x3, waiting for transfers between devices, swap_z(): lax.ppermute(value, 'expert', [(i, i ^ step) for i in range(NZ * NX * NC)])  15.7 us
    ppermute x5, starting transfers between devices, along_z(): return lax.ppermute(value, 'expert', perm)  15.5 us
    pallas_call x5, Pallas kernels, back(): pl.pallas_call(functools.partial(back_kernel, slots, first), grid=(width...  12.6 us
    ppermute x8, starting transfers between devices, swap_x(): lax.ppermute(value, 'expert', [(i, i ^ NC) for i in range(NZ * NX * NC)])  8.37 us
  transfers between devices with their start and end apart: 34, of which 16 were waited for; matrix products, arithmetic and copies ran while one was open for 2% of the time, Pallas kernels for 27%

profile of v8, /device:TPU:8, one launch (start us, length us, event | category | flops | bytes accessed | tf_op | source)
XLA Modules:
  0.0 188.2 jit_solution(3463419286409552280)
XLA Ops:
  5.5 4.6 %collective-permute-start.6 = (bf16[128,3712]{1,0:T(8,128)(2,1)S(1)}, bf16[128,3712]{1,0:T(8,128)(2,1)}, u32[]{:S(2)}, u32[]{:S(2)}) collective-permute-start(bf16[128,3712]{1,0:T(8,128)(2,1)S(1)} %pad_maximum_fusion.refs_0_.refs_4_.refs_8_), channel_id=1, source_target_pairs={{4,8},{5,9},{6,10},{7,11},{8,4},{9,5},{10,6},{11,7},{20,24},{21,25... | collective-permute-start | bytes 2850824 | tf_op jit(solution)/shard_map/ppermute | solution.py:32
  10.2 16.3 %collective-permute-done.1.refs_2_.refs_6_.refs_10_ = bf16[128,3712]{1,0:T(8,128)(2,1)} collective-permute-done((bf16[128,3712]{1,0:T(8,128)(2,1)S(1)}, bf16[128,3712]{1,0:T(8,128)(2,1)}, u32[]{:S(2)}, u32[]{:S(2)}) %collective-permute-start.1) | collective-permute-done | bytes 950304 | tf_op jit(solution)/shard_map/ppermute | solution.py:41
  27.6 3.1 %collective-permute-done.6 = bf16[128,3712]{1,0:T(8,128)(2,1)} collective-permute-done((bf16[128,3712]{1,0:T(8,128)(2,1)S(1)}, bf16[128,3712]{1,0:T(8,128)(2,1)}, u32[]{:S(2)}, u32[]{:S(2)}) %collective-permute-start.6) | collective-permute-done | bytes 950304 | tf_op jit(solution)/shard_map/ppermute | solution.py:32
  31.3 3.6 %collective-permute-start.7 = (bf16[128,3712]{1,0:T(8,128)(2,1)S(1)}, bf16[128,3712]{1,0:T(8,128)(2,1)}, u32[]{:S(2)}, u32[]{:S(2)}) collective-permute-start(bf16[128,3712]{1,0:T(8,128)(2,1)S(1)} %collective-permute-done.5.refs_0_.refs_4_.refs_8_), channel_id=1, source_target_pairs={{4,8},{5,9},{6,10},{7,11},{8,4},{9,5},{10,6},{11,7},{20,24},{21,25... | collective-permute-start | bytes 2850824 | tf_op jit(solution)/shard_map/ppermute | solution.py:32
  34.9 2.2 %collective-permute-start.8 = (bf16[128,3712]{1,0:T(8,128)(2,1)}, bf16[128,3712]{1,0:T(8,128)(2,1)}, u32[]{:S(2)}, u32[]{:S(2)}) collective-permute-start(bf16[128,3712]{1,0:T(8,128)(2,1)} %collective-permute-done.6), channel_id=1, source_target_pairs={{4,0},{5,1},{6,2},{7,3},{8,12},{9,13},{10,14},{11,15},{20,16},{21,... | collective-permute-start | bytes 2850824 | tf_op jit(solution)/shard_map/ppermute | solution.py:32
  37.2 2.0 %copy-done = bf16[1,1792,1024]{2,1,0:T(8,128)(2,1)S(1)} copy-done((bf16[1,1792,1024]{2,1,0:T(8,128)(2,1)S(1)}, bf16[1,1792,1024]{2,1,0:T(8,128)(2,1)}, u32[]{:S(2)}) %copy-start) | copy-done | bytes 3670040
  39.2 2.0 %copy-done.2 = bf16[1,1792,1024]{2,1,0:T(8,128)(2,1)S(1)} copy-done((bf16[1,1792,1024]{2,1,0:T(8,128)(2,1)S(1)}, bf16[1,1792,1024]{2,1,0:T(8,128)(2,1)}, u32[]{:S(2)}) %copy-start.2) | copy-done | bytes 3670040
  41.2 6.0 %shard_map.94 = (bf16[256,1792]{1,0:T(8,128)(2,1)S(1)}, bf16[256,1792]{1,0:T(8,128)(2,1)S(1)}, s32[4,8,128]{2,1,0:T(8,128)S(1)}, bf16[256,2048]{1,0:T(8,128)(2,1)S(1)}) custom-call(s32[1]{0:T(128)} %bitcast.own_ref, s32[16]{0:T(128)S(1)} %copy-done.10, bf16[128,3712]{1,0:T(8,128)(2,1)S(1)} %pad_maximum_fusion.refs_0_.refs_4_.refs_8_, ...), custom_call_target="tpu_custom_call" | custom-call | tf_op jit(solution)/shard_map/pallas_call | solution.py:146
  48.9 3.4 %collective-permute-done.9.refs_2_.refs_6_.refs_10_ = bf16[128,3712]{1,0:T(8,128)(2,1)S(1)} collective-permute-done((bf16[128,3712]{1,0:T(8,128)(2,1)S(1)}, bf16[128,3712]{1,0:T(8,128)(2,1)S(1)}, u32[]{:S(2)}, u32[]{:S(2)}) %collective-permute-start.9) | collective-permute-done | bytes 950304 | tf_op jit(solution)/shard_map/ppermute | solution.py:41
  52.3 2.2 %collective-permute-done.7 = bf16[128,3712]{1,0:T(8,128)(2,1)} collective-permute-done((bf16[128,3712]{1,0:T(8,128)(2,1)S(1)}, bf16[128,3712]{1,0:T(8,128)(2,1)}, u32[]{:S(2)}, u32[]{:S(2)}) %collective-permute-start.7) | collective-permute-done | bytes 950304 | tf_op jit(solution)/shard_map/ppermute | solution.py:32
  57.9 4.6 %collective-permute-start.10 = (bf16[128,3712]{1,0:T(8,128)(2,1)}, bf16[128,3712]{1,0:T(8,128)(2,1)S(1)}, u32[]{:S(2)}, u32[]{:S(2)}) collective-permute-start(bf16[128,3712]{1,0:T(8,128)(2,1)} %collective-permute-done.7), channel_id=1, source_target_pairs={{4,0},{5,1},{6,2},{7,3},{8,12},{9,13},{10,14},{11,15},{20,16},{21,... | collective-permute-start | bytes 2850824 | tf_op jit(solution)/shard_map/ppermute | solution.py:32
  62.6 5.6 %shard_map.96 = (bf16[256,1792]{1,0:T(8,128)(2,1)S(1)}, bf16[256,1792]{1,0:T(8,128)(2,1)S(1)}, s32[4,8,128]{2,1,0:T(8,128)S(1)}, bf16[256,2048]{1,0:T(8,128)(2,1)S(1)}) custom-call(s32[1]{0:T(128)} %bitcast.own_ref, s32[16]{0:T(128)S(1)} %copy-done.10, bf16[128,3712]{1,0:T(8,128)(2,1)S(1)} %collective-permute-done.5.refs_0_.refs_4_.refs_8_, ...), custom_call_target="tpu_custom_call" | custom-call | tf_op jit(solution)/shard_map/pallas_call | solution.py:146
  69.8 7.4 %collective-permute-done.11.refs_2_.refs_6_.refs_10_ = bf16[128,3712]{1,0:T(8,128)(2,1)S(1)} collective-permute-done((bf16[128,3712]{1,0:T(8,128)(2,1)S(1)}, bf16[128,3712]{1,0:T(8,128)(2,1)S(1)}, u32[]{:S(2)}, u32[]{:S(2)}) %collective-permute-start.11) | collective-permute-done | bytes 950304 | tf_op jit(solution)/shard_map/ppermute | solution.py:41
  77.2 2.7 %shard_map.95 = (bf16[256,1024]{1,0:T(8,128)(2,1)S(1)}, bf16[2,128,1792]{2,1,0:T(8,128)(2,1)S(1)}, bf16[2,128,1792]{2,1,0:T(8,128)(2,1)S(1)}) custom-call(s32[4,8,128]{2,1,0:T(8,128)S(1)} %get-tuple-element.61.slot_ref, bf16[256,2048]{1,0:T(8,128)(2,1)S(1)} %get-tuple-element.63.part_a.refs_5_, bf16[256,2048]{1,0:T(8,128)(2,1)S(1)} %collective-permute-done.3.part_b.refs_10_, ...), custom_call_target="tpu_custom_call" | custom-call | tf_op jit(solution)/shard_map/pallas_call | solution.py:201
  82.8 5.5 %shard_map.97 = (bf16[256,1792]{1,0:T(8,128)(2,1)S(1)}, bf16[256,1792]{1,0:T(8,128)(2,1)S(1)}, s32[4,8,128]{2,1,0:T(8,128)S(1)}, bf16[256,2048]{1,0:T(8,128)(2,1)S(1)}) custom-call(s32[1]{0:T(128)} %bitcast.own_ref, s32[16]{0:T(128)S(1)} %copy-done.10, bf16[128,3712]{1,0:T(8,128)(2,1)S(1)} %broadcast_select_fusion.1.refs_0_.refs_4_.refs_8_, ...), custom_call_target="tpu_custom_call" | custom-call | tf_op jit(solution)/shard_map/pallas_call | solution.py:146
  89.9 5.9 %collective-permute-done.17.part_b.refs_11_ = bf16[256,2048]{1,0:T(8,128)(2,1)S(1)} collective-permute-done((bf16[256,2048]{1,0:T(8,128)(2,1)S(1)}, bf16[256,2048]{1,0:T(8,128)(2,1)S(1)}, u32[]{:S(2)}, u32[]{:S(2)}) %collective-permute-start.17) | collective-permute-done | bytes 1048608 | tf_op jit(solution)/shard_map/ppermute | solution.py:49
  95.8 2.7 %shard_map.98 = (bf16[256,1024]{1,0:T(8,128)(2,1)S(1)}, bf16[2,128,1792]{2,1,0:T(8,128)(2,1)S(1)}, bf16[2,128,1792]{2,1,0:T(8,128)(2,1)S(1)}) custom-call(s32[4,8,128]{2,1,0:T(8,128)S(1)} %get-tuple-element.76.slot_ref, bf16[256,2048]{1,0:T(8,128)(2,1)S(1)} %get-tuple-element.77.part_a.refs_6_, ...), custom_call_target="tpu_custom_call" | custom-call | tf_op jit(solution)/shard_map/pallas_call | solution.py:201
  98.9 6.5 %collective-permute-done.14.refs_2_.refs_6_.refs_10_ = bf16[128,3712]{1,0:T(8,128)(2,1)S(1)} collective-permute-done((bf16[128,3712]{1,0:T(8,128)(2,1)S(1)}, bf16[128,3712]{1,0:T(8,128)(2,1)S(1)}, u32[]{:S(2)}, u32[]{:S(2)}) %collective-permute-start.14) | collective-permute-done | bytes 950304 | tf_op jit(solution)/shard_map/ppermute | solution.py:41
  106.5 2.2 %collective-permute-done.21.refs_3_.refs_7_.refs_11_ = bf16[128,3712]{1,0:T(8,128)(2,1)S(1)} collective-permute-done((bf16[128,3712]{1,0:T(8,128)(2,1)S(1)}, bf16[128,3712]{1,0:T(8,128)(2,1)S(1)}, u32[]{:S(2)}, u32[]{:S(2)}) %collective-permute-start.21) | collective-permute-done | bytes 950304 | tf_op jit(solution)/shard_map/ppermute | solution.py:45
  108.7 5.5 %shard_map.99 = (bf16[256,1792]{1,0:T(8,128)(2,1)S(1)}, bf16[256,1792]{1,0:T(8,128)(2,1)S(1)}, s32[4,8,128]{2,1,0:T(8,128)S(1)}, bf16[128,2048]{1,0:T(8,128)(2,1)S(1)}, bf16[128,2048]{1,0:T(8,128)(2,1)S(1)}) custom-call(s32[1]{0:T(128)} %bitcast.own_ref, s32[16]{0:T(128)S(1)} %copy-done.10, ...), custom_call_target="tpu_custom_call" | custom-call | tf_op jit(solution)/shard_map/pallas_call | solution.py:146
  114.2 3.2 %collective-permute-done.18 = bf16[128,1792]{1,0:T(8,128)(2,1)S(1)} collective-permute-done((bf16[128,1792]{1,0:T(8,128)(2,1)S(1)}, bf16[128,1792]{1,0:T(8,128)(2,1)S(1)}, u32[]{:S(2)}, u32[]{:S(2)}) %collective-permute-start.18) | collective-permute-done | bytes 458784 | tf_op jit(solution)/shard_map/ppermute | solution.py:41
  118.3 2.7 %shard_map.100 = (bf16[256,1024]{1,0:T(8,128)(2,1)S(1)}, bf16[2,128,1792]{2,1,0:T(8,128)(2,1)S(1)}, bf16[2,128,1792]{2,1,0:T(8,128)(2,1)S(1)}) custom-call(s32[4,8,128]{2,1,0:T(8,128)S(1)} %get-tuple-element.83.slot_ref, bf16[256,2048]{1,0:T(8,128)(2,1)S(1)} %get-tuple-element.84.part_a.refs_7_, ...), custom_call_target="tpu_custom_call" | custom-call | tf_op jit(solution)/shard_map/pallas_call | solution.py:201
  122.6 6.0 %collective-permute-done.22 = bf16[128,1792]{1,0:T(8,128)(2,1)S(1)} collective-permute-done((bf16[128,1792]{1,0:T(8,128)(2,1)S(1)}, bf16[128,1792]{1,0:T(8,128)(2,1)S(1)}, u32[]{:S(2)}, u32[]{:S(2)}) %collective-permute-start.22) | collective-permute-done | bytes 458784 | tf_op jit(solution)/shard_map/ppermute | solution.py:41
  129.9 5.5 %collective-permute-done.28.part_b.refs_14_ = bf16[128,2048]{1,0:T(8,128)(2,1)S(1)} collective-permute-done((bf16[128,2048]{1,0:T(8,128)(2,1)S(1)}, bf16[128,2048]{1,0:T(8,128)(2,1)S(1)}, u32[]{:S(2)}, u32[]{:S(2)}) %collective-permute-start.28) | collective-permute-done | bytes 524320 | tf_op jit(solution)/shard_map/ppermute | solution.py:49
  136.9 2.3 %shard_map.101 = (bf16[128,1024]{1,0:T(8,128)(2,1)S(1)}, bf16[1,128,1792]{2,1,0:T(8,128)(2,1)S(1)}, bf16[1,128,1792]{2,1,0:T(8,128)(2,1)S(1)}) custom-call(s32[4,8,128]{2,1,0:T(8,128)S(1)} %get-tuple-element.89.slot_ref, bf16[128,2048]{1,0:T(8,128)(2,1)S(1)} %get-tuple-element.92.part_a.refs_9_, ...), custom_call_target="tpu_custom_call" | custom-call | tf_op jit(solution)/shard_map/pallas_call | solution.py:201
  142.4 6.4 %collective-permute-done.29.part_b.refs_13_ = bf16[128,2048]{1,0:T(8,128)(2,1)S(1)} collective-permute-done((bf16[128,2048]{1,0:T(8,128)(2,1)S(1)}, bf16[128,2048]{1,0:T(8,128)(2,1)S(1)}, u32[]{:S(2)}, u32[]{:S(2)}) %collective-permute-start.29) | collective-permute-done | bytes 524320 | tf_op jit(solution)/shard_map/ppermute | solution.py:49
  148.9 2.3 %shard_map.102 = (bf16[128,1024]{1,0:T(8,128)(2,1)S(1)}, bf16[1,128,1792]{2,1,0:T(8,128)(2,1)S(1)}, bf16[1,128,1792]{2,1,0:T(8,128)(2,1)S(1)}) custom-call(s32[4,8,128]{2,1,0:T(8,128)S(1)} %get-tuple-element.89.slot_ref, bf16[128,2048]{1,0:T(8,128)(2,1)S(1)} %get-tuple-element.96.part_a.refs_8_, ...), custom_call_target="tpu_custom_call" | custom-call | tf_op jit(solution)/shard_map/pallas_call | solution.py:201
  151.2 10.2 %collective-permute-done.27 = bf16[128,1792]{1,0:T(8,128)(2,1)S(1)} collective-permute-done((bf16[128,1792]{1,0:T(8,128)(2,1)S(1)}, bf16[128,1792]{1,0:T(8,128)(2,1)S(1)}, u32[]{:S(2)}, u32[]{:S(2)}) %collective-permute-start.27) | collective-permute-done | bytes 458784 | tf_op jit(solution)/shard_map/ppermute | solution.py:37
  161.3 3.1 %collective-permute-start.23 = (bf16[128,1792]{1,0:T(8,128)(2,1)S(1)}, bf16[128,1792]{1,0:T(8,128)(2,1)S(1)}, u32[]{:S(2)}, u32[]{:S(2)}) collective-permute-start(bf16[128,1792]{1,0:T(8,128)(2,1)S(1)} %fusion.2), channel_id=1, source_target_pairs={{0,4},{1,5},{2,6},{3,7},{4,0},{5,1},{6,2},{7,3},{8,12},{9,13},{10,... | collective-permute-start | bytes 1376264 | tf_op jit(solution)/shard_map/ppermute | solution.py:37
  165.5 7.3 %shard_map.103 = bf16[1792,1024]{1,0:T(8,128)(2,1)} custom-call(bf16[256,1792]{1,0:T(8,128)(2,1)S(1)} %copy-done.5, bf16[256,1792]{1,0:T(8,128)(2,1)S(1)} %get-tuple-element.103.refs_1_, bf16[256,1792]{1,0:T(8,128)(2,1)S(1)} %get-tuple-element.104.refs_2_, bf16[256,1792]{1,0:T(8,128)(2,1)S(1)} %get-tuple-element.105.refs_3_.refs_4_, ...), custom_call_target="tpu_custom_call" | custom-call | tf_op jit(solution)/shard_map/pallas_call | solution.py:258
  172.8 8.7 %shard_map.104 = bf16[1792,1024]{1,0:T(8,128)(2,1)} custom-call(bf16[256,1792]{1,0:T(8,128)(2,1)S(1)} %copy-done.7, bf16[256,1792]{1,0:T(8,128)(2,1)S(1)} %copy-done.9, bf16[256,1792]{1,0:T(8,128)(2,1)S(1)} %get-tuple-element.117.refs_2_, bf16[256,1792]{1,0:T(8,128)(2,1)S(1)} %get-tuple-element.118.refs_3_.refs_4_, ...), custom_call_target="tpu_custom_call" | custom-call | tf_op jit(solution)/shard_map/pallas_call | solution.py:258
  181.5 5.6 %collective-permute-done.33 = bf16[128,1792]{1,0:T(8,128)(2,1)S(1)} collective-permute-done((bf16[128,1792]{1,0:T(8,128)(2,1)S(1)}, bf16[128,1792]{1,0:T(8,128)(2,1)S(1)}, u32[]{:S(2)}, u32[]{:S(2)}) %collective-permute-start.33) | collective-permute-done | bytes 458784 | tf_op jit(solution)/shard_map/ppermute | solution.py:37
  (86 shorter events, 29.8 us)
Async XLA Ops:
  3.5 23.0 %collective-permute-start.1 = (bf16[128,3712]{1,0:T(8,128)(2,1)S(1)}, bf16[128,3712]{1,0:T(8,128)(2,1)}, u32[]{:S(2)}, u32[]{:S(2)}) collective-permute-start(bf16[128,3712]{1,0:T(8,128)(2,1)S(1)} %pad_maximum_fusion.refs_0_.refs_4_.refs_8_), channel_id=1, source_target_pairs={{0,2},{1,3},{2,0},{3,1},{4,6},{5,7},{6,4},{7,5},{8,10},{9,11},{10,... | collective-permute-start | bytes 2850824 | tf_op jit(solution)/shard_map/ppermute | solution.py:41
  5.1 22.5 %collective-permute-start.5 = (bf16[128,3712]{1,0:T(8,128)(2,1)S(1)}, bf16[128,3712]{1,0:T(8,128)(2,1)S(1)}, u32[]{:S(2)}, u32[]{:S(2)}) collective-permute-start(bf16[128,3712]{1,0:T(8,128)(2,1)S(1)} %pad_maximum_fusion.refs_0_.refs_4_.refs_8_), channel_id=1, source_target_pairs={{0,4},{1,5},{2,6},{3,7},{4,0},{5,1},{6,2},{7,3},{8,12},{9,13},{10,... | collective-permute-start | bytes 2850824 | tf_op jit(solution)/shard_map/ppermute | solution.py:32
  5.5 25.2 %collective-permute-start.6 = (bf16[128,3712]{1,0:T(8,128)(2,1)S(1)}, bf16[128,3712]{1,0:T(8,128)(2,1)}, u32[]{:S(2)}, u32[]{:S(2)}) collective-permute-start(bf16[128,3712]{1,0:T(8,128)(2,1)S(1)} %pad_maximum_fusion.refs_0_.refs_4_.refs_8_), channel_id=1, source_target_pairs={{4,8},{5,9},{6,10},{7,11},{8,4},{9,5},{10,6},{11,7},{20,24},{21,25... | collective-permute-start | bytes 2850824 | tf_op jit(solution)/shard_map/ppermute | solution.py:32
  10.2 27.0 %collective-permute-start = (bf16[128,3712]{1,0:T(8,128)(2,1)S(1)}, bf16[128,3712]{1,0:T(8,128)(2,1)}, u32[]{:S(2)}, u32[]{:S(2)}) collective-permute-start(bf16[128,3712]{1,0:T(8,128)(2,1)S(1)} %pad_maximum_fusion.refs_0_.refs_4_.refs_8_), channel_id=1, source_target_pairs={{0,1},{1,0},{2,3},{3,2},{4,5},{5,4},{6,7},{7,6},{8,9},{9,8},{10,11... | collective-permute-start | bytes 2850824 | tf_op jit(solution)/shard_map/ppermute | solution.py:45
  26.5 10.6 %collective-permute-start.2 = (bf16[128,3712]{1,0:T(8,128)(2,1)}, bf16[128,3712]{1,0:T(8,128)(2,1)}, u32[]{:S(2)}, u32[]{:S(2)}) collective-permute-start(bf16[128,3712]{1,0:T(8,128)(2,1)} %collective-permute-done.1.refs_2_.refs_6_.refs_10_), channel_id=1, source_target_pairs={{0,1},{1,0},{2,3},{3,2},{4,5},{5,4},{6,7},{7,6},{8,9},{9,8},{10,11... | collective-permute-start | bytes 2850824 | tf_op jit(solution)/shard_map/ppermute | solution.py:45
  30.7 21.6 %collective-permute-start.9 = (bf16[128,3712]{1,0:T(8,128)(2,1)S(1)}, bf16[128,3712]{1,0:T(8,128)(2,1)S(1)}, u32[]{:S(2)}, u32[]{:S(2)}) collective-permute-start(bf16[128,3712]{1,0:T(8,128)(2,1)S(1)} %collective-permute-done.5.refs_0_.refs_4_.refs_8_), channel_id=1, source_target_pairs={{0,2},{1,3},{2,0},{3,1},{4,6},{5,7},{6,4},{7,5},{8,10},{9,11},{10,... | collective-permute-start | bytes 2850824 | tf_op jit(solution)/shard_map/ppermute | solution.py:41
  31.3 23.3 %collective-permute-start.7 = (bf16[128,3712]{1,0:T(8,128)(2,1)S(1)}, bf16[128,3712]{1,0:T(8,128)(2,1)}, u32[]{:S(2)}, u32[]{:S(2)}) collective-permute-start(bf16[128,3712]{1,0:T(8,128)(2,1)S(1)} %collective-permute-done.5.refs_0_.refs_4_.refs_8_), channel_id=1, source_target_pairs={{4,8},{5,9},{6,10},{7,11},{8,4},{9,5},{10,6},{11,7},{20,24},{21,25... | collective-permute-start | bytes 2850824 | tf_op jit(solution)/shard_map/ppermute | solution.py:32
  34.9 20.1 %collective-permute-start.8 = (bf16[128,3712]{1,0:T(8,128)(2,1)}, bf16[128,3712]{1,0:T(8,128)(2,1)}, u32[]{:S(2)}, u32[]{:S(2)}) collective-permute-start(bf16[128,3712]{1,0:T(8,128)(2,1)} %collective-permute-done.6), channel_id=1, source_target_pairs={{4,0},{5,1},{6,2},{7,3},{8,12},{9,13},{10,14},{11,15},{20,16},{21,... | collective-permute-start | bytes 2850824 | tf_op jit(solution)/shard_map/ppermute | solution.py:32
  37.1 25.4 %collective-permute-start.12 = (bf16[128,3712]{1,0:T(8,128)(2,1)S(1)}, bf16[128,3712]{1,0:T(8,128)(2,1)S(1)}, u32[]{:S(2)}, u32[]{:S(2)}) collective-permute-start(bf16[128,3712]{1,0:T(8,128)(2,1)S(1)} %collective-permute-done.5.refs_0_.refs_4_.refs_8_), channel_id=1, source_target_pairs={{0,1},{1,0},{2,3},{3,2},{4,5},{5,4},{6,7},{7,6},{8,9},{9,8},{10,11... | collective-permute-start | bytes 2850824 | tf_op jit(solution)/shard_map/ppermute | solution.py:45
  47.3 29.9 %collective-permute-start.3 = (bf16[256,2048]{1,0:T(8,128)(2,1)S(1)}, bf16[256,2048]{1,0:T(8,128)(2,1)S(1)}, u32[]{:S(2)}, u32[]{:S(2)}) collective-permute-start(bf16[256,2048]{1,0:T(8,128)(2,1)S(1)} %get-tuple-element.63.part_a.refs_5_), channel_id=1, source_target_pairs={{0,16},{16,0},{1,17},{17,1},{2,18},{18,2},{3,19},{19,3},{4,20},{20... | collective-permute-start | bytes 3145736 | tf_op jit(solution)/shard_map/ppermute | solution.py:49
  52.3 10.2 %collective-permute-start.13 = (bf16[128,3712]{1,0:T(8,128)(2,1)S(1)}, bf16[128,3712]{1,0:T(8,128)(2,1)S(1)}, u32[]{:S(2)}, u32[]{:S(2)}) collective-permute-start(bf16[128,3712]{1,0:T(8,128)(2,1)S(1)} %collective-permute-done.9.refs_2_.refs_6_.refs_10_), channel_id=1, source_target_pairs={{0,1},{1,0},{2,3},{3,2},{4,5},{5,4},{6,7},{7,6},{8,9},{9,8},{10,11... | collective-permute-start | bytes 2850824 | tf_op jit(solution)/shard_map/ppermute | solution.py:45
  56.4 20.8 %collective-permute-start.11 = (bf16[128,3712]{1,0:T(8,128)(2,1)S(1)}, bf16[128,3712]{1,0:T(8,128)(2,1)S(1)}, u32[]{:S(2)}, u32[]{:S(2)}) collective-permute-start(bf16[128,3712]{1,0:T(8,128)(2,1)S(1)} %broadcast_select_fusion.1.refs_0_.refs_4_.refs_8_), channel_id=1, source_target_pairs={{0,2},{1,3},{2,0},{3,1},{4,6},{5,7},{6,4},{7,5},{8,10},{9,11},{10,... | collective-permute-start | bytes 2850824 | tf_op jit(solution)/shard_map/ppermute | solution.py:41
  57.9 22.6 %collective-permute-start.10 = (bf16[128,3712]{1,0:T(8,128)(2,1)}, bf16[128,3712]{1,0:T(8,128)(2,1)S(1)}, u32[]{:S(2)}, u32[]{:S(2)}) collective-permute-start(bf16[128,3712]{1,0:T(8,128)(2,1)} %collective-permute-done.7), channel_id=1, source_target_pairs={{4,0},{5,1},{6,2},{7,3},{8,12},{9,13},{10,14},{11,15},{20,16},{21,... | collective-permute-start | bytes 2850824 | tf_op jit(solution)/shard_map/ppermute | solution.py:32
  68.2 27.6 %collective-permute-start.17 = (bf16[256,2048]{1,0:T(8,128)(2,1)S(1)}, bf16[256,2048]{1,0:T(8,128)(2,1)S(1)}, u32[]{:S(2)}, u32[]{:S(2)}) collective-permute-start(bf16[256,2048]{1,0:T(8,128)(2,1)S(1)} %get-tuple-element.77.part_a.refs_6_), channel_id=1, source_target_pairs={{0,16},{16,0},{1,17},{17,1},{2,18},{18,2},{3,19},{19,3},{4,20},{20... | collective-permute-start | bytes 3145736 | tf_op jit(solution)/shard_map/ppermute | solution.py:49
  69.8 12.1 %collective-permute-start.15 = (bf16[128,3712]{1,0:T(8,128)(2,1)S(1)}, bf16[128,3712]{1,0:T(8,128)(2,1)S(1)}, u32[]{:S(2)}, u32[]{:S(2)}) collective-permute-start(bf16[128,3712]{1,0:T(8,128)(2,1)S(1)} %broadcast_select_fusion.1.refs_0_.refs_4_.refs_8_), channel_id=1, source_target_pairs={{0,1},{1,0},{2,3},{3,2},{4,5},{5,4},{6,7},{7,6},{8,9},{9,8},{10,11... | collective-permute-start | bytes 2850824 | tf_op jit(solution)/shard_map/ppermute | solution.py:45
  77.2 5.6 %collective-permute-start.16 = (bf16[128,3712]{1,0:T(8,128)(2,1)S(1)}, bf16[128,3712]{1,0:T(8,128)(2,1)S(1)}, u32[]{:S(2)}, u32[]{:S(2)}) collective-permute-start(bf16[128,3712]{1,0:T(8,128)(2,1)S(1)} %collective-permute-done.11.refs_2_.refs_6_.refs_10_), channel_id=1, source_target_pairs={{0,1},{1,0},{2,3},{3,2},{4,5},{5,4},{6,7},{7,6},{8,9},{9,8},{10,11... | collective-permute-start | bytes 2850824 | tf_op jit(solution)/shard_map/ppermute | solution.py:45
  79.9 18.6 %collective-permute-start.4 = (bf16[2,128,1792]{2,1,0:T(8,128)(2,1)S(1)}, bf16[2,128,1792]{2,1,0:T(8,128)(2,1)S(1)}, u32[]{:S(2)}, u32[]{:S(2)}) collective-permute-start(bf16[2,128,1792]{2,1,0:T(8,128)(2,1)S(1)} %get-tuple-element.66), channel_id=1, source_target_pairs={{0,1},{1,0},{2,3},{3,2},{4,5},{5,4},{6,7},{7,6},{8,9},{9,8},{10,11... | collective-permute-start | bytes 2752520 | tf_op jit(solution)/shard_map/ppermute | solution.py:45
  81.8 24.7 %collective-permute-start.20 = (bf16[128,3712]{1,0:T(8,128)(2,1)S(1)}, bf16[128,3712]{1,0:T(8,128)(2,1)S(1)}, u32[]{:S(2)}, u32[]{:S(2)}) collective-permute-start(bf16[128,3712]{1,0:T(8,128)(2,1)S(1)} %broadcast_select_fusion.refs_0_.refs_4_.refs_8_), channel_id=1, source_target_pairs={{0,1},{1,0},{2,3},{3,2},{4,5},{5,4},{6,7},{7,6},{8,9},{9,8},{10,11... | collective-permute-start | bytes 2850824 | tf_op jit(solution)/shard_map/ppermute | solution.py:45
  81.9 23.5 %collective-permute-start.14 = (bf16[128,3712]{1,0:T(8,128)(2,1)S(1)}, bf16[128,3712]{1,0:T(8,128)(2,1)S(1)}, u32[]{:S(2)}, u32[]{:S(2)}) collective-permute-start(bf16[128,3712]{1,0:T(8,128)(2,1)S(1)} %broadcast_select_fusion.refs_0_.refs_4_.refs_8_), channel_id=1, source_target_pairs={{0,2},{1,3},{2,0},{3,1},{4,6},{5,7},{6,4},{7,5},{8,10},{9,11},{10,... | collective-permute-start | bytes 2850824 | tf_op jit(solution)/shard_map/ppermute | solution.py:41
  88.3 29.9 %collective-permute-start.24 = (bf16[256,2048]{1,0:T(8,128)(2,1)S(1)}, bf16[256,2048]{1,0:T(8,128)(2,1)S(1)}, u32[]{:S(2)}, u32[]{:S(2)}) collective-permute-start(bf16[256,2048]{1,0:T(8,128)(2,1)S(1)} %get-tuple-element.84.part_a.refs_7_), channel_id=1, source_target_pairs={{0,16},{16,0},{1,17},{17,1},{2,18},{18,2},{3,19},{19,3},{4,20},{20... | collective-permute-start | bytes 3145736 | tf_op jit(solution)/shard_map/ppermute | solution.py:49
  98.5 7.7 %collective-permute-start.19 = (bf16[2,128,1792]{2,1,0:T(8,128)(2,1)S(1)}, bf16[2,128,1792]{2,1,0:T(8,128)(2,1)S(1)}, u32[]{:S(2)}, u32[]{:S(2)}) collective-permute-start(bf16[2,128,1792]{2,1,0:T(8,128)(2,1)S(1)} %get-tuple-element.80), channel_id=1, source_target_pairs={{0,1},{1,0},{2,3},{3,2},{4,5},{5,4},{6,7},{7,6},{8,9},{9,8},{10,11... | collective-permute-start | bytes 2752520 | tf_op jit(solution)/shard_map/ppermute | solution.py:45
  105.4 12.1 %collective-permute-start.18 = (bf16[128,1792]{1,0:T(8,128)(2,1)S(1)}, bf16[128,1792]{1,0:T(8,128)(2,1)S(1)}, u32[]{:S(2)}, u32[]{:S(2)}) collective-permute-start(bf16[128,1792]{1,0:T(8,128)(2,1)S(1)} %slice_bitcast_fusion.4), channel_id=1, source_target_pairs={{0,2},{1,3},{2,0},{3,1},{4,6},{5,7},{6,4},{7,5},{8,10},{9,11},{10,... | collective-permute-start | bytes 1376264 | tf_op jit(solution)/shard_map/ppermute | solution.py:41
  117.4 11.2 %collective-permute-start.22 = (bf16[128,1792]{1,0:T(8,128)(2,1)S(1)}, bf16[128,1792]{1,0:T(8,128)(2,1)S(1)}, u32[]{:S(2)}, u32[]{:S(2)}) collective-permute-start(bf16[128,1792]{1,0:T(8,128)(2,1)S(1)} %slice_bitcast_fusion.2), channel_id=1, source_target_pairs={{0,2},{1,3},{2,0},{3,1},{4,6},{5,7},{6,4},{7,5},{8,10},{9,11},{10,... | collective-permute-start | bytes 1376264 | tf_op jit(solution)/shard_map/ppermute | solution.py:41
  121.0 7.8 %collective-permute-start.25 = (bf16[2,128,1792]{2,1,0:T(8,128)(2,1)S(1)}, bf16[2,128,1792]{2,1,0:T(8,128)(2,1)S(1)}, u32[]{:S(2)}, u32[]{:S(2)}) collective-permute-start(bf16[2,128,1792]{2,1,0:T(8,128)(2,1)S(1)} %get-tuple-element.87), channel_id=1, source_target_pairs={{0,1},{1,0},{2,3},{3,2},{4,5},{5,4},{6,7},{7,6},{8,9},{9,8},{10,11... | collective-permute-start | bytes 2752520 | tf_op jit(solution)/shard_map/ppermute | solution.py:45
  121.0 14.3 %collective-permute-start.28 = (bf16[128,2048]{1,0:T(8,128)(2,1)S(1)}, bf16[128,2048]{1,0:T(8,128)(2,1)S(1)}, u32[]{:S(2)}, u32[]{:S(2)}) collective-permute-start(bf16[128,2048]{1,0:T(8,128)(2,1)S(1)} %get-tuple-element.92.part_a.refs_9_), channel_id=1, source_target_pairs={{0,16},{16,0},{1,17},{17,1},{2,18},{18,2},{3,19},{19,3},{4,20},{20... | collective-permute-start | bytes 1572872 | tf_op jit(solution)/shard_map/ppermute | solution.py:49
  129.0 10.3 %collective-permute-start.26 = (bf16[128,1792]{1,0:T(8,128)(2,1)S(1)}, bf16[128,1792]{1,0:T(8,128)(2,1)S(1)}, u32[]{:S(2)}, u32[]{:S(2)}) collective-permute-start(bf16[128,1792]{1,0:T(8,128)(2,1)S(1)} %slice_bitcast_fusion), channel_id=1, source_target_pairs={{0,2},{1,3},{2,0},{3,1},{4,6},{5,7},{6,4},{7,5},{8,10},{9,11},{10,... | collective-permute-start | bytes 1376264 | tf_op jit(solution)/shard_map/ppermute | solution.py:41
  135.4 13.5 %collective-permute-start.29 = (bf16[128,2048]{1,0:T(8,128)(2,1)S(1)}, bf16[128,2048]{1,0:T(8,128)(2,1)S(1)}, u32[]{:S(2)}, u32[]{:S(2)}) collective-permute-start(bf16[128,2048]{1,0:T(8,128)(2,1)S(1)} %get-tuple-element.96.part_a.refs_8_), channel_id=1, source_target_pairs={{0,16},{16,0},{1,17},{17,1},{2,18},{18,2},{3,19},{19,3},{4,20},{20... | collective-permute-start | bytes 1572872 | tf_op jit(solution)/shard_map/ppermute | solution.py:49
  139.4 21.9 %collective-permute-start.27 = (bf16[128,1792]{1,0:T(8,128)(2,1)S(1)}, bf16[128,1792]{1,0:T(8,128)(2,1)S(1)}, u32[]{:S(2)}, u32[]{:S(2)}) collective-permute-start(bf16[128,1792]{1,0:T(8,128)(2,1)S(1)} %fusion.1), channel_id=1, source_target_pairs={{0,8},{1,9},{2,10},{3,11},{4,12},{5,13},{6,14},{7,15},{8,0},{9,1},... | collective-permute-start | bytes 1376264 | tf_op jit(solution)/shard_map/ppermute | solution.py:37
  141.2 23.2 %collective-permute-start.32 = (bf16[128,1792]{1,0:T(8,128)(2,1)S(1)}, bf16[128,1792]{1,0:T(8,128)(2,1)S(1)}, u32[]{:S(2)}, u32[]{:S(2)}) collective-permute-start(bf16[128,1792]{1,0:T(8,128)(2,1)S(1)} %fusion.7), channel_id=1, source_target_pairs={{0,2},{1,3},{2,0},{3,1},{4,6},{5,7},{6,4},{7,5},{8,10},{9,11},{10,... | collective-permute-start | bytes 1376264 | tf_op jit(solution)/shard_map/ppermute | solution.py:41
  161.3 3.1 %collective-permute-start.31 = (bf16[1,128,1792]{2,1,0:T(8,128)(2,1)S(1)}, bf16[1,128,1792]{2,1,0:T(8,128)(2,1)S(1)}, u32[]{:S(2)}, u32[]{:S(2)}) collective-permute-start(bf16[1,128,1792]{2,1,0:T(8,128)(2,1)S(1)} %get-tuple-element.100), channel_id=1, source_target_pairs={{0,1},{1,0},{2,3},{3,2},{4,5},{5,4},{6,7},{7,6},{8,9},{9,8},{10,11... | collective-permute-start | bytes 1376264 | tf_op jit(solution)/shard_map/ppermute | solution.py:45
  161.3 20.2 %collective-permute-start.23 = (bf16[128,1792]{1,0:T(8,128)(2,1)S(1)}, bf16[128,1792]{1,0:T(8,128)(2,1)S(1)}, u32[]{:S(2)}, u32[]{:S(2)}) collective-permute-start(bf16[128,1792]{1,0:T(8,128)(2,1)S(1)} %fusion.2), channel_id=1, source_target_pairs={{0,4},{1,5},{2,6},{3,7},{4,0},{5,1},{6,2},{7,3},{8,12},{9,13},{10,... | collective-permute-start | bytes 1376264 | tf_op jit(solution)/shard_map/ppermute | solution.py:37
  164.6 22.5 %collective-permute-start.33 = (bf16[128,1792]{1,0:T(8,128)(2,1)S(1)}, bf16[128,1792]{1,0:T(8,128)(2,1)S(1)}, u32[]{:S(2)}, u32[]{:S(2)}) collective-permute-start(bf16[128,1792]{1,0:T(8,128)(2,1)S(1)} %fusion), channel_id=1, source_target_pairs={{0,12},{1,13},{2,14},{3,15},{4,8},{5,9},{6,10},{7,11},{8,4},{9,5},... | collective-permute-start | bytes 1376264 | tf_op jit(solution)/shard_map/ppermute | solution.py:37
  (13 other events, 136.4 us)

commit v9 on v8

--- a/solution.py
+++ b/solution.py
@@ -357,7 +357,7 @@
     far_send = tie(other_sum, two_sum)
     back_far = swap_x(far_send)
     act_own, keep, send = back(slot_of[3], tie((part_own, dp_own), other_sum), weight_up, slots)
-    far_sum = add(add(keep[0], swap_core(tie(send, hop_two))[0]), back_far)
+    far_sum = add(add(keep[0], swap_core(tie(send, hop_two, hop_near))[0]), back_far)
     hop_far = swap_z(far_sum, 3)
     whole = parts[:3]
     down_grad = weight_grad(

time: 190 us -> 187 us (0.984)
  transfers between devices with their start and end apart: 34 -> 34, of which waited for: 16 -> 17; matrix products, arithmetic and copies ran while one was open for 2% -> 2% of each run, Pallas kernels for 27% -> 27%
where the time goes in v9:
time: 187 us
  waiting for transfers between devices  85.8 us (46%)
  Pallas kernels  51.3 us (27%)
  starting transfers between devices  36.8 us (20%)
  other arithmetic  6.17 us (3%)
  local copies, waits for them, and re-layouts  5.79 us (3%)
    ppermute x8, waiting for transfers between devices, swap_x(): lax.ppermute(value, 'expert', [(i, i ^ NC) for i in range(NZ * NX * NC)])  42.8 us
    pallas_call x4, Pallas kernels, front(): pl.pallas_call(functools.partial(front_kernel, top_count, slots), grid=(w...  22.7 us
    ppermute x5, waiting for transfers between devices, swap_dp(): return lax.ppermute(value, 'dp', [(0, 1), (1, 0)])  16.5 us
    pallas_call x2, Pallas kernels, weight_grad(): pl.pallas_call(kernel, grid=(width // tile,), in_specs=in_specs, out_spec...  16 us
    ppermute x5, starting transfers between devices, along_z(): return lax.ppermute(value, 'expert', perm)  15.5 us
    ppermute x3, waiting for transfers between devices, swap_z(): lax.ppermute(value, 'expert', [(i, i ^ step) for i in range(NZ * NX * NC)])  15.4 us
    pallas_call x5, Pallas kernels, back(): pl.pallas_call(functools.partial(back_kernel, slots, first), grid=(width...  12.6 us
    ppermute x8, starting transfers between devices, swap_x(): lax.ppermute(value, 'expert', [(i, i ^ NC) for i in range(NZ * NX * NC)])  8.37 us
  transfers between devices with their start and end apart: 34, of which 17 were waited for; matrix products, arithmetic and copies ran while one was open for 2% of the time, Pallas kernels for 27%

profile of v9, /device:TPU:8, one launch (start us, length us, event | category | flops | bytes accessed | tf_op | source)
XLA Modules:
  0.0 186.9 jit_solution(14710491819996586278)
XLA Ops:
  5.5 4.6 %collective-permute-start.6 = (bf16[128,3712]{1,0:T(8,128)(2,1)S(1)}, bf16[128,3712]{1,0:T(8,128)(2,1)}, u32[]{:S(2)}, u32[]{:S(2)}) collective-permute-start(bf16[128,3712]{1,0:T(8,128)(2,1)S(1)} %pad_maximum_fusion.refs_0_.refs_4_.refs_8_), channel_id=1, source_target_pairs={{4,8},{5,9},{6,10},{7,11},{8,4},{9,5},{10,6},{11,7},{20,24},{21,25... | collective-permute-start | bytes 2850824 | tf_op jit(solution)/shard_map/ppermute | solution.py:32
  10.2 16.3 %collective-permute-done.1.refs_2_.refs_6_.refs_10_ = bf16[128,3712]{1,0:T(8,128)(2,1)} collective-permute-done((bf16[128,3712]{1,0:T(8,128)(2,1)S(1)}, bf16[128,3712]{1,0:T(8,128)(2,1)}, u32[]{:S(2)}, u32[]{:S(2)}) %collective-permute-start.1) | collective-permute-done | bytes 950304 | tf_op jit(solution)/shard_map/ppermute | solution.py:41
  27.6 3.1 %collective-permute-done.6 = bf16[128,3712]{1,0:T(8,128)(2,1)} collective-permute-done((bf16[128,3712]{1,0:T(8,128)(2,1)S(1)}, bf16[128,3712]{1,0:T(8,128)(2,1)}, u32[]{:S(2)}, u32[]{:S(2)}) %collective-permute-start.6) | collective-permute-done | bytes 950304 | tf_op jit(solution)/shard_map/ppermute | solution.py:32
  31.3 3.6 %collective-permute-start.7 = (bf16[128,3712]{1,0:T(8,128)(2,1)S(1)}, bf16[128,3712]{1,0:T(8,128)(2,1)}, u32[]{:S(2)}, u32[]{:S(2)}) collective-permute-start(bf16[128,3712]{1,0:T(8,128)(2,1)S(1)} %collective-permute-done.5.refs_0_.refs_4_.refs_8_), channel_id=1, source_target_pairs={{4,8},{5,9},{6,10},{7,11},{8,4},{9,5},{10,6},{11,7},{20,24},{21,25... | collective-permute-start | bytes 2850824 | tf_op jit(solution)/shard_map/ppermute | solution.py:32
  34.9 2.2 %collective-permute-start.8 = (bf16[128,3712]{1,0:T(8,128)(2,1)}, bf16[128,3712]{1,0:T(8,128)(2,1)}, u32[]{:S(2)}, u32[]{:S(2)}) collective-permute-start(bf16[128,3712]{1,0:T(8,128)(2,1)} %collective-permute-done.6), channel_id=1, source_target_pairs={{4,0},{5,1},{6,2},{7,3},{8,12},{9,13},{10,14},{11,15},{20,16},{21,... | collective-permute-start | bytes 2850824 | tf_op jit(solution)/shard_map/ppermute | solution.py:32
  37.2 2.0 %copy-done = bf16[1,1792,1024]{2,1,0:T(8,128)(2,1)S(1)} copy-done((bf16[1,1792,1024]{2,1,0:T(8,128)(2,1)S(1)}, bf16[1,1792,1024]{2,1,0:T(8,128)(2,1)}, u32[]{:S(2)}) %copy-start) | copy-done | bytes 3670040
  39.2 2.0 %copy-done.2 = bf16[1,1792,1024]{2,1,0:T(8,128)(2,1)S(1)} copy-done((bf16[1,1792,1024]{2,1,0:T(8,128)(2,1)S(1)}, bf16[1,1792,1024]{2,1,0:T(8,128)(2,1)}, u32[]{:S(2)}) %copy-start.2) | copy-done | bytes 3670040
  41.2 6.0 %shard_map.94 = (bf16[256,1792]{1,0:T(8,128)(2,1)S(1)}, bf16[256,1792]{1,0:T(8,128)(2,1)S(1)}, s32[4,8,128]{2,1,0:T(8,128)S(1)}, bf16[256,2048]{1,0:T(8,128)(2,1)S(1)}) custom-call(s32[1]{0:T(128)} %bitcast.own_ref, s32[16]{0:T(128)S(1)} %copy-done.10, bf16[128,3712]{1,0:T(8,128)(2,1)S(1)} %pad_maximum_fusion.refs_0_.refs_4_.refs_8_, ...), custom_call_target="tpu_custom_call" | custom-call | tf_op jit(solution)/shard_map/pallas_call | solution.py:146
  48.9 3.4 %collective-permute-done.9.refs_2_.refs_6_.refs_10_ = bf16[128,3712]{1,0:T(8,128)(2,1)S(1)} collective-permute-done((bf16[128,3712]{1,0:T(8,128)(2,1)S(1)}, bf16[128,3712]{1,0:T(8,128)(2,1)S(1)}, u32[]{:S(2)}, u32[]{:S(2)}) %collective-permute-start.9) | collective-permute-done | bytes 950304 | tf_op jit(solution)/shard_map/ppermute | solution.py:41
  52.3 2.2 %collective-permute-done.7 = bf16[128,3712]{1,0:T(8,128)(2,1)} collective-permute-done((bf16[128,3712]{1,0:T(8,128)(2,1)S(1)}, bf16[128,3712]{1,0:T(8,128)(2,1)}, u32[]{:S(2)}, u32[]{:S(2)}) %collective-permute-start.7) | collective-permute-done | bytes 950304 | tf_op jit(solution)/shard_map/ppermute | solution.py:32
  57.9 4.6 %collective-permute-start.10 = (bf16[128,3712]{1,0:T(8,128)(2,1)}, bf16[128,3712]{1,0:T(8,128)(2,1)S(1)}, u32[]{:S(2)}, u32[]{:S(2)}) collective-permute-start(bf16[128,3712]{1,0:T(8,128)(2,1)} %collective-permute-done.7), channel_id=1, source_target_pairs={{4,0},{5,1},{6,2},{7,3},{8,12},{9,13},{10,14},{11,15},{20,16},{21,... | collective-permute-start | bytes 2850824 | tf_op jit(solution)/shard_map/ppermute | solution.py:32
  62.6 5.6 %shard_map.96 = (bf16[256,1792]{1,0:T(8,128)(2,1)S(1)}, bf16[256,1792]{1,0:T(8,128)(2,1)S(1)}, s32[4,8,128]{2,1,0:T(8,128)S(1)}, bf16[256,2048]{1,0:T(8,128)(2,1)S(1)}) custom-call(s32[1]{0:T(128)} %bitcast.own_ref, s32[16]{0:T(128)S(1)} %copy-done.10, bf16[128,3712]{1,0:T(8,128)(2,1)S(1)} %collective-permute-done.5.refs_0_.refs_4_.refs_8_, ...), custom_call_target="tpu_custom_call" | custom-call | tf_op jit(solution)/shard_map/pallas_call | solution.py:146
  69.8 7.4 %collective-permute-done.11.refs_2_.refs_6_.refs_10_ = bf16[128,3712]{1,0:T(8,128)(2,1)S(1)} collective-permute-done((bf16[128,3712]{1,0:T(8,128)(2,1)S(1)}, bf16[128,3712]{1,0:T(8,128)(2,1)S(1)}, u32[]{:S(2)}, u32[]{:S(2)}) %collective-permute-start.11) | collective-permute-done | bytes 950304 | tf_op jit(solution)/shard_map/ppermute | solution.py:41
  77.2 2.7 %shard_map.95 = (bf16[256,1024]{1,0:T(8,128)(2,1)S(1)}, bf16[2,128,1792]{2,1,0:T(8,128)(2,1)S(1)}, bf16[2,128,1792]{2,1,0:T(8,128)(2,1)S(1)}) custom-call(s32[4,8,128]{2,1,0:T(8,128)S(1)} %get-tuple-element.61.slot_ref, bf16[256,2048]{1,0:T(8,128)(2,1)S(1)} %get-tuple-element.63.part_a.refs_5_, bf16[256,2048]{1,0:T(8,128)(2,1)S(1)} %collective-permute-done.3.part_b.refs_10_, ...), custom_call_target="tpu_custom_call" | custom-call | tf_op jit(solution)/shard_map/pallas_call | solution.py:201
  82.8 5.5 %shard_map.97 = (bf16[256,1792]{1,0:T(8,128)(2,1)S(1)}, bf16[256,1792]{1,0:T(8,128)(2,1)S(1)}, s32[4,8,128]{2,1,0:T(8,128)S(1)}, bf16[256,2048]{1,0:T(8,128)(2,1)S(1)}) custom-call(s32[1]{0:T(128)} %bitcast.own_ref, s32[16]{0:T(128)S(1)} %copy-done.10, bf16[128,3712]{1,0:T(8,128)(2,1)S(1)} %broadcast_select_fusion.1.refs_0_.refs_4_.refs_8_, ...), custom_call_target="tpu_custom_call" | custom-call | tf_op jit(solution)/shard_map/pallas_call | solution.py:146
  89.9 5.9 %collective-permute-done.17.part_b.refs_11_ = bf16[256,2048]{1,0:T(8,128)(2,1)S(1)} collective-permute-done((bf16[256,2048]{1,0:T(8,128)(2,1)S(1)}, bf16[256,2048]{1,0:T(8,128)(2,1)S(1)}, u32[]{:S(2)}, u32[]{:S(2)}) %collective-permute-start.17) | collective-permute-done | bytes 1048608 | tf_op jit(solution)/shard_map/ppermute | solution.py:49
  95.8 2.7 %shard_map.98 = (bf16[256,1024]{1,0:T(8,128)(2,1)S(1)}, bf16[2,128,1792]{2,1,0:T(8,128)(2,1)S(1)}, bf16[2,128,1792]{2,1,0:T(8,128)(2,1)S(1)}) custom-call(s32[4,8,128]{2,1,0:T(8,128)S(1)} %get-tuple-element.76.slot_ref, bf16[256,2048]{1,0:T(8,128)(2,1)S(1)} %get-tuple-element.77.part_a.refs_6_, ...), custom_call_target="tpu_custom_call" | custom-call | tf_op jit(solution)/shard_map/pallas_call | solution.py:201
  98.9 6.5 %collective-permute-done.14.refs_2_.refs_6_.refs_10_ = bf16[128,3712]{1,0:T(8,128)(2,1)S(1)} collective-permute-done((bf16[128,3712]{1,0:T(8,128)(2,1)S(1)}, bf16[128,3712]{1,0:T(8,128)(2,1)S(1)}, u32[]{:S(2)}, u32[]{:S(2)}) %collective-permute-start.14) | collective-permute-done | bytes 950304 | tf_op jit(solution)/shard_map/ppermute | solution.py:41
  106.5 2.2 %collective-permute-done.21.refs_3_.refs_7_.refs_11_ = bf16[128,3712]{1,0:T(8,128)(2,1)S(1)} collective-permute-done((bf16[128,3712]{1,0:T(8,128)(2,1)S(1)}, bf16[128,3712]{1,0:T(8,128)(2,1)S(1)}, u32[]{:S(2)}, u32[]{:S(2)}) %collective-permute-start.21) | collective-permute-done | bytes 950304 | tf_op jit(solution)/shard_map/ppermute | solution.py:45
  108.7 5.5 %shard_map.99 = (bf16[256,1792]{1,0:T(8,128)(2,1)S(1)}, bf16[256,1792]{1,0:T(8,128)(2,1)S(1)}, s32[4,8,128]{2,1,0:T(8,128)S(1)}, bf16[128,2048]{1,0:T(8,128)(2,1)S(1)}, bf16[128,2048]{1,0:T(8,128)(2,1)S(1)}) custom-call(s32[1]{0:T(128)} %bitcast.own_ref, s32[16]{0:T(128)S(1)} %copy-done.10, ...), custom_call_target="tpu_custom_call" | custom-call | tf_op jit(solution)/shard_map/pallas_call | solution.py:146
  114.2 3.2 %collective-permute-done.18 = bf16[128,1792]{1,0:T(8,128)(2,1)S(1)} collective-permute-done((bf16[128,1792]{1,0:T(8,128)(2,1)S(1)}, bf16[128,1792]{1,0:T(8,128)(2,1)S(1)}, u32[]{:S(2)}, u32[]{:S(2)}) %collective-permute-start.18) | collective-permute-done | bytes 458784 | tf_op jit(solution)/shard_map/ppermute | solution.py:41
  118.3 2.7 %shard_map.100 = (bf16[256,1024]{1,0:T(8,128)(2,1)S(1)}, bf16[2,128,1792]{2,1,0:T(8,128)(2,1)S(1)}, bf16[2,128,1792]{2,1,0:T(8,128)(2,1)S(1)}) custom-call(s32[4,8,128]{2,1,0:T(8,128)S(1)} %get-tuple-element.83.slot_ref, bf16[256,2048]{1,0:T(8,128)(2,1)S(1)} %get-tuple-element.84.part_a.refs_7_, ...), custom_call_target="tpu_custom_call" | custom-call | tf_op jit(solution)/shard_map/pallas_call | solution.py:201
  122.6 6.0 %collective-permute-done.22 = bf16[128,1792]{1,0:T(8,128)(2,1)S(1)} collective-permute-done((bf16[128,1792]{1,0:T(8,128)(2,1)S(1)}, bf16[128,1792]{1,0:T(8,128)(2,1)S(1)}, u32[]{:S(2)}, u32[]{:S(2)}) %collective-permute-start.22) | collective-permute-done | bytes 458784 | tf_op jit(solution)/shard_map/ppermute | solution.py:41
  131.2 4.2 %collective-permute-done.28.part_b.refs_14_ = bf16[128,2048]{1,0:T(8,128)(2,1)S(1)} collective-permute-done((bf16[128,2048]{1,0:T(8,128)(2,1)S(1)}, bf16[128,2048]{1,0:T(8,128)(2,1)S(1)}, u32[]{:S(2)}, u32[]{:S(2)}) %collective-permute-start.28) | collective-permute-done | bytes 524320 | tf_op jit(solution)/shard_map/ppermute | solution.py:49
  136.9 2.3 %shard_map.101 = (bf16[128,1024]{1,0:T(8,128)(2,1)S(1)}, bf16[1,128,1792]{2,1,0:T(8,128)(2,1)S(1)}, bf16[1,128,1792]{2,1,0:T(8,128)(2,1)S(1)}) custom-call(s32[4,8,128]{2,1,0:T(8,128)S(1)} %get-tuple-element.89.slot_ref, bf16[128,2048]{1,0:T(8,128)(2,1)S(1)} %get-tuple-element.92.part_a.refs_9_, ...), custom_call_target="tpu_custom_call" | custom-call | tf_op jit(solution)/shard_map/pallas_call | solution.py:201
  142.4 6.4 %collective-permute-done.29.part_b.refs_13_ = bf16[128,2048]{1,0:T(8,128)(2,1)S(1)} collective-permute-done((bf16[128,2048]{1,0:T(8,128)(2,1)S(1)}, bf16[128,2048]{1,0:T(8,128)(2,1)S(1)}, u32[]{:S(2)}, u32[]{:S(2)}) %collective-permute-start.29) | collective-permute-done | bytes 524320 | tf_op jit(solution)/shard_map/ppermute | solution.py:49
  148.9 2.3 %shard_map.102 = (bf16[128,1024]{1,0:T(8,128)(2,1)S(1)}, bf16[1,128,1792]{2,1,0:T(8,128)(2,1)S(1)}, bf16[1,128,1792]{2,1,0:T(8,128)(2,1)S(1)}) custom-call(s32[4,8,128]{2,1,0:T(8,128)S(1)} %get-tuple-element.89.slot_ref, bf16[128,2048]{1,0:T(8,128)(2,1)S(1)} %get-tuple-element.96.part_a.refs_8_, ...), custom_call_target="tpu_custom_call" | custom-call | tf_op jit(solution)/shard_map/pallas_call | solution.py:201
  151.2 10.2 %collective-permute-done.27 = bf16[128,1792]{1,0:T(8,128)(2,1)S(1)} collective-permute-done((bf16[128,1792]{1,0:T(8,128)(2,1)S(1)}, bf16[128,1792]{1,0:T(8,128)(2,1)S(1)}, u32[]{:S(2)}, u32[]{:S(2)}) %collective-permute-start.27) | collective-permute-done | bytes 458784 | tf_op jit(solution)/shard_map/ppermute | solution.py:37
  161.3 1.8 collective-permute-done.31
  164.5 7.3 %shard_map.103 = bf16[1792,1024]{1,0:T(8,128)(2,1)} custom-call(bf16[256,1792]{1,0:T(8,128)(2,1)S(1)} %copy-done.5, bf16[256,1792]{1,0:T(8,128)(2,1)S(1)} %get-tuple-element.103.refs_1_, bf16[256,1792]{1,0:T(8,128)(2,1)S(1)} %get-tuple-element.104.refs_2_, bf16[256,1792]{1,0:T(8,128)(2,1)S(1)} %get-tuple-element.105.refs_3_.refs_4_, ...), custom_call_target="tpu_custom_call" | custom-call | tf_op jit(solution)/shard_map/pallas_call | solution.py:258
  171.8 8.7 %shard_map.104 = bf16[1792,1024]{1,0:T(8,128)(2,1)} custom-call(bf16[256,1792]{1,0:T(8,128)(2,1)S(1)} %copy-done.7, bf16[256,1792]{1,0:T(8,128)(2,1)S(1)} %copy-done.9, bf16[256,1792]{1,0:T(8,128)(2,1)S(1)} %get-tuple-element.117.refs_2_, bf16[256,1792]{1,0:T(8,128)(2,1)S(1)} %get-tuple-element.118.refs_3_.refs_4_, ...), custom_call_target="tpu_custom_call" | custom-call | tf_op jit(solution)/shard_map/pallas_call | solution.py:258
  180.5 5.2 %collective-permute-done.33 = bf16[128,1792]{1,0:T(8,128)(2,1)S(1)} collective-permute-done((bf16[128,1792]{1,0:T(8,128)(2,1)S(1)}, bf16[128,1792]{1,0:T(8,128)(2,1)S(1)}, u32[]{:S(2)}, u32[]{:S(2)}) %collective-permute-start.33) | collective-permute-done | bytes 458784 | tf_op jit(solution)/shard_map/ppermute | solution.py:37
  (86 shorter events, 31.3 us)
Async XLA Ops:
  3.5 23.0 %collective-permute-start.1 = (bf16[128,3712]{1,0:T(8,128)(2,1)S(1)}, bf16[128,3712]{1,0:T(8,128)(2,1)}, u32[]{:S(2)}, u32[]{:S(2)}) collective-permute-start(bf16[128,3712]{1,0:T(8,128)(2,1)S(1)} %pad_maximum_fusion.refs_0_.refs_4_.refs_8_), channel_id=1, source_target_pairs={{0,2},{1,3},{2,0},{3,1},{4,6},{5,7},{6,4},{7,5},{8,10},{9,11},{10,... | collective-permute-start | bytes 2850824 | tf_op jit(solution)/shard_map/ppermute | solution.py:41
  5.1 22.5 %collective-permute-start.5 = (bf16[128,3712]{1,0:T(8,128)(2,1)S(1)}, bf16[128,3712]{1,0:T(8,128)(2,1)S(1)}, u32[]{:S(2)}, u32[]{:S(2)}) collective-permute-start(bf16[128,3712]{1,0:T(8,128)(2,1)S(1)} %pad_maximum_fusion.refs_0_.refs_4_.refs_8_), channel_id=1, source_target_pairs={{0,4},{1,5},{2,6},{3,7},{4,0},{5,1},{6,2},{7,3},{8,12},{9,13},{10,... | collective-permute-start | bytes 2850824 | tf_op jit(solution)/shard_map/ppermute | solution.py:32
  5.5 25.2 %collective-permute-start.6 = (bf16[128,3712]{1,0:T(8,128)(2,1)S(1)}, bf16[128,3712]{1,0:T(8,128)(2,1)}, u32[]{:S(2)}, u32[]{:S(2)}) collective-permute-start(bf16[128,3712]{1,0:T(8,128)(2,1)S(1)} %pad_maximum_fusion.refs_0_.refs_4_.refs_8_), channel_id=1, source_target_pairs={{4,8},{5,9},{6,10},{7,11},{8,4},{9,5},{10,6},{11,7},{20,24},{21,25... | collective-permute-start | bytes 2850824 | tf_op jit(solution)/shard_map/ppermute | solution.py:32
  10.2 27.0 %collective-permute-start = (bf16[128,3712]{1,0:T(8,128)(2,1)S(1)}, bf16[128,3712]{1,0:T(8,128)(2,1)}, u32[]{:S(2)}, u32[]{:S(2)}) collective-permute-start(bf16[128,3712]{1,0:T(8,128)(2,1)S(1)} %pad_maximum_fusion.refs_0_.refs_4_.refs_8_), channel_id=1, source_target_pairs={{0,1},{1,0},{2,3},{3,2},{4,5},{5,4},{6,7},{7,6},{8,9},{9,8},{10,11... | collective-permute-start | bytes 2850824 | tf_op jit(solution)/shard_map/ppermute | solution.py:45
  26.5 10.6 %collective-permute-start.2 = (bf16[128,3712]{1,0:T(8,128)(2,1)}, bf16[128,3712]{1,0:T(8,128)(2,1)}, u32[]{:S(2)}, u32[]{:S(2)}) collective-permute-start(bf16[128,3712]{1,0:T(8,128)(2,1)} %collective-permute-done.1.refs_2_.refs_6_.refs_10_), channel_id=1, source_target_pairs={{0,1},{1,0},{2,3},{3,2},{4,5},{5,4},{6,7},{7,6},{8,9},{9,8},{10,11... | collective-permute-start | bytes 2850824 | tf_op jit(solution)/shard_map/ppermute | solution.py:45
  30.7 21.6 %collective-permute-start.9 = (bf16[128,3712]{1,0:T(8,128)(2,1)S(1)}, bf16[128,3712]{1,0:T(8,128)(2,1)S(1)}, u32[]{:S(2)}, u32[]{:S(2)}) collective-permute-start(bf16[128,3712]{1,0:T(8,128)(2,1)S(1)} %collective-permute-done.5.refs_0_.refs_4_.refs_8_), channel_id=1, source_target_pairs={{0,2},{1,3},{2,0},{3,1},{4,6},{5,7},{6,4},{7,5},{8,10},{9,11},{10,... | collective-permute-start | bytes 2850824 | tf_op jit(solution)/shard_map/ppermute | solution.py:41
  31.3 23.3 %collective-permute-start.7 = (bf16[128,3712]{1,0:T(8,128)(2,1)S(1)}, bf16[128,3712]{1,0:T(8,128)(2,1)}, u32[]{:S(2)}, u32[]{:S(2)}) collective-permute-start(bf16[128,3712]{1,0:T(8,128)(2,1)S(1)} %collective-permute-done.5.refs_0_.refs_4_.refs_8_), channel_id=1, source_target_pairs={{4,8},{5,9},{6,10},{7,11},{8,4},{9,5},{10,6},{11,7},{20,24},{21,25... | collective-permute-start | bytes 2850824 | tf_op jit(solution)/shard_map/ppermute | solution.py:32
  34.9 20.1 %collective-permute-start.8 = (bf16[128,3712]{1,0:T(8,128)(2,1)}, bf16[128,3712]{1,0:T(8,128)(2,1)}, u32[]{:S(2)}, u32[]{:S(2)}) collective-permute-start(bf16[128,3712]{1,0:T(8,128)(2,1)} %collective-permute-done.6), channel_id=1, source_target_pairs={{4,0},{5,1},{6,2},{7,3},{8,12},{9,13},{10,14},{11,15},{20,16},{21,... | collective-permute-start | bytes 2850824 | tf_op jit(solution)/shard_map/ppermute | solution.py:32
  37.1 25.4 %collective-permute-start.12 = (bf16[128,3712]{1,0:T(8,128)(2,1)S(1)}, bf16[128,3712]{1,0:T(8,128)(2,1)S(1)}, u32[]{:S(2)}, u32[]{:S(2)}) collective-permute-start(bf16[128,3712]{1,0:T(8,128)(2,1)S(1)} %collective-permute-done.5.refs_0_.refs_4_.refs_8_), channel_id=1, source_target_pairs={{0,1},{1,0},{2,3},{3,2},{4,5},{5,4},{6,7},{7,6},{8,9},{9,8},{10,11... | collective-permute-start | bytes 2850824 | tf_op jit(solution)/shard_map/ppermute | solution.py:45
  47.3 29.9 %collective-permute-start.3 = (bf16[256,2048]{1,0:T(8,128)(2,1)S(1)}, bf16[256,2048]{1,0:T(8,128)(2,1)S(1)}, u32[]{:S(2)}, u32[]{:S(2)}) collective-permute-start(bf16[256,2048]{1,0:T(8,128)(2,1)S(1)} %get-tuple-element.63.part_a.refs_5_), channel_id=1, source_target_pairs={{0,16},{16,0},{1,17},{17,1},{2,18},{18,2},{3,19},{19,3},{4,20},{20... | collective-permute-start | bytes 3145736 | tf_op jit(solution)/shard_map/ppermute | solution.py:49
  52.3 10.2 %collective-permute-start.13 = (bf16[128,3712]{1,0:T(8,128)(2,1)S(1)}, bf16[128,3712]{1,0:T(8,128)(2,1)S(1)}, u32[]{:S(2)}, u32[]{:S(2)}) collective-permute-start(bf16[128,3712]{1,0:T(8,128)(2,1)S(1)} %collective-permute-done.9.refs_2_.refs_6_.refs_10_), channel_id=1, source_target_pairs={{0,1},{1,0},{2,3},{3,2},{4,5},{5,4},{6,7},{7,6},{8,9},{9,8},{10,11... | collective-permute-start | bytes 2850824 | tf_op jit(solution)/shard_map/ppermute | solution.py:45
  56.4 20.8 %collective-permute-start.11 = (bf16[128,3712]{1,0:T(8,128)(2,1)S(1)}, bf16[128,3712]{1,0:T(8,128)(2,1)S(1)}, u32[]{:S(2)}, u32[]{:S(2)}) collective-permute-start(bf16[128,3712]{1,0:T(8,128)(2,1)S(1)} %broadcast_select_fusion.1.refs_0_.refs_4_.refs_8_), channel_id=1, source_target_pairs={{0,2},{1,3},{2,0},{3,1},{4,6},{5,7},{6,4},{7,5},{8,10},{9,11},{10,... | collective-permute-start | bytes 2850824 | tf_op jit(solution)/shard_map/ppermute | solution.py:41
  57.9 22.6 %collective-permute-start.10 = (bf16[128,3712]{1,0:T(8,128)(2,1)}, bf16[128,3712]{1,0:T(8,128)(2,1)S(1)}, u32[]{:S(2)}, u32[]{:S(2)}) collective-permute-start(bf16[128,3712]{1,0:T(8,128)(2,1)} %collective-permute-done.7), channel_id=1, source_target_pairs={{4,0},{5,1},{6,2},{7,3},{8,12},{9,13},{10,14},{11,15},{20,16},{21,... | collective-permute-start | bytes 2850824 | tf_op jit(solution)/shard_map/ppermute | solution.py:32
  68.2 27.6 %collective-permute-start.17 = (bf16[256,2048]{1,0:T(8,128)(2,1)S(1)}, bf16[256,2048]{1,0:T(8,128)(2,1)S(1)}, u32[]{:S(2)}, u32[]{:S(2)}) collective-permute-start(bf16[256,2048]{1,0:T(8,128)(2,1)S(1)} %get-tuple-element.77.part_a.refs_6_), channel_id=1, source_target_pairs={{0,16},{16,0},{1,17},{17,1},{2,18},{18,2},{3,19},{19,3},{4,20},{20... | collective-permute-start | bytes 3145736 | tf_op jit(solution)/shard_map/ppermute | solution.py:49
  69.8 12.1 %collective-permute-start.15 = (bf16[128,3712]{1,0:T(8,128)(2,1)S(1)}, bf16[128,3712]{1,0:T(8,128)(2,1)S(1)}, u32[]{:S(2)}, u32[]{:S(2)}) collective-permute-start(bf16[128,3712]{1,0:T(8,128)(2,1)S(1)} %broadcast_select_fusion.1.refs_0_.refs_4_.refs_8_), channel_id=1, source_target_pairs={{0,1},{1,0},{2,3},{3,2},{4,5},{5,4},{6,7},{7,6},{8,9},{9,8},{10,11... | collective-permute-start | bytes 2850824 | tf_op jit(solution)/shard_map/ppermute | solution.py:45
  77.2 5.6 %collective-permute-start.16 = (bf16[128,3712]{1,0:T(8,128)(2,1)S(1)}, bf16[128,3712]{1,0:T(8,128)(2,1)S(1)}, u32[]{:S(2)}, u32[]{:S(2)}) collective-permute-start(bf16[128,3712]{1,0:T(8,128)(2,1)S(1)} %collective-permute-done.11.refs_2_.refs_6_.refs_10_), channel_id=1, source_target_pairs={{0,1},{1,0},{2,3},{3,2},{4,5},{5,4},{6,7},{7,6},{8,9},{9,8},{10,11... | collective-permute-start | bytes 2850824 | tf_op jit(solution)/shard_map/ppermute | solution.py:45
  79.9 18.6 %collective-permute-start.4 = (bf16[2,128,1792]{2,1,0:T(8,128)(2,1)S(1)}, bf16[2,128,1792]{2,1,0:T(8,128)(2,1)S(1)}, u32[]{:S(2)}, u32[]{:S(2)}) collective-permute-start(bf16[2,128,1792]{2,1,0:T(8,128)(2,1)S(1)} %get-tuple-element.66), channel_id=1, source_target_pairs={{0,1},{1,0},{2,3},{3,2},{4,5},{5,4},{6,7},{7,6},{8,9},{9,8},{10,11... | collective-permute-start | bytes 2752520 | tf_op jit(solution)/shard_map/ppermute | solution.py:45
  81.8 24.7 %collective-permute-start.20 = (bf16[128,3712]{1,0:T(8,128)(2,1)S(1)}, bf16[128,3712]{1,0:T(8,128)(2,1)S(1)}, u32[]{:S(2)}, u32[]{:S(2)}) collective-permute-start(bf16[128,3712]{1,0:T(8,128)(2,1)S(1)} %broadcast_select_fusion.refs_0_.refs_4_.refs_8_), channel_id=1, source_target_pairs={{0,1},{1,0},{2,3},{3,2},{4,5},{5,4},{6,7},{7,6},{8,9},{9,8},{10,11... | collective-permute-start | bytes 2850824 | tf_op jit(solution)/shard_map/ppermute | solution.py:45
  81.9 23.5 %collective-permute-start.14 = (bf16[128,3712]{1,0:T(8,128)(2,1)S(1)}, bf16[128,3712]{1,0:T(8,128)(2,1)S(1)}, u32[]{:S(2)}, u32[]{:S(2)}) collective-permute-start(bf16[128,3712]{1,0:T(8,128)(2,1)S(1)} %broadcast_select_fusion.refs_0_.refs_4_.refs_8_), channel_id=1, source_target_pairs={{0,2},{1,3},{2,0},{3,1},{4,6},{5,7},{6,4},{7,5},{8,10},{9,11},{10,... | collective-permute-start | bytes 2850824 | tf_op jit(solution)/shard_map/ppermute | solution.py:41
  88.3 29.9 %collective-permute-start.24 = (bf16[256,2048]{1,0:T(8,128)(2,1)S(1)}, bf16[256,2048]{1,0:T(8,128)(2,1)S(1)}, u32[]{:S(2)}, u32[]{:S(2)}) collective-permute-start(bf16[256,2048]{1,0:T(8,128)(2,1)S(1)} %get-tuple-element.84.part_a.refs_7_), channel_id=1, source_target_pairs={{0,16},{16,0},{1,17},{17,1},{2,18},{18,2},{3,19},{19,3},{4,20},{20... | collective-permute-start | bytes 3145736 | tf_op jit(solution)/shard_map/ppermute | solution.py:49
  98.5 7.7 %collective-permute-start.19 = (bf16[2,128,1792]{2,1,0:T(8,128)(2,1)S(1)}, bf16[2,128,1792]{2,1,0:T(8,128)(2,1)S(1)}, u32[]{:S(2)}, u32[]{:S(2)}) collective-permute-start(bf16[2,128,1792]{2,1,0:T(8,128)(2,1)S(1)} %get-tuple-element.80), channel_id=1, source_target_pairs={{0,1},{1,0},{2,3},{3,2},{4,5},{5,4},{6,7},{7,6},{8,9},{9,8},{10,11... | collective-permute-start | bytes 2752520 | tf_op jit(solution)/shard_map/ppermute | solution.py:45
  105.4 12.1 %collective-permute-start.18 = (bf16[128,1792]{1,0:T(8,128)(2,1)S(1)}, bf16[128,1792]{1,0:T(8,128)(2,1)S(1)}, u32[]{:S(2)}, u32[]{:S(2)}) collective-permute-start(bf16[128,1792]{1,0:T(8,128)(2,1)S(1)} %slice_bitcast_fusion.4), channel_id=1, source_target_pairs={{0,2},{1,3},{2,0},{3,1},{4,6},{5,7},{6,4},{7,5},{8,10},{9,11},{10,... | collective-permute-start | bytes 1376264 | tf_op jit(solution)/shard_map/ppermute | solution.py:41
  106.2 2.5 %collective-permute-start.21 = (bf16[128,3712]{1,0:T(8,128)(2,1)S(1)}, bf16[128,3712]{1,0:T(8,128)(2,1)S(1)}, u32[]{:S(2)}, u32[]{:S(2)}) collective-permute-start(bf16[128,3712]{1,0:T(8,128)(2,1)S(1)} %collective-permute-done.14.refs_2_.refs_6_.refs_10_), channel_id=1, source_target_pairs={{0,1},{1,0},{2,3},{3,2},{4,5},{5,4},{6,7},{7,6},{8,9},{9,8},{10,11... | collective-permute-start | bytes 2850824 | tf_op jit(solution)/shard_map/ppermute | solution.py:45
  117.4 11.2 %collective-permute-start.22 = (bf16[128,1792]{1,0:T(8,128)(2,1)S(1)}, bf16[128,1792]{1,0:T(8,128)(2,1)S(1)}, u32[]{:S(2)}, u32[]{:S(2)}) collective-permute-start(bf16[128,1792]{1,0:T(8,128)(2,1)S(1)} %slice_bitcast_fusion.2), channel_id=1, source_target_pairs={{0,2},{1,3},{2,0},{3,1},{4,6},{5,7},{6,4},{7,5},{8,10},{9,11},{10,... | collective-permute-start | bytes 1376264 | tf_op jit(solution)/shard_map/ppermute | solution.py:41
  121.0 7.8 %collective-permute-start.25 = (bf16[2,128,1792]{2,1,0:T(8,128)(2,1)S(1)}, bf16[2,128,1792]{2,1,0:T(8,128)(2,1)S(1)}, u32[]{:S(2)}, u32[]{:S(2)}) collective-permute-start(bf16[2,128,1792]{2,1,0:T(8,128)(2,1)S(1)} %get-tuple-element.87), channel_id=1, source_target_pairs={{0,1},{1,0},{2,3},{3,2},{4,5},{5,4},{6,7},{7,6},{8,9},{9,8},{10,11... | collective-permute-start | bytes 2752520 | tf_op jit(solution)/shard_map/ppermute | solution.py:45
  121.0 14.3 %collective-permute-start.28 = (bf16[128,2048]{1,0:T(8,128)(2,1)S(1)}, bf16[128,2048]{1,0:T(8,128)(2,1)S(1)}, u32[]{:S(2)}, u32[]{:S(2)}) collective-permute-start(bf16[128,2048]{1,0:T(8,128)(2,1)S(1)} %get-tuple-element.92.part_a.refs_9_), channel_id=1, source_target_pairs={{0,16},{16,0},{1,17},{17,1},{2,18},{18,2},{3,19},{19,3},{4,20},{20... | collective-permute-start | bytes 1572872 | tf_op jit(solution)/shard_map/ppermute | solution.py:49
  129.0 10.3 %collective-permute-start.26 = (bf16[128,1792]{1,0:T(8,128)(2,1)S(1)}, bf16[128,1792]{1,0:T(8,128)(2,1)S(1)}, u32[]{:S(2)}, u32[]{:S(2)}) collective-permute-start(bf16[128,1792]{1,0:T(8,128)(2,1)S(1)} %slice_bitcast_fusion), channel_id=1, source_target_pairs={{0,2},{1,3},{2,0},{3,1},{4,6},{5,7},{6,4},{7,5},{8,10},{9,11},{10,... | collective-permute-start | bytes 1376264 | tf_op jit(solution)/shard_map/ppermute | solution.py:41
  129.9 21.3 %collective-permute-start.23 = (bf16[128,1792]{1,0:T(8,128)(2,1)S(1)}, bf16[128,1792]{1,0:T(8,128)(2,1)S(1)}, u32[]{:S(2)}, u32[]{:S(2)}) collective-permute-start(bf16[128,1792]{1,0:T(8,128)(2,1)S(1)} %fusion.2), channel_id=1, source_target_pairs={{0,4},{1,5},{2,6},{3,7},{4,0},{5,1},{6,2},{7,3},{8,12},{9,13},{10,... | collective-permute-start | bytes 1376264 | tf_op jit(solution)/shard_map/ppermute | solution.py:37
  135.4 13.5 %collective-permute-start.29 = (bf16[128,2048]{1,0:T(8,128)(2,1)S(1)}, bf16[128,2048]{1,0:T(8,128)(2,1)S(1)}, u32[]{:S(2)}, u32[]{:S(2)}) collective-permute-start(bf16[128,2048]{1,0:T(8,128)(2,1)S(1)} %get-tuple-element.96.part_a.refs_8_), channel_id=1, source_target_pairs={{0,16},{16,0},{1,17},{17,1},{2,18},{18,2},{3,19},{19,3},{4,20},{20... | collective-permute-start | bytes 1572872 | tf_op jit(solution)/shard_map/ppermute | solution.py:49
  139.4 21.9 %collective-permute-start.27 = (bf16[128,1792]{1,0:T(8,128)(2,1)S(1)}, bf16[128,1792]{1,0:T(8,128)(2,1)S(1)}, u32[]{:S(2)}, u32[]{:S(2)}) collective-permute-start(bf16[128,1792]{1,0:T(8,128)(2,1)S(1)} %fusion.1), channel_id=1, source_target_pairs={{0,8},{1,9},{2,10},{3,11},{4,12},{5,13},{6,14},{7,15},{8,0},{9,1},... | collective-permute-start | bytes 1376264 | tf_op jit(solution)/shard_map/ppermute | solution.py:37
  141.2 20.2 %collective-permute-start.32 = (bf16[128,1792]{1,0:T(8,128)(2,1)S(1)}, bf16[128,1792]{1,0:T(8,128)(2,1)S(1)}, u32[]{:S(2)}, u32[]{:S(2)}) collective-permute-start(bf16[128,1792]{1,0:T(8,128)(2,1)S(1)} %fusion.7), channel_id=1, source_target_pairs={{0,2},{1,3},{2,0},{3,1},{4,6},{5,7},{6,4},{7,5},{8,10},{9,11},{10,... | collective-permute-start | bytes 1376264 | tf_op jit(solution)/shard_map/ppermute | solution.py:41
  163.3 22.5 %collective-permute-start.33 = (bf16[128,1792]{1,0:T(8,128)(2,1)S(1)}, bf16[128,1792]{1,0:T(8,128)(2,1)S(1)}, u32[]{:S(2)}, u32[]{:S(2)}) collective-permute-start(bf16[128,1792]{1,0:T(8,128)(2,1)S(1)} %fusion), channel_id=1, source_target_pairs={{0,12},{1,13},{2,14},{3,15},{4,8},{5,9},{6,10},{7,11},{8,4},{9,5},... | collective-permute-start | bytes 1376264 | tf_op jit(solution)/shard_map/ppermute | solution.py:37
  (13 other events, 134.7 us)
